TPU v7x, 128 devices: a whole 4x4x4 slice. The times are simulated.
128 devices in a mesh: dp: 4 (over z), tensor: 32 (over x, y, core).
Axes of the slice: x: 4, y: 4, z: 4, core: 2. Of those that a mesh axis runs over, the one named last changes fastest.
Arguments:
- tokens: bfloat16 [2048, 8192], P(('dp', 'tensor')), parts along dimension 0, may hold values from -6 to 6
- gate_weight: bfloat16 [8192, 14336], P(None, 'tensor'), may hold values from -0.0625 to 0.0625
- up_weight: bfloat16 [8192, 14336], P(None, 'tensor'), may hold values from -0.0625 to 0.0625
- down_weight: bfloat16 [14336, 8192], P('tensor'), may hold values from -0.046875 to 0.046875
- block_mixing_matrix: bfloat16 [448, 448], replicated, may hold values from -0.25 to 0.25
Outputs:
- mixed: bfloat16 [2048, 8192], P(('dp', 'tensor')), parts along dimension 0
There are 4 independent parts, one for each index of `dp`. A program takes and returns all parts, laid end to end along the dimension named above; an argument that names none is the same for every part. Nothing has to cross between parts.
All inputs are finite; a program needn't handle non-finite values.
Results may differ from a plain program's by a relative error of at most 0.025.
Values may be sent and summed in bfloat16 or wider, within the bound.
No kernel may reach another device: no remote copies, remote signals or barrier semaphores. Data moves between devices by JAX's collectives and lax.ppermute only.
A program may use at most 128 MiB of HBM per device.

v0:
```python
import math

import jax
import jax.numpy as jnp
from jax import lax
from jax.sharding import PartitionSpec as P


def shortened(x):

    def short(part):
        return part.astype(jnp.bfloat16) if part.dtype == jnp.float32 else part

    return jax.tree.map(short, x)


def walsh_table(block_members):
    indices = jnp.arange(block_members, dtype=jnp.int32)
    common = jnp.bitwise_and(indices[:, None], indices[None, :])
    parity = jnp.zeros((block_members, block_members), jnp.int32)
    for position in range(block_members.bit_length() - 1):
        parity = jnp.bitwise_xor(parity, jnp.bitwise_and(jnp.right_shift(common, position), 1))
    return (1.0 - 2.0 * parity.astype(jnp.float32)) / math.sqrt(block_members)


def body(tokens, gate_weight, up_weight, down_weight, block_mixing_matrix):
    block_members = lax.axis_size("tensor")
    piece = lax.all_gather(tokens, "tensor", axis=0, tiled=True)
    gate_part = jnp.dot(piece, gate_weight, preferred_element_type=jnp.float32)
    up_part = jnp.dot(piece, up_weight, preferred_element_type=jnp.float32)
    hidden = (jax.nn.silu(gate_part) * up_part).astype(jnp.bfloat16)
    local_block_values = jnp.dot(hidden, block_mixing_matrix, preferred_element_type=jnp.float32)
    sign_table = walsh_table(block_members)
    spread = jnp.einsum(
        "kb,btm->ktm",
        sign_table,
        lax.all_to_all(
            local_block_values[None].astype(jnp.bfloat16),
            "tensor",
            split_axis=1,
            concat_axis=0,
            tiled=True,
        ).astype(jnp.float32),
        precision=lax.Precision.HIGHEST,
    )
    rotated_hidden = lax.all_to_all(
        shortened(spread), "tensor", split_axis=0, concat_axis=1, tiled=True
    ).astype(spread.dtype)[0]
    rotated_hidden = rotated_hidden.astype(jnp.bfloat16)
    return lax.psum_scatter(
        jnp.dot(rotated_hidden, down_weight, preferred_element_type=jnp.float32).astype(
            jnp.bfloat16
        ),
        "tensor",
        scatter_dimension=0,
        tiled=True,
    )


def solution(mesh):
    in_specs = (
        P(("dp", "tensor"), None),
        P(None, "tensor"),
        P(None, "tensor"),
        P("tensor", None),
        P(),
    )
    out_specs = P(("dp", "tensor"), None)
    return jax.shard_map(body, mesh=mesh, in_specs=in_specs, out_specs=out_specs, check_vma=False)
```

profile of v0, /device:TPU:0, one launch (start us, length us, event | category | flops | bytes accessed | tf_op | source)
XLA Modules:
  0.0 229.7 jit_solution(13208000654466066742)
XLA Ops:
  6.5 0.0 copy-start
  6.5 0.0 all-gather.2.cloned.1.call-start
  6.5 0.7 all-gather.2.cloned.1.call-update
  7.3 0.0 reduce-scatter.2.cloned.1.call-start
  7.3 57.6 %all-gather.2.cloned.1.call-done = bf16[512,8192]{1,0:T(8,128)(2,1)} async-done(((bf16[16,8192]{1,0:T(8,128)(2,1)}), bf16[512,8192]{1,0:T(8,128)(2,1)}) %all-gather.2.cloned.1.call-update) | async-done | bytes 8388624 | tf_op jit(solution)/shard_map/all_gather | solution.py:28
  64.9 8.6 %fusion.50 = f32[512,448]{0,1:T(8,128)S(1)} fusion(bf16[512,8192]{1,0:T(8,128)(2,1)} %all-gather.2.cloned.1.call-done, bf16[8192,448]{0,1:T(8,128)(2,1)} %param.6), kind=kOutput, calls=%fused_computation.53 | convolution fusion | flops 3758096384 | bytes 16646144 | tf_op jit(solution)/shard_map/dot_general | solution.py:29
  73.5 0.0 copy-done
  73.5 9.8 %fusion.3 = bf16[1,512,448]{1,2,0:T(8,128)(2,1)S(1)} fusion(bf16[448,448]{1,0:T(8,128)(2,1)S(1)} %copy-done, bf16[512,8192]{1,0:T(8,128)(2,1)} %all-gather.2.cloned.1.call-done, bf16[8192,448]{0,1:T(8,128)(2,1)} %param.7, f32[512,448]{0,1:T(8,128)S(1)} %fusion.50), kind=kOutput, calls=%fused_computation.6 | convolution fusion | flops 3965222912 | bytes 17506304 | tf_op jit(solution)/shard_map/dot_general | solution.py:32
  83.3 0.9 copy.10
  84.2 0.5 broadcast.11
  84.8 4.0 %reduce = bf16[512,448]{1,0:T(8,128)(2,1)S(1)} reduce(bf16[512,1,448]{2,1,0:T(2,128)(2,1)S(1)} %bitcast.16, bf16[]{:T(256)} %broadcast.11), dimensions={1}, to_apply=%bitcast.7.reduce_sub_computation | reduce | bytes 917506
  88.8 0.6 reshape.12
  89.3 15.8 %all_to_all.24 = bf16[32,2,3584]{2,1,0:T(2,128)(2,1)S(1)} all-to-all(bf16[32,2,3584]{2,1,0:T(2,128)(2,1)S(1)} %reshape.12), channel_id=1, replica_groups=mesh['dp'=4,'tensor'=32] {'tensor'}, dimensions={0} | all-to-all | bytes 917504 | tf_op jit(solution)/shard_map/all_to_all | solution.py:37
  105.2 0.7 reshape.13
  105.9 0.1 copy.13
  106.0 0.8 convolution_convert_fusion.1
  106.8 0.3 copy.12
  107.1 15.0 %all_to_all.25 = bf16[32,16,448]{2,1,0:T(8,128)(2,1)S(1)} all-to-all(bf16[32,16,448]{2,1,0:T(8,128)(2,1)S(1)} %copy.12), channel_id=1, replica_groups=mesh['dp'=4,'tensor'=32] {'tensor'}, dimensions={0} | all-to-all | bytes 917504 | tf_op jit(solution)/shard_map/all_to_all | solution.py:46
  122.1 9.7 %convolution_convert_fusion = bf16[512,8192]{1,0:T(8,128)(2,1)} fusion(bf16[512,448]{1,0:T(8,128)(2,1)S(1)} %bitcast.19, bf16[448,8192]{1,0:T(8,128)(2,1)} %param.8), kind=kOutput, calls=%fused_computation | convolution fusion | flops 3762290688 | bytes 16187392 | tf_op jit(solution)/shard_map/dot_general | solution.py:51
  131.9 0.0 reduce-scatter.2.cloned.1.call-update
  131.9 91.0 %reduce-scatter.2.cloned.1.call-done = bf16[16,8192]{1,0:T(8,128)(2,1)} async-done(((bf16[512,8192]{1,0:T(8,128)(2,1)}), bf16[16,8192]{1,0:T(8,128)(2,1)}) %reduce-scatter.2.cloned.1.call-update) | async-done | bytes 262160 | tf_op jit(solution)/shard_map/reduce_scatter | solution.py:50
Async XLA Ops:
  6.5 67.0 %copy-start = (bf16[448,448]{1,0:T(8,128)(2,1)S(1)}, bf16[448,448]{1,0:T(8,128)(2,1)}, u32[]{:S(2)}) copy-start(bf16[448,448]{1,0:T(8,128)(2,1)} %param.9) | copy-start | bytes 1204228
  6.5 58.3 %all-gather.2.cloned.1.call-start = ((), (), s32[]{:S(2)}) async-start(), calls=%async_computation.3 | async-start | bytes 8650752 | tf_op jit(solution)/shard_map/all_gather | solution.py:28
  7.3 215.6 %reduce-scatter.2.cloned.1.call-start = ((), (), s32[]{:S(2)}) async-start(), calls=%async_computation.4 | async-start | bytes 8650752 | tf_op jit(solution)/shard_map/reduce_scatter | solution.py:50
Sparse Core Ops, SparseCore 0:
  9.6 55.2 all-gather.1
  132.0 90.8 reduce-scatter.1
where the time goes:
time: 230 us
  waiting for transfers between devices  149 us (65%)
  blocking collectives  30.8 us (13%)
  matrix products  29 us (13%)
  between operations  13.5 us (6%)
  other arithmetic  3.99 us (2%)
  local copies, waits for them, and re-layouts  3.12 us (1%)
    reduce_scatter x1, waiting for transfers between devices, body(): lax.psum_scatter(jnp.dot(rotated_hidden, down_weight, preferred_element_t...  91 us
    all_gather x1, waiting for transfers between devices, body(): piece = lax.all_gather(tokens, 'tensor', axis=0, tiled=True)  57.6 us
    all_to_all x1, blocking collectives, body(): lax.all_to_all(local_block_values[None].astype(jnp.bfloat16), 'tensor', s...  15.8 us
    all_to_all x1, blocking collectives, body(): lax.all_to_all(shortened(spread), 'tensor', split_axis=0, concat_axis=1,...  15 us
    dot_general x1, matrix products, body(): jnp.dot(hidden, block_mixing_matrix, preferred_element_type=jnp.float32)  9.81 us
    dot_general x1, matrix products, body(): jnp.dot(rotated_hidden, down_weight, preferred_element_type=jnp.float32)  9.75 us
    dot_general x1, matrix products, body(): gate_part = jnp.dot(piece, gate_weight, preferred_element_type=jnp.float32)  8.63 us
  transfers between devices with their start and end apart: 2, of which 2 were waited for; matrix products, arithmetic and copies ran while one was open for 0% of the time, Pallas kernels for 0%

commit v1 on v0

v1 whole, which is shorter than its diff:
```python
import math

import jax
import jax.numpy as jnp
from jax import lax
from jax.sharding import PartitionSpec as P

RING = 4
PLACES = [(x, y, c) for x in range(RING) for y in range(RING) for c in range(2)]


def place(x, y, c):
    return (x % RING) * RING * 2 + (y % RING) * 2 + c


def along_first(d):
    return [
        (place(x, y, c), place(x + d, y, c) if c == 0 else place(x, y + d, c))
        for x, y, c in PLACES
    ]


def along_second(d):
    return [
        (place(x, y, c), place(x + d, y, c) if c == 1 else place(x, y + d, c))
        for x, y, c in PLACES
    ]


SIBLING = [(place(x, y, c), place(x, y, 1 - c)) for x, y, c in PLACES]


def send(value, pairs):
    return lax.ppermute(value, "tensor", pairs)


def dot(a, b):
    return jnp.dot(a, b, preferred_element_type=jnp.float32)


def sign(row, column):
    common = jnp.bitwise_and(row, column)
    parity = jnp.bitwise_xor(common, jnp.right_shift(common, 1)) & 1
    return 1.0 - 2.0 * parity.astype(jnp.float32)


def rotate(value, along, position, axis, scale):
    came = {0: value, 1: send(value, along(-1)), 2: send(value, along(2)), 3: send(value, along(1))}
    total = 0.0
    for step, part in came.items():
        factor = sign(position, (position + step) % RING) * scale
        total = total + factor * jnp.roll(part, step, axis=axis).astype(jnp.float32)
    return total.astype(jnp.bfloat16)


def body(tokens, gate_weight, up_weight, down_weight, mixing):
    rows, width = tokens.shape
    units = gate_weight.shape[1]
    index = lax.axis_index("tensor")
    core = index % 2
    x, y = index // (2 * RING), (index // 2) % RING
    first = jnp.where(core == 0, x, y)
    second = jnp.where(core == 0, y, x)

    gate_other = send(gate_weight, SIBLING)
    up_other = send(up_weight, SIBLING)
    down_other = send(down_weight, SIBLING)

    chunks = 2
    span = width // chunks
    blocks = []
    for at in range(chunks):
        own = tokens[:, at * span : (at + 1) * span]
        blocks.append(
            jnp.concatenate(
                [own, send(own, along_first(-1)), send(own, along_first(2)), send(own, along_first(1))]
            )
        )
    sums = [0.0] * 4
    for at in range(chunks):
        block = blocks[at]
        ahead = send(block, along_second(-1))
        behind = send(block, along_second(1))
        if at % 2 == 0:
            across = send(behind, along_second(1))
        else:
            across = send(ahead, along_second(-1))
        piece = jnp.concatenate([block, ahead, across, behind])
        part = slice(at * span, (at + 1) * span)
        for n, weight in enumerate((gate_weight, up_weight, gate_other, up_other)):
            sums[n] = sums[n] + dot(piece, weight[part])

    def local(gate, up):
        hidden = (jax.nn.silu(gate) * up).astype(jnp.bfloat16)
        return dot(hidden, mixing)

    local_own = local(sums[0], sums[1])
    local_other = local(sums[2], sums[3])
    turn = 1.0 - 2.0 * core.astype(jnp.float32)
    value = jnp.concatenate(
        [local_other + turn * local_own, local_own - turn * local_other], axis=1
    ).astype(jnp.bfloat16)
    value = value.reshape(RING, RING, rows, 2 * units)
    value = rotate(value, along_first, first, 1, 1.0)
    value = rotate(value, along_second, second, 0, 1.0 / math.sqrt(2 * RING * RING))
    value = value.reshape(RING * RING * rows, 2 * units)

    outs = []
    for at in range(chunks):
        part = slice(at * span, (at + 1) * span)
        partial = dot(value[:, :units], down_weight[:, part]) + dot(
            value[:, units:], down_other[:, part]
        )
        partial = partial.astype(jnp.bfloat16).reshape(RING, RING * rows, span)
        if at % 2 == 0:
            forward, back = 1, 3
        else:
            forward, back = 3, 1
        step = 1 if forward == 1 else -1
        far = send(partial[2], along_second(step))
        near = send(partial[back], along_second(-step))
        onward = (partial[forward].astype(jnp.float32) + far.astype(jnp.float32)).astype(jnp.bfloat16)
        onward = send(onward, along_second(step))
        total = (
            partial[0].astype(jnp.float32) + near.astype(jnp.float32) + onward.astype(jnp.float32)
        )
        total = total.astype(jnp.bfloat16).reshape(RING, rows, span)
        came = [
            send(total[1], along_first(1)),
            send(total[2], along_first(2)),
            send(total[3], along_first(-1)),
        ]
        last = total[0].astype(jnp.float32)
        for part_sum in came:
            last = last + part_sum.astype(jnp.float32)
        outs.append(last.astype(jnp.bfloat16))
    return jnp.concatenate(outs, axis=1)


def solution(mesh):
    in_specs = (
        P(("dp", "tensor"), None),
        P(None, "tensor"),
        P(None, "tensor"),
        P("tensor", None),
        P(),
    )
    out_specs = P(("dp", "tensor"), None)
    return jax.shard_map(body, mesh=mesh, in_specs=in_specs, out_specs=out_specs, check_vma=False)
```

time: 230 us -> 172 us (0.75)
  waiting for transfers between devices: 149 us -> 68.3 us
  starting transfers between devices: 0.04 us -> 43.2 us
  blocking collectives: 30.8 us -> 0 us
  local copies, waits for them, and re-layouts: 3.12 us -> 16.6 us
  between operations: 13.5 us -> 0.52 us
  matrix products: 29 us -> 36.8 us
    reduce_scatter x1 -> x0, waiting for transfers between devices: 91 us -> none  [body(): lax.psum_scatter(jnp.dot(rotated_hidden, down_weight, preferred_element_t...]
    ppermute x0 -> x33, waiting for transfers between devices: none -> 68.3 us  [send(): return lax.ppermute(value, 'tensor', pairs)]
    all_gather x1 -> x0, waiting for transfers between devices: 57.6 us -> none  [body(): piece = lax.all_gather(tokens, 'tensor', axis=0, tiled=True)]
    ppermute x0 -> x33, starting transfers between devices: none -> 43.2 us  [send(): return lax.ppermute(value, 'tensor', pairs)]
    all_to_all x2 -> x0, blocking collectives: 30.8 us -> none  [the longest x1 15.8 us: body(): lax.all_to_all(local_block_values[None].astype(jnp.bfloat16), 'tensor', s...]
    dot_general x4 -> x12, matrix products: 29 us -> 36.8 us  [dot(): return jnp.dot(a, b, preferred_element_type=jnp.float32)]
    slice x0 -> x15, local copies, waits for them, and re-layouts: none -> 6.99 us  [the longest x10 5.03 us: rotate(): total = total + factor * jnp.roll(part, step, axis=axis).astype(jnp.float32)]
    mul x0 -> x6, local copies, waits for them, and re-layouts: none -> 6.56 us  [rotate(): total = total + factor * jnp.roll(part, step, axis=axis).astype(jnp.float32)]
  transfers between devices with their start and end apart: 2 -> 33, of which waited for: 2 -> 16; matrix products, arithmetic and copies ran while one was open for 0% -> 30% of each run, Pallas kernels for 0% -> 0%
where the time goes in v1:
time: 172 us; the launch traced here: 171 us
  waiting for transfers between devices  68.3 us (40%)
  starting transfers between devices  43.2 us (25%)
  matrix products  36.8 us (21%)
  local copies, waits for them, and re-layouts  16.6 us (10%)
  other arithmetic  5.75 us (3%)
    ppermute x33, waiting for transfers between devices, send(): return lax.ppermute(value, 'tensor', pairs)  68.3 us
    ppermute x33, starting transfers between devices, send(): return lax.ppermute(value, 'tensor', pairs)  43.2 us
    dot_general x12, matrix products, dot(): return jnp.dot(a, b, preferred_element_type=jnp.float32)  36.8 us
    mul x6, local copies, waits for them, and re-layouts, rotate(): total = total + factor * jnp.roll(part, step, axis=axis).astype(jnp.float32)  6.56 us
    slice x10, local copies, waits for them, and re-layouts, rotate(): total = total + factor * jnp.roll(part, step, axis=axis).astype(jnp.float32)  5.03 us
  transfers between devices with their start and end apart: 33, of which 16 were waited for; matrix products, arithmetic and copies ran while one was open for 30% of the time, Pallas kernels for 0%

profile of v1, /device:TPU:0, one launch (start us, length us, event | category | flops | bytes accessed | tf_op | source)
XLA Modules:
  0.0 171.1 jit_solution(259258519405667156)
XLA Ops:
  0.0 1.7 %fusion.58 = (bf16[16,4096]{1,0:T(8,128)(2,1)S(1)}, bf16[256,4096]{1,0:T(8,128)(2,1)}, bf16[256,4096]{1,0:T(8,128)(2,1)S(1)}, bf16[16,4096]{1,0:T(8,128)(2,1)S(1)}) fusion(bf16[16,8192]{1,0:T(8,128)(2,1)} %param.5), kind=kLoop, calls=%fused_computation.81 | loop fusion | bytes 786432 | tf_op jit(solution)/shard_map/slice | solution.py:73
  1.7 2.8 %collective-permute-start = (bf16[16,4096]{1,0:T(8,128)(2,1)S(1)}, bf16[16,4096]{1,0:T(8,128)(2,1)S(1)}, u32[]{:S(2)}, u32[]{:S(2)}) collective-permute-start(bf16[16,4096]{1,0:T(8,128)(2,1)S(1)} %get-tuple-element.25), channel_id=1, source_target_pairs={{0,24},{1,7},{2,26},{3,1},{4,28},{5,3},{6,30},{7,5},{8,0},{9,15},{... | collective-permute-start | bytes 393224 | tf_op jit(solution)/shard_map/ppermute | solution.py:34
  4.6 0.8 collective-permute-start.1
  5.4 0.9 collective-permute-start.2
  6.2 2.4 %collective-permute-start.7 = (bf16[16,4096]{1,0:T(8,128)(2,1)S(1)}, bf16[16,4096]{1,0:T(8,128)(2,1)S(1)}, u32[]{:S(2)}, u32[]{:S(2)}) collective-permute-start(bf16[16,4096]{1,0:T(8,128)(2,1)S(1)} %get-tuple-element.28), channel_id=1, source_target_pairs={{0,24},{1,7},{2,26},{3,1},{4,28},{5,3},{6,30},{7,5},{8,0},{9,15},{... | collective-permute-start | bytes 393224 | tf_op jit(solution)/shard_map/ppermute | solution.py:34
  8.6 1.5 collective-permute-start.8
  10.1 1.0 collective-permute-done.1
  11.1 1.3 collective-permute-done.2
  12.5 3.1 %collective-permute-start.3 = (bf16[64,4096]{1,0:T(8,128)(2,1)S(1)}, bf16[64,4096]{1,0:T(8,128)(2,1)S(1)}, u32[]{:S(2)}, u32[]{:S(2)}) collective-permute-start(bf16[64,4096]{1,0:T(8,128)(2,1)S(1)} %pad_maximum_fusion), channel_id=1, source_target_pairs={{0,6},{1,25},{2,0},{3,27},{4,2},{5,29},{6,4},{7,31},{8,14},{9,1},{... | collective-permute-start | bytes 1572872 | tf_op jit(solution)/shard_map/ppermute | solution.py:34
  15.6 1.1 collective-permute-start.4
  16.7 2.9 %collective-permute-start.10 = (bf16[64,4096]{1,0:T(8,128)(2,1)S(1)}, bf16[64,4096]{1,0:T(8,128)(2,1)S(1)}, u32[]{:S(2)}, u32[]{:S(2)}) collective-permute-start(bf16[64,4096]{1,0:T(8,128)(2,1)S(1)} %pad_maximum_fusion.1), channel_id=1, source_target_pairs={{0,6},{1,25},{2,0},{3,27},{4,2},{5,29},{6,4},{7,31},{8,14},{9,1},{... | collective-permute-start | bytes 1572872 | tf_op jit(solution)/shard_map/ppermute | solution.py:34
  19.7 6.3 %collective-permute-done.4 = bf16[64,4096]{1,0:T(8,128)(2,1)S(1)} collective-permute-done((bf16[64,4096]{1,0:T(8,128)(2,1)S(1)}, bf16[64,4096]{1,0:T(8,128)(2,1)S(1)}, u32[]{:S(2)}, u32[]{:S(2)}) %collective-permute-start.4) | collective-permute-done | bytes 524320 | tf_op jit(solution)/shard_map/ppermute | solution.py:34
  26.0 1.9 %collective-permute-done.10 = bf16[64,4096]{1,0:T(8,128)(2,1)S(1)} collective-permute-done((bf16[64,4096]{1,0:T(8,128)(2,1)S(1)}, bf16[64,4096]{1,0:T(8,128)(2,1)S(1)}, u32[]{:S(2)}, u32[]{:S(2)}) %collective-permute-start.10) | collective-permute-done | bytes 524320 | tf_op jit(solution)/shard_map/ppermute | solution.py:34
  27.9 1.0 collective-permute-start.5
  29.0 2.7 %collective-permute-start.11 = (bf16[64,4096]{1,0:T(8,128)(2,1)S(1)}, bf16[64,4096]{1,0:T(8,128)(2,1)S(1)}, u32[]{:S(2)}, u32[]{:S(2)}) collective-permute-start(bf16[64,4096]{1,0:T(8,128)(2,1)S(1)} %collective-permute-done.10), channel_id=1, source_target_pairs={{0,6},{1,25},{2,0},{3,27},{4,2},{5,29},{6,4},{7,31},{8,14},{9,1},{... | collective-permute-start | bytes 1572872 | tf_op jit(solution)/shard_map/ppermute | solution.py:34
  31.7 7.0 %collective-permute-done.5 = bf16[64,4096]{1,0:T(8,128)(2,1)S(1)} collective-permute-done((bf16[64,4096]{1,0:T(8,128)(2,1)S(1)}, bf16[64,4096]{1,0:T(8,128)(2,1)S(1)}, u32[]{:S(2)}, u32[]{:S(2)}) %collective-permute-start.5) | collective-permute-done | bytes 524320 | tf_op jit(solution)/shard_map/ppermute | solution.py:34
  38.8 10.3 %collective-permute-done.12 = bf16[64,4096]{1,0:T(8,128)(2,1)S(1)} collective-permute-done((bf16[64,4096]{1,0:T(8,128)(2,1)S(1)}, bf16[64,4096]{1,0:T(8,128)(2,1)S(1)}, u32[]{:S(2)}, u32[]{:S(2)}) %collective-permute-start.12) | collective-permute-done | bytes 524320 | tf_op jit(solution)/shard_map/ppermute | solution.py:34
  49.2 3.3 %fusion.20 = f32[256,448]{0,1:T(8,128)S(1)} fusion(bf16[256,4096]{1,0:T(8,128)(2,1)S(1)} %constant_dynamic-update-slice_fusion.7, bf16[8192,448]{0,1:T(8,128)(2,1)} %param.6), kind=kOutput, calls=%fused_computation.22 | convolution fusion | flops 939524096 | bytes 6225920 | tf_op jit(solution)/shard_map/dot_general | solution.py:38
  53.3 1.3 fusion.16
  55.1 1.2 slice-done.3
  56.3 1.1 fusion.24
  57.5 5.1 %fusion.41 = f32[256,448]{0,1:T(8,128)} fusion(bf16[448,448]{1,0:T(8,128)(2,1)S(1)} %copy-done, f32[256,448]{0,1:T(8,128)S(1)} %fusion.24, f32[256,448]{0,1:T(8,128)S(1)} %fusion.16, bf16[256,4096]{1,0:T(8,128)(2,1)} %copy-done.7, bf16[8192,448]{0,1:T(8,128)(2,1)} %param.7), kind=kOutput, calls=%fused_computation.54 | convolution fusion | flops 1043087360 | bytes 7544832 | tf_op jit(solution)/shard_map/dot_general | solution.py:38
  62.5 3.2 %fusion.8 = f32[256,448]{0,1:T(8,128)S(1)} fusion(bf16[256,4096]{1,0:T(8,128)(2,1)S(1)} %constant_dynamic-update-slice_fusion.7, bf16[8192,448]{0,1:T(8,128)(2,1)} %collective-permute-done.6), kind=kOutput, calls=%fused_computation.10 | convolution fusion | flops 939524096 | bytes 6225920 | tf_op jit(solution)/shard_map/dot_general | solution.py:38
  65.7 4.2 %fusion.4 = f32[256,448]{0,1:T(8,128)} fusion(bf16[256,4096]{1,0:T(8,128)(2,1)S(1)} %constant_dynamic-update-slice_fusion.7, bf16[8192,448]{0,1:T(8,128)(2,1)} %collective-permute-done.13), kind=kOutput, calls=%fused_computation.6 | convolution fusion | flops 939524096 | bytes 6225920 | tf_op jit(solution)/shard_map/dot_general | solution.py:38
  69.9 3.3 %fusion.30 = f32[256,448]{0,1:T(8,128)S(1)} fusion(f32[256,448]{0,1:T(8,128)S(1)} %fusion.8, bf16[256,4096]{1,0:T(8,128)(2,1)S(1)} %copy-done.8, bf16[8192,448]{0,1:T(8,128)(2,1)} %collective-permute-done.6), kind=kOutput, calls=%fused_computation.28 | convolution fusion | flops 939638784 | bytes 6684672 | tf_op jit(solution)/shard_map/dot_general | solution.py:38
  73.3 3.8 %add_convert_fusion.7 = (bf16[256,448]{0,1:T(8,128)(2,1)S(1)}, bf16[256,448]{0,1:T(8,128)(2,1)S(1)}) fusion(f32[256,448]{0,1:T(8,128)} %fusion.41, f32[]{:T(128)S(6)} %sub.41, bf16[448,448]{1,0:T(8,128)(2,1)S(1)} %copy-done, f32[256,448]{0,1:T(8,128)S(1)} %fusion.30, f32[256,448]{0,1:T(8,128)} %fusion.4, bf16[256,4096]{1,0:T(8,128)(2,1)S(1)} %copy-done.9, ...), kind=kOutput, calls=%fused_computation.47 | convolution fusion | flops 1043775488 | bytes 8003588 | tf_op jit(solution)/shard_map/dot_general | solution.py:38
  77.6 3.7 %collective-permute-start.14 = (bf16[4,4,16,896]{3,2,1,0:T(8,128)(2,1)S(1)}, bf16[4,4,16,896]{3,2,1,0:T(8,128)(2,1)S(1)}, u32[]{:S(2)}, u32[]{:S(2)}) collective-permute-start(bf16[4,4,16,896]{3,2,1,0:T(8,128)(2,1)S(1)} %pad_maximum_fusion.2), channel_id=1, source_target_pairs={{0,24},{1,7},{2,26},{3,1},{4,28},{5,3},{6,30},{7,5},{8,0},{9,15},{... | collective-permute-start | bytes 1376264 | tf_op jit(solution)/shard_map/ppermute | solution.py:34
  81.3 1.5 collective-permute-start.15
  82.8 9.4 %collective-permute-done.14 = bf16[4,4,16,896]{3,2,1,0:T(8,128)(2,1)S(1)} collective-permute-done((bf16[4,4,16,896]{3,2,1,0:T(8,128)(2,1)S(1)}, bf16[4,4,16,896]{3,2,1,0:T(8,128)(2,1)S(1)}, u32[]{:S(2)}, u32[]{:S(2)}) %collective-permute-start.14) | collective-permute-done | bytes 458784 | tf_op jit(solution)/shard_map/ppermute | solution.py:34
  92.2 3.6 %collective-permute-done.16 = bf16[4,4,16,896]{3,2,1,0:T(8,128)(2,1)S(1)} collective-permute-done((bf16[4,4,16,896]{3,2,1,0:T(8,128)(2,1)S(1)}, bf16[4,4,16,896]{3,2,1,0:T(8,128)(2,1)S(1)}, u32[]{:S(2)}, u32[]{:S(2)}) %collective-permute-start.16) | collective-permute-done | bytes 458784 | tf_op jit(solution)/shard_map/ppermute | solution.py:34
  96.0 1.2 convert_multiply_fusion.5
  97.3 0.8 collective-permute-start.17
  98.1 1.2 collective-permute-start.19
  99.3 1.2 copy.10
  100.8 1.3 copy.9
  102.1 3.9 %collective-permute-done.17 = bf16[4,4,16,896]{3,2,1,0:T(8,128)(2,1)} collective-permute-done((bf16[4,4,16,896]{3,2,1,0:T(8,128)(2,1)}, bf16[4,4,16,896]{3,2,1,0:T(8,128)(2,1)}, u32[]{:S(2)}, u32[]{:S(2)}) %collective-permute-start.17) | collective-permute-done | bytes 458784 | tf_op jit(solution)/shard_map/ppermute | solution.py:34
  106.0 1.0 slice.217
  107.1 0.9 slice.216
  108.0 1.2 copy.11
  109.3 1.1 fusion.56
  110.5 1.2 copy.12
  111.7 1.6 collective-permute-done.19
  113.3 1.0 slice.220
  114.3 0.9 slice.221
  115.3 1.3 copy.13
  116.5 2.6 %add_convert_fusion.4 = bf16[256,896]{0,1:T(8,128)(2,1)S(1)} fusion(f32[256,896]{0,1:T(8,128)} %copy.13, f32[256,896]{0,1:T(8,128)} %copy.12, f32[256,896]{0,1:T(8,128)} %copy.11, f32[256,896]{0,1:T(8,128)S(1)} %copy-done.2, f32[256,896]{0,1:T(8,128)} %copy.9, f32[256,896]{0,1:T(8,128)S(1)} %copy.8, bf16[256,448]{0,1:T(8,128)(2,1)} %copy-done.5, ...), kind=kLoop, calls=%fused_computation.34 | loop fusion | flops 3440640 | bytes 6422536 | tf_op jit(solution)/shard_map/convert_element_type | solution.py:53
  119.1 3.5 %fusion.14 = f32[256,4096]{1,0:T(8,128)S(1)} fusion(bf16[448,8192]{1,0:T(8,128)(2,1)} %param.8, bf16[256,896]{0,1:T(8,128)(2,1)S(1)} %add_convert_fusion.4), kind=kOutput, calls=%fused_computation.16 | convolution fusion | flops 939524096 | bytes 8093696 | tf_op jit(solution)/shard_map/dot_general | solution.py:38
  122.6 1.3 fusion.12
  124.0 3.3 %fusion = bf16[256,4096]{1,0:T(8,128)(2,1)S(1)} fusion(f32[256,4096]{1,0:T(8,128)S(1)} %fusion.14, bf16[448,8192]{1,0:T(8,128)(2,1)} %collective-permute-done.20, bf16[256,896]{0,1:T(8,128)(2,1)S(1)} %add_convert_fusion.4), kind=kOutput, calls=%fused_computation.2 | convolution fusion | flops 941621248 | bytes 10190848 | tf_op jit(solution)/shard_map/dot_general | solution.py:38
  127.5 3.2 %collective-permute-start.21 = (bf16[64,4096]{1,0:T(8,128)(2,1)S(1)}, bf16[64,4096]{1,0:T(8,128)(2,1)S(1)}, u32[]{:S(2)}, u32[]{:S(2)}) collective-permute-start(bf16[64,4096]{1,0:T(8,128)(2,1)S(1)} %get-tuple-element.5), channel_id=1, source_target_pairs={{0,6},{1,25},{2,0},{3,27},{4,2},{5,29},{6,4},{7,31},{8,14},{9,1},{... | collective-permute-start | bytes 1572872 | tf_op jit(solution)/shard_map/ppermute | solution.py:34
  130.7 3.3 %fusion.1 = bf16[256,4096]{1,0:T(8,128)(2,1)S(1)} fusion(f32[256,4096]{1,0:T(8,128)S(1)} %fusion.12, bf16[448,8192]{1,0:T(8,128)(2,1)} %collective-permute-done.20, bf16[256,896]{0,1:T(8,128)(2,1)S(1)} %add_convert_fusion.4), kind=kOutput, calls=%fused_computation.3 | convolution fusion | flops 941621248 | bytes 10190848 | tf_op jit(solution)/shard_map/dot_general | solution.py:38
  134.1 1.7 %collective-permute-start.28 = (bf16[64,4096]{1,0:T(8,128)(2,1)S(1)}, bf16[64,4096]{1,0:T(8,128)(2,1)S(1)}, u32[]{:S(2)}, u32[]{:S(2)}) collective-permute-start(bf16[64,4096]{1,0:T(8,128)(2,1)S(1)} %get-tuple-element.8), channel_id=1, source_target_pairs={{0,6},{1,25},{2,0},{3,27},{4,2},{5,29},{6,4},{7,31},{8,14},{9,1},{... | collective-permute-start | bytes 1572872 | tf_op jit(solution)/shard_map/ppermute | solution.py:34
  136.2 1.6 collective-permute-done.22
  138.1 5.3 %collective-permute-done.28 = bf16[64,4096]{1,0:T(8,128)(2,1)S(1)} collective-permute-done((bf16[64,4096]{1,0:T(8,128)(2,1)S(1)}, bf16[64,4096]{1,0:T(8,128)(2,1)S(1)}, u32[]{:S(2)}, u32[]{:S(2)}) %collective-permute-start.28) | collective-permute-done | bytes 524320 | tf_op jit(solution)/shard_map/ppermute | solution.py:34
  143.5 3.4 %collective-permute-start.29 = (bf16[64,4096]{1,0:T(8,128)(2,1)S(1)}, bf16[64,4096]{1,0:T(8,128)(2,1)S(1)}, u32[]{:S(2)}, u32[]{:S(2)}) collective-permute-start(bf16[64,4096]{1,0:T(8,128)(2,1)S(1)} %add_convert_fusion.1), channel_id=1, source_target_pairs={{0,6},{1,25},{2,0},{3,27},{4,2},{5,29},{6,4},{7,31},{8,14},{9,1},{... | collective-permute-start | bytes 1572872 | tf_op jit(solution)/shard_map/ppermute | solution.py:34
  146.9 10.6 %collective-permute-done.23 = bf16[64,4096]{1,0:T(8,128)(2,1)S(1)} collective-permute-done((bf16[64,4096]{1,0:T(8,128)(2,1)S(1)}, bf16[64,4096]{1,0:T(8,128)(2,1)S(1)}, u32[]{:S(2)}, u32[]{:S(2)}) %collective-permute-start.23) | collective-permute-done | bytes 524320 | tf_op jit(solution)/shard_map/ppermute | solution.py:34
  157.8 1.5 collective-permute-start.25
  159.3 1.7 collective-permute-start.26
  161.3 0.9 collective-permute-start.30
  162.2 2.1 %collective-permute-start.31 = (bf16[16,4096]{1,0:T(8,128)(2,1)S(1)}, bf16[16,4096]{1,0:T(8,128)(2,1)S(1)}, u32[]{:S(2)}, u32[]{:S(2)}) collective-permute-start(bf16[16,4096]{1,0:T(8,128)(2,1)S(1)} %get-tuple-element.16), channel_id=1, source_target_pairs={{0,16},{1,5},{2,18},{3,7},{4,20},{5,1},{6,22},{7,3},{8,24},{9,13},... | collective-permute-start | bytes 393224 | tf_op jit(solution)/shard_map/ppermute | solution.py:34
  164.3 1.0 collective-permute-done.24
  165.4 1.5 collective-permute-start.32
  167.0 1.9 %collective-permute-done.30 = bf16[16,4096]{1,0:T(8,128)(2,1)S(1)} collective-permute-done((bf16[16,4096]{1,0:T(8,128)(2,1)S(1)}, bf16[16,4096]{1,0:T(8,128)(2,1)S(1)}, u32[]{:S(2)}, u32[]{:S(2)}) %collective-permute-start.30) | collective-permute-done | bytes 131104 | tf_op jit(solution)/shard_map/ppermute | solution.py:34
  168.9 1.4 collective-permute-done.32
  (96 shorter events, 5.2 us)
Async XLA Ops:
  0.0 57.5 %copy-start = (bf16[448,448]{1,0:T(8,128)(2,1)S(1)}, bf16[448,448]{1,0:T(8,128)(2,1)}, u32[]{:S(2)}) copy-start(bf16[448,448]{1,0:T(8,128)(2,1)} %param.9) | copy-start | bytes 1204228
  1.7 8.4 %collective-permute-start = (bf16[16,4096]{1,0:T(8,128)(2,1)S(1)}, bf16[16,4096]{1,0:T(8,128)(2,1)S(1)}, u32[]{:S(2)}, u32[]{:S(2)}) collective-permute-start(bf16[16,4096]{1,0:T(8,128)(2,1)S(1)} %get-tuple-element.25), channel_id=1, source_target_pairs={{0,24},{1,7},{2,26},{3,1},{4,28},{5,3},{6,30},{7,5},{8,0},{9,15},{... | collective-permute-start | bytes 393224 | tf_op jit(solution)/shard_map/ppermute | solution.py:34
  4.6 6.6 %collective-permute-start.1 = (bf16[16,4096]{1,0:T(8,128)(2,1)S(1)}, bf16[16,4096]{1,0:T(8,128)(2,1)S(1)}, u32[]{:S(2)}, u32[]{:S(2)}) collective-permute-start(bf16[16,4096]{1,0:T(8,128)(2,1)S(1)} %get-tuple-element.25), channel_id=1, source_target_pairs={{0,16},{1,5},{2,18},{3,7},{4,20},{5,1},{6,22},{7,3},{8,24},{9,13},... | collective-permute-start | bytes 393224 | tf_op jit(solution)/shard_map/ppermute | solution.py:34
  5.4 7.1 %collective-permute-start.2 = (bf16[16,4096]{1,0:T(8,128)(2,1)S(1)}, bf16[16,4096]{1,0:T(8,128)(2,1)S(1)}, u32[]{:S(2)}, u32[]{:S(2)}) collective-permute-start(bf16[16,4096]{1,0:T(8,128)(2,1)S(1)} %get-tuple-element.25), channel_id=1, source_target_pairs={{0,8},{1,3},{2,10},{3,5},{4,12},{5,7},{6,14},{7,1},{8,16},{9,11},{... | collective-permute-start | bytes 393224 | tf_op jit(solution)/shard_map/ppermute | solution.py:34
  6.2 6.3 %collective-permute-start.7 = (bf16[16,4096]{1,0:T(8,128)(2,1)S(1)}, bf16[16,4096]{1,0:T(8,128)(2,1)S(1)}, u32[]{:S(2)}, u32[]{:S(2)}) collective-permute-start(bf16[16,4096]{1,0:T(8,128)(2,1)S(1)} %get-tuple-element.28), channel_id=1, source_target_pairs={{0,24},{1,7},{2,26},{3,1},{4,28},{5,3},{6,30},{7,5},{8,0},{9,15},{... | collective-permute-start | bytes 393224 | tf_op jit(solution)/shard_map/ppermute | solution.py:34
  8.6 7.0 %collective-permute-start.8 = (bf16[16,4096]{1,0:T(8,128)(2,1)S(1)}, bf16[16,4096]{1,0:T(8,128)(2,1)S(1)}, u32[]{:S(2)}, u32[]{:S(2)}) collective-permute-start(bf16[16,4096]{1,0:T(8,128)(2,1)S(1)} %get-tuple-element.28), channel_id=1, source_target_pairs={{0,16},{1,5},{2,18},{3,7},{4,20},{5,1},{6,22},{7,3},{8,24},{9,13},... | collective-permute-start | bytes 393224 | tf_op jit(solution)/shard_map/ppermute | solution.py:34
  10.1 9.5 %copy-start.6 = (bf16[256,4096]{1,0:T(8,128)(2,1)S(1)}, bf16[256,4096]{1,0:T(8,128)(2,1)}, u32[]{:S(2)}) copy-start(bf16[256,4096]{1,0:T(8,128)(2,1)} %get-tuple-element.26) | copy-start | bytes 6291460
  10.1 6.5 %collective-permute-start.9 = (bf16[16,4096]{1,0:T(8,128)(2,1)S(1)}, bf16[16,4096]{1,0:T(8,128)(2,1)S(1)}, u32[]{:S(2)}, u32[]{:S(2)}) collective-permute-start(bf16[16,4096]{1,0:T(8,128)(2,1)S(1)} %get-tuple-element.28), channel_id=1, source_target_pairs={{0,8},{1,3},{2,10},{3,5},{4,12},{5,7},{6,14},{7,1},{8,16},{9,11},{... | collective-permute-start | bytes 393224 | tf_op jit(solution)/shard_map/ppermute | solution.py:34
  11.1 51.4 %collective-permute-start.6 = (bf16[8192,448]{0,1:T(8,128)(2,1)}, bf16[8192,448]{0,1:T(8,128)(2,1)}, u32[]{:S(2)}, u32[]{:S(2)}) collective-permute-start(bf16[8192,448]{0,1:T(8,128)(2,1)} %param.6), channel_id=1, source_target_pairs={{0,1},{1,0},{2,3},{3,2},{4,5},{5,4},{6,7},{7,6},{8,9},{9,8},{10,11... | collective-permute-start | bytes 22020104 | tf_op jit(solution)/shard_map/ppermute | solution.py:34
  12.4 53.3 %collective-permute-start.13 = (bf16[8192,448]{0,1:T(8,128)(2,1)}, bf16[8192,448]{0,1:T(8,128)(2,1)}, u32[]{:S(2)}, u32[]{:S(2)}) collective-permute-start(bf16[8192,448]{0,1:T(8,128)(2,1)} %param.7), channel_id=1, source_target_pairs={{0,1},{1,0},{2,3},{3,2},{4,5},{5,4},{6,7},{7,6},{8,9},{9,8},{10,11... | collective-permute-start | bytes 22020104 | tf_op jit(solution)/shard_map/ppermute | solution.py:34
  12.5 16.5 %collective-permute-start.3 = (bf16[64,4096]{1,0:T(8,128)(2,1)S(1)}, bf16[64,4096]{1,0:T(8,128)(2,1)S(1)}, u32[]{:S(2)}, u32[]{:S(2)}) collective-permute-start(bf16[64,4096]{1,0:T(8,128)(2,1)S(1)} %pad_maximum_fusion), channel_id=1, source_target_pairs={{0,6},{1,25},{2,0},{3,27},{4,2},{5,29},{6,4},{7,31},{8,14},{9,1},{... | collective-permute-start | bytes 1572872 | tf_op jit(solution)/shard_map/ppermute | solution.py:34
  15.6 10.4 %collective-permute-start.4 = (bf16[64,4096]{1,0:T(8,128)(2,1)S(1)}, bf16[64,4096]{1,0:T(8,128)(2,1)S(1)}, u32[]{:S(2)}, u32[]{:S(2)}) collective-permute-start(bf16[64,4096]{1,0:T(8,128)(2,1)S(1)} %pad_maximum_fusion), channel_id=1, source_target_pairs={{0,2},{1,9},{2,4},{3,11},{4,6},{5,13},{6,0},{7,15},{8,10},{9,17},{... | collective-permute-start | bytes 1572872 | tf_op jit(solution)/shard_map/ppermute | solution.py:34
  16.7 11.2 %collective-permute-start.10 = (bf16[64,4096]{1,0:T(8,128)(2,1)S(1)}, bf16[64,4096]{1,0:T(8,128)(2,1)S(1)}, u32[]{:S(2)}, u32[]{:S(2)}) collective-permute-start(bf16[64,4096]{1,0:T(8,128)(2,1)S(1)} %pad_maximum_fusion.1), channel_id=1, source_target_pairs={{0,6},{1,25},{2,0},{3,27},{4,2},{5,29},{6,4},{7,31},{8,14},{9,1},{... | collective-permute-start | bytes 1572872 | tf_op jit(solution)/shard_map/ppermute | solution.py:34
  26.0 98.0 %collective-permute-start.20 = (bf16[448,8192]{1,0:T(8,128)(2,1)}, bf16[448,8192]{1,0:T(8,128)(2,1)}, u32[]{:S(2)}, u32[]{:S(2)}) collective-permute-start(bf16[448,8192]{1,0:T(8,128)(2,1)} %param.8), channel_id=1, source_target_pairs={{0,1},{1,0},{2,3},{3,2},{4,5},{5,4},{6,7},{7,6},{8,9},{9,8},{10,11... | collective-permute-start | bytes 22020104 | tf_op jit(solution)/shard_map/ppermute | solution.py:34
  27.9 10.8 %collective-permute-start.5 = (bf16[64,4096]{1,0:T(8,128)(2,1)S(1)}, bf16[64,4096]{1,0:T(8,128)(2,1)S(1)}, u32[]{:S(2)}, u32[]{:S(2)}) collective-permute-start(bf16[64,4096]{1,0:T(8,128)(2,1)S(1)} %collective-permute-done.4), channel_id=1, source_target_pairs={{0,2},{1,9},{2,4},{3,11},{4,6},{5,13},{6,0},{7,15},{8,10},{9,17},{... | collective-permute-start | bytes 1572872 | tf_op jit(solution)/shard_map/ppermute | solution.py:34
  29.0 9.8 %collective-permute-start.11 = (bf16[64,4096]{1,0:T(8,128)(2,1)S(1)}, bf16[64,4096]{1,0:T(8,128)(2,1)S(1)}, u32[]{:S(2)}, u32[]{:S(2)}) collective-permute-start(bf16[64,4096]{1,0:T(8,128)(2,1)S(1)} %collective-permute-done.10), channel_id=1, source_target_pairs={{0,6},{1,25},{2,0},{3,27},{4,2},{5,29},{6,4},{7,31},{8,14},{9,1},{... | collective-permute-start | bytes 1572872 | tf_op jit(solution)/shard_map/ppermute | solution.py:34
  38.7 10.4 %collective-permute-start.12 = (bf16[64,4096]{1,0:T(8,128)(2,1)S(1)}, bf16[64,4096]{1,0:T(8,128)(2,1)S(1)}, u32[]{:S(2)}, u32[]{:S(2)}) collective-permute-start(bf16[64,4096]{1,0:T(8,128)(2,1)S(1)} %pad_maximum_fusion.1), channel_id=1, source_target_pairs={{0,2},{1,9},{2,4},{3,11},{4,6},{5,13},{6,0},{7,15},{8,10},{9,17},{... | collective-permute-start | bytes 1572872 | tf_op jit(solution)/shard_map/ppermute | solution.py:34
  49.1 4.2 %copy-start.10 = (bf16[8192,448]{0,1:T(8,128)(2,1)S(1)}, bf16[8192,448]{0,1:T(8,128)(2,1)}, u32[]{:S(2)}) copy-start(bf16[8192,448]{0,1:T(8,128)(2,1)} %param.7) | copy-start | bytes 22020100
  49.2 6.0 %slice-start.2 = ((s8[7340032]{0:T(1024)(128)(4,1)}), s8[4194304]{0:T(1024)(128)(4,1)S(1)}, s32[]{:S(2)}) async-start(s8[7340032]{0:T(1024)(128)(4,1)} %bitcast.30), calls=%async_computation.2 | async-start | bytes 8388608
  52.5 3.8 %slice-start.3 = ((s8[7340032]{0:T(1024)(128)(4,1)}), s8[3145728]{0:T(1024)(128)(4,1)S(1)}, s32[]{:S(2)}) async-start(s8[7340032]{0:T(1024)(128)(4,1)} %bitcast.30), calls=%async_computation.3 | async-start | bytes 6291456
  53.3 1.3 copy-start.7
  65.7 4.2 %copy-start.8 = (bf16[256,4096]{1,0:T(8,128)(2,1)S(1)}, bf16[256,4096]{1,0:T(8,128)(2,1)}, u32[]{:S(2)}) copy-start(bf16[256,4096]{1,0:T(8,128)(2,1)} %copy-done.7) | copy-start | bytes 6291460
  69.9 3.3 %copy-start.9 = (bf16[256,4096]{1,0:T(8,128)(2,1)S(1)}, bf16[256,4096]{1,0:T(8,128)(2,1)}, u32[]{:S(2)}) copy-start(bf16[256,4096]{1,0:T(8,128)(2,1)} %copy-done.7) | copy-start | bytes 6291460
  77.1 18.9 %copy-start.3 = (bf16[256,448]{0,1:T(8,128)(2,1)}, bf16[256,448]{0,1:T(8,128)(2,1)S(1)}, u32[]{:S(2)}) copy-start(bf16[256,448]{0,1:T(8,128)(2,1)S(1)} %get-tuple-element.9) | copy-start | bytes 688132
  77.1 18.9 %copy-start.5 = (bf16[256,448]{0,1:T(8,128)(2,1)}, bf16[256,448]{0,1:T(8,128)(2,1)S(1)}, u32[]{:S(2)}) copy-start(bf16[256,448]{0,1:T(8,128)(2,1)S(1)} %get-tuple-element.10) | copy-start | bytes 688132
  77.6 14.6 %collective-permute-start.14 = (bf16[4,4,16,896]{3,2,1,0:T(8,128)(2,1)S(1)}, bf16[4,4,16,896]{3,2,1,0:T(8,128)(2,1)S(1)}, u32[]{:S(2)}, u32[]{:S(2)}) collective-permute-start(bf16[4,4,16,896]{3,2,1,0:T(8,128)(2,1)S(1)} %pad_maximum_fusion.2), channel_id=1, source_target_pairs={{0,24},{1,7},{2,26},{3,1},{4,28},{5,3},{6,30},{7,5},{8,0},{9,15},{... | collective-permute-start | bytes 1376264 | tf_op jit(solution)/shard_map/ppermute | solution.py:34
  81.3 14.6 %collective-permute-start.16 = (bf16[4,4,16,896]{3,2,1,0:T(8,128)(2,1)S(1)}, bf16[4,4,16,896]{3,2,1,0:T(8,128)(2,1)S(1)}, u32[]{:S(2)}, u32[]{:S(2)}) collective-permute-start(bf16[4,4,16,896]{3,2,1,0:T(8,128)(2,1)S(1)} %pad_maximum_fusion.2), channel_id=1, source_target_pairs={{0,8},{1,3},{2,10},{3,5},{4,12},{5,7},{6,14},{7,1},{8,16},{9,11},{... | collective-permute-start | bytes 1376264 | tf_op jit(solution)/shard_map/ppermute | solution.py:34
  81.3 14.7 %collective-permute-start.15 = (bf16[4,4,16,896]{3,2,1,0:T(8,128)(2,1)S(1)}, bf16[4,4,16,896]{3,2,1,0:T(8,128)(2,1)S(1)}, u32[]{:S(2)}, u32[]{:S(2)}) collective-permute-start(bf16[4,4,16,896]{3,2,1,0:T(8,128)(2,1)S(1)} %pad_maximum_fusion.2), channel_id=1, source_target_pairs={{0,16},{1,5},{2,18},{3,7},{4,20},{5,1},{6,22},{7,3},{8,24},{9,13},... | collective-permute-start | bytes 1376264 | tf_op jit(solution)/shard_map/ppermute | solution.py:34
  97.3 8.8 %collective-permute-start.17 = (bf16[4,4,16,896]{3,2,1,0:T(8,128)(2,1)}, bf16[4,4,16,896]{3,2,1,0:T(8,128)(2,1)}, u32[]{:S(2)}, u32[]{:S(2)}) collective-permute-start(bf16[4,4,16,896]{3,2,1,0:T(8,128)(2,1)} %get-tuple-element.18), channel_id=1, source_target_pairs={{0,6},{1,25},{2,0},{3,27},{4,2},{5,29},{6,4},{7,31},{8,14},{9,1},{... | collective-permute-start | bytes 1376264 | tf_op jit(solution)/shard_map/ppermute | solution.py:34
  98.1 11.2 %collective-permute-start.18 = (bf16[4,4,16,896]{3,2,1,0:T(8,128)(2,1)}, bf16[4,4,16,896]{3,2,1,0:T(8,128)(2,1)}, u32[]{:S(2)}, u32[]{:S(2)}) collective-permute-start(bf16[4,4,16,896]{3,2,1,0:T(8,128)(2,1)} %get-tuple-element.18), channel_id=1, source_target_pairs={{0,4},{1,17},{2,6},{3,19},{4,0},{5,21},{6,2},{7,23},{8,12},{9,25},... | collective-permute-start | bytes 1376264 | tf_op jit(solution)/shard_map/ppermute | solution.py:34
  98.1 15.2 %collective-permute-start.19 = (bf16[4,4,16,896]{3,2,1,0:T(8,128)(2,1)}, bf16[4,4,16,896]{3,2,1,0:T(8,128)(2,1)}, u32[]{:S(2)}, u32[]{:S(2)}) collective-permute-start(bf16[4,4,16,896]{3,2,1,0:T(8,128)(2,1)} %get-tuple-element.18), channel_id=1, source_target_pairs={{0,2},{1,9},{2,4},{3,11},{4,6},{5,13},{6,0},{7,15},{8,10},{9,17},{... | collective-permute-start | bytes 1376264 | tf_op jit(solution)/shard_map/ppermute | solution.py:34
  111.7 4.8 %copy-start.2 = (f32[256,896]{0,1:T(8,128)S(1)}, f32[256,896]{0,1:T(8,128)}, u32[]{:S(2)}) copy-start(f32[256,896]{0,1:T(8,128)} %copy.10) | copy-start | bytes 2752516
  111.7 4.8 %copy-start.4 = (bf16[256,448]{0,1:T(8,128)(2,1)S(1)}, bf16[256,448]{0,1:T(8,128)(2,1)}, u32[]{:S(2)}) copy-start(bf16[256,448]{0,1:T(8,128)(2,1)} %copy-done.3) | copy-start | bytes 688132
  116.5 6.1 %slice-start = ((s8[7340032]{0:T(1024)(128)(4,1)}), s8[3145728]{0:T(1024)(128)(4,1)S(1)}, s32[]{:S(2)}) async-start(s8[7340032]{0:T(1024)(128)(4,1)} %bitcast.18), calls=%async_computation | async-start | bytes 6291456
  119.1 3.5 %slice-start.1 = ((s8[7340032]{0:T(1024)(128)(4,1)}), s8[4194304]{0:T(1024)(128)(4,1)S(1)}, s32[]{:S(2)}) async-start(s8[7340032]{0:T(1024)(128)(4,1)} %bitcast.18), calls=%async_computation.1 | async-start | bytes 8388608
  127.4 10.5 %collective-permute-start.22 = (bf16[64,4096]{1,0:T(8,128)(2,1)S(1)}, bf16[64,4096]{1,0:T(8,128)(2,1)S(1)}, u32[]{:S(2)}, u32[]{:S(2)}) collective-permute-start(bf16[64,4096]{1,0:T(8,128)(2,1)S(1)} %get-tuple-element.6), channel_id=1, source_target_pairs={{0,2},{1,9},{2,4},{3,11},{4,6},{5,13},{6,0},{7,15},{8,10},{9,17},{... | collective-permute-start | bytes 1572872 | tf_op jit(solution)/shard_map/ppermute | solution.py:34
  127.5 19.4 %collective-permute-start.21 = (bf16[64,4096]{1,0:T(8,128)(2,1)S(1)}, bf16[64,4096]{1,0:T(8,128)(2,1)S(1)}, u32[]{:S(2)}, u32[]{:S(2)}) collective-permute-start(bf16[64,4096]{1,0:T(8,128)(2,1)S(1)} %get-tuple-element.5), channel_id=1, source_target_pairs={{0,6},{1,25},{2,0},{3,27},{4,2},{5,29},{6,4},{7,31},{8,14},{9,1},{... | collective-permute-start | bytes 1572872 | tf_op jit(solution)/shard_map/ppermute | solution.py:34
  134.1 9.2 %collective-permute-start.28 = (bf16[64,4096]{1,0:T(8,128)(2,1)S(1)}, bf16[64,4096]{1,0:T(8,128)(2,1)S(1)}, u32[]{:S(2)}, u32[]{:S(2)}) collective-permute-start(bf16[64,4096]{1,0:T(8,128)(2,1)S(1)} %get-tuple-element.8), channel_id=1, source_target_pairs={{0,6},{1,25},{2,0},{3,27},{4,2},{5,29},{6,4},{7,31},{8,14},{9,1},{... | collective-permute-start | bytes 1572872 | tf_op jit(solution)/shard_map/ppermute | solution.py:34
  135.9 25.2 %collective-permute-start.27 = (bf16[64,4096]{1,0:T(8,128)(2,1)S(1)}, bf16[64,4096]{1,0:T(8,128)(2,1)S(1)}, u32[]{:S(2)}, u32[]{:S(2)}) collective-permute-start(bf16[64,4096]{1,0:T(8,128)(2,1)S(1)} %get-tuple-element.7), channel_id=1, source_target_pairs={{0,2},{1,9},{2,4},{3,11},{4,6},{5,13},{6,0},{7,15},{8,10},{9,17},{... | collective-permute-start | bytes 1572872 | tf_op jit(solution)/shard_map/ppermute | solution.py:34
  138.0 19.5 %collective-permute-start.23 = (bf16[64,4096]{1,0:T(8,128)(2,1)S(1)}, bf16[64,4096]{1,0:T(8,128)(2,1)S(1)}, u32[]{:S(2)}, u32[]{:S(2)}) collective-permute-start(bf16[64,4096]{1,0:T(8,128)(2,1)S(1)} %add_convert_fusion.3), channel_id=1, source_target_pairs={{0,2},{1,9},{2,4},{3,11},{4,6},{5,13},{6,0},{7,15},{8,10},{9,17},{... | collective-permute-start | bytes 1572872 | tf_op jit(solution)/shard_map/ppermute | solution.py:34
  143.5 17.5 %collective-permute-start.29 = (bf16[64,4096]{1,0:T(8,128)(2,1)S(1)}, bf16[64,4096]{1,0:T(8,128)(2,1)S(1)}, u32[]{:S(2)}, u32[]{:S(2)}) collective-permute-start(bf16[64,4096]{1,0:T(8,128)(2,1)S(1)} %add_convert_fusion.1), channel_id=1, source_target_pairs={{0,6},{1,25},{2,0},{3,27},{4,2},{5,29},{6,4},{7,31},{8,14},{9,1},{... | collective-permute-start | bytes 1572872 | tf_op jit(solution)/shard_map/ppermute | solution.py:34
  157.7 7.7 %collective-permute-start.24 = (bf16[16,4096]{1,0:T(8,128)(2,1)S(1)}, bf16[16,4096]{1,0:T(8,128)(2,1)S(1)}, u32[]{:S(2)}, u32[]{:S(2)}) collective-permute-start(bf16[16,4096]{1,0:T(8,128)(2,1)S(1)} %get-tuple-element.11), channel_id=1, source_target_pairs={{0,8},{1,3},{2,10},{3,5},{4,12},{5,7},{6,14},{7,1},{8,16},{9,11},{... | collective-permute-start | bytes 393224 | tf_op jit(solution)/shard_map/ppermute | solution.py:34
  157.8 9.1 %collective-permute-start.25 = (bf16[16,4096]{1,0:T(8,128)(2,1)S(1)}, bf16[16,4096]{1,0:T(8,128)(2,1)S(1)}, u32[]{:S(2)}, u32[]{:S(2)}) collective-permute-start(bf16[16,4096]{1,0:T(8,128)(2,1)S(1)} %get-tuple-element.13), channel_id=1, source_target_pairs={{0,16},{1,5},{2,18},{3,7},{4,20},{5,1},{6,22},{7,3},{8,24},{9,13},... | collective-permute-start | bytes 393224 | tf_op jit(solution)/shard_map/ppermute | solution.py:34
  159.3 11.8 %copy-start.1 = (bf16[448,448]{1,0:T(8,128)(2,1)S(1)}, bf16[448,448]{1,0:T(8,128)(2,1)}, u32[]{:S(2)}) copy-start(bf16[448,448]{1,0:T(8,128)(2,1)} %param.9) | copy-start | bytes 1204228
  159.3 7.6 %collective-permute-start.26 = (bf16[16,4096]{1,0:T(8,128)(2,1)S(1)}, bf16[16,4096]{1,0:T(8,128)(2,1)S(1)}, u32[]{:S(2)}, u32[]{:S(2)}) collective-permute-start(bf16[16,4096]{1,0:T(8,128)(2,1)S(1)} %get-tuple-element.12), channel_id=1, source_target_pairs={{0,24},{1,7},{2,26},{3,1},{4,28},{5,3},{6,30},{7,5},{8,0},{9,15},{... | collective-permute-start | bytes 393224 | tf_op jit(solution)/shard_map/ppermute | solution.py:34
  161.3 7.7 %collective-permute-start.30 = (bf16[16,4096]{1,0:T(8,128)(2,1)S(1)}, bf16[16,4096]{1,0:T(8,128)(2,1)S(1)}, u32[]{:S(2)}, u32[]{:S(2)}) collective-permute-start(bf16[16,4096]{1,0:T(8,128)(2,1)S(1)} %get-tuple-element.14), channel_id=1, source_target_pairs={{0,8},{1,3},{2,10},{3,5},{4,12},{5,7},{6,14},{7,1},{8,16},{9,11},{... | collective-permute-start | bytes 393224 | tf_op jit(solution)/shard_map/ppermute | solution.py:34
  162.2 6.7 %collective-permute-start.31 = (bf16[16,4096]{1,0:T(8,128)(2,1)S(1)}, bf16[16,4096]{1,0:T(8,128)(2,1)S(1)}, u32[]{:S(2)}, u32[]{:S(2)}) collective-permute-start(bf16[16,4096]{1,0:T(8,128)(2,1)S(1)} %get-tuple-element.16), channel_id=1, source_target_pairs={{0,16},{1,5},{2,18},{3,7},{4,20},{5,1},{6,22},{7,3},{8,24},{9,13},... | collective-permute-start | bytes 393224 | tf_op jit(solution)/shard_map/ppermute | solution.py:34
  165.4 5.0 %collective-permute-start.32 = (bf16[16,4096]{1,0:T(8,128)(2,1)S(1)}, bf16[16,4096]{1,0:T(8,128)(2,1)S(1)}, u32[]{:S(2)}, u32[]{:S(2)}) collective-permute-start(bf16[16,4096]{1,0:T(8,128)(2,1)S(1)} %get-tuple-element.15), channel_id=1, source_target_pairs={{0,24},{1,7},{2,26},{3,1},{4,28},{5,3},{6,30},{7,5},{8,0},{9,15},{... | collective-permute-start | bytes 393224 | tf_op jit(solution)/shard_map/ppermute | solution.py:34

commit v2 on v0

v2 whole, which is shorter than its diff:
```python
import functools
import math

import jax
import jax.numpy as jnp
import numpy as np
from jax import lax
from jax.experimental import pallas as pl
from jax.experimental.pallas import tpu as pltpu
from jax.sharding import PartitionSpec as P

RING = 4
PLACES = [(x, y, c) for x in range(RING) for y in range(RING) for c in range(2)]
GATHER_SPANS = (3072, 3072, 2048)
OUT_SPANS = (4096, 4096)
LIMIT = 40 * 2**20
BY_ROWS = (((1,), (1,)), ((), ()))


def place(x, y, c):
    return (x % RING) * RING * 2 + (y % RING) * 2 + c


def along_first(d):
    return [
        (place(x, y, c), place(x + d, y, c) if c == 0 else place(x, y + d, c))
        for x, y, c in PLACES
    ]


def along_second(d):
    return [
        (place(x, y, c), place(x + d, y, c) if c == 1 else place(x, y + d, c))
        for x, y, c in PLACES
    ]


SIBLING = [(place(x, y, c), place(x, y, 1 - c)) for x, y, c in PLACES]


def send(value, pairs):
    return lax.ppermute(value, "tensor", pairs)


def from_steps(value, along):
    return send(value, along(-1)), send(value, along(2)), send(value, along(1))


def dot(a, b):
    return jnp.dot(a, b, preferred_element_type=jnp.float32)


def scalar_table():
    def sign(row, column):
        return 1.0 - 2.0 * (bin(row & column).count("1") % 2)

    rows = []
    for x, y, c in PLACES:
        first, second = (x, y) if c == 0 else (y, x)
        row = [1.0 - 2.0 * c]
        row += [sign(first, (first + s) % RING) for s in range(RING)]
        row += [
            sign(second, (second + s) % RING) / math.sqrt(2 * RING * RING) for s in range(RING)
        ]
        rows.append(row + [0.0] * (16 - len(row)))
    return np.array(rows, np.float32)


def spans(widths, total):
    cut = [w * total // sum(widths) for w in widths]
    starts = [sum(cut[:n]) for n in range(len(cut))]
    return list(zip(starts, cut))


def step_of(span):
    for size in (2048, 1536, 1024, 512, 256, 128):
        if span % size == 0 and span // size >= 2:
            return size
    return span


def call(kernel, name, flops, size, **kwargs):
    return pl.pallas_call(
        kernel,
        name=name,
        compiler_params=pltpu.CompilerParams(vmem_limit_bytes=LIMIT),
        cost_estimate=pl.CostEstimate(flops=flops, bytes_accessed=size, transcendentals=0),
        **kwargs,
    )


SCALARS = pl.BlockSpec(memory_space=pltpu.SMEM)


def gate_up(pieces, weights, at, span, sums, finish):
    rows = RING * pieces[0].shape[0]
    units = weights[0].shape[0]
    block = step_of(span)
    steps = span // block
    offset = at // block
    opening, closing = sums is None, finish is not None

    def kernel(*refs):
        refs = list(refs)
        parts, loads = refs[:4], refs[4:8]
        refs = refs[8:]
        before = None if opening else refs.pop(0)
        if closing:
            mixing, scalars, out, held = refs
        else:
            (held,) = refs
        step = pl.program_id(0)
        x = jnp.concatenate([part[...] for part in parts], axis=0)
        for n, load in enumerate(loads):
            product = lax.dot_general(x, load[...], BY_ROWS, preferred_element_type=jnp.float32)

            @pl.when(step == 0)
            def _():
                held[n] = product if opening else before[n] + product

            @pl.when(step > 0)
            def _():
                held[n] = held[n] + product

        if closing:

            @pl.when(step == steps - 1)
            def _():
                local = []
                for n in (0, 2):
                    gate, up = held[n], held[n + 1]
                    hidden = (gate / (1.0 + jnp.exp(-gate)) * up).astype(jnp.bfloat16)
                    local.append(dot(hidden, mixing[...]))
                own, other = local
                turn = scalars[0]
                out[:, :units] = (other + turn * own).astype(jnp.bfloat16)
                out[:, units:] = (own - turn * other).astype(jnp.bfloat16)

    whole = (4, rows, units)
    in_specs = [pl.BlockSpec((rows // RING, block), lambda k: (0, k))] * 4
    in_specs += [pl.BlockSpec((units, block), lambda k: (0, k + offset))] * 4
    operands = [*pieces, *weights]
    if not opening:
        in_specs.append(pl.BlockSpec(whole, lambda k: (0, 0, 0)))
        operands.append(sums)
    if closing:
        mixing, scalars = finish
        in_specs += [pl.BlockSpec(mixing.shape, lambda k: (0, 0)), SCALARS]
        operands += [mixing, scalars]
        extra = dict(
            out_shape=jax.ShapeDtypeStruct((rows, 2 * units), jnp.bfloat16),
            out_specs=pl.BlockSpec((rows, 2 * units), lambda k: (0, 0)),
            scratch_shapes=[pltpu.VMEM(whole, jnp.float32)],
        )
    else:
        extra = dict(
            out_shape=jax.ShapeDtypeStruct(whole, jnp.float32),
            out_specs=pl.BlockSpec(whole, lambda k: (0, 0, 0)),
            input_output_aliases={} if opening else {8: 0},
        )
    return call(
        kernel,
        "gate_up",
        8 * rows * units * span,
        8 * units * span + 2 * rows * span,
        grid=(steps,),
        in_specs=in_specs,
        **extra,
    )(*operands)


def combine(parts, scalars, first_scalar, major):
    rows, width = parts[0].shape
    slot = rows // (RING * RING)

    def kernel(own, one, two, three, factors, out):
        came = (own, one, two, three)
        for i in range(RING):
            for j in range(RING):
                total = 0.0
                for s in range(RING):
                    where = ((i - s) % RING, j) if major else (i, (j - s) % RING)
                    at = (where[0] * RING + where[1]) * slot
                    total = total + factors[first_scalar + s] * came[s][at : at + slot].astype(
                        jnp.float32
                    )
                at = (i * RING + j) * slot
                out[at : at + slot] = total.astype(jnp.bfloat16)

    return call(
        kernel,
        "combine",
        0,
        10 * rows * width,
        in_specs=[pl.BlockSpec(memory_space=pltpu.VMEM)] * 4 + [SCALARS],
        out_specs=pl.BlockSpec(memory_space=pltpu.VMEM),
        out_shape=jax.ShapeDtypeStruct((rows, width), jnp.bfloat16),
    )(*parts, scalars)


def down(value, weight, other, at, span):
    rows = value.shape[0]
    units = weight.shape[0]
    block = step_of(span)
    offset = at // block

    def kernel(held, load, load_other, *outs):
        product = dot(held[:, :units], load[...]) + dot(held[:, units:], load_other[...])
        product = product.astype(jnp.bfloat16)
        for n, out in enumerate(outs):
            out[...] = product[n * (rows // RING) : (n + 1) * (rows // RING)]

    return call(
        kernel,
        "down",
        4 * rows * units * span,
        4 * units * span + 2 * rows * span,
        grid=(span // block,),
        in_specs=[pl.BlockSpec(value.shape, lambda k: (0, 0))]
        + [pl.BlockSpec((units, block), lambda k: (0, k + offset))] * 2,
        out_specs=[pl.BlockSpec((rows // RING, block), lambda k: (0, k))] * RING,
        out_shape=[jax.ShapeDtypeStruct((rows // RING, span), jnp.bfloat16)] * RING,
    )(value, weight, other)


def fold(own, near, onward):
    rows, width = own.shape

    def kernel(own, near, onward, *outs):
        for n, out in enumerate(outs):
            at = slice(n * (rows // RING), (n + 1) * (rows // RING))
            total = (
                own[at].astype(jnp.float32)
                + near[at].astype(jnp.float32)
                + onward[at].astype(jnp.float32)
            )
            out[...] = total.astype(jnp.bfloat16)

    return call(
        kernel,
        "fold",
        0,
        8 * rows * width,
        in_specs=[pl.BlockSpec(memory_space=pltpu.VMEM)] * 3,
        out_specs=[pl.BlockSpec(memory_space=pltpu.VMEM)] * RING,
        out_shape=[jax.ShapeDtypeStruct((rows // RING, width), jnp.bfloat16)] * RING,
    )(own, near, onward)


def body(tokens, gate_weight, up_weight, down_weight, mixing):
    width = tokens.shape[1]
    index = lax.axis_index("tensor")
    scalars = lax.dynamic_index_in_dim(jnp.asarray(scalar_table()), index, keepdims=False)

    gate, up = gate_weight.T, up_weight.T
    near = from_steps(tokens, along_first)
    weights = [gate, up, send(gate, SIBLING), send(up, SIBLING)]
    down_other = send(down_weight, SIBLING)

    sums = None
    cuts = spans(GATHER_SPANS, width)
    for n, (at, span) in enumerate(cuts):
        part = slice(at, at + span)
        block = jnp.concatenate([tokens[:, part]] + [piece[:, part] for piece in near])
        ahead, across, behind = from_steps(block, along_second)
        finish = (mixing, scalars) if n == len(cuts) - 1 else None
        sums = gate_up((block, ahead, across, behind), weights, at, span, sums, finish)

    value = sums
    value = combine((value, *from_steps(value, along_first)), scalars, 1, False)
    value = combine((value, *from_steps(value, along_second)), scalars, 1 + RING, True)

    came = []
    for n, (at, span) in enumerate(spans(OUT_SPANS, width)):
        parts = down(value, down_weight, down_other, at, span)
        forward, back, step = (1, 3, 1) if n % 2 == 0 else (3, 1, -1)
        far = send(parts[2], along_second(step))
        near = send(parts[back], along_second(-step))
        onward = (parts[forward].astype(jnp.float32) + far.astype(jnp.float32)).astype(jnp.bfloat16)
        onward = send(onward, along_second(step))
        total = fold(parts[0], near, onward)
        came.append(
            [
                total[0],
                send(total[1], along_first(1)),
                send(total[2], along_first(2)),
                send(total[3], along_first(-1)),
            ]
        )
    outs = []
    for parts in came:
        outs.append(sum(part.astype(jnp.float32) for part in parts).astype(jnp.bfloat16))
    return jnp.concatenate(outs, axis=1)


def solution(mesh):
    in_specs = (
        P(("dp", "tensor"), None),
        P(None, "tensor"),
        P(None, "tensor"),
        P("tensor", None),
        P(),
    )
    out_specs = P(("dp", "tensor"), None)
    return jax.shard_map(body, mesh=mesh, in_specs=in_specs, out_specs=out_specs, check_vma=False)
```

time: 230 us -> 159 us (0.69)
  waiting for transfers between devices: 149 us -> 77.7 us
  starting transfers between devices: 0.04 us -> 38.2 us
  Pallas kernels: 0 us -> 32.7 us
  blocking collectives: 30.8 us -> 0 us
  matrix products: 29 us -> 0 us
  between operations: 13.5 us -> 0.24 us
  local copies, waits for them, and re-layouts: 3.12 us -> 8.74 us
  other arithmetic: 3.99 us -> 1.18 us
    reduce_scatter x1 -> x0, waiting for transfers between devices: 91 us -> none  [body(): lax.psum_scatter(jnp.dot(rotated_hidden, down_weight, preferred_element_t...]
    ppermute x0 -> x33, waiting for transfers between devices: none -> 77.7 us  [send(): return lax.ppermute(value, 'tensor', pairs)]
    all_gather x1 -> x0, waiting for transfers between devices: 57.6 us -> none  [body(): piece = lax.all_gather(tokens, 'tensor', axis=0, tiled=True)]
    ppermute x0 -> x33, starting transfers between devices: none -> 38.2 us  [send(): return lax.ppermute(value, 'tensor', pairs)]
    pallas_call x0 -> x9, Pallas kernels: none -> 32.7 us  [the longest x3 21.9 us: gate_up(): call(kernel, 'gate_up', 8 * rows * units * span, 8 * units * span + 2 * r...]
    all_to_all x2 -> x0, blocking collectives: 30.8 us -> none  [the longest x1 15.8 us: body(): lax.all_to_all(local_block_values[None].astype(jnp.bfloat16), 'tensor', s...]
    dot_general x4 -> x0, matrix products: 29 us -> none  [the longest x1 9.81 us: body(): jnp.dot(hidden, block_mixing_matrix, preferred_element_type=jnp.float32)]
    unnamed x6 -> x8, local copies, waits for them, and re-layouts: 1.95 us -> 6.17 us
  transfers between devices with their start and end apart: 2 -> 33, of which waited for: 2 -> 18; matrix products, arithmetic and copies ran while one was open for 0% -> 2% of each run, Pallas kernels for 0% -> 18%
where the time goes in v2:
time: 159 us
  waiting for transfers between devices  77.7 us (49%)
  starting transfers between devices  38.2 us (24%)
  Pallas kernels  32.7 us (21%)
  local copies, waits for them, and re-layouts  8.74 us (5%)
    ppermute x33, waiting for transfers between devices, send(): return lax.ppermute(value, 'tensor', pairs)  77.7 us
    ppermute x33, starting transfers between devices, send(): return lax.ppermute(value, 'tensor', pairs)  38.2 us
    pallas_call x3, Pallas kernels, gate_up(): call(kernel, 'gate_up', 8 * rows * units * span, 8 * units * span + 2 * r...  21.9 us
    pallas_call x2, Pallas kernels, down(): call(kernel, 'down', 4 * rows * units * span, 4 * units * span + 2 * rows...  8.69 us
    unnamed x8, local copies, waits for them, and re-layouts  6.17 us
  transfers between devices with their start and end apart: 33, of which 18 were waited for; matrix products, arithmetic and copies ran while one was open for 2% of the time, Pallas kernels for 18%

profile of v2, /device:TPU:0, one launch (start us, length us, event | category | flops | bytes accessed | tf_op | source)
XLA Modules:
  0.0 158.9 jit_solution(3189961410196982209)
XLA Ops:
  0.0 0.5 collective-permute-start.7
  0.5 2.8 %collective-permute-start = (bf16[16,8192]{1,0:T(8,128)(2,1)}, bf16[16,8192]{1,0:T(8,128)(2,1)S(1)}, u32[]{:S(2)}, u32[]{:S(2)}) collective-permute-start(bf16[16,8192]{1,0:T(8,128)(2,1)} %param.6), channel_id=1, source_target_pairs={{0,24},{1,7},{2,26},{3,1},{4,28},{5,3},{6,30},{7,5},{8,0},{9,15},{... | collective-permute-start | bytes 786440 | tf_op jit(solution)/shard_map/ppermute | solution.py:42
  3.4 0.8 collective-permute-start.1
  4.2 1.0 fusion
  5.1 5.2 %collective-permute-done = bf16[16,8192]{1,0:T(8,128)(2,1)S(1)} collective-permute-done((bf16[16,8192]{1,0:T(8,128)(2,1)}, bf16[16,8192]{1,0:T(8,128)(2,1)S(1)}, u32[]{:S(2)}, u32[]{:S(2)}) %collective-permute-start) | collective-permute-done | bytes 262176 | tf_op jit(solution)/shard_map/ppermute | solution.py:42
  10.4 1.1 collective-permute-done.1
  11.5 7.1 %collective-permute-done.2 = bf16[16,8192]{1,0:T(8,128)(2,1)S(1)} collective-permute-done((bf16[16,8192]{1,0:T(8,128)(2,1)}, bf16[16,8192]{1,0:T(8,128)(2,1)S(1)}, u32[]{:S(2)}, u32[]{:S(2)}) %collective-permute-start.2) | collective-permute-done | bytes 262176 | tf_op jit(solution)/shard_map/ppermute | solution.py:42
  18.6 3.1 %collective-permute-start.11 = (bf16[64,3072]{1,0:T(8,128)(2,1)S(1)}, bf16[64,3072]{1,0:T(8,128)(2,1)S(1)}, u32[]{:S(2)}, u32[]{:S(2)}) collective-permute-start(bf16[64,3072]{1,0:T(8,128)(2,1)S(1)} %pad_maximum_fusion.1.refs_0_), channel_id=1, source_target_pairs={{0,6},{1,25},{2,0},{3,27},{4,2},{5,29},{6,4},{7,31},{8,14},{9,1},{... | collective-permute-start | bytes 1179656 | tf_op jit(solution)/shard_map/ppermute | solution.py:42
  21.7 0.6 collective-permute-start.12
  22.3 8.9 %collective-permute-done.11.refs_1_ = bf16[64,3072]{1,0:T(8,128)(2,1)S(1)} collective-permute-done((bf16[64,3072]{1,0:T(8,128)(2,1)S(1)}, bf16[64,3072]{1,0:T(8,128)(2,1)S(1)}, u32[]{:S(2)}, u32[]{:S(2)}) %collective-permute-start.11) | collective-permute-done | bytes 393248 | tf_op jit(solution)/shard_map/ppermute | solution.py:42
  31.2 0.7 dynamic-slice_bitcast_fusion.refs_10_.factors
  31.9 0.8 slice.36
  32.8 0.4 collective-permute-start.10
  33.2 7.4 %collective-permute-done.13.refs_3_ = bf16[64,3072]{1,0:T(8,128)(2,1)S(1)} collective-permute-done((bf16[64,3072]{1,0:T(8,128)(2,1)S(1)}, bf16[64,3072]{1,0:T(8,128)(2,1)S(1)}, u32[]{:S(2)}, u32[]{:S(2)}) %collective-permute-start.13) | collective-permute-done | bytes 393248 | tf_op jit(solution)/shard_map/ppermute | solution.py:42
  40.6 2.0 %collective-permute-start.8 = (bf16[64,3072]{1,0:T(8,128)(2,1)S(1)}, bf16[64,3072]{1,0:T(8,128)(2,1)S(1)}, u32[]{:S(2)}, u32[]{:S(2)}) collective-permute-start(bf16[64,3072]{1,0:T(8,128)(2,1)S(1)} %pad_maximum_fusion.refs_0_), channel_id=1, source_target_pairs={{0,6},{1,25},{2,0},{3,27},{4,2},{5,29},{6,4},{7,31},{8,14},{9,1},{... | collective-permute-start | bytes 1179656 | tf_op jit(solution)/shard_map/ppermute | solution.py:42
  42.7 2.7 %collective-permute-start.3 = (bf16[64,2048]{1,0:T(8,128)(2,1)S(1)}, bf16[64,2048]{1,0:T(8,128)(2,1)S(1)}, u32[]{:S(2)}, u32[]{:S(2)}) collective-permute-start(bf16[64,2048]{1,0:T(8,128)(2,1)S(1)} %pad_maximum_fusion.2.refs_0_), channel_id=1, source_target_pairs={{0,6},{1,25},{2,0},{3,27},{4,2},{5,29},{6,4},{7,31},{8,14},{9,1},{... | collective-permute-start | bytes 786440 | tf_op jit(solution)/shard_map/ppermute | solution.py:42
  45.4 3.1 %copy-done = bf16[8192,448]{0,1:T(8,128)(2,1)S(1)} copy-done((bf16[8192,448]{0,1:T(8,128)(2,1)S(1)}, bf16[8192,448]{0,1:T(8,128)(2,1)}, u32[]{:S(2)}) %copy-start) | copy-done | bytes 7340056
  48.5 7.6 %gate_up.3.refs_8_ = f32[4,256,448]{2,1,0:T(8,128)S(1)} custom-call(bf16[64,3072]{1,0:T(8,128)(2,1)S(1)} %pad_maximum_fusion.1.refs_0_, bf16[64,3072]{1,0:T(8,128)(2,1)S(1)} %collective-permute-done.11.refs_1_, bf16[64,3072]{1,0:T(8,128)(2,1)S(1)} %collective-permute-done.12.refs_2_, bf16[64,3072]{1,0:T(8,128)(2,1)S(1)} %collective-permute-done.13.refs_3_, ...), custom_call_target="tpu_custom_call" | custom-call | flops 2818572288 | bytes 12582912 | tf_op jit(solution)/shard_map/gate_up/pallas_call | solution.py:161
  56.1 1.0 collective-permute-start.4
  57.1 1.4 collective-permute-start.5
  58.5 7.7 %gate_up.4.refs_8_ = f32[4,256,448]{2,1,0:T(8,128)S(1)} custom-call(bf16[64,3072]{1,0:T(8,128)(2,1)S(1)} %pad_maximum_fusion.refs_0_, bf16[64,3072]{1,0:T(8,128)(2,1)S(1)} %collective-permute-done.8.refs_1_, bf16[64,3072]{1,0:T(8,128)(2,1)S(1)} %collective-permute-done.9.refs_2_, ...), custom_call_target="tpu_custom_call", output_to_operand_aliasing={{}: (8, {})} | custom-call | flops 2818572288 | bytes 12582912 | tf_op jit(solution)/shard_map/gate_up/pallas_call | solution.py:161
  66.2 0.7 collective-permute-done.5.refs_3_
  66.9 6.6 %gate_up.5.own = bf16[256,896]{1,0:T(8,128)(2,1)S(1)} custom-call(bf16[64,2048]{1,0:T(8,128)(2,1)S(1)} %pad_maximum_fusion.2.refs_0_, bf16[64,2048]{1,0:T(8,128)(2,1)S(1)} %collective-permute-done.3.refs_1_, bf16[64,2048]{1,0:T(8,128)(2,1)S(1)} %collective-permute-done.4.refs_2_, bf16[64,2048]{1,0:T(8,128)(2,1)S(1)} %collective-permute-done.5.refs_3_, ...), custom_call_target="tpu_custom_call" | custom-call | flops 1879048192 | bytes 8388608 | tf_op jit(solution)/shard_map/gate_up/pallas_call | solution.py:161
  73.5 2.3 %collective-permute-start.14 = (bf16[256,896]{1,0:T(8,128)(2,1)S(1)}, bf16[256,896]{1,0:T(8,128)(2,1)S(1)}, u32[]{:S(2)}, u32[]{:S(2)}) collective-permute-start(bf16[256,896]{1,0:T(8,128)(2,1)S(1)} %gate_up.5.own), channel_id=1, source_target_pairs={{0,24},{1,7},{2,26},{3,1},{4,28},{5,3},{6,30},{7,5},{8,0},{9,15},{... | collective-permute-start | bytes 1376264 | tf_op jit(solution)/shard_map/ppermute | solution.py:42
  75.8 0.9 collective-permute-start.16
  76.8 10.0 %collective-permute-done.14.one = bf16[256,896]{1,0:T(8,128)(2,1)S(1)} collective-permute-done((bf16[256,896]{1,0:T(8,128)(2,1)S(1)}, bf16[256,896]{1,0:T(8,128)(2,1)S(1)}, u32[]{:S(2)}, u32[]{:S(2)}) %collective-permute-start.14) | collective-permute-done | bytes 458784 | tf_op jit(solution)/shard_map/ppermute | solution.py:42
  86.8 3.7 %collective-permute-done.16.three = bf16[256,896]{1,0:T(8,128)(2,1)S(1)} collective-permute-done((bf16[256,896]{1,0:T(8,128)(2,1)S(1)}, bf16[256,896]{1,0:T(8,128)(2,1)S(1)}, u32[]{:S(2)}, u32[]{:S(2)}) %collective-permute-start.16) | collective-permute-done | bytes 458784 | tf_op jit(solution)/shard_map/ppermute | solution.py:42
  90.4 0.9 combine.2.own
  91.3 1.3 collective-permute-start.17
  92.6 2.5 %collective-permute-start.18 = (bf16[256,896]{1,0:T(8,128)(2,1)S(1)}, bf16[256,896]{1,0:T(8,128)(2,1)S(1)}, u32[]{:S(2)}, u32[]{:S(2)}) collective-permute-start(bf16[256,896]{1,0:T(8,128)(2,1)S(1)} %combine.2.own), channel_id=1, source_target_pairs={{0,4},{1,17},{2,6},{3,19},{4,0},{5,21},{6,2},{7,23},{8,12},{9,25},... | collective-permute-start | bytes 1376264 | tf_op jit(solution)/shard_map/ppermute | solution.py:42
  95.1 4.8 %collective-permute-done.17.one = bf16[256,896]{1,0:T(8,128)(2,1)S(1)} collective-permute-done((bf16[256,896]{1,0:T(8,128)(2,1)S(1)}, bf16[256,896]{1,0:T(8,128)(2,1)S(1)}, u32[]{:S(2)}, u32[]{:S(2)}) %collective-permute-start.17) | collective-permute-done | bytes 458784 | tf_op jit(solution)/shard_map/ppermute | solution.py:42
  99.9 2.8 %collective-permute-done.18.two = bf16[256,896]{1,0:T(8,128)(2,1)S(1)} collective-permute-done((bf16[256,896]{1,0:T(8,128)(2,1)S(1)}, bf16[256,896]{1,0:T(8,128)(2,1)S(1)}, u32[]{:S(2)}, u32[]{:S(2)}) %collective-permute-start.18) | collective-permute-done | bytes 458784 | tf_op jit(solution)/shard_map/ppermute | solution.py:42
  102.7 4.8 %collective-permute-done.19.three = bf16[256,896]{1,0:T(8,128)(2,1)S(1)} collective-permute-done((bf16[256,896]{1,0:T(8,128)(2,1)S(1)}, bf16[256,896]{1,0:T(8,128)(2,1)S(1)}, u32[]{:S(2)}, u32[]{:S(2)}) %collective-permute-start.19) | collective-permute-done | bytes 458784 | tf_op jit(solution)/shard_map/ppermute | solution.py:42
  107.5 0.9 combine.3.held
  108.4 0.0 copy-start.2
  108.4 3.1 %copy-done.2 = bf16[448,8192]{1,0:T(8,128)(2,1)S(1)} copy-done((bf16[448,8192]{1,0:T(8,128)(2,1)S(1)}, bf16[448,8192]{1,0:T(8,128)(2,1)}, u32[]{:S(2)}) %copy-start.2) | copy-done | bytes 7340056
  111.5 4.3 %down.2 = (bf16[64,4096]{1,0:T(8,128)(2,1)S(1)}, bf16[64,4096]{1,0:T(8,128)(2,1)S(1)}, bf16[64,4096]{1,0:T(8,128)(2,1)S(1)}, bf16[64,4096]{1,0:T(8,128)(2,1)S(1)}) custom-call(bf16[256,896]{1,0:T(8,128)(2,1)S(1)} %combine.3.held, bf16[448,8192]{1,0:T(8,128)(2,1)S(1)} %copy-done.2, bf16[448,8192]{1,0:T(8,128)(2,1)} %collective-permute-done.20.load_other), custom_call_target="tpu_custom_call" | custom-call | flops 1879048192 | bytes 9437184 | tf_op jit(solution)/shard_map/down/pallas_call | solution.py:213
  115.8 1.1 collective-permute-start.22
  116.9 2.2 %collective-permute-start.21 = (bf16[64,4096]{1,0:T(8,128)(2,1)S(1)}, bf16[64,4096]{1,0:T(8,128)(2,1)S(1)}, u32[]{:S(2)}, u32[]{:S(2)}) collective-permute-start(bf16[64,4096]{1,0:T(8,128)(2,1)S(1)} %get-tuple-element.22), channel_id=1, source_target_pairs={{0,6},{1,25},{2,0},{3,27},{4,2},{5,29},{6,4},{7,31},{8,14},{9,1},{... | collective-permute-start | bytes 1572872 | tf_op jit(solution)/shard_map/ppermute | solution.py:42
  119.1 4.3 %down.3 = (bf16[64,4096]{1,0:T(8,128)(2,1)S(1)}, bf16[64,4096]{1,0:T(8,128)(2,1)S(1)}, bf16[64,4096]{1,0:T(8,128)(2,1)S(1)}, bf16[64,4096]{1,0:T(8,128)(2,1)S(1)}) custom-call(bf16[256,896]{1,0:T(8,128)(2,1)S(1)} %combine.3.held, bf16[448,8192]{1,0:T(8,128)(2,1)S(1)} %copy-done.2, bf16[448,8192]{1,0:T(8,128)(2,1)} %collective-permute-done.20.load_other), custom_call_target="tpu_custom_call" | custom-call | flops 1879048192 | bytes 9437184 | tf_op jit(solution)/shard_map/down/pallas_call | solution.py:213
  123.5 0.1 collective-permute-start.28
  123.6 2.0 %collective-permute-start.27 = (bf16[64,4096]{1,0:T(8,128)(2,1)S(1)}, bf16[64,4096]{1,0:T(8,128)(2,1)S(1)}, u32[]{:S(2)}, u32[]{:S(2)}) collective-permute-start(bf16[64,4096]{1,0:T(8,128)(2,1)S(1)} %get-tuple-element.30), channel_id=1, source_target_pairs={{0,2},{1,9},{2,4},{3,11},{4,6},{5,13},{6,0},{7,15},{8,10},{9,17},{... | collective-permute-start | bytes 1572872 | tf_op jit(solution)/shard_map/ppermute | solution.py:42
  125.6 0.7 collective-permute-done.22
  126.3 0.1 add_convert_fusion.1
  126.4 0.1 collective-permute-start.23
  126.5 6.2 %collective-permute-done.28 = bf16[64,4096]{1,0:T(8,128)(2,1)S(1)} collective-permute-done((bf16[64,4096]{1,0:T(8,128)(2,1)S(1)}, bf16[64,4096]{1,0:T(8,128)(2,1)S(1)}, u32[]{:S(2)}, u32[]{:S(2)}) %collective-permute-start.28) | collective-permute-done | bytes 524320 | tf_op jit(solution)/shard_map/ppermute | solution.py:42
  132.7 0.1 add_convert_fusion
  132.9 2.5 %collective-permute-start.29 = (bf16[64,4096]{1,0:T(8,128)(2,1)S(1)}, bf16[64,4096]{1,0:T(8,128)(2,1)S(1)}, u32[]{:S(2)}, u32[]{:S(2)}) collective-permute-start(bf16[64,4096]{1,0:T(8,128)(2,1)S(1)} %add_convert_fusion), channel_id=1, source_target_pairs={{0,6},{1,25},{2,0},{3,27},{4,2},{5,29},{6,4},{7,31},{8,14},{9,1},{... | collective-permute-start | bytes 1572872 | tf_op jit(solution)/shard_map/ppermute | solution.py:42
  135.3 9.9 %collective-permute-done.23.onward = bf16[64,4096]{1,0:T(8,128)(2,1)S(1)} collective-permute-done((bf16[64,4096]{1,0:T(8,128)(2,1)S(1)}, bf16[64,4096]{1,0:T(8,128)(2,1)S(1)}, u32[]{:S(2)}, u32[]{:S(2)}) %collective-permute-start.23) | collective-permute-done | bytes 524320 | tf_op jit(solution)/shard_map/ppermute | solution.py:42
  145.3 0.2 fold.2
  145.4 0.1 collective-permute-start.24
  145.5 2.4 %collective-permute-start.25 = (bf16[16,4096]{1,0:T(8,128)(2,1)S(1)}, bf16[16,4096]{1,0:T(8,128)(2,1)S(1)}, u32[]{:S(2)}, u32[]{:S(2)}) collective-permute-start(bf16[16,4096]{1,0:T(8,128)(2,1)S(1)} %get-tuple-element.27), channel_id=1, source_target_pairs={{0,16},{1,5},{2,18},{3,7},{4,20},{5,1},{6,22},{7,3},{8,24},{9,13},... | collective-permute-start | bytes 393224 | tf_op jit(solution)/shard_map/ppermute | solution.py:42
  147.9 0.9 collective-permute-start.26
  148.8 0.2 fold.3
  149.0 1.2 collective-permute-start.30
  150.2 1.9 %collective-permute-start.31 = (bf16[16,4096]{1,0:T(8,128)(2,1)S(1)}, bf16[16,4096]{1,0:T(8,128)(2,1)S(1)}, u32[]{:S(2)}, u32[]{:S(2)}) collective-permute-start(bf16[16,4096]{1,0:T(8,128)(2,1)S(1)} %get-tuple-element.35), channel_id=1, source_target_pairs={{0,16},{1,5},{2,18},{3,7},{4,20},{5,1},{6,22},{7,3},{8,24},{9,13},... | collective-permute-start | bytes 393224 | tf_op jit(solution)/shard_map/ppermute | solution.py:42
  152.0 1.1 collective-permute-done.24
  153.1 1.5 collective-permute-start.32
  154.6 0.1 add_convert_fusion.3
  154.7 0.5 collective-permute-done.30
  155.2 1.4 collective-permute-done.31
  156.7 1.4 collective-permute-done.32
  158.1 0.1 add_convert_fusion.2
  158.1 0.7 pad_maximum_fusion.3
  (36 shorter events, 0.2 us)
Async XLA Ops:
  0.0 42.6 %collective-permute-start.6 = (bf16[448,8192]{1,0:T(8,128)(2,1)}, bf16[448,8192]{1,0:T(8,128)(2,1)}, u32[]{:S(2)}, u32[]{:S(2)}) collective-permute-start(bf16[448,8192]{1,0:T(8,128)(2,1)} %bitcast.4), channel_id=1, source_target_pairs={{0,1},{1,0},{2,3},{3,2},{4,5},{5,4},{6,7},{7,6},{8,9},{9,8},{10,11... | collective-permute-start | bytes 22020104 | tf_op jit(solution)/shard_map/ppermute | solution.py:42
  0.0 42.7 %collective-permute-start.7 = (bf16[448,8192]{1,0:T(8,128)(2,1)}, bf16[448,8192]{1,0:T(8,128)(2,1)}, u32[]{:S(2)}, u32[]{:S(2)}) collective-permute-start(bf16[448,8192]{1,0:T(8,128)(2,1)} %bitcast.8), channel_id=1, source_target_pairs={{0,1},{1,0},{2,3},{3,2},{4,5},{5,4},{6,7},{7,6},{8,9},{9,8},{10,11... | collective-permute-start | bytes 22020104 | tf_op jit(solution)/shard_map/ppermute | solution.py:42
  0.5 107.9 %collective-permute-start.20 = (bf16[448,8192]{1,0:T(8,128)(2,1)}, bf16[448,8192]{1,0:T(8,128)(2,1)}, u32[]{:S(2)}, u32[]{:S(2)}) collective-permute-start(bf16[448,8192]{1,0:T(8,128)(2,1)} %load.3), channel_id=1, source_target_pairs={{0,1},{1,0},{2,3},{3,2},{4,5},{5,4},{6,7},{7,6},{8,9},{9,8},{10,11... | collective-permute-start | bytes 22020104 | tf_op jit(solution)/shard_map/ppermute | solution.py:42
  0.5 9.9 %collective-permute-start = (bf16[16,8192]{1,0:T(8,128)(2,1)}, bf16[16,8192]{1,0:T(8,128)(2,1)S(1)}, u32[]{:S(2)}, u32[]{:S(2)}) collective-permute-start(bf16[16,8192]{1,0:T(8,128)(2,1)} %param.6), channel_id=1, source_target_pairs={{0,24},{1,7},{2,26},{3,1},{4,28},{5,3},{6,30},{7,5},{8,0},{9,15},{... | collective-permute-start | bytes 786440 | tf_op jit(solution)/shard_map/ppermute | solution.py:42
  3.4 8.1 %collective-permute-start.1 = (bf16[16,8192]{1,0:T(8,128)(2,1)}, bf16[16,8192]{1,0:T(8,128)(2,1)S(1)}, u32[]{:S(2)}, u32[]{:S(2)}) collective-permute-start(bf16[16,8192]{1,0:T(8,128)(2,1)} %param.6), channel_id=1, source_target_pairs={{0,16},{1,5},{2,18},{3,7},{4,20},{5,1},{6,22},{7,3},{8,24},{9,13},... | collective-permute-start | bytes 786440 | tf_op jit(solution)/shard_map/ppermute | solution.py:42
  10.4 8.1 %collective-permute-start.2 = (bf16[16,8192]{1,0:T(8,128)(2,1)}, bf16[16,8192]{1,0:T(8,128)(2,1)S(1)}, u32[]{:S(2)}, u32[]{:S(2)}) collective-permute-start(bf16[16,8192]{1,0:T(8,128)(2,1)} %param.6), channel_id=1, source_target_pairs={{0,8},{1,3},{2,10},{3,5},{4,12},{5,7},{6,14},{7,1},{8,16},{9,11},{... | collective-permute-start | bytes 786440 | tf_op jit(solution)/shard_map/ppermute | solution.py:42
  18.6 12.6 %collective-permute-start.11 = (bf16[64,3072]{1,0:T(8,128)(2,1)S(1)}, bf16[64,3072]{1,0:T(8,128)(2,1)S(1)}, u32[]{:S(2)}, u32[]{:S(2)}) collective-permute-start(bf16[64,3072]{1,0:T(8,128)(2,1)S(1)} %pad_maximum_fusion.1.refs_0_), channel_id=1, source_target_pairs={{0,6},{1,25},{2,0},{3,27},{4,2},{5,29},{6,4},{7,31},{8,14},{9,1},{... | collective-permute-start | bytes 1179656 | tf_op jit(solution)/shard_map/ppermute | solution.py:42
  21.7 11.1 %collective-permute-start.12 = (bf16[64,3072]{1,0:T(8,128)(2,1)S(1)}, bf16[64,3072]{1,0:T(8,128)(2,1)S(1)}, u32[]{:S(2)}, u32[]{:S(2)}) collective-permute-start(bf16[64,3072]{1,0:T(8,128)(2,1)S(1)} %pad_maximum_fusion.1.refs_0_), channel_id=1, source_target_pairs={{0,4},{1,17},{2,6},{3,19},{4,0},{5,21},{6,2},{7,23},{8,12},{9,25},... | collective-permute-start | bytes 1179656 | tf_op jit(solution)/shard_map/ppermute | solution.py:42
  31.2 9.4 %collective-permute-start.13 = (bf16[64,3072]{1,0:T(8,128)(2,1)S(1)}, bf16[64,3072]{1,0:T(8,128)(2,1)S(1)}, u32[]{:S(2)}, u32[]{:S(2)}) collective-permute-start(bf16[64,3072]{1,0:T(8,128)(2,1)S(1)} %pad_maximum_fusion.1.refs_0_), channel_id=1, source_target_pairs={{0,2},{1,9},{2,4},{3,11},{4,6},{5,13},{6,0},{7,15},{8,10},{9,17},{... | collective-permute-start | bytes 1179656 | tf_op jit(solution)/shard_map/ppermute | solution.py:42
  32.8 23.3 %collective-permute-start.10 = (bf16[64,3072]{1,0:T(8,128)(2,1)S(1)}, bf16[64,3072]{1,0:T(8,128)(2,1)S(1)}, u32[]{:S(2)}, u32[]{:S(2)}) collective-permute-start(bf16[64,3072]{1,0:T(8,128)(2,1)S(1)} %pad_maximum_fusion.refs_0_), channel_id=1, source_target_pairs={{0,2},{1,9},{2,4},{3,11},{4,6},{5,13},{6,0},{7,15},{8,10},{9,17},{... | collective-permute-start | bytes 1179656 | tf_op jit(solution)/shard_map/ppermute | solution.py:42
  40.6 16.5 %collective-permute-start.8 = (bf16[64,3072]{1,0:T(8,128)(2,1)S(1)}, bf16[64,3072]{1,0:T(8,128)(2,1)S(1)}, u32[]{:S(2)}, u32[]{:S(2)}) collective-permute-start(bf16[64,3072]{1,0:T(8,128)(2,1)S(1)} %pad_maximum_fusion.refs_0_), channel_id=1, source_target_pairs={{0,6},{1,25},{2,0},{3,27},{4,2},{5,29},{6,4},{7,31},{8,14},{9,1},{... | collective-permute-start | bytes 1179656 | tf_op jit(solution)/shard_map/ppermute | solution.py:42
  42.6 15.9 %collective-permute-start.9 = (bf16[64,3072]{1,0:T(8,128)(2,1)S(1)}, bf16[64,3072]{1,0:T(8,128)(2,1)S(1)}, u32[]{:S(2)}, u32[]{:S(2)}) collective-permute-start(bf16[64,3072]{1,0:T(8,128)(2,1)S(1)} %pad_maximum_fusion.refs_0_), channel_id=1, source_target_pairs={{0,4},{1,17},{2,6},{3,19},{4,0},{5,21},{6,2},{7,23},{8,12},{9,25},... | collective-permute-start | bytes 1179656 | tf_op jit(solution)/shard_map/ppermute | solution.py:42
  42.7 23.5 %collective-permute-start.3 = (bf16[64,2048]{1,0:T(8,128)(2,1)S(1)}, bf16[64,2048]{1,0:T(8,128)(2,1)S(1)}, u32[]{:S(2)}, u32[]{:S(2)}) collective-permute-start(bf16[64,2048]{1,0:T(8,128)(2,1)S(1)} %pad_maximum_fusion.2.refs_0_), channel_id=1, source_target_pairs={{0,6},{1,25},{2,0},{3,27},{4,2},{5,29},{6,4},{7,31},{8,14},{9,1},{... | collective-permute-start | bytes 786440 | tf_op jit(solution)/shard_map/ppermute | solution.py:42
  45.4 3.1 %copy-start = (bf16[8192,448]{0,1:T(8,128)(2,1)S(1)}, bf16[8192,448]{0,1:T(8,128)(2,1)}, u32[]{:S(2)}) copy-start(bf16[8192,448]{0,1:T(8,128)(2,1)} %param.7) | copy-start | bytes 22020100
  48.5 10.0 %copy-start.1 = (bf16[8192,448]{0,1:T(8,128)(2,1)S(1)}, bf16[8192,448]{0,1:T(8,128)(2,1)}, u32[]{:S(2)}) copy-start(bf16[8192,448]{0,1:T(8,128)(2,1)} %param.7) | copy-start | bytes 22020100
  56.1 10.8 %copy-start.3 = (bf16[448,448]{1,0:T(8,128)(2,1)S(1)}, bf16[448,448]{1,0:T(8,128)(2,1)}, u32[]{:S(2)}) copy-start(bf16[448,448]{1,0:T(8,128)(2,1)} %refs_9_.1) | copy-start | bytes 1204228
  56.1 10.1 %collective-permute-start.4 = (bf16[64,2048]{1,0:T(8,128)(2,1)S(1)}, bf16[64,2048]{1,0:T(8,128)(2,1)S(1)}, u32[]{:S(2)}, u32[]{:S(2)}) collective-permute-start(bf16[64,2048]{1,0:T(8,128)(2,1)S(1)} %pad_maximum_fusion.2.refs_0_), channel_id=1, source_target_pairs={{0,4},{1,17},{2,6},{3,19},{4,0},{5,21},{6,2},{7,23},{8,12},{9,25},... | collective-permute-start | bytes 786440 | tf_op jit(solution)/shard_map/ppermute | solution.py:42
  57.1 9.8 %collective-permute-start.5 = (bf16[64,2048]{1,0:T(8,128)(2,1)S(1)}, bf16[64,2048]{1,0:T(8,128)(2,1)S(1)}, u32[]{:S(2)}, u32[]{:S(2)}) collective-permute-start(bf16[64,2048]{1,0:T(8,128)(2,1)S(1)} %pad_maximum_fusion.2.refs_0_), channel_id=1, source_target_pairs={{0,2},{1,9},{2,4},{3,11},{4,6},{5,13},{6,0},{7,15},{8,10},{9,17},{... | collective-permute-start | bytes 786440 | tf_op jit(solution)/shard_map/ppermute | solution.py:42
  73.5 13.2 %collective-permute-start.14 = (bf16[256,896]{1,0:T(8,128)(2,1)S(1)}, bf16[256,896]{1,0:T(8,128)(2,1)S(1)}, u32[]{:S(2)}, u32[]{:S(2)}) collective-permute-start(bf16[256,896]{1,0:T(8,128)(2,1)S(1)} %gate_up.5.own), channel_id=1, source_target_pairs={{0,24},{1,7},{2,26},{3,1},{4,28},{5,3},{6,30},{7,5},{8,0},{9,15},{... | collective-permute-start | bytes 1376264 | tf_op jit(solution)/shard_map/ppermute | solution.py:42
  75.8 10.9 %collective-permute-start.15 = (bf16[256,896]{1,0:T(8,128)(2,1)S(1)}, bf16[256,896]{1,0:T(8,128)(2,1)S(1)}, u32[]{:S(2)}, u32[]{:S(2)}) collective-permute-start(bf16[256,896]{1,0:T(8,128)(2,1)S(1)} %gate_up.5.own), channel_id=1, source_target_pairs={{0,16},{1,5},{2,18},{3,7},{4,20},{5,1},{6,22},{7,3},{8,24},{9,13},... | collective-permute-start | bytes 1376264 | tf_op jit(solution)/shard_map/ppermute | solution.py:42
  75.8 14.6 %collective-permute-start.16 = (bf16[256,896]{1,0:T(8,128)(2,1)S(1)}, bf16[256,896]{1,0:T(8,128)(2,1)S(1)}, u32[]{:S(2)}, u32[]{:S(2)}) collective-permute-start(bf16[256,896]{1,0:T(8,128)(2,1)S(1)} %gate_up.5.own), channel_id=1, source_target_pairs={{0,8},{1,3},{2,10},{3,5},{4,12},{5,7},{6,14},{7,1},{8,16},{9,11},{... | collective-permute-start | bytes 1376264 | tf_op jit(solution)/shard_map/ppermute | solution.py:42
  91.3 8.5 %collective-permute-start.17 = (bf16[256,896]{1,0:T(8,128)(2,1)S(1)}, bf16[256,896]{1,0:T(8,128)(2,1)S(1)}, u32[]{:S(2)}, u32[]{:S(2)}) collective-permute-start(bf16[256,896]{1,0:T(8,128)(2,1)S(1)} %combine.2.own), channel_id=1, source_target_pairs={{0,6},{1,25},{2,0},{3,27},{4,2},{5,29},{6,4},{7,31},{8,14},{9,1},{... | collective-permute-start | bytes 1376264 | tf_op jit(solution)/shard_map/ppermute | solution.py:42
  92.6 10.1 %collective-permute-start.18 = (bf16[256,896]{1,0:T(8,128)(2,1)S(1)}, bf16[256,896]{1,0:T(8,128)(2,1)S(1)}, u32[]{:S(2)}, u32[]{:S(2)}) collective-permute-start(bf16[256,896]{1,0:T(8,128)(2,1)S(1)} %combine.2.own), channel_id=1, source_target_pairs={{0,4},{1,17},{2,6},{3,19},{4,0},{5,21},{6,2},{7,23},{8,12},{9,25},... | collective-permute-start | bytes 1376264 | tf_op jit(solution)/shard_map/ppermute | solution.py:42
  95.1 12.4 %collective-permute-start.19 = (bf16[256,896]{1,0:T(8,128)(2,1)S(1)}, bf16[256,896]{1,0:T(8,128)(2,1)S(1)}, u32[]{:S(2)}, u32[]{:S(2)}) collective-permute-start(bf16[256,896]{1,0:T(8,128)(2,1)S(1)} %combine.2.own), channel_id=1, source_target_pairs={{0,2},{1,9},{2,4},{3,11},{4,6},{5,13},{6,0},{7,15},{8,10},{9,17},{... | collective-permute-start | bytes 1376264 | tf_op jit(solution)/shard_map/ppermute | solution.py:42
  108.4 3.1 %copy-start.2 = (bf16[448,8192]{1,0:T(8,128)(2,1)S(1)}, bf16[448,8192]{1,0:T(8,128)(2,1)}, u32[]{:S(2)}) copy-start(bf16[448,8192]{1,0:T(8,128)(2,1)} %load.3) | copy-start | bytes 22020100
  115.8 10.5 %collective-permute-start.22 = (bf16[64,4096]{1,0:T(8,128)(2,1)S(1)}, bf16[64,4096]{1,0:T(8,128)(2,1)S(1)}, u32[]{:S(2)}, u32[]{:S(2)}) collective-permute-start(bf16[64,4096]{1,0:T(8,128)(2,1)S(1)} %get-tuple-element.24), channel_id=1, source_target_pairs={{0,2},{1,9},{2,4},{3,11},{4,6},{5,13},{6,0},{7,15},{8,10},{9,17},{... | collective-permute-start | bytes 1572872 | tf_op jit(solution)/shard_map/ppermute | solution.py:42
  116.9 18.4 %collective-permute-start.21 = (bf16[64,4096]{1,0:T(8,128)(2,1)S(1)}, bf16[64,4096]{1,0:T(8,128)(2,1)S(1)}, u32[]{:S(2)}, u32[]{:S(2)}) collective-permute-start(bf16[64,4096]{1,0:T(8,128)(2,1)S(1)} %get-tuple-element.22), channel_id=1, source_target_pairs={{0,6},{1,25},{2,0},{3,27},{4,2},{5,29},{6,4},{7,31},{8,14},{9,1},{... | collective-permute-start | bytes 1572872 | tf_op jit(solution)/shard_map/ppermute | solution.py:42
  123.5 9.2 %collective-permute-start.28 = (bf16[64,4096]{1,0:T(8,128)(2,1)S(1)}, bf16[64,4096]{1,0:T(8,128)(2,1)S(1)}, u32[]{:S(2)}, u32[]{:S(2)}) collective-permute-start(bf16[64,4096]{1,0:T(8,128)(2,1)S(1)} %get-tuple-element.32), channel_id=1, source_target_pairs={{0,6},{1,25},{2,0},{3,27},{4,2},{5,29},{6,4},{7,31},{8,14},{9,1},{... | collective-permute-start | bytes 1572872 | tf_op jit(solution)/shard_map/ppermute | solution.py:42
  123.6 25.2 %collective-permute-start.27 = (bf16[64,4096]{1,0:T(8,128)(2,1)S(1)}, bf16[64,4096]{1,0:T(8,128)(2,1)S(1)}, u32[]{:S(2)}, u32[]{:S(2)}) collective-permute-start(bf16[64,4096]{1,0:T(8,128)(2,1)S(1)} %get-tuple-element.30), channel_id=1, source_target_pairs={{0,2},{1,9},{2,4},{3,11},{4,6},{5,13},{6,0},{7,15},{8,10},{9,17},{... | collective-permute-start | bytes 1572872 | tf_op jit(solution)/shard_map/ppermute | solution.py:42
  126.4 18.9 %collective-permute-start.23 = (bf16[64,4096]{1,0:T(8,128)(2,1)S(1)}, bf16[64,4096]{1,0:T(8,128)(2,1)S(1)}, u32[]{:S(2)}, u32[]{:S(2)}) collective-permute-start(bf16[64,4096]{1,0:T(8,128)(2,1)S(1)} %add_convert_fusion.1), channel_id=1, source_target_pairs={{0,2},{1,9},{2,4},{3,11},{4,6},{5,13},{6,0},{7,15},{8,10},{9,17},{... | collective-permute-start | bytes 1572872 | tf_op jit(solution)/shard_map/ppermute | solution.py:42
  132.9 15.9 %collective-permute-start.29 = (bf16[64,4096]{1,0:T(8,128)(2,1)S(1)}, bf16[64,4096]{1,0:T(8,128)(2,1)S(1)}, u32[]{:S(2)}, u32[]{:S(2)}) collective-permute-start(bf16[64,4096]{1,0:T(8,128)(2,1)S(1)} %add_convert_fusion), channel_id=1, source_target_pairs={{0,6},{1,25},{2,0},{3,27},{4,2},{5,29},{6,4},{7,31},{8,14},{9,1},{... | collective-permute-start | bytes 1572872 | tf_op jit(solution)/shard_map/ppermute | solution.py:42
  145.4 7.7 %collective-permute-start.24 = (bf16[16,4096]{1,0:T(8,128)(2,1)S(1)}, bf16[16,4096]{1,0:T(8,128)(2,1)S(1)}, u32[]{:S(2)}, u32[]{:S(2)}) collective-permute-start(bf16[16,4096]{1,0:T(8,128)(2,1)S(1)} %get-tuple-element.26), channel_id=1, source_target_pairs={{0,8},{1,3},{2,10},{3,5},{4,12},{5,7},{6,14},{7,1},{8,16},{9,11},{... | collective-permute-start | bytes 393224 | tf_op jit(solution)/shard_map/ppermute | solution.py:42
  145.5 9.1 %collective-permute-start.25 = (bf16[16,4096]{1,0:T(8,128)(2,1)S(1)}, bf16[16,4096]{1,0:T(8,128)(2,1)S(1)}, u32[]{:S(2)}, u32[]{:S(2)}) collective-permute-start(bf16[16,4096]{1,0:T(8,128)(2,1)S(1)} %get-tuple-element.27), channel_id=1, source_target_pairs={{0,16},{1,5},{2,18},{3,7},{4,20},{5,1},{6,22},{7,3},{8,24},{9,13},... | collective-permute-start | bytes 393224 | tf_op jit(solution)/shard_map/ppermute | solution.py:42
  147.9 6.7 %collective-permute-start.26 = (bf16[16,4096]{1,0:T(8,128)(2,1)S(1)}, bf16[16,4096]{1,0:T(8,128)(2,1)S(1)}, u32[]{:S(2)}, u32[]{:S(2)}) collective-permute-start(bf16[16,4096]{1,0:T(8,128)(2,1)S(1)} %get-tuple-element.28), channel_id=1, source_target_pairs={{0,24},{1,7},{2,26},{3,1},{4,28},{5,3},{6,30},{7,5},{8,0},{9,15},{... | collective-permute-start | bytes 393224 | tf_op jit(solution)/shard_map/ppermute | solution.py:42
  149.0 6.2 %collective-permute-start.30 = (bf16[16,4096]{1,0:T(8,128)(2,1)S(1)}, bf16[16,4096]{1,0:T(8,128)(2,1)S(1)}, u32[]{:S(2)}, u32[]{:S(2)}) collective-permute-start(bf16[16,4096]{1,0:T(8,128)(2,1)S(1)} %get-tuple-element.34), channel_id=1, source_target_pairs={{0,8},{1,3},{2,10},{3,5},{4,12},{5,7},{6,14},{7,1},{8,16},{9,11},{... | collective-permute-start | bytes 393224 | tf_op jit(solution)/shard_map/ppermute | solution.py:42
  150.2 6.5 %collective-permute-start.31 = (bf16[16,4096]{1,0:T(8,128)(2,1)S(1)}, bf16[16,4096]{1,0:T(8,128)(2,1)S(1)}, u32[]{:S(2)}, u32[]{:S(2)}) collective-permute-start(bf16[16,4096]{1,0:T(8,128)(2,1)S(1)} %get-tuple-element.35), channel_id=1, source_target_pairs={{0,16},{1,5},{2,18},{3,7},{4,20},{5,1},{6,22},{7,3},{8,24},{9,13},... | collective-permute-start | bytes 393224 | tf_op jit(solution)/shard_map/ppermute | solution.py:42
  153.1 5.0 %collective-permute-start.32 = (bf16[16,4096]{1,0:T(8,128)(2,1)S(1)}, bf16[16,4096]{1,0:T(8,128)(2,1)S(1)}, u32[]{:S(2)}, u32[]{:S(2)}) collective-permute-start(bf16[16,4096]{1,0:T(8,128)(2,1)S(1)} %get-tuple-element.36), channel_id=1, source_target_pairs={{0,24},{1,7},{2,26},{3,1},{4,28},{5,3},{6,30},{7,5},{8,0},{9,15},{... | collective-permute-start | bytes 393224 | tf_op jit(solution)/shard_map/ppermute | solution.py:42

commit v3 on v0

v3 whole, which is shorter than its diff:
```python
import math

import jax
import jax.numpy as jnp
import numpy as np
from jax import lax
from jax.experimental import pallas as pl
from jax.experimental.pallas import tpu as pltpu
from jax.sharding import PartitionSpec as P

RING = 4
PLACES = [(x, y, c) for x in range(RING) for y in range(RING) for c in range(2)]
GATHER_SPANS = (3, 3, 2)
LIMIT = 14 * 2**20
BY_ROWS = (((1,), (1,)), ((), ()))


def place(x, y, c):
    return (x % RING) * RING * 2 + (y % RING) * 2 + c


def along_first(d):
    return [
        (place(x, y, c), place(x + d, y, c) if c == 0 else place(x, y + d, c))
        for x, y, c in PLACES
    ]


def along_second(d):
    return [
        (place(x, y, c), place(x + d, y, c) if c == 1 else place(x, y + d, c))
        for x, y, c in PLACES
    ]


PAIRS = [[place(x, y, 0), place(x, y, 1)] for x in range(RING) for y in range(RING)]
SIBLING = [(place(x, y, c), place(x, y, 1 - c)) for x, y, c in PLACES]


def send(value, pairs):
    return lax.ppermute(value, "tensor", pairs)


def from_steps(value, along):
    return send(value, along(-1)), send(value, along(2)), send(value, along(1))


def after(value, *others):
    return lax.optimization_barrier((value, *others))[0]


def dot(a, b):
    return jnp.dot(a, b, preferred_element_type=jnp.float32)


def scalar_table():
    def sign(row, column):
        return 1.0 - 2.0 * (bin(row & column).count("1") % 2)

    rows = []
    for x, y, c in PLACES:
        first, second = (x, y) if c == 0 else (y, x)
        row = [1.0 - 2.0 * c]
        row += [sign(first, (first + s) % RING) for s in range(RING)]
        row += [
            sign(second, (second + s) % RING) / math.sqrt(2 * RING * RING) for s in range(RING)
        ]
        rows.append(row + [0.0] * (16 - len(row)))
    return np.array(rows, np.float32)


def cuts_of(shares, total):
    widths = [w * total // sum(shares) for w in shares]
    starts = [sum(widths[:n]) for n in range(len(widths))]
    return list(zip(starts, widths))


VMEM = pl.BlockSpec(memory_space=pltpu.VMEM)
SCALARS = pl.BlockSpec(memory_space=pltpu.SMEM)


def call(kernel, name, flops, size, operands, outs, specs=None, **kwargs):
    return pl.pallas_call(
        kernel,
        name=name,
        compiler_params=pltpu.CompilerParams(vmem_limit_bytes=LIMIT),
        cost_estimate=pl.CostEstimate(flops=flops, bytes_accessed=size, transcendentals=0),
        in_specs=specs or [VMEM] * len(operands),
        out_specs=[VMEM] * len(outs),
        out_shape=outs,
        **kwargs,
    )(*operands)


def load(first, second, at, span, rows, skip):
    def kernel(first, second, first_out, second_out, sems):
        columns = pl.ds(at, span)
        copies = [
            pltpu.make_async_copy(first.at[:rows, columns], first_out, sems.at[0]),
            pltpu.make_async_copy(second.at[skip : skip + rows, columns], second_out, sems.at[1]),
        ]
        for copy in copies:
            copy.start()
        for copy in copies:
            copy.wait()

    return pl.pallas_call(
        kernel,
        name="load",
        compiler_params=pltpu.CompilerParams(vmem_limit_bytes=LIMIT),
        cost_estimate=pl.CostEstimate(flops=0, bytes_accessed=4 * rows * span, transcendentals=0),
        in_specs=[pl.BlockSpec(memory_space=pltpu.HBM)] * 2,
        out_specs=[VMEM] * 2,
        out_shape=[pltpu.VMEM((rows, span), first.dtype)] * 2,
        scratch_shapes=[pltpu.SemaphoreType.DMA((2,))],
    )(
        pltpu.with_memory_space_constraint(first, pltpu.HBM),
        pltpu.with_memory_space_constraint(second, pltpu.HBM),
    )


def gate_up(pieces, weights, at, span, sums, mixing, streamed):
    rows = RING * pieces[0].shape[0]
    units = weights[0].shape[0]
    block = math.gcd(span, 1024) if streamed else span
    steps = span // block
    opening, closing = sums is None, mixing is not None

    def kernel(*refs):
        refs = list(refs)
        held = refs.pop()
        parts, loads, refs = refs[:RING], refs[RING : RING + 2], refs[RING + 2 :]
        before = None if opening else refs.pop(0)
        mix = refs.pop(0) if closing else None
        (out,) = refs
        total = held if closing else out
        step = pl.program_id(0)
        x = jnp.concatenate([part[...] for part in parts], axis=0)
        for m in range(2):
            product = lax.dot_general(
                x, loads[m][...], BY_ROWS, preferred_element_type=jnp.float32
            )

            @pl.when(step == 0)
            def _():
                total[m] = product if opening else before[m] + product

            @pl.when(step > 0)
            def _():
                total[m] = total[m] + product

        if closing:

            @pl.when(step == steps - 1)
            def _():
                gate, up = total[0], total[1]
                hidden = (gate / (1.0 + jnp.exp(-gate)) * up).astype(jnp.bfloat16)
                out[...] = dot(hidden, mix[...]).astype(jnp.bfloat16)

    operands = [*pieces, *weights]
    if streamed:
        specs = [pl.BlockSpec((rows // RING, block), lambda k: (0, k))] * RING
        specs += [pl.BlockSpec((units, block), lambda k: (0, k + at // block))] * 2
    else:
        specs = [VMEM] * (RING + 2)
    if not opening:
        operands.append(sums)
        specs.append(VMEM)
    if closing:
        operands.append(mixing)
        specs.append(VMEM)
        out = jax.ShapeDtypeStruct((rows, units), jnp.bfloat16)
    else:
        out = jax.ShapeDtypeStruct((2, rows, units), jnp.float32)
    return call(
        kernel,
        "gate_up",
        4 * rows * units * span,
        4 * units * span,
        operands,
        [out],
        specs,
        grid=(steps,),
        scratch_shapes=[pltpu.VMEM((2, rows, units), jnp.float32)],
    )[0]


def turned(came, factors, first_scalar, i, j, major, slot):
    total = 0.0
    for s in range(RING):
        where = ((i - s) % RING, j) if major else (i, (j - s) % RING)
        at = (where[0] * RING + where[1]) * slot
        total = total + factors[first_scalar + s] * came[s][at : at + slot].astype(jnp.float32)
    return total


def first_ring(parts, scalars):
    rows, width = parts[0].shape
    slot = rows // (RING * RING)

    def kernel(own, one, two, three, factors, out):
        for i in range(RING):
            for j in range(RING):
                at = (i * RING + j) * slot
                out[at : at + slot] = turned(
                    (own, one, two, three), factors, 1, i, j, False, slot
                ).astype(jnp.bfloat16)

    return call(
        kernel,
        "first_ring",
        0,
        10 * rows * width,
        [*parts, scalars],
        [jax.ShapeDtypeStruct((rows, width), jnp.bfloat16)],
        [VMEM] * 4 + [SCALARS],
    )[0]


def second_ring(own_parts, other_parts, scalars):
    rows, width = own_parts[0].shape
    slot = rows // (RING * RING)

    def kernel(*refs):
        factors, sum_out, difference_out = refs[8:]
        turn = factors[0]
        for i in range(RING):
            for j in range(RING):
                at = (i * RING + j) * slot
                own = turned(refs[:4], factors, 1 + RING, i, j, True, slot)
                other = turned(refs[4:8], factors, 1 + RING, i, j, True, slot)
                sum_out[at : at + slot] = (own + other).astype(jnp.bfloat16)
                difference_out[at : at + slot] = (turn * (own - other)).astype(jnp.bfloat16)

    return call(
        kernel,
        "second_ring",
        0,
        20 * rows * width,
        [*own_parts, *other_parts, scalars],
        [jax.ShapeDtypeStruct((rows, width), jnp.bfloat16)] * 2,
        [VMEM] * 8 + [SCALARS],
    )


def down(values, weights, span):
    rows, units = values[0].shape
    group = rows // RING
    block = min(span, 512)

    def kernel(zero, one, loaded, loaded_one, *outs):
        for start in range(0, span, block):
            where = slice(start, start + block)
            product = dot(zero[...], loaded[:, where]) + dot(one[...], loaded_one[:, where])
            product = product.astype(jnp.bfloat16)
            for n, out in enumerate(outs):
                out[:, where] = product[n * group : (n + 1) * group]

    return call(
        kernel,
        "down",
        4 * rows * units * span,
        4 * units * span,
        [*values, *weights],
        [jax.ShapeDtypeStruct((group, span), jnp.bfloat16)] * RING,
    )


def added(a, b):
    return (a.astype(jnp.float32) + b.astype(jnp.float32)).astype(jnp.bfloat16)


def fold(thirds):
    group = thirds[0][0].shape[0]
    rows = group // RING
    width = sum(parts[0].shape[1] for parts in thirds)

    def kernel(*refs):
        ins, outs = refs[: 3 * len(thirds)], refs[3 * len(thirds) :]
        start = 0
        for n in range(len(thirds)):
            parts = ins[3 * n : 3 * n + 3]
            stop = start + parts[0].shape[1]
            for m, out in enumerate(outs):
                at = slice(m * rows, (m + 1) * rows)
                total = sum(part[at].astype(jnp.float32) for part in parts)
                out[:, start:stop] = total.astype(jnp.bfloat16)
            start = stop

    return call(
        kernel,
        "fold",
        0,
        8 * group * width,
        [part for parts in thirds for part in parts],
        [jax.ShapeDtypeStruct((rows, width), jnp.bfloat16)] * RING,
    )


def body(tokens, gate_weight, up_weight, down_weight, mixing):
    width = tokens.shape[1]
    index = lax.axis_index("tensor")
    scalars = lax.dynamic_index_in_dim(jnp.asarray(scalar_table()), index, keepdims=False)

    gate, up = gate_weight.T, up_weight.T
    near = from_steps(tokens, along_first)
    gate_other = send(gate, SIBLING)
    up_other = send(up, SIBLING)
    both_down = lax.all_gather(down_weight, "tensor", axis=0, tiled=True, axis_index_groups=PAIRS)
    cuts = cuts_of(GATHER_SPANS, width)
    units = gate.shape[0]
    own_weights = [load(gate, up, *cut, units, 0) for cut in cuts]
    tokens = after(tokens, *own_weights[0])

    own = other = None
    for n, (at, span) in enumerate(cuts):
        part = slice(at, at + span)
        block = jnp.concatenate([tokens[:, part]] + [piece[:, part] for piece in near])
        ahead, behind = send(block, along_second(-1)), send(block, along_second(1))
        if n == 0:
            across = send(behind, along_second(1))
        elif n == 1:
            across = send(ahead, along_second(-1))
        else:
            across = send(block, along_second(2))
        pieces = (block, ahead, across, behind)
        mix = mixing if n == len(cuts) - 1 else None
        own = gate_up(pieces, own_weights[n], at, span, own, mix, False)
        other = gate_up(pieces, (gate_other, up_other), at, span, other, mix, True)

    own = first_ring((own, *from_steps(own, along_first)), scalars)
    other = first_ring((other, *from_steps(other, along_first)), scalars)
    both = second_ring(
        (own, *from_steps(own, along_second)), (other, *from_steps(other, along_second)), scalars
    )

    half = width // 2
    halves = (both_down, both_down)
    left = down(both, load(*halves, 0, half, units, units), half)
    right = down(both, load(*halves, half, half, units, units), half)
    left_far = send(left[2], along_second(1))
    right_far = send(right[2], along_second(-1))
    right_near = send(right[1], along_second(1))
    left_near = send(left[3], along_second(-1))
    left_on = send(added(left[1], left_far), along_second(1))
    right_on = send(added(right[3], right_far), along_second(-1))
    parts = fold([(left[0], left_near, left_on), (right[0], right_near, right_on)])
    came = [
        parts[0],
        send(parts[1], along_first(1)),
        send(parts[2], along_first(2)),
        send(parts[3], along_first(-1)),
    ]
    return sum(part.astype(jnp.float32) for part in came).astype(jnp.bfloat16)


def solution(mesh):
    in_specs = (
        P(("dp", "tensor"), None),
        P(None, "tensor"),
        P(None, "tensor"),
        P("tensor", None),
        P(),
    )
    out_specs = P(("dp", "tensor"), None)
    return jax.shard_map(body, mesh=mesh, in_specs=in_specs, out_specs=out_specs, check_vma=False)
```

time: 230 us -> 179 us (0.78)
  waiting for transfers between devices: 149 us -> 54.1 us
  starting transfers between devices: 0.04 us -> 50.6 us
  Pallas kernels: 0 us -> 43.6 us
  blocking collectives: 30.8 us -> 0 us
  matrix products: 29 us -> 0 us
  local copies, waits for them, and re-layouts: 3.12 us -> 13.6 us
    reduce_scatter x1 -> x0, waiting for transfers between devices: 91 us -> none  [body(): lax.psum_scatter(jnp.dot(rotated_hidden, down_weight, preferred_element_t...]
    all_gather x1, waiting for transfers between devices: 57.6 us -> 0.02 us  [body(): lax.all_gather(down_weight, 'tensor', axis=0, tiled=True, axis_index_grou...]
    ppermute x0 -> x35, waiting for transfers between devices: none -> 53.4 us  [send(): return lax.ppermute(value, 'tensor', pairs)]
    ppermute x0 -> x35, starting transfers between devices: none -> 50.6 us  [send(): return lax.ppermute(value, 'tensor', pairs)]
    pallas_call x0 -> x17, Pallas kernels: none -> 43.6 us  [the longest x12 29.9 us: call(): pl.pallas_call(kernel, name=name, compiler_params=pltpu.CompilerParams(vm...]
    all_to_all x2 -> x0, blocking collectives: 30.8 us -> none  [the longest x1 15.8 us: body(): lax.all_to_all(local_block_values[None].astype(jnp.bfloat16), 'tensor', s...]
    dot_general x4 -> x0, matrix products: 29 us -> none  [the longest x1 9.81 us: body(): jnp.dot(hidden, block_mixing_matrix, preferred_element_type=jnp.float32)]
    unnamed x6 -> x34, local copies, waits for them, and re-layouts: 1.95 us -> 8.89 us
  transfers between devices with their start and end apart: 2 -> 36, of which waited for: 2 -> 15; matrix products, arithmetic and copies ran while one was open for 0% -> 3% of each run, Pallas kernels for 0% -> 21%
where the time goes in v3:
time: 179 us; the launch traced here: 178 us
  waiting for transfers between devices  54.1 us (30%)
  starting transfers between devices  50.6 us (28%)
  Pallas kernels  43.6 us (24%)
  between operations  13.8 us (8%)
  local copies, waits for them, and re-layouts  13.6 us (8%)
  other arithmetic  2.05 us (1%)
    ppermute x35, waiting for transfers between devices, send(): return lax.ppermute(value, 'tensor', pairs)  53.4 us
    ppermute x35, starting transfers between devices, send(): return lax.ppermute(value, 'tensor', pairs)  50.6 us
    pallas_call x12, Pallas kernels, call(): pl.pallas_call(kernel, name=name, compiler_params=pltpu.CompilerParams(vm...  29.9 us
    pallas_call x5, Pallas kernels, load(): pl.pallas_call(kernel, name='load', compiler_params=pltpu.CompilerParams(...  13.7 us
    unnamed x34, local copies, waits for them, and re-layouts  8.89 us
  transfers between devices with their start and end apart: 36, of which 15 were waited for; matrix products, arithmetic and copies ran while one was open for 3% of the time, Pallas kernels for 21%

profile of v3, /device:TPU:0, one launch (start us, length us, event | category | flops | bytes accessed | tf_op | source)
XLA Modules:
  0.0 177.7 jit_solution(1975579316286101252)
XLA Ops:
  7.9 1.6 collective-permute-start.2
  9.4 2.7 %collective-permute-start.1 = (bf16[16,8192]{1,0:T(8,128)(2,1)S(1)}, bf16[16,8192]{1,0:T(8,128)(2,1)S(1)}, u32[]{:S(2)}, u32[]{:S(2)}) collective-permute-start(bf16[16,8192]{1,0:T(8,128)(2,1)S(1)} %copy-done.13), channel_id=1, source_target_pairs={{0,16},{1,5},{2,18},{3,7},{4,20},{5,1},{6,22},{7,3},{8,24},{9,13},... | collective-permute-start | bytes 786440 | tf_op jit(solution)/shard_map/ppermute | solution.py:41
  12.2 1.4 collective-permute-start
  13.6 2.6 %load.5 = (bf16[448,3072]{1,0:T(8,128)(2,1)S(1)}, bf16[448,3072]{1,0:T(8,128)(2,1)S(1)}) custom-call(bf16[448,8192]{1,0:T(8,128)(2,1)} %bitcast.5, bf16[448,8192]{1,0:T(8,128)(2,1)} %bitcast.9), custom_call_target="tpu_custom_call" | custom-call | bytes 5505024 | tf_op jit(solution)/shard_map/load/pallas_call | solution.py:107
  17.0 2.3 %collective-permute-done.1 = bf16[16,8192]{1,0:T(8,128)(2,1)S(1)} collective-permute-done((bf16[16,8192]{1,0:T(8,128)(2,1)S(1)}, bf16[16,8192]{1,0:T(8,128)(2,1)S(1)}, u32[]{:S(2)}, u32[]{:S(2)}) %collective-permute-start.1) | collective-permute-done | bytes 262176 | tf_op jit(solution)/shard_map/ppermute | solution.py:41
  19.4 3.1 %collective-permute-start.6 = (bf16[64,3072]{1,0:T(8,128)(2,1)S(1)}, bf16[64,3072]{1,0:T(8,128)(2,1)}, u32[]{:S(2)}, u32[]{:S(2)}) collective-permute-start(bf16[64,3072]{1,0:T(8,128)(2,1)S(1)} %pad_maximum_fusion.refs_0_), channel_id=1, source_target_pairs={{0,6},{1,25},{2,0},{3,27},{4,2},{5,29},{6,4},{7,31},{8,14},{9,1},{... | collective-permute-start | bytes 1179656 | tf_op jit(solution)/shard_map/ppermute | solution.py:41
  23.2 4.6 %collective-permute-done.6.refs_1_ = bf16[64,3072]{1,0:T(8,128)(2,1)} collective-permute-done((bf16[64,3072]{1,0:T(8,128)(2,1)S(1)}, bf16[64,3072]{1,0:T(8,128)(2,1)}, u32[]{:S(2)}, u32[]{:S(2)}) %collective-permute-start.6) | collective-permute-done | bytes 393248 | tf_op jit(solution)/shard_map/ppermute | solution.py:41
  27.8 3.8 %collective-permute-start.9 = (bf16[64,3072]{1,0:T(8,128)(2,1)S(1)}, bf16[64,3072]{1,0:T(8,128)(2,1)}, u32[]{:S(2)}, u32[]{:S(2)}) collective-permute-start(bf16[64,3072]{1,0:T(8,128)(2,1)S(1)} %pad_maximum_fusion.1.refs_0_), channel_id=1, source_target_pairs={{0,6},{1,25},{2,0},{3,27},{4,2},{5,29},{6,4},{7,31},{8,14},{9,1},{... | collective-permute-start | bytes 1179656 | tf_op jit(solution)/shard_map/ppermute | solution.py:41
  31.6 0.7 copy-done.11
  32.3 3.5 %collective-permute-done.10.refs_3_ = bf16[64,3072]{1,0:T(8,128)(2,1)} collective-permute-done((bf16[64,3072]{1,0:T(8,128)(2,1)S(1)}, bf16[64,3072]{1,0:T(8,128)(2,1)}, u32[]{:S(2)}, u32[]{:S(2)}) %collective-permute-start.10) | collective-permute-done | bytes 393248 | tf_op jit(solution)/shard_map/ppermute | solution.py:41
  35.8 1.5 slice.36
  37.3 2.1 %load.6 = (bf16[448,2048]{1,0:T(8,128)(2,1)S(1)}, bf16[448,2048]{1,0:T(8,128)(2,1)S(1)}) custom-call(bf16[448,8192]{1,0:T(8,128)(2,1)} %bitcast.6, bf16[448,8192]{1,0:T(8,128)(2,1)} %bitcast.10), custom_call_target="tpu_custom_call" | custom-call | bytes 3670016 | tf_op jit(solution)/shard_map/load/pallas_call | solution.py:107
  39.4 1.2 copy-done.7
  40.6 1.3 copy-done.9
  41.9 2.6 %load.7 = (bf16[448,3072]{1,0:T(8,128)(2,1)S(1)}, bf16[448,3072]{1,0:T(8,128)(2,1)S(1)}) custom-call(bf16[448,8192]{1,0:T(8,128)(2,1)} %bitcast.7, bf16[448,8192]{1,0:T(8,128)(2,1)} %bitcast.11), custom_call_target="tpu_custom_call" | custom-call | bytes 5505024 | tf_op jit(solution)/shard_map/load/pallas_call | solution.py:107
  44.5 1.5 copy-done.2
  46.0 1.6 copy-done.4
  48.3 0.8 slice.50
  49.2 0.8 slice.49
  50.0 0.8 slice.48
  50.8 0.9 pad_maximum_fusion.2.refs_0_
  51.8 3.3 %collective-permute-start.3 = (bf16[64,2048]{1,0:T(8,128)(2,1)S(1)}, bf16[64,2048]{1,0:T(8,128)(2,1)S(1)}, u32[]{:S(2)}, u32[]{:S(2)}) collective-permute-start(bf16[64,2048]{1,0:T(8,128)(2,1)S(1)} %pad_maximum_fusion.2.refs_0_), channel_id=1, source_target_pairs={{0,6},{1,25},{2,0},{3,27},{4,2},{5,29},{6,4},{7,31},{8,14},{9,1},{... | collective-permute-start | bytes 786440 | tf_op jit(solution)/shard_map/ppermute | solution.py:41
  55.1 1.0 collective-permute-start.5
  56.0 1.8 copy-done.1
  57.8 3.2 %gate_up.6.refs_6_ = f32[2,256,448]{2,1,0:T(8,128)S(1)} custom-call(bf16[64,3072]{1,0:T(8,128)(2,1)S(1)} %pad_maximum_fusion.1.refs_0_, bf16[64,3072]{1,0:T(8,128)(2,1)} %collective-permute-done.9.refs_1_, bf16[64,3072]{1,0:T(8,128)(2,1)} %collective-permute-done.11.refs_2_, bf16[64,3072]{1,0:T(8,128)(2,1)} %collective-permute-done.10.refs_3_, ...), custom_call_target="tpu_custom_call" | custom-call | flops 1409286144 | bytes 5505024 | tf_op jit(solution)/shard_map/gate_up/pallas_call | solution.py:83
  61.1 3.1 %gate_up.7.refs_6_ = f32[2,256,448]{2,1,0:T(8,128)S(1)} custom-call(bf16[64,3072]{1,0:T(8,128)(2,1)S(1)} %pad_maximum_fusion.refs_0_, bf16[64,3072]{1,0:T(8,128)(2,1)} %collective-permute-done.6.refs_1_, bf16[64,3072]{1,0:T(8,128)(2,1)} %collective-permute-done.7.refs_2_, bf16[64,3072]{1,0:T(8,128)(2,1)S(1)} %copy-done.12, bf16[448,3072]{1,0:T(8,128)(2,1)S(1)} %copy-done.3, ...), custom_call_target="tpu_custom_call" | custom-call | flops 1409286144 | bytes 5505024 | tf_op jit(solution)/shard_map/gate_up/pallas_call | solution.py:83
  64.2 1.4 collective-permute-done.5.refs_3_
  65.5 1.5 gate_up.8.own
  67.1 2.6 %collective-permute-start.12 = (bf16[256,448]{1,0:T(8,128)(2,1)S(1)}, bf16[256,448]{1,0:T(8,128)(2,1)S(1)}, u32[]{:S(2)}, u32[]{:S(2)}) collective-permute-start(bf16[256,448]{1,0:T(8,128)(2,1)S(1)} %gate_up.8.own), channel_id=1, source_target_pairs={{0,24},{1,7},{2,26},{3,1},{4,28},{5,3},{6,30},{7,5},{8,0},{9,15},{... | collective-permute-start | bytes 688136 | tf_op jit(solution)/shard_map/ppermute | solution.py:41
  69.6 1.4 collective-permute-start.13
  71.4 5.3 %gate_up.9.refs_6_ = f32[2,256,448]{2,1,0:T(8,128)S(1)} custom-call(bf16[64,3072]{1,0:T(8,128)(2,1)S(1)} %pad_maximum_fusion.1.refs_0_, bf16[64,3072]{1,0:T(8,128)(2,1)} %collective-permute-done.9.refs_1_, bf16[64,3072]{1,0:T(8,128)(2,1)} %collective-permute-done.11.refs_2_, bf16[64,3072]{1,0:T(8,128)(2,1)} %collective-permute-done.10.refs_3_, ...), custom_call_target="tpu_custom_call" | custom-call | flops 1409286144 | bytes 5505024 | tf_op jit(solution)/shard_map/gate_up/pallas_call | solution.py:83
  76.8 5.4 %gate_up.10.refs_6_ = f32[2,256,448]{2,1,0:T(8,128)S(1)} custom-call(bf16[64,3072]{1,0:T(8,128)(2,1)S(1)} %pad_maximum_fusion.refs_0_, bf16[64,3072]{1,0:T(8,128)(2,1)} %collective-permute-done.6.refs_1_, bf16[64,3072]{1,0:T(8,128)(2,1)} %collective-permute-done.7.refs_2_, bf16[64,3072]{1,0:T(8,128)(2,1)S(1)} %copy-done.12, ...), custom_call_target="tpu_custom_call" | custom-call | flops 1409286144 | bytes 5505024 | tf_op jit(solution)/shard_map/gate_up/pallas_call | solution.py:83
  82.1 4.0 %gate_up.11.own = bf16[256,448]{1,0:T(8,128)(2,1)S(1)} custom-call(bf16[64,2048]{1,0:T(8,128)(2,1)S(1)} %pad_maximum_fusion.2.refs_0_, bf16[64,2048]{1,0:T(8,128)(2,1)S(1)} %collective-permute-done.3.refs_1_, bf16[64,2048]{1,0:T(8,128)(2,1)S(1)} %collective-permute-done.4.refs_2_, bf16[64,2048]{1,0:T(8,128)(2,1)S(1)} %collective-permute-done.5.refs_3_, ...), custom_call_target="tpu_custom_call" | custom-call | flops 939524096 | bytes 3670016 | tf_op jit(solution)/shard_map/gate_up/pallas_call | solution.py:83
  86.1 2.9 %collective-permute-start.20 = (bf16[256,448]{1,0:T(8,128)(2,1)S(1)}, bf16[256,448]{1,0:T(8,128)(2,1)S(1)}, u32[]{:S(2)}, u32[]{:S(2)}) collective-permute-start(bf16[256,448]{1,0:T(8,128)(2,1)S(1)} %gate_up.11.own), channel_id=1, source_target_pairs={{0,24},{1,7},{2,26},{3,1},{4,28},{5,3},{6,30},{7,5},{8,0},{9,15},{... | collective-permute-start | bytes 688136 | tf_op jit(solution)/shard_map/ppermute | solution.py:41
  89.0 0.9 collective-permute-start.21
  90.0 0.7 first_ring.2.refs_0_
  90.7 1.1 collective-permute-start.15
  91.8 2.2 %collective-permute-start.16 = (bf16[256,448]{1,0:T(8,128)(2,1)S(1)}, bf16[256,448]{1,0:T(8,128)(2,1)S(1)}, u32[]{:S(2)}, u32[]{:S(2)}) collective-permute-start(bf16[256,448]{1,0:T(8,128)(2,1)S(1)} %first_ring.2.refs_0_), channel_id=1, source_target_pairs={{0,4},{1,17},{2,6},{3,19},{4,0},{5,21},{6,2},{7,23},{8,12},{9,25},... | collective-permute-start | bytes 688136 | tf_op jit(solution)/shard_map/ppermute | solution.py:41
  94.1 2.9 %collective-permute-done.20.one = bf16[256,448]{1,0:T(8,128)(2,1)S(1)} collective-permute-done((bf16[256,448]{1,0:T(8,128)(2,1)S(1)}, bf16[256,448]{1,0:T(8,128)(2,1)S(1)}, u32[]{:S(2)}, u32[]{:S(2)}) %collective-permute-start.20) | collective-permute-done | bytes 229408 | tf_op jit(solution)/shard_map/ppermute | solution.py:41
  97.0 2.4 %collective-permute-start.17 = (bf16[256,448]{1,0:T(8,128)(2,1)S(1)}, bf16[256,448]{1,0:T(8,128)(2,1)S(1)}, u32[]{:S(2)}, u32[]{:S(2)}) collective-permute-start(bf16[256,448]{1,0:T(8,128)(2,1)S(1)} %first_ring.2.refs_0_), channel_id=1, source_target_pairs={{0,2},{1,9},{2,4},{3,11},{4,6},{5,13},{6,0},{7,15},{8,10},{9,17},{... | collective-permute-start | bytes 688136 | tf_op jit(solution)/shard_map/ppermute | solution.py:41
  99.4 6.3 %collective-permute-done.22.three = bf16[256,448]{1,0:T(8,128)(2,1)S(1)} collective-permute-done((bf16[256,448]{1,0:T(8,128)(2,1)S(1)}, bf16[256,448]{1,0:T(8,128)(2,1)S(1)}, u32[]{:S(2)}, u32[]{:S(2)}) %collective-permute-start.22) | collective-permute-done | bytes 229408 | tf_op jit(solution)/shard_map/ppermute | solution.py:41
  105.7 0.7 first_ring.3.refs_4_
  107.0 2.8 %collective-permute-start.24 = (bf16[256,448]{1,0:T(8,128)(2,1)S(1)}, bf16[256,448]{1,0:T(8,128)(2,1)S(1)}, u32[]{:S(2)}, u32[]{:S(2)}) collective-permute-start(bf16[256,448]{1,0:T(8,128)(2,1)S(1)} %first_ring.3.refs_4_), channel_id=1, source_target_pairs={{0,4},{1,17},{2,6},{3,19},{4,0},{5,21},{6,2},{7,23},{8,12},{9,25},... | collective-permute-start | bytes 688136 | tf_op jit(solution)/shard_map/ppermute | solution.py:41
  109.8 3.1 %collective-permute-done.23.refs_5_ = bf16[256,448]{1,0:T(8,128)(2,1)S(1)} collective-permute-done((bf16[256,448]{1,0:T(8,128)(2,1)S(1)}, bf16[256,448]{1,0:T(8,128)(2,1)S(1)}, u32[]{:S(2)}, u32[]{:S(2)}) %collective-permute-start.23) | collective-permute-done | bytes 229408 | tf_op jit(solution)/shard_map/ppermute | solution.py:41
  112.9 2.0 %collective-permute-done.24.refs_6_ = bf16[256,448]{1,0:T(8,128)(2,1)S(1)} collective-permute-done((bf16[256,448]{1,0:T(8,128)(2,1)S(1)}, bf16[256,448]{1,0:T(8,128)(2,1)S(1)}, u32[]{:S(2)}, u32[]{:S(2)}) %collective-permute-start.24) | collective-permute-done | bytes 229408 | tf_op jit(solution)/shard_map/ppermute | solution.py:41
  114.9 2.8 %collective-permute-done.25.refs_7_ = bf16[256,448]{1,0:T(8,128)(2,1)S(1)} collective-permute-done((bf16[256,448]{1,0:T(8,128)(2,1)S(1)}, bf16[256,448]{1,0:T(8,128)(2,1)S(1)}, u32[]{:S(2)}, u32[]{:S(2)}) %collective-permute-start.25) | collective-permute-done | bytes 229408 | tf_op jit(solution)/shard_map/ppermute | solution.py:41
  117.6 1.0 second_ring.1
  118.7 3.2 %load.8 = (bf16[448,4096]{1,0:T(8,128)(2,1)S(1)}, bf16[448,4096]{1,0:T(8,128)(2,1)S(1)}) custom-call(bf16[896,8192]{1,0:T(8,128)(2,1)} %all-gather.2.cloned.1.call-done.first.second, bf16[896,8192]{1,0:T(8,128)(2,1)} %all-gather.2.cloned.1.call-done.first.second), custom_call_target="tpu_custom_call" | custom-call | bytes 7340032 | tf_op jit(solution)/shard_map/load/pallas_call | solution.py:107
  121.9 2.3 %down.2 = (bf16[64,4096]{1,0:T(8,128)(2,1)S(1)}, bf16[64,4096]{1,0:T(8,128)(2,1)S(1)}, bf16[64,4096]{1,0:T(8,128)(2,1)S(1)}, bf16[64,4096]{1,0:T(8,128)(2,1)S(1)}) custom-call(bf16[256,448]{1,0:T(8,128)(2,1)S(1)} %get-tuple-element.37.zero, bf16[256,448]{1,0:T(8,128)(2,1)S(1)} %get-tuple-element.38.one, bf16[448,4096]{1,0:T(8,128)(2,1)S(1)} %get-tuple-element.39.loaded, ...), custom_call_target="tpu_custom_call" | custom-call | flops 1879048192 | bytes 7340032 | tf_op jit(solution)/shard_map/down/pallas_call | solution.py:83
  124.2 1.4 collective-permute-start.27
  125.6 1.9 %collective-permute-start.26 = (bf16[64,4096]{1,0:T(8,128)(2,1)S(1)}, bf16[64,4096]{1,0:T(8,128)(2,1)S(1)}, u32[]{:S(2)}, u32[]{:S(2)}) collective-permute-start(bf16[64,4096]{1,0:T(8,128)(2,1)S(1)} %get-tuple-element.42), channel_id=1, source_target_pairs={{0,6},{1,25},{2,0},{3,27},{4,2},{5,29},{6,4},{7,31},{8,14},{9,1},{... | collective-permute-start | bytes 1572872 | tf_op jit(solution)/shard_map/ppermute | solution.py:41
  127.5 3.2 %load.9 = (bf16[448,4096]{1,0:T(8,128)(2,1)S(1)}, bf16[448,4096]{1,0:T(8,128)(2,1)S(1)}) custom-call(bf16[896,8192]{1,0:T(8,128)(2,1)} %all-gather.2.cloned.1.call-done.first.second, bf16[896,8192]{1,0:T(8,128)(2,1)} %all-gather.2.cloned.1.call-done.first.second), custom_call_target="tpu_custom_call" | custom-call | bytes 7340032 | tf_op jit(solution)/shard_map/load/pallas_call | solution.py:107
  130.7 2.3 %down.3 = (bf16[64,4096]{1,0:T(8,128)(2,1)S(1)}, bf16[64,4096]{1,0:T(8,128)(2,1)S(1)}, bf16[64,4096]{1,0:T(8,128)(2,1)S(1)}, bf16[64,4096]{1,0:T(8,128)(2,1)S(1)}) custom-call(bf16[256,448]{1,0:T(8,128)(2,1)S(1)} %get-tuple-element.37.zero, bf16[256,448]{1,0:T(8,128)(2,1)S(1)} %get-tuple-element.38.one, bf16[448,4096]{1,0:T(8,128)(2,1)S(1)} %get-tuple-element.45.loaded, ...), custom_call_target="tpu_custom_call" | custom-call | flops 1879048192 | bytes 7340032 | tf_op jit(solution)/shard_map/down/pallas_call | solution.py:83
  133.2 3.1 %collective-permute-start.30 = (bf16[64,4096]{1,0:T(8,128)(2,1)S(1)}, bf16[64,4096]{1,0:T(8,128)(2,1)S(1)}, u32[]{:S(2)}, u32[]{:S(2)}) collective-permute-start(bf16[64,4096]{1,0:T(8,128)(2,1)S(1)} %get-tuple-element.50), channel_id=1, source_target_pairs={{0,6},{1,25},{2,0},{3,27},{4,2},{5,29},{6,4},{7,31},{8,14},{9,1},{... | collective-permute-start | bytes 1572872 | tf_op jit(solution)/shard_map/ppermute | solution.py:41
  136.5 6.5 %collective-permute-done.30 = bf16[64,4096]{1,0:T(8,128)(2,1)S(1)} collective-permute-done((bf16[64,4096]{1,0:T(8,128)(2,1)S(1)}, bf16[64,4096]{1,0:T(8,128)(2,1)S(1)}, u32[]{:S(2)}, u32[]{:S(2)}) %collective-permute-start.30) | collective-permute-done | bytes 524320 | tf_op jit(solution)/shard_map/ppermute | solution.py:41
  143.1 3.8 %collective-permute-start.31 = (bf16[64,4096]{1,0:T(8,128)(2,1)S(1)}, bf16[64,4096]{1,0:T(8,128)(2,1)S(1)}, u32[]{:S(2)}, u32[]{:S(2)}) collective-permute-start(bf16[64,4096]{1,0:T(8,128)(2,1)S(1)} %add_convert_fusion), channel_id=1, source_target_pairs={{0,6},{1,25},{2,0},{3,27},{4,2},{5,29},{6,4},{7,31},{8,14},{9,1},{... | collective-permute-start | bytes 1572872 | tf_op jit(solution)/shard_map/ppermute | solution.py:41
  146.9 5.9 %collective-permute-done.28.refs_2_ = bf16[64,4096]{1,0:T(8,128)(2,1)S(1)} collective-permute-done((bf16[64,4096]{1,0:T(8,128)(2,1)S(1)}, bf16[64,4096]{1,0:T(8,128)(2,1)S(1)}, u32[]{:S(2)}, u32[]{:S(2)}) %collective-permute-start.28) | collective-permute-done | bytes 524320 | tf_op jit(solution)/shard_map/ppermute | solution.py:41
  152.8 2.7 %collective-permute-done.31.refs_5_ = bf16[64,4096]{1,0:T(8,128)(2,1)S(1)} collective-permute-done((bf16[64,4096]{1,0:T(8,128)(2,1)S(1)}, bf16[64,4096]{1,0:T(8,128)(2,1)S(1)}, u32[]{:S(2)}, u32[]{:S(2)}) %collective-permute-start.31) | collective-permute-done | bytes 524320 | tf_op jit(solution)/shard_map/ppermute | solution.py:41
  155.9 3.8 %collective-permute-start.34 = (bf16[16,8192]{1,0:T(8,128)(2,1)S(1)}, bf16[16,8192]{1,0:T(8,128)(2,1)S(1)}, u32[]{:S(2)}, u32[]{:S(2)}) collective-permute-start(bf16[16,8192]{1,0:T(8,128)(2,1)S(1)} %get-tuple-element.54), channel_id=1, source_target_pairs={{0,24},{1,7},{2,26},{3,1},{4,28},{5,3},{6,30},{7,5},{8,0},{9,15},{... | collective-permute-start | bytes 786440 | tf_op jit(solution)/shard_map/ppermute | solution.py:41
  159.7 0.9 collective-permute-start.32
  160.6 5.7 %collective-permute-done.34 = bf16[16,8192]{1,0:T(8,128)(2,1)S(1)} collective-permute-done((bf16[16,8192]{1,0:T(8,128)(2,1)S(1)}, bf16[16,8192]{1,0:T(8,128)(2,1)S(1)}, u32[]{:S(2)}, u32[]{:S(2)}) %collective-permute-start.34) | collective-permute-done | bytes 262176 | tf_op jit(solution)/shard_map/ppermute | solution.py:41
  166.4 1.3 collective-permute-done.33
  167.6 2.4 %collective-permute-done.32 = bf16[16,8192]{1,0:T(8,128)(2,1)S(1)} collective-permute-done((bf16[16,8192]{1,0:T(8,128)(2,1)S(1)}, bf16[16,8192]{1,0:T(8,128)(2,1)S(1)}, u32[]{:S(2)}, u32[]{:S(2)}) %collective-permute-start.32) | collective-permute-done | bytes 262176 | tf_op jit(solution)/shard_map/ppermute | solution.py:41
  170.1 0.8 add_convert_fusion.2
  (75 shorter events, 5.5 us)
Async XLA Ops:
  6.5 1.3 copy-start.13
  6.5 112.1 %all-gather.2.cloned.1.call-start = ((), (), s32[]{:S(2)}) async-start(), calls=%async_computation | async-start | bytes 22020096 | tf_op jit(solution)/shard_map/all_gather | solution.py:309
  7.3 64.2 %collective-permute-start.18 = (bf16[448,8192]{1,0:T(8,128)(2,1)}, bf16[448,8192]{1,0:T(8,128)(2,1)}, u32[]{:S(2)}, u32[]{:S(2)}) collective-permute-start(bf16[448,8192]{1,0:T(8,128)(2,1)} %bitcast.4), channel_id=1, source_target_pairs={{0,1},{1,0},{2,3},{3,2},{4,5},{5,4},{6,7},{7,6},{8,9},{9,8},{10,11... | collective-permute-start | bytes 22020104 | tf_op jit(solution)/shard_map/ppermute | solution.py:41
  7.4 64.1 %collective-permute-start.19 = (bf16[448,8192]{1,0:T(8,128)(2,1)}, bf16[448,8192]{1,0:T(8,128)(2,1)}, u32[]{:S(2)}, u32[]{:S(2)}) collective-permute-start(bf16[448,8192]{1,0:T(8,128)(2,1)} %bitcast.8), channel_id=1, source_target_pairs={{0,1},{1,0},{2,3},{3,2},{4,5},{5,4},{6,7},{7,6},{8,9},{9,8},{10,11... | collective-permute-start | bytes 22020104 | tf_op jit(solution)/shard_map/ppermute | solution.py:41
  7.9 8.4 %collective-permute-start.2 = (bf16[16,8192]{1,0:T(8,128)(2,1)S(1)}, bf16[16,8192]{1,0:T(8,128)(2,1)S(1)}, u32[]{:S(2)}, u32[]{:S(2)}) collective-permute-start(bf16[16,8192]{1,0:T(8,128)(2,1)S(1)} %copy-done.13), channel_id=1, source_target_pairs={{0,8},{1,3},{2,10},{3,5},{4,12},{5,7},{6,14},{7,1},{8,16},{9,11},{... | collective-permute-start | bytes 786440 | tf_op jit(solution)/shard_map/ppermute | solution.py:41
  9.4 9.9 %collective-permute-start.1 = (bf16[16,8192]{1,0:T(8,128)(2,1)S(1)}, bf16[16,8192]{1,0:T(8,128)(2,1)S(1)}, u32[]{:S(2)}, u32[]{:S(2)}) collective-permute-start(bf16[16,8192]{1,0:T(8,128)(2,1)S(1)} %copy-done.13), channel_id=1, source_target_pairs={{0,16},{1,5},{2,18},{3,7},{4,20},{5,1},{6,22},{7,3},{8,24},{9,13},... | collective-permute-start | bytes 786440 | tf_op jit(solution)/shard_map/ppermute | solution.py:41
  12.2 7.2 %collective-permute-start = (bf16[16,8192]{1,0:T(8,128)(2,1)S(1)}, bf16[16,8192]{1,0:T(8,128)(2,1)S(1)}, u32[]{:S(2)}, u32[]{:S(2)}) collective-permute-start(bf16[16,8192]{1,0:T(8,128)(2,1)S(1)} %copy-done.13), channel_id=1, source_target_pairs={{0,24},{1,7},{2,26},{3,1},{4,28},{5,3},{6,30},{7,5},{8,0},{9,15},{... | collective-permute-start | bytes 786440 | tf_op jit(solution)/shard_map/ppermute | solution.py:41
  16.2 19.6 %copy-start = (bf16[448,3072]{1,0:T(8,128)(2,1)}, bf16[448,3072]{1,0:T(8,128)(2,1)S(1)}, u32[]{:S(2)}) copy-start(bf16[448,3072]{1,0:T(8,128)(2,1)S(1)} %get-tuple-element.31.refs_5_) | copy-start | bytes 8257540
  16.3 0.8 copy-start.14
  19.3 16.5 %copy-start.15 = (bf16[16,8192]{1,0:T(8,128)(2,1)}, bf16[16,8192]{1,0:T(8,128)(2,1)S(1)}, u32[]{:S(2)}) copy-start(bf16[16,8192]{1,0:T(8,128)(2,1)S(1)} %collective-permute-done.1) | copy-start | bytes 786436
  19.3 16.5 %copy-start.16 = (bf16[16,8192]{1,0:T(8,128)(2,1)}, bf16[16,8192]{1,0:T(8,128)(2,1)S(1)}, u32[]{:S(2)}) copy-start(bf16[16,8192]{1,0:T(8,128)(2,1)S(1)} %collective-permute-done) | copy-start | bytes 786436
  19.4 8.4 %collective-permute-start.6 = (bf16[64,3072]{1,0:T(8,128)(2,1)S(1)}, bf16[64,3072]{1,0:T(8,128)(2,1)}, u32[]{:S(2)}, u32[]{:S(2)}) collective-permute-start(bf16[64,3072]{1,0:T(8,128)(2,1)S(1)} %pad_maximum_fusion.refs_0_), channel_id=1, source_target_pairs={{0,6},{1,25},{2,0},{3,27},{4,2},{5,29},{6,4},{7,31},{8,14},{9,1},{... | collective-permute-start | bytes 1179656 | tf_op jit(solution)/shard_map/ppermute | solution.py:41
  22.5 9.1 %collective-permute-start.8 = (bf16[64,3072]{1,0:T(8,128)(2,1)S(1)}, bf16[64,3072]{1,0:T(8,128)(2,1)S(1)}, u32[]{:S(2)}, u32[]{:S(2)}) collective-permute-start(bf16[64,3072]{1,0:T(8,128)(2,1)S(1)} %pad_maximum_fusion.refs_0_), channel_id=1, source_target_pairs={{0,2},{1,9},{2,4},{3,11},{4,6},{5,13},{6,0},{7,15},{8,10},{9,17},{... | collective-permute-start | bytes 1179656 | tf_op jit(solution)/shard_map/ppermute | solution.py:41
  22.5 13.3 %collective-permute-start.10 = (bf16[64,3072]{1,0:T(8,128)(2,1)S(1)}, bf16[64,3072]{1,0:T(8,128)(2,1)}, u32[]{:S(2)}, u32[]{:S(2)}) collective-permute-start(bf16[64,3072]{1,0:T(8,128)(2,1)S(1)} %pad_maximum_fusion.1.refs_0_), channel_id=1, source_target_pairs={{0,2},{1,9},{2,4},{3,11},{4,6},{5,13},{6,0},{7,15},{8,10},{9,17},{... | collective-permute-start | bytes 1179656 | tf_op jit(solution)/shard_map/ppermute | solution.py:41
  27.8 24.0 %collective-permute-start.9 = (bf16[64,3072]{1,0:T(8,128)(2,1)S(1)}, bf16[64,3072]{1,0:T(8,128)(2,1)}, u32[]{:S(2)}, u32[]{:S(2)}) collective-permute-start(bf16[64,3072]{1,0:T(8,128)(2,1)S(1)} %pad_maximum_fusion.1.refs_0_), channel_id=1, source_target_pairs={{0,6},{1,25},{2,0},{3,27},{4,2},{5,29},{6,4},{7,31},{8,14},{9,1},{... | collective-permute-start | bytes 1179656 | tf_op jit(solution)/shard_map/ppermute | solution.py:41
  31.6 0.7 copy-start.11
  32.3 22.7 %collective-permute-start.7 = (bf16[64,3072]{1,0:T(8,128)(2,1)}, bf16[64,3072]{1,0:T(8,128)(2,1)}, u32[]{:S(2)}, u32[]{:S(2)}) collective-permute-start(bf16[64,3072]{1,0:T(8,128)(2,1)} %collective-permute-done.6.refs_1_), channel_id=1, source_target_pairs={{0,6},{1,25},{2,0},{3,27},{4,2},{5,29},{6,4},{7,31},{8,14},{9,1},{... | collective-permute-start | bytes 1179656 | tf_op jit(solution)/shard_map/ppermute | solution.py:41
  35.8 19.3 %collective-permute-start.11 = (bf16[64,3072]{1,0:T(8,128)(2,1)}, bf16[64,3072]{1,0:T(8,128)(2,1)}, u32[]{:S(2)}, u32[]{:S(2)}) collective-permute-start(bf16[64,3072]{1,0:T(8,128)(2,1)} %collective-permute-done.10.refs_3_), channel_id=1, source_target_pairs={{0,2},{1,9},{2,4},{3,11},{4,6},{5,13},{6,0},{7,15},{8,10},{9,17},{... | collective-permute-start | bytes 1179656 | tf_op jit(solution)/shard_map/ppermute | solution.py:41
  39.4 1.2 copy-start.7
  40.6 1.3 copy-start.9
  44.5 1.5 copy-start.2
  46.0 1.6 copy-start.4
  50.8 10.2 %copy-start.12 = (bf16[64,3072]{1,0:T(8,128)(2,1)S(1)}, bf16[64,3072]{1,0:T(8,128)(2,1)}, u32[]{:S(2)}) copy-start(bf16[64,3072]{1,0:T(8,128)(2,1)} %copy-done.11) | copy-start | bytes 1179652
  51.8 12.4 %collective-permute-start.3 = (bf16[64,2048]{1,0:T(8,128)(2,1)S(1)}, bf16[64,2048]{1,0:T(8,128)(2,1)S(1)}, u32[]{:S(2)}, u32[]{:S(2)}) collective-permute-start(bf16[64,2048]{1,0:T(8,128)(2,1)S(1)} %pad_maximum_fusion.2.refs_0_), channel_id=1, source_target_pairs={{0,6},{1,25},{2,0},{3,27},{4,2},{5,29},{6,4},{7,31},{8,14},{9,1},{... | collective-permute-start | bytes 786440 | tf_op jit(solution)/shard_map/ppermute | solution.py:41
  55.1 9.1 %collective-permute-start.4 = (bf16[64,2048]{1,0:T(8,128)(2,1)S(1)}, bf16[64,2048]{1,0:T(8,128)(2,1)S(1)}, u32[]{:S(2)}, u32[]{:S(2)}) collective-permute-start(bf16[64,2048]{1,0:T(8,128)(2,1)S(1)} %pad_maximum_fusion.2.refs_0_), channel_id=1, source_target_pairs={{0,4},{1,17},{2,6},{3,19},{4,0},{5,21},{6,2},{7,23},{8,12},{9,25},... | collective-permute-start | bytes 786440 | tf_op jit(solution)/shard_map/ppermute | solution.py:41
  55.1 10.5 %collective-permute-start.5 = (bf16[64,2048]{1,0:T(8,128)(2,1)S(1)}, bf16[64,2048]{1,0:T(8,128)(2,1)S(1)}, u32[]{:S(2)}, u32[]{:S(2)}) collective-permute-start(bf16[64,2048]{1,0:T(8,128)(2,1)S(1)} %pad_maximum_fusion.2.refs_0_), channel_id=1, source_target_pairs={{0,2},{1,9},{2,4},{3,11},{4,6},{5,13},{6,0},{7,15},{8,10},{9,17},{... | collective-permute-start | bytes 786440 | tf_op jit(solution)/shard_map/ppermute | solution.py:41
  56.0 1.8 copy-start.1
  57.8 3.2 %copy-start.3 = (bf16[448,3072]{1,0:T(8,128)(2,1)S(1)}, bf16[448,3072]{1,0:T(8,128)(2,1)}, u32[]{:S(2)}) copy-start(bf16[448,3072]{1,0:T(8,128)(2,1)} %copy-done.2) | copy-start | bytes 8257540
  57.8 3.2 %copy-start.5 = (bf16[448,3072]{1,0:T(8,128)(2,1)S(1)}, bf16[448,3072]{1,0:T(8,128)(2,1)}, u32[]{:S(2)}) copy-start(bf16[448,3072]{1,0:T(8,128)(2,1)} %copy-done.4) | copy-start | bytes 8257540
  61.0 4.5 %copy-start.6 = (bf16[448,448]{1,0:T(8,128)(2,1)S(1)}, bf16[448,448]{1,0:T(8,128)(2,1)}, u32[]{:S(2)}) copy-start(bf16[448,448]{1,0:T(8,128)(2,1)} %refs_7_.3) | copy-start | bytes 1204228
  61.0 4.5 %copy-start.8 = (bf16[448,2048]{1,0:T(8,128)(2,1)S(1)}, bf16[448,2048]{1,0:T(8,128)(2,1)}, u32[]{:S(2)}) copy-start(bf16[448,2048]{1,0:T(8,128)(2,1)} %copy-done.7) | copy-start | bytes 5505028
  61.0 4.5 %copy-start.10 = (bf16[448,2048]{1,0:T(8,128)(2,1)S(1)}, bf16[448,2048]{1,0:T(8,128)(2,1)}, u32[]{:S(2)}) copy-start(bf16[448,2048]{1,0:T(8,128)(2,1)} %copy-done.9) | copy-start | bytes 5505028
  67.1 22.8 %collective-permute-start.12 = (bf16[256,448]{1,0:T(8,128)(2,1)S(1)}, bf16[256,448]{1,0:T(8,128)(2,1)S(1)}, u32[]{:S(2)}, u32[]{:S(2)}) collective-permute-start(bf16[256,448]{1,0:T(8,128)(2,1)S(1)} %gate_up.8.own), channel_id=1, source_target_pairs={{0,24},{1,7},{2,26},{3,1},{4,28},{5,3},{6,30},{7,5},{8,0},{9,15},{... | collective-permute-start | bytes 688136 | tf_op jit(solution)/shard_map/ppermute | solution.py:41
  69.6 20.3 %collective-permute-start.13 = (bf16[256,448]{1,0:T(8,128)(2,1)S(1)}, bf16[256,448]{1,0:T(8,128)(2,1)S(1)}, u32[]{:S(2)}, u32[]{:S(2)}) collective-permute-start(bf16[256,448]{1,0:T(8,128)(2,1)S(1)} %gate_up.8.own), channel_id=1, source_target_pairs={{0,16},{1,5},{2,18},{3,7},{4,20},{5,1},{6,22},{7,3},{8,24},{9,13},... | collective-permute-start | bytes 688136 | tf_op jit(solution)/shard_map/ppermute | solution.py:41
  71.0 18.9 %collective-permute-start.14 = (bf16[256,448]{1,0:T(8,128)(2,1)S(1)}, bf16[256,448]{1,0:T(8,128)(2,1)S(1)}, u32[]{:S(2)}, u32[]{:S(2)}) collective-permute-start(bf16[256,448]{1,0:T(8,128)(2,1)S(1)} %gate_up.8.own), channel_id=1, source_target_pairs={{0,8},{1,3},{2,10},{3,5},{4,12},{5,7},{6,14},{7,1},{8,16},{9,11},{... | collective-permute-start | bytes 688136 | tf_op jit(solution)/shard_map/ppermute | solution.py:41
  86.1 10.9 %collective-permute-start.20 = (bf16[256,448]{1,0:T(8,128)(2,1)S(1)}, bf16[256,448]{1,0:T(8,128)(2,1)S(1)}, u32[]{:S(2)}, u32[]{:S(2)}) collective-permute-start(bf16[256,448]{1,0:T(8,128)(2,1)S(1)} %gate_up.11.own), channel_id=1, source_target_pairs={{0,24},{1,7},{2,26},{3,1},{4,28},{5,3},{6,30},{7,5},{8,0},{9,15},{... | collective-permute-start | bytes 688136 | tf_op jit(solution)/shard_map/ppermute | solution.py:41
  89.0 10.4 %collective-permute-start.21 = (bf16[256,448]{1,0:T(8,128)(2,1)S(1)}, bf16[256,448]{1,0:T(8,128)(2,1)S(1)}, u32[]{:S(2)}, u32[]{:S(2)}) collective-permute-start(bf16[256,448]{1,0:T(8,128)(2,1)S(1)} %gate_up.11.own), channel_id=1, source_target_pairs={{0,16},{1,5},{2,18},{3,7},{4,20},{5,1},{6,22},{7,3},{8,24},{9,13},... | collective-permute-start | bytes 688136 | tf_op jit(solution)/shard_map/ppermute | solution.py:41
  89.9 15.8 %collective-permute-start.22 = (bf16[256,448]{1,0:T(8,128)(2,1)S(1)}, bf16[256,448]{1,0:T(8,128)(2,1)S(1)}, u32[]{:S(2)}, u32[]{:S(2)}) collective-permute-start(bf16[256,448]{1,0:T(8,128)(2,1)S(1)} %gate_up.11.own), channel_id=1, source_target_pairs={{0,8},{1,3},{2,10},{3,5},{4,12},{5,7},{6,14},{7,1},{8,16},{9,11},{... | collective-permute-start | bytes 688136 | tf_op jit(solution)/shard_map/ppermute | solution.py:41
  90.7 19.0 %collective-permute-start.15 = (bf16[256,448]{1,0:T(8,128)(2,1)S(1)}, bf16[256,448]{1,0:T(8,128)(2,1)S(1)}, u32[]{:S(2)}, u32[]{:S(2)}) collective-permute-start(bf16[256,448]{1,0:T(8,128)(2,1)S(1)} %first_ring.2.refs_0_), channel_id=1, source_target_pairs={{0,6},{1,25},{2,0},{3,27},{4,2},{5,29},{6,4},{7,31},{8,14},{9,1},{... | collective-permute-start | bytes 688136 | tf_op jit(solution)/shard_map/ppermute | solution.py:41
  91.8 17.9 %collective-permute-start.16 = (bf16[256,448]{1,0:T(8,128)(2,1)S(1)}, bf16[256,448]{1,0:T(8,128)(2,1)S(1)}, u32[]{:S(2)}, u32[]{:S(2)}) collective-permute-start(bf16[256,448]{1,0:T(8,128)(2,1)S(1)} %first_ring.2.refs_0_), channel_id=1, source_target_pairs={{0,4},{1,17},{2,6},{3,19},{4,0},{5,21},{6,2},{7,23},{8,12},{9,25},... | collective-permute-start | bytes 688136 | tf_op jit(solution)/shard_map/ppermute | solution.py:41
  97.0 12.8 %collective-permute-start.17 = (bf16[256,448]{1,0:T(8,128)(2,1)S(1)}, bf16[256,448]{1,0:T(8,128)(2,1)S(1)}, u32[]{:S(2)}, u32[]{:S(2)}) collective-permute-start(bf16[256,448]{1,0:T(8,128)(2,1)S(1)} %first_ring.2.refs_0_), channel_id=1, source_target_pairs={{0,2},{1,9},{2,4},{3,11},{4,6},{5,13},{6,0},{7,15},{8,10},{9,17},{... | collective-permute-start | bytes 688136 | tf_op jit(solution)/shard_map/ppermute | solution.py:41
  106.4 6.4 %collective-permute-start.23 = (bf16[256,448]{1,0:T(8,128)(2,1)S(1)}, bf16[256,448]{1,0:T(8,128)(2,1)S(1)}, u32[]{:S(2)}, u32[]{:S(2)}) collective-permute-start(bf16[256,448]{1,0:T(8,128)(2,1)S(1)} %first_ring.3.refs_4_), channel_id=1, source_target_pairs={{0,6},{1,25},{2,0},{3,27},{4,2},{5,29},{6,4},{7,31},{8,14},{9,1},{... | collective-permute-start | bytes 688136 | tf_op jit(solution)/shard_map/ppermute | solution.py:41
  107.0 7.9 %collective-permute-start.24 = (bf16[256,448]{1,0:T(8,128)(2,1)S(1)}, bf16[256,448]{1,0:T(8,128)(2,1)S(1)}, u32[]{:S(2)}, u32[]{:S(2)}) collective-permute-start(bf16[256,448]{1,0:T(8,128)(2,1)S(1)} %first_ring.3.refs_4_), channel_id=1, source_target_pairs={{0,4},{1,17},{2,6},{3,19},{4,0},{5,21},{6,2},{7,23},{8,12},{9,25},... | collective-permute-start | bytes 688136 | tf_op jit(solution)/shard_map/ppermute | solution.py:41
  109.7 7.9 %collective-permute-start.25 = (bf16[256,448]{1,0:T(8,128)(2,1)S(1)}, bf16[256,448]{1,0:T(8,128)(2,1)S(1)}, u32[]{:S(2)}, u32[]{:S(2)}) collective-permute-start(bf16[256,448]{1,0:T(8,128)(2,1)S(1)} %first_ring.3.refs_4_), channel_id=1, source_target_pairs={{0,2},{1,9},{2,4},{3,11},{4,6},{5,13},{6,0},{7,15},{8,10},{9,17},{... | collective-permute-start | bytes 688136 | tf_op jit(solution)/shard_map/ppermute | solution.py:41
  124.2 12.1 %collective-permute-start.27 = (bf16[64,4096]{1,0:T(8,128)(2,1)S(1)}, bf16[64,4096]{1,0:T(8,128)(2,1)S(1)}, u32[]{:S(2)}, u32[]{:S(2)}) collective-permute-start(bf16[64,4096]{1,0:T(8,128)(2,1)S(1)} %get-tuple-element.44), channel_id=1, source_target_pairs={{0,2},{1,9},{2,4},{3,11},{4,6},{5,13},{6,0},{7,15},{8,10},{9,17},{... | collective-permute-start | bytes 1572872 | tf_op jit(solution)/shard_map/ppermute | solution.py:41
  125.6 21.3 %collective-permute-start.26 = (bf16[64,4096]{1,0:T(8,128)(2,1)S(1)}, bf16[64,4096]{1,0:T(8,128)(2,1)S(1)}, u32[]{:S(2)}, u32[]{:S(2)}) collective-permute-start(bf16[64,4096]{1,0:T(8,128)(2,1)S(1)} %get-tuple-element.42), channel_id=1, source_target_pairs={{0,6},{1,25},{2,0},{3,27},{4,2},{5,29},{6,4},{7,31},{8,14},{9,1},{... | collective-permute-start | bytes 1572872 | tf_op jit(solution)/shard_map/ppermute | solution.py:41
  133.0 13.9 %collective-permute-start.29 = (bf16[64,4096]{1,0:T(8,128)(2,1)S(1)}, bf16[64,4096]{1,0:T(8,128)(2,1)S(1)}, u32[]{:S(2)}, u32[]{:S(2)}) collective-permute-start(bf16[64,4096]{1,0:T(8,128)(2,1)S(1)} %get-tuple-element.48), channel_id=1, source_target_pairs={{0,2},{1,9},{2,4},{3,11},{4,6},{5,13},{6,0},{7,15},{8,10},{9,17},{... | collective-permute-start | bytes 1572872 | tf_op jit(solution)/shard_map/ppermute | solution.py:41
  133.2 9.8 %collective-permute-start.30 = (bf16[64,4096]{1,0:T(8,128)(2,1)S(1)}, bf16[64,4096]{1,0:T(8,128)(2,1)S(1)}, u32[]{:S(2)}, u32[]{:S(2)}) collective-permute-start(bf16[64,4096]{1,0:T(8,128)(2,1)S(1)} %get-tuple-element.50), channel_id=1, source_target_pairs={{0,6},{1,25},{2,0},{3,27},{4,2},{5,29},{6,4},{7,31},{8,14},{9,1},{... | collective-permute-start | bytes 1572872 | tf_op jit(solution)/shard_map/ppermute | solution.py:41
  136.4 16.4 %collective-permute-start.28 = (bf16[64,4096]{1,0:T(8,128)(2,1)S(1)}, bf16[64,4096]{1,0:T(8,128)(2,1)S(1)}, u32[]{:S(2)}, u32[]{:S(2)}) collective-permute-start(bf16[64,4096]{1,0:T(8,128)(2,1)S(1)} %add_convert_fusion.1), channel_id=1, source_target_pairs={{0,2},{1,9},{2,4},{3,11},{4,6},{5,13},{6,0},{7,15},{8,10},{9,17},{... | collective-permute-start | bytes 1572872 | tf_op jit(solution)/shard_map/ppermute | solution.py:41
  143.1 12.4 %collective-permute-start.31 = (bf16[64,4096]{1,0:T(8,128)(2,1)S(1)}, bf16[64,4096]{1,0:T(8,128)(2,1)S(1)}, u32[]{:S(2)}, u32[]{:S(2)}) collective-permute-start(bf16[64,4096]{1,0:T(8,128)(2,1)S(1)} %add_convert_fusion), channel_id=1, source_target_pairs={{0,6},{1,25},{2,0},{3,27},{4,2},{5,29},{6,4},{7,31},{8,14},{9,1},{... | collective-permute-start | bytes 1572872 | tf_op jit(solution)/shard_map/ppermute | solution.py:41
  155.9 10.5 %collective-permute-start.34 = (bf16[16,8192]{1,0:T(8,128)(2,1)S(1)}, bf16[16,8192]{1,0:T(8,128)(2,1)S(1)}, u32[]{:S(2)}, u32[]{:S(2)}) collective-permute-start(bf16[16,8192]{1,0:T(8,128)(2,1)S(1)} %get-tuple-element.54), channel_id=1, source_target_pairs={{0,24},{1,7},{2,26},{3,1},{4,28},{5,3},{6,30},{7,5},{8,0},{9,15},{... | collective-permute-start | bytes 786440 | tf_op jit(solution)/shard_map/ppermute | solution.py:41
  159.7 8.0 %collective-permute-start.33 = (bf16[16,8192]{1,0:T(8,128)(2,1)S(1)}, bf16[16,8192]{1,0:T(8,128)(2,1)S(1)}, u32[]{:S(2)}, u32[]{:S(2)}) collective-permute-start(bf16[16,8192]{1,0:T(8,128)(2,1)S(1)} %get-tuple-element.53), channel_id=1, source_target_pairs={{0,16},{1,5},{2,18},{3,7},{4,20},{5,1},{6,22},{7,3},{8,24},{9,13},... | collective-permute-start | bytes 786440 | tf_op jit(solution)/shard_map/ppermute | solution.py:41
  159.7 10.4 %collective-permute-start.32 = (bf16[16,8192]{1,0:T(8,128)(2,1)S(1)}, bf16[16,8192]{1,0:T(8,128)(2,1)S(1)}, u32[]{:S(2)}, u32[]{:S(2)}) collective-permute-start(bf16[16,8192]{1,0:T(8,128)(2,1)S(1)} %get-tuple-element.52), channel_id=1, source_target_pairs={{0,8},{1,3},{2,10},{3,5},{4,12},{5,7},{6,14},{7,1},{8,16},{9,11},{... | collective-permute-start | bytes 786440 | tf_op jit(solution)/shard_map/ppermute | solution.py:41
Sparse Core Ops, SparseCore 0:
  9.0 32.1 all-gather.1

commit v4 on v3

v4 whole, which is shorter than its diff:
```python
import math

import jax
import jax.numpy as jnp
import numpy as np
from jax import lax
from jax.experimental import pallas as pl
from jax.experimental.pallas import tpu as pltpu
from jax.sharding import PartitionSpec as P

RING = 4
PLACES = [(x, y, c) for x in range(RING) for y in range(RING) for c in range(2)]
GATHER_SPANS = (3, 3, 2)
LIMIT = 24 * 2**20
BY_ROWS = (((1,), (1,)), ((), ()))


def place(x, y, c):
    return (x % RING) * RING * 2 + (y % RING) * 2 + c


def along_first(d):
    return [
        (place(x, y, c), place(x + d, y, c) if c == 0 else place(x, y + d, c))
        for x, y, c in PLACES
    ]


def along_second(d):
    return [
        (place(x, y, c), place(x + d, y, c) if c == 1 else place(x, y + d, c))
        for x, y, c in PLACES
    ]


SIBLING = [(place(x, y, c), place(x, y, 1 - c)) for x, y, c in PLACES]


def send(value, pairs):
    return lax.ppermute(value, "tensor", pairs)


def from_steps(value, along):
    return send(value, along(-1)), send(value, along(2)), send(value, along(1))


def after(value, *others):
    return lax.optimization_barrier((value, *others))[0]


def dot(a, b):
    return jnp.dot(a, b, preferred_element_type=jnp.float32)


def scalar_table():
    def sign(row, column):
        return 1.0 - 2.0 * (bin(row & column).count("1") % 2)

    rows = []
    for x, y, c in PLACES:
        first, second = (x, y) if c == 0 else (y, x)
        row = [1.0 - 2.0 * c]
        row += [sign(first, (first + s) % RING) for s in range(RING)]
        row += [
            sign(second, (second + s) % RING) / math.sqrt(2 * RING * RING) for s in range(RING)
        ]
        rows.append(row + [0.0] * (16 - len(row)))
    return np.array(rows, np.float32)


def cuts_of(shares, total):
    widths = [w * total // sum(shares) for w in shares]
    starts = [sum(widths[:n]) for n in range(len(widths))]
    return list(zip(starts, widths))


VMEM = pl.BlockSpec(memory_space=pltpu.VMEM)
SCALARS = pl.BlockSpec(memory_space=pltpu.SMEM)


def call(kernel, name, flops, size, operands, outs, specs=None, **kwargs):
    return pl.pallas_call(
        kernel,
        name=name,
        compiler_params=pltpu.CompilerParams(vmem_limit_bytes=LIMIT),
        cost_estimate=pl.CostEstimate(flops=flops, bytes_accessed=size, transcendentals=0),
        in_specs=specs or [VMEM] * len(operands),
        out_specs=[VMEM] * len(outs),
        out_shape=outs,
        **kwargs,
    )(*operands)


def in_hbm(value):
    return pltpu.with_memory_space_constraint(value, pltpu.HBM)


def load(value):
    def kernel(value, out, sem):
        copy = pltpu.make_async_copy(value, out, sem)
        copy.start()
        copy.wait()

    return pl.pallas_call(
        kernel,
        name="load",
        compiler_params=pltpu.CompilerParams(vmem_limit_bytes=LIMIT),
        cost_estimate=pl.CostEstimate(
            flops=0, bytes_accessed=2 * value.size, transcendentals=0
        ),
        in_specs=[pl.BlockSpec(memory_space=pltpu.HBM)],
        out_specs=VMEM,
        out_shape=pltpu.VMEM(value.shape, value.dtype),
        scratch_shapes=[pltpu.SemaphoreType.DMA],
    )(in_hbm(value))


def stack(parts, cuts):
    rows = parts[0].shape[0]

    def kernel(*refs):
        ins, outs = refs[: len(parts)], refs[len(parts) :]
        for (at, span), out in zip(cuts, outs):
            for n, part in enumerate(ins):
                out[n * rows : (n + 1) * rows] = part[:, at : at + span]

    return call(
        kernel,
        "stack",
        0,
        sum(4 * rows * len(parts) * span for _, span in cuts),
        parts,
        [jax.ShapeDtypeStruct((rows * len(parts), span), jnp.bfloat16) for _, span in cuts],
    )


def gate_up(tokens, weights, at, span, sums, mixing):
    rows = tokens[0].shape[0]
    units = weights[0].shape[0]
    block = math.gcd(span, 1024)
    steps = span // block
    count = len(tokens)
    opening, closing = sums is None, mixing is not None

    def kernel(*refs):
        refs = list(refs)
        parts, loads, refs = refs[:count], refs[count : count + 2], refs[count + 2 :]
        before, refs = (None, refs) if opening else (refs[:count], refs[count:])
        mix = refs.pop(0) if closing else None
        outs, totals = refs[:count], refs[count:] if closing else refs[:count]
        step = pl.program_id(0)

        @pl.when(step == 0)
        def _():
            for n, total in enumerate(totals):
                total[...] = jnp.zeros(total.shape, total.dtype) if opening else before[n][...]

        for part, total in zip(parts, totals):
            for m in range(2):
                total[m] += lax.dot_general(
                    part[...], loads[m][...], BY_ROWS, preferred_element_type=jnp.float32
                )

        if closing:

            @pl.when(step == steps - 1)
            def _():
                for total, out in zip(totals, outs):
                    gate, up = total[0], total[1]
                    hidden = (gate / (1.0 + jnp.exp(-gate)) * up).astype(jnp.bfloat16)
                    out[...] = dot(hidden, mix[...]).astype(jnp.bfloat16)

    operands = [*tokens, *[in_hbm(w) for w in weights]]
    specs = [pl.BlockSpec((rows, block), lambda k: (0, k))] * count
    specs += [pl.BlockSpec((units, block), lambda k: (0, k + at // block))] * 2
    if not opening:
        operands += sums
        specs += [VMEM] * count
    kwargs = {}
    if closing:
        operands.append(mixing)
        specs.append(VMEM)
        outs = [jax.ShapeDtypeStruct((rows, units), jnp.bfloat16)] * count
        kwargs["scratch_shapes"] = [pltpu.VMEM((2, rows, units), jnp.float32)] * count
    else:
        outs = [jax.ShapeDtypeStruct((2, rows, units), jnp.float32)] * count
    return call(
        kernel,
        "gate_up",
        4 * count * rows * units * span,
        4 * units * span,
        operands,
        outs,
        specs,
        grid=(steps,),
        **kwargs,
    )


def turned(came, factors, first_scalar, i, j, major, slot):
    total = 0.0
    for s in range(RING):
        where = ((i - s) % RING, j) if major else (i, (j - s) % RING)
        at = (where[0] * RING + where[1]) * slot
        total = total + factors[first_scalar + s] * came[s][at : at + slot].astype(jnp.float32)
    return total


def first_ring(parts, scalars):
    rows, width = parts[0].shape
    slot = rows // (RING * RING)

    def kernel(own, one, two, three, factors, out):
        for i in range(RING):
            for j in range(RING):
                at = (i * RING + j) * slot
                out[at : at + slot] = turned(
                    (own, one, two, three), factors, 1, i, j, False, slot
                ).astype(jnp.bfloat16)

    return call(
        kernel,
        "first_ring",
        0,
        10 * rows * width,
        [*parts, scalars],
        [jax.ShapeDtypeStruct((rows, width), jnp.bfloat16)],
        [VMEM] * 4 + [SCALARS],
    )[0]


def second_ring(own_parts, other_parts, scalars):
    rows, width = own_parts[0].shape
    slot = rows // (RING * RING)

    def kernel(*refs):
        factors, own_out, other_out = refs[8:]
        turn = factors[0]
        for i in range(RING):
            for j in range(RING):
                at = (i * RING + j) * slot
                own = turned(refs[:4], factors, 1 + RING, i, j, True, slot)
                other = turned(refs[4:8], factors, 1 + RING, i, j, True, slot)
                own_out[at : at + slot] = (other + turn * own).astype(jnp.bfloat16)
                other_out[at : at + slot] = (own - turn * other).astype(jnp.bfloat16)

    return call(
        kernel,
        "second_ring",
        0,
        20 * rows * width,
        [*own_parts, *other_parts, scalars],
        [jax.ShapeDtypeStruct((rows, width), jnp.bfloat16)] * 2,
        [VMEM] * 8 + [SCALARS],
    )


def down(values, weights, at, span):
    rows, units = values[0].shape
    group = rows // RING
    block = min(span, 512)

    def kernel(held, held_other, loaded, loaded_other, *outs):
        for start in range(0, span, block):
            where = slice(at + start, at + start + block)
            product = dot(held[...], loaded[:, where]) + dot(
                held_other[...], loaded_other[:, where]
            )
            product = product.astype(jnp.bfloat16)
            for n, out in enumerate(outs):
                out[:, start : start + block] = product[n * group : (n + 1) * group]

    return call(
        kernel,
        "down",
        4 * rows * units * span,
        4 * units * span,
        [*values, *weights],
        [jax.ShapeDtypeStruct((group, span), jnp.bfloat16)] * RING,
    )


def fold(sides):
    count = len(sides[0])
    group = sides[0][0].shape[0]
    rows = group // RING
    width = sum(parts[0].shape[1] for parts in sides)

    def kernel(*refs):
        ins, outs = refs[: count * len(sides)], refs[count * len(sides) :]
        start = 0
        for n in range(len(sides)):
            parts = ins[count * n : count * (n + 1)]
            stop = start + parts[0].shape[1]
            for m, out in enumerate(outs):
                at = slice(m * rows, (m + 1) * rows)
                total = sum(part[at].astype(jnp.float32) for part in parts)
                out[:, start:stop] = total.astype(jnp.bfloat16)
            start = stop

    return call(
        kernel,
        "fold",
        0,
        10 * group * width,
        [part for parts in sides for part in parts],
        [jax.ShapeDtypeStruct((rows, width), jnp.bfloat16)] * RING,
    )


def to_steps(parts, along):
    return parts[0], send(parts[1], along(1)), send(parts[2], along(2)), send(parts[3], along(-1))


def body(tokens, gate_weight, up_weight, down_weight, mixing):
    width = tokens.shape[1]
    index = lax.axis_index("tensor")
    scalars = lax.dynamic_index_in_dim(jnp.asarray(scalar_table()), index, keepdims=False)

    weights = (gate_weight.T, up_weight.T)
    down_other = send(down_weight, SIBLING)

    cuts = cuts_of(GATHER_SPANS, width)
    blocks = stack((tokens, *from_steps(tokens, along_first)), cuts)
    sums, held = None, None
    for n, (at, span) in enumerate(cuts):
        parts = (blocks[n], *from_steps(blocks[n], along_second))
        if n == 2:
            parts = after(parts, sums)
        (mine,) = stack(parts, [(0, span)])
        if n == 0:
            mine = after(mine, down_other)
        theirs = send(mine, SIBLING)
        if n > 0:
            sums = gate_up(held, weights, *cuts[n - 1], sums, None)
        held = (mine, theirs)
    (own,) = gate_up((mine,), weights, at, span, sums[:1], mixing)
    (other,) = gate_up((after(theirs, own),), weights, at, span, sums[1:], mixing)
    other = send(other, SIBLING)

    own = first_ring((own, *from_steps(own, along_first)), scalars)
    other = first_ring((other, *from_steps(other, along_first)), scalars)
    loaded = (load(down_weight), pltpu.with_memory_space_constraint(down_other, pltpu.VMEM))
    own = after(own, loaded[0])
    both = second_ring(
        (own, *from_steps(own, along_second)), (other, *from_steps(other, along_second)), scalars
    )
    half = width // 2
    sides = [to_steps(down(both, loaded, at, half), along_second) for at in (0, half)]
    parts = to_steps(fold(sides), along_first)
    return sum(part.astype(jnp.float32) for part in parts).astype(jnp.bfloat16)


def solution(mesh):
    in_specs = (
        P(("dp", "tensor"), None),
        P(None, "tensor"),
        P(None, "tensor"),
        P("tensor", None),
        P(),
    )
    out_specs = P(("dp", "tensor"), None)
    return jax.shard_map(body, mesh=mesh, in_specs=in_specs, out_specs=out_specs, check_vma=False)
```

time: 179 us -> 169 us (0.944)
  waiting for transfers between devices: 54.1 us -> 85.3 us
  Pallas kernels: 43.6 us -> 29.5 us
  between operations: 13.8 us -> 0.24 us
  starting transfers between devices: 50.6 us -> 37.6 us
    ppermute x35 -> x38, waiting for transfers between devices: 53.4 us -> 85.3 us  [send(): return lax.ppermute(value, 'tensor', pairs)]
    ppermute x35 -> x38, starting transfers between devices: 50.6 us -> 37.6 us  [send(): return lax.ppermute(value, 'tensor', pairs)]
    pallas_call x5 -> x1, Pallas kernels: 13.7 us -> 3.09 us  [load(): pl.pallas_call(kernel, name='load', compiler_params=pltpu.CompilerParams(...]
    unnamed x34 -> x12, local copies, waits for them, and re-layouts: 8.89 us -> 13 us
    slice x8 -> x0, local copies, waits for them, and re-layouts: 4.06 us -> none  [the longest x6 2.58 us: body(): piece[:, part]]
    pallas_call x12 -> x14, Pallas kernels: 29.9 us -> 26.4 us  [call(): pl.pallas_call(kernel, name=name, compiler_params=pltpu.CompilerParams(vm...]
  transfers between devices with their start and end apart: 36 -> 38, of which waited for: 15 -> 23; matrix products, arithmetic and copies ran while one was open for 3% -> 0% of each run, Pallas kernels for 21% -> 13%
where the time goes in v4:
time: 169 us; the launch traced here: 167 us
  waiting for transfers between devices  85.3 us (50%)
  starting transfers between devices  37.6 us (22%)
  Pallas kernels  29.5 us (17%)
  local copies, waits for them, and re-layouts  13.7 us (8%)
    ppermute x38, waiting for transfers between devices, send(): return lax.ppermute(value, 'tensor', pairs)  85.3 us
    ppermute x38, starting transfers between devices, send(): return lax.ppermute(value, 'tensor', pairs)  37.6 us
    pallas_call x14, Pallas kernels, call(): pl.pallas_call(kernel, name=name, compiler_params=pltpu.CompilerParams(vm...  26.4 us
    unnamed x12, local copies, waits for them, and re-layouts  13 us
  transfers between devices with their start and end apart: 38, of which 23 were waited for; matrix products, arithmetic and copies ran while one was open for 0% of the time, Pallas kernels for 13%

profile of v4, /device:TPU:0, one launch (start us, length us, event | category | flops | bytes accessed | tf_op | source)
XLA Modules:
  0.0 167.1 jit_solution(4649064481355013844)
XLA Ops:
  0.0 2.8 %collective-permute-start = (bf16[16,8192]{1,0:T(8,128)(2,1)}, bf16[16,8192]{1,0:T(8,128)(2,1)S(1)}, u32[]{:S(2)}, u32[]{:S(2)}) collective-permute-start(bf16[16,8192]{1,0:T(8,128)(2,1)} %refs_0_.1), channel_id=1, source_target_pairs={{0,24},{1,7},{2,26},{3,1},{4,28},{5,3},{6,30},{7,5},{8,0},{9,15},{... | collective-permute-start | bytes 786440 | tf_op jit(solution)/shard_map/ppermute | solution.py:40
  2.8 0.8 collective-permute-start.1
  3.6 0.9 collective-permute-start.2
  4.5 5.3 %collective-permute-done.refs_1_ = bf16[16,8192]{1,0:T(8,128)(2,1)S(1)} collective-permute-done((bf16[16,8192]{1,0:T(8,128)(2,1)}, bf16[16,8192]{1,0:T(8,128)(2,1)S(1)}, u32[]{:S(2)}, u32[]{:S(2)}) %collective-permute-start) | collective-permute-done | bytes 262176 | tf_op jit(solution)/shard_map/ppermute | solution.py:40
  9.9 1.2 collective-permute-done.1.refs_2_
  11.0 2.7 %collective-permute-done.2.refs_3_ = bf16[16,8192]{1,0:T(8,128)(2,1)S(1)} collective-permute-done((bf16[16,8192]{1,0:T(8,128)(2,1)}, bf16[16,8192]{1,0:T(8,128)(2,1)S(1)}, u32[]{:S(2)}, u32[]{:S(2)}) %collective-permute-start.2) | collective-permute-done | bytes 262176 | tf_op jit(solution)/shard_map/ppermute | solution.py:40
  13.7 0.9 copy-done.5
  14.8 3.1 %collective-permute-start.6 = (bf16[64,3072]{1,0:T(8,128)(2,1)S(1)}, bf16[64,3072]{1,0:T(8,128)(2,1)S(1)}, u32[]{:S(2)}, u32[]{:S(2)}) collective-permute-start(bf16[64,3072]{1,0:T(8,128)(2,1)S(1)} %get-tuple-element.34.refs_0_), channel_id=1, source_target_pairs={{0,6},{1,25},{2,0},{3,27},{4,2},{5,29},{6,4},{7,31},{8,14},{9,1},{... | collective-permute-start | bytes 1179656 | tf_op jit(solution)/shard_map/ppermute | solution.py:40
  17.8 0.6 collective-permute-start.7
  18.5 1.0 collective-permute-start.8
  19.4 7.9 %collective-permute-done.6.refs_1_ = bf16[64,3072]{1,0:T(8,128)(2,1)S(1)} collective-permute-done((bf16[64,3072]{1,0:T(8,128)(2,1)S(1)}, bf16[64,3072]{1,0:T(8,128)(2,1)S(1)}, u32[]{:S(2)}, u32[]{:S(2)}) %collective-permute-start.6) | collective-permute-done | bytes 393248 | tf_op jit(solution)/shard_map/ppermute | solution.py:40
  27.4 4.0 %collective-permute-done.8.refs_3_ = bf16[64,3072]{1,0:T(8,128)(2,1)S(1)} collective-permute-done((bf16[64,3072]{1,0:T(8,128)(2,1)S(1)}, bf16[64,3072]{1,0:T(8,128)(2,1)S(1)}, u32[]{:S(2)}, u32[]{:S(2)}) %collective-permute-start.8) | collective-permute-done | bytes 393248 | tf_op jit(solution)/shard_map/ppermute | solution.py:40
  31.5 2.9 %copy-done.2 = bf16[448,8192]{1,0:T(8,128)(2,1)} copy-done((bf16[448,8192]{1,0:T(8,128)(2,1)}, bf16[448,8192]{1,0:T(8,128)(2,1)S(1)}, u32[]{:S(2)}) %copy-start.2) | copy-done | bytes 7340056
  35.0 0.6 collective-permute-start.12
  35.6 0.8 collective-permute-start.13
  36.4 5.7 %collective-permute-done.11.refs_1_ = bf16[64,3072]{1,0:T(8,128)(2,1)S(1)} collective-permute-done((bf16[64,3072]{1,0:T(8,128)(2,1)S(1)}, bf16[64,3072]{1,0:T(8,128)(2,1)S(1)}, u32[]{:S(2)}, u32[]{:S(2)}) %collective-permute-start.11) | collective-permute-done | bytes 393248 | tf_op jit(solution)/shard_map/ppermute | solution.py:40
  42.1 2.2 %collective-permute-done.12.refs_2_ = bf16[64,3072]{1,0:T(8,128)(2,1)S(1)} collective-permute-done((bf16[64,3072]{1,0:T(8,128)(2,1)S(1)}, bf16[64,3072]{1,0:T(8,128)(2,1)S(1)}, u32[]{:S(2)}, u32[]{:S(2)}) %collective-permute-start.12) | collective-permute-done | bytes 393248 | tf_op jit(solution)/shard_map/ppermute | solution.py:40
  44.3 4.1 %collective-permute-done.13.refs_3_ = bf16[64,3072]{1,0:T(8,128)(2,1)S(1)} collective-permute-done((bf16[64,3072]{1,0:T(8,128)(2,1)S(1)}, bf16[64,3072]{1,0:T(8,128)(2,1)S(1)}, u32[]{:S(2)}, u32[]{:S(2)}) %collective-permute-start.13) | collective-permute-done | bytes 393248 | tf_op jit(solution)/shard_map/ppermute | solution.py:40
  48.6 0.7 collective-permute-start.3
  49.3 0.6 collective-permute-start.4
  50.0 0.8 collective-permute-start.5
  50.8 5.8 %gate_up.4 = (f32[2,256,448]{2,1,0:T(8,128)S(1)}, f32[2,256,448]{2,1,0:T(8,128)S(1)}) custom-call(bf16[256,3072]{1,0:T(8,128)(2,1)S(1)} %stack.5.refs_0_, bf16[256,3072]{1,0:T(8,128)(2,1)S(1)} %collective-permute-done.10.refs_1_, bf16[448,8192]{1,0:T(8,128)(2,1)} %bitcast.4, bf16[448,8192]{1,0:T(8,128)(2,1)} %bitcast.8), custom_call_target="tpu_custom_call" | custom-call | flops 2818572288 | bytes 5505024 | tf_op jit(solution)/shard_map/gate_up/pallas_call | solution.py:82
  56.6 0.7 collective-permute-done.4.refs_2_
  57.3 2.7 %collective-permute-done.5.refs_3_ = bf16[64,2048]{1,0:T(8,128)(2,1)S(1)} collective-permute-done((bf16[64,2048]{1,0:T(8,128)(2,1)S(1)}, bf16[64,2048]{1,0:T(8,128)(2,1)S(1)}, u32[]{:S(2)}, u32[]{:S(2)}) %collective-permute-start.5) | collective-permute-done | bytes 262176 | tf_op jit(solution)/shard_map/ppermute | solution.py:40
  60.2 5.8 %gate_up.5 = (f32[2,256,448]{2,1,0:T(8,128)S(1)}, f32[2,256,448]{2,1,0:T(8,128)S(1)}) custom-call(bf16[256,3072]{1,0:T(8,128)(2,1)S(1)} %stack.7.refs_0_, bf16[256,3072]{1,0:T(8,128)(2,1)S(1)} %collective-permute-done.14.refs_1_, bf16[448,8192]{1,0:T(8,128)(2,1)} %bitcast.5, bf16[448,8192]{1,0:T(8,128)(2,1)} %bitcast.9, ...), custom_call_target="tpu_custom_call" | custom-call | flops 2818572288 | bytes 5505024 | tf_op jit(solution)/shard_map/gate_up/pallas_call | solution.py:82
  66.0 3.4 %gate_up.6.own = bf16[256,448]{1,0:T(8,128)(2,1)S(1)} custom-call(bf16[256,2048]{1,0:T(8,128)(2,1)S(1)} %stack.6.refs_0_, bf16[448,8192]{1,0:T(8,128)(2,1)} %bitcast.6, bf16[448,8192]{1,0:T(8,128)(2,1)} %bitcast.10, f32[2,256,448]{2,1,0:T(8,128)S(1)} %get-tuple-element.43.refs_3_, bf16[448,448]{1,0:T(8,128)(2,1)S(1)} %copy-done.4), custom_call_target="tpu_custom_call" | custom-call | flops 939524096 | bytes 3670016 | tf_op jit(solution)/shard_map/gate_up/pallas_call | solution.py:82
  69.4 3.4 %gate_up.7 = bf16[256,448]{1,0:T(8,128)(2,1)S(1)} custom-call(bf16[256,2048]{1,0:T(8,128)(2,1)S(1)} %collective-permute-done.21.refs_0_, bf16[448,8192]{1,0:T(8,128)(2,1)} %bitcast.7, bf16[448,8192]{1,0:T(8,128)(2,1)} %bitcast.11, f32[2,256,448]{2,1,0:T(8,128)S(1)} %get-tuple-element.46.refs_3_, bf16[448,448]{1,0:T(8,128)(2,1)S(1)} %copy-done.4), custom_call_target="tpu_custom_call" | custom-call | flops 939524096 | bytes 3670016 | tf_op jit(solution)/shard_map/gate_up/pallas_call | solution.py:82
  74.0 0.8 collective-permute-start.16
  74.8 0.9 collective-permute-start.17
  75.6 3.1 %load.1.loaded = bf16[448,8192]{1,0:T(8,128)(2,1)S(1)} custom-call(bf16[448,8192]{1,0:T(8,128)(2,1)} %value.1), custom_call_target="tpu_custom_call" | custom-call | bytes 7340032 | tf_op jit(solution)/shard_map/load/pallas_call | solution.py:104
  78.7 3.0 %copy-done = bf16[448,8192]{1,0:T(8,128)(2,1)} copy-done((bf16[448,8192]{1,0:T(8,128)(2,1)}, bf16[448,8192]{1,0:T(8,128)(2,1)S(1)}, u32[]{:S(2)}) %copy-start) | copy-done | bytes 7340056
  81.7 0.7 dynamic-slice_bitcast_fusion.factors.refs_8_
  82.4 2.5 %collective-permute-start.23 = (bf16[256,448]{1,0:T(8,128)(2,1)S(1)}, bf16[256,448]{1,0:T(8,128)(2,1)S(1)}, u32[]{:S(2)}, u32[]{:S(2)}) collective-permute-start(bf16[256,448]{1,0:T(8,128)(2,1)S(1)} %collective-permute-done.22.own), channel_id=1, source_target_pairs={{0,24},{1,7},{2,26},{3,1},{4,28},{5,3},{6,30},{7,5},{8,0},{9,15},{... | collective-permute-start | bytes 688136 | tf_op jit(solution)/shard_map/ppermute | solution.py:40
  84.9 0.7 first_ring.2.refs_0_
  85.6 1.6 collective-permute-start.24
  87.2 1.4 collective-permute-start.25
  90.0 0.8 collective-permute-start.20
  90.7 5.2 %collective-permute-done.24.two = bf16[256,448]{1,0:T(8,128)(2,1)S(1)} collective-permute-done((bf16[256,448]{1,0:T(8,128)(2,1)S(1)}, bf16[256,448]{1,0:T(8,128)(2,1)S(1)}, u32[]{:S(2)}, u32[]{:S(2)}) %collective-permute-start.24) | collective-permute-done | bytes 229408 | tf_op jit(solution)/shard_map/ppermute | solution.py:40
  95.9 6.1 %collective-permute-done.25.three = bf16[256,448]{1,0:T(8,128)(2,1)S(1)} collective-permute-done((bf16[256,448]{1,0:T(8,128)(2,1)S(1)}, bf16[256,448]{1,0:T(8,128)(2,1)S(1)}, u32[]{:S(2)}, u32[]{:S(2)}) %collective-permute-start.25) | collective-permute-done | bytes 229408 | tf_op jit(solution)/shard_map/ppermute | solution.py:40
  102.0 0.7 first_ring.3.refs_4_
  102.9 1.1 collective-permute-start.27
  103.9 0.9 collective-permute-start.28
  104.9 4.3 %collective-permute-done.26.refs_5_ = bf16[256,448]{1,0:T(8,128)(2,1)S(1)} collective-permute-done((bf16[256,448]{1,0:T(8,128)(2,1)S(1)}, bf16[256,448]{1,0:T(8,128)(2,1)S(1)}, u32[]{:S(2)}, u32[]{:S(2)}) %collective-permute-start.26) | collective-permute-done | bytes 229408 | tf_op jit(solution)/shard_map/ppermute | solution.py:40
  109.2 1.7 %collective-permute-done.27.refs_6_ = bf16[256,448]{1,0:T(8,128)(2,1)S(1)} collective-permute-done((bf16[256,448]{1,0:T(8,128)(2,1)S(1)}, bf16[256,448]{1,0:T(8,128)(2,1)S(1)}, u32[]{:S(2)}, u32[]{:S(2)}) %collective-permute-start.27) | collective-permute-done | bytes 229408 | tf_op jit(solution)/shard_map/ppermute | solution.py:40
  110.9 2.7 %collective-permute-done.28.refs_7_ = bf16[256,448]{1,0:T(8,128)(2,1)S(1)} collective-permute-done((bf16[256,448]{1,0:T(8,128)(2,1)S(1)}, bf16[256,448]{1,0:T(8,128)(2,1)S(1)}, u32[]{:S(2)}, u32[]{:S(2)}) %collective-permute-start.28) | collective-permute-done | bytes 229408 | tf_op jit(solution)/shard_map/ppermute | solution.py:40
  113.6 1.0 second_ring.1
  114.6 3.1 %copy-done.1 = bf16[448,8192]{1,0:T(8,128)(2,1)S(1)} copy-done((bf16[448,8192]{1,0:T(8,128)(2,1)S(1)}, bf16[448,8192]{1,0:T(8,128)(2,1)}, u32[]{:S(2)}) %copy-start.1) | copy-done | bytes 7340056
  117.7 3.1 %copy-done.3 = bf16[448,8192]{1,0:T(8,128)(2,1)S(1)} copy-done((bf16[448,8192]{1,0:T(8,128)(2,1)S(1)}, bf16[448,8192]{1,0:T(8,128)(2,1)}, u32[]{:S(2)}) %copy-start.3) | copy-done | bytes 7340056
  120.8 2.3 %down.3 = (bf16[64,4096]{1,0:T(8,128)(2,1)S(1)}, bf16[64,4096]{1,0:T(8,128)(2,1)S(1)}, bf16[64,4096]{1,0:T(8,128)(2,1)S(1)}, bf16[64,4096]{1,0:T(8,128)(2,1)S(1)}) custom-call(bf16[256,448]{1,0:T(8,128)(2,1)S(1)} %get-tuple-element.47.held, bf16[256,448]{1,0:T(8,128)(2,1)S(1)} %get-tuple-element.48.held_other, bf16[448,8192]{1,0:T(8,128)(2,1)S(1)} %copy-done.1, ...), custom_call_target="tpu_custom_call" | custom-call | flops 1879048192 | bytes 7340032 | tf_op jit(solution)/shard_map/down/pallas_call | solution.py:82
  123.2 2.5 %collective-permute-start.33 = (bf16[64,4096]{1,0:T(8,128)(2,1)S(1)}, bf16[64,4096]{1,0:T(8,128)(2,1)S(1)}, u32[]{:S(2)}, u32[]{:S(2)}) collective-permute-start(bf16[64,4096]{1,0:T(8,128)(2,1)S(1)} %get-tuple-element.55), channel_id=1, source_target_pairs={{0,4},{1,17},{2,6},{3,19},{4,0},{5,21},{6,2},{7,23},{8,12},{9,25},... | collective-permute-start | bytes 1572872 | tf_op jit(solution)/shard_map/ppermute | solution.py:40
  125.7 1.1 collective-permute-start.34
  126.8 2.3 %down.2 = (bf16[64,4096]{1,0:T(8,128)(2,1)S(1)}, bf16[64,4096]{1,0:T(8,128)(2,1)S(1)}, bf16[64,4096]{1,0:T(8,128)(2,1)S(1)}, bf16[64,4096]{1,0:T(8,128)(2,1)S(1)}) custom-call(bf16[256,448]{1,0:T(8,128)(2,1)S(1)} %get-tuple-element.47.held, bf16[256,448]{1,0:T(8,128)(2,1)S(1)} %get-tuple-element.48.held_other, bf16[448,8192]{1,0:T(8,128)(2,1)S(1)} %copy-done.1, ...), custom_call_target="tpu_custom_call" | custom-call | flops 1879048192 | bytes 7340032 | tf_op jit(solution)/shard_map/down/pallas_call | solution.py:82
  129.2 1.0 collective-permute-start.29
  130.2 1.7 %collective-permute-start.30 = (bf16[64,4096]{1,0:T(8,128)(2,1)S(1)}, bf16[64,4096]{1,0:T(8,128)(2,1)S(1)}, u32[]{:S(2)}, u32[]{:S(2)}) collective-permute-start(bf16[64,4096]{1,0:T(8,128)(2,1)S(1)} %get-tuple-element.51), channel_id=1, source_target_pairs={{0,4},{1,17},{2,6},{3,19},{4,0},{5,21},{6,2},{7,23},{8,12},{9,25},... | collective-permute-start | bytes 1572872 | tf_op jit(solution)/shard_map/ppermute | solution.py:40
  131.9 7.4 %collective-permute-done.32.refs_5_ = bf16[64,4096]{1,0:T(8,128)(2,1)S(1)} collective-permute-done((bf16[64,4096]{1,0:T(8,128)(2,1)S(1)}, bf16[64,4096]{1,0:T(8,128)(2,1)S(1)}, u32[]{:S(2)}, u32[]{:S(2)}) %collective-permute-start.32) | collective-permute-done | bytes 524320 | tf_op jit(solution)/shard_map/ppermute | solution.py:40
  139.2 0.9 collective-permute-done.34.refs_7_
  140.1 10.3 %collective-permute-done.29.refs_1_ = bf16[64,4096]{1,0:T(8,128)(2,1)S(1)} collective-permute-done((bf16[64,4096]{1,0:T(8,128)(2,1)S(1)}, bf16[64,4096]{1,0:T(8,128)(2,1)S(1)}, u32[]{:S(2)}, u32[]{:S(2)}) %collective-permute-start.29) | collective-permute-done | bytes 524320 | tf_op jit(solution)/shard_map/ppermute | solution.py:40
  150.4 1.0 collective-permute-done.30.refs_2_
  151.4 3.0 %collective-permute-done.31.refs_3_ = bf16[64,4096]{1,0:T(8,128)(2,1)S(1)} collective-permute-done((bf16[64,4096]{1,0:T(8,128)(2,1)S(1)}, bf16[64,4096]{1,0:T(8,128)(2,1)S(1)}, u32[]{:S(2)}, u32[]{:S(2)}) %collective-permute-start.31) | collective-permute-done | bytes 524320 | tf_op jit(solution)/shard_map/ppermute | solution.py:40
  155.0 2.7 %collective-permute-start.36 = (bf16[16,8192]{1,0:T(8,128)(2,1)S(1)}, bf16[16,8192]{1,0:T(8,128)(2,1)S(1)}, u32[]{:S(2)}, u32[]{:S(2)}) collective-permute-start(bf16[16,8192]{1,0:T(8,128)(2,1)S(1)} %get-tuple-element.59), channel_id=1, source_target_pairs={{0,16},{1,5},{2,18},{3,7},{4,20},{5,1},{6,22},{7,3},{8,24},{9,13},... | collective-permute-start | bytes 786440 | tf_op jit(solution)/shard_map/ppermute | solution.py:40
  157.7 2.5 %collective-permute-start.37 = (bf16[16,8192]{1,0:T(8,128)(2,1)S(1)}, bf16[16,8192]{1,0:T(8,128)(2,1)S(1)}, u32[]{:S(2)}, u32[]{:S(2)}) collective-permute-start(bf16[16,8192]{1,0:T(8,128)(2,1)S(1)} %get-tuple-element.60), channel_id=1, source_target_pairs={{0,24},{1,7},{2,26},{3,1},{4,28},{5,3},{6,30},{7,5},{8,0},{9,15},{... | collective-permute-start | bytes 786440 | tf_op jit(solution)/shard_map/ppermute | solution.py:40
  160.3 5.1 %collective-permute-done.35 = bf16[16,8192]{1,0:T(8,128)(2,1)S(1)} collective-permute-done((bf16[16,8192]{1,0:T(8,128)(2,1)S(1)}, bf16[16,8192]{1,0:T(8,128)(2,1)S(1)}, u32[]{:S(2)}, u32[]{:S(2)}) %collective-permute-start.35) | collective-permute-done | bytes 262176 | tf_op jit(solution)/shard_map/ppermute | solution.py:40
  165.4 0.9 collective-permute-done.37
  166.3 0.8 add_convert_fusion
  (41 shorter events, 4.4 us)
Async XLA Ops:
  0.0 31.5 %collective-permute-start.9 = (bf16[448,8192]{1,0:T(8,128)(2,1)}, bf16[448,8192]{1,0:T(8,128)(2,1)S(1)}, u32[]{:S(2)}, u32[]{:S(2)}) collective-permute-start(bf16[448,8192]{1,0:T(8,128)(2,1)} %value.1), channel_id=1, source_target_pairs={{0,1},{1,0},{2,3},{3,2},{4,5},{5,4},{6,7},{7,6},{8,9},{9,8},{10,11... | collective-permute-start | bytes 22020104 | tf_op jit(solution)/shard_map/ppermute | solution.py:40
  0.0 9.9 %collective-permute-start = (bf16[16,8192]{1,0:T(8,128)(2,1)}, bf16[16,8192]{1,0:T(8,128)(2,1)S(1)}, u32[]{:S(2)}, u32[]{:S(2)}) collective-permute-start(bf16[16,8192]{1,0:T(8,128)(2,1)} %refs_0_.1), channel_id=1, source_target_pairs={{0,24},{1,7},{2,26},{3,1},{4,28},{5,3},{6,30},{7,5},{8,0},{9,15},{... | collective-permute-start | bytes 786440 | tf_op jit(solution)/shard_map/ppermute | solution.py:40
  2.8 8.2 %collective-permute-start.1 = (bf16[16,8192]{1,0:T(8,128)(2,1)}, bf16[16,8192]{1,0:T(8,128)(2,1)S(1)}, u32[]{:S(2)}, u32[]{:S(2)}) collective-permute-start(bf16[16,8192]{1,0:T(8,128)(2,1)} %refs_0_.1), channel_id=1, source_target_pairs={{0,16},{1,5},{2,18},{3,7},{4,20},{5,1},{6,22},{7,3},{8,24},{9,13},... | collective-permute-start | bytes 786440 | tf_op jit(solution)/shard_map/ppermute | solution.py:40
  3.6 10.1 %collective-permute-start.2 = (bf16[16,8192]{1,0:T(8,128)(2,1)}, bf16[16,8192]{1,0:T(8,128)(2,1)S(1)}, u32[]{:S(2)}, u32[]{:S(2)}) collective-permute-start(bf16[16,8192]{1,0:T(8,128)(2,1)} %refs_0_.1), channel_id=1, source_target_pairs={{0,8},{1,3},{2,10},{3,5},{4,12},{5,7},{6,14},{7,1},{8,16},{9,11},{... | collective-permute-start | bytes 786440 | tf_op jit(solution)/shard_map/ppermute | solution.py:40
  13.7 1.0 copy-start.5
  14.8 12.6 %collective-permute-start.6 = (bf16[64,3072]{1,0:T(8,128)(2,1)S(1)}, bf16[64,3072]{1,0:T(8,128)(2,1)S(1)}, u32[]{:S(2)}, u32[]{:S(2)}) collective-permute-start(bf16[64,3072]{1,0:T(8,128)(2,1)S(1)} %get-tuple-element.34.refs_0_), channel_id=1, source_target_pairs={{0,6},{1,25},{2,0},{3,27},{4,2},{5,29},{6,4},{7,31},{8,14},{9,1},{... | collective-permute-start | bytes 1179656 | tf_op jit(solution)/shard_map/ppermute | solution.py:40
  17.8 9.5 %collective-permute-start.7 = (bf16[64,3072]{1,0:T(8,128)(2,1)S(1)}, bf16[64,3072]{1,0:T(8,128)(2,1)S(1)}, u32[]{:S(2)}, u32[]{:S(2)}) collective-permute-start(bf16[64,3072]{1,0:T(8,128)(2,1)S(1)} %get-tuple-element.34.refs_0_), channel_id=1, source_target_pairs={{0,4},{1,17},{2,6},{3,19},{4,0},{5,21},{6,2},{7,23},{8,12},{9,25},... | collective-permute-start | bytes 1179656 | tf_op jit(solution)/shard_map/ppermute | solution.py:40
  18.5 12.9 %collective-permute-start.8 = (bf16[64,3072]{1,0:T(8,128)(2,1)S(1)}, bf16[64,3072]{1,0:T(8,128)(2,1)S(1)}, u32[]{:S(2)}, u32[]{:S(2)}) collective-permute-start(bf16[64,3072]{1,0:T(8,128)(2,1)S(1)} %get-tuple-element.34.refs_0_), channel_id=1, source_target_pairs={{0,2},{1,9},{2,4},{3,11},{4,6},{5,13},{6,0},{7,15},{8,10},{9,17},{... | collective-permute-start | bytes 1179656 | tf_op jit(solution)/shard_map/ppermute | solution.py:40
  31.5 2.9 %copy-start.2 = (bf16[448,8192]{1,0:T(8,128)(2,1)}, bf16[448,8192]{1,0:T(8,128)(2,1)S(1)}, u32[]{:S(2)}) copy-start(bf16[448,8192]{1,0:T(8,128)(2,1)S(1)} %collective-permute-done.9.loaded_other) | copy-start | bytes 22020100
  34.3 16.4 %collective-permute-start.10 = (bf16[256,3072]{1,0:T(8,128)(2,1)S(1)}, bf16[256,3072]{1,0:T(8,128)(2,1)S(1)}, u32[]{:S(2)}, u32[]{:S(2)}) collective-permute-start(bf16[256,3072]{1,0:T(8,128)(2,1)S(1)} %stack.5.refs_0_), channel_id=1, source_target_pairs={{0,1},{1,0},{2,3},{3,2},{4,5},{5,4},{6,7},{7,6},{8,9},{9,8},{10,11... | collective-permute-start | bytes 4718600 | tf_op jit(solution)/shard_map/ppermute | solution.py:40
  34.3 7.8 %collective-permute-start.11 = (bf16[64,3072]{1,0:T(8,128)(2,1)S(1)}, bf16[64,3072]{1,0:T(8,128)(2,1)S(1)}, u32[]{:S(2)}, u32[]{:S(2)}) collective-permute-start(bf16[64,3072]{1,0:T(8,128)(2,1)S(1)} %get-tuple-element.42.refs_0_), channel_id=1, source_target_pairs={{0,6},{1,25},{2,0},{3,27},{4,2},{5,29},{6,4},{7,31},{8,14},{9,1},{... | collective-permute-start | bytes 1179656 | tf_op jit(solution)/shard_map/ppermute | solution.py:40
  35.0 9.4 %collective-permute-start.12 = (bf16[64,3072]{1,0:T(8,128)(2,1)S(1)}, bf16[64,3072]{1,0:T(8,128)(2,1)S(1)}, u32[]{:S(2)}, u32[]{:S(2)}) collective-permute-start(bf16[64,3072]{1,0:T(8,128)(2,1)S(1)} %get-tuple-element.42.refs_0_), channel_id=1, source_target_pairs={{0,4},{1,17},{2,6},{3,19},{4,0},{5,21},{6,2},{7,23},{8,12},{9,25},... | collective-permute-start | bytes 1179656 | tf_op jit(solution)/shard_map/ppermute | solution.py:40
  35.6 12.9 %collective-permute-start.13 = (bf16[64,3072]{1,0:T(8,128)(2,1)S(1)}, bf16[64,3072]{1,0:T(8,128)(2,1)S(1)}, u32[]{:S(2)}, u32[]{:S(2)}) collective-permute-start(bf16[64,3072]{1,0:T(8,128)(2,1)S(1)} %get-tuple-element.42.refs_0_), channel_id=1, source_target_pairs={{0,2},{1,9},{2,4},{3,11},{4,6},{5,13},{6,0},{7,15},{8,10},{9,17},{... | collective-permute-start | bytes 1179656 | tf_op jit(solution)/shard_map/ppermute | solution.py:40
  48.6 11.6 %collective-permute-start.14 = (bf16[256,3072]{1,0:T(8,128)(2,1)S(1)}, bf16[256,3072]{1,0:T(8,128)(2,1)S(1)}, u32[]{:S(2)}, u32[]{:S(2)}) collective-permute-start(bf16[256,3072]{1,0:T(8,128)(2,1)S(1)} %stack.7.refs_0_), channel_id=1, source_target_pairs={{0,1},{1,0},{2,3},{3,2},{4,5},{5,4},{6,7},{7,6},{8,9},{9,8},{10,11... | collective-permute-start | bytes 4718600 | tf_op jit(solution)/shard_map/ppermute | solution.py:40
  48.6 7.9 %collective-permute-start.3 = (bf16[64,2048]{1,0:T(8,128)(2,1)S(1)}, bf16[64,2048]{1,0:T(8,128)(2,1)S(1)}, u32[]{:S(2)}, u32[]{:S(2)}) collective-permute-start(bf16[64,2048]{1,0:T(8,128)(2,1)S(1)} %get-tuple-element.38.refs_0_), channel_id=1, source_target_pairs={{0,6},{1,25},{2,0},{3,27},{4,2},{5,29},{6,4},{7,31},{8,14},{9,1},{... | collective-permute-start | bytes 786440 | tf_op jit(solution)/shard_map/ppermute | solution.py:40
  49.3 8.0 %collective-permute-start.4 = (bf16[64,2048]{1,0:T(8,128)(2,1)S(1)}, bf16[64,2048]{1,0:T(8,128)(2,1)S(1)}, u32[]{:S(2)}, u32[]{:S(2)}) collective-permute-start(bf16[64,2048]{1,0:T(8,128)(2,1)S(1)} %get-tuple-element.38.refs_0_), channel_id=1, source_target_pairs={{0,4},{1,17},{2,6},{3,19},{4,0},{5,21},{6,2},{7,23},{8,12},{9,25},... | collective-permute-start | bytes 786440 | tf_op jit(solution)/shard_map/ppermute | solution.py:40
  50.0 10.1 %collective-permute-start.5 = (bf16[64,2048]{1,0:T(8,128)(2,1)S(1)}, bf16[64,2048]{1,0:T(8,128)(2,1)S(1)}, u32[]{:S(2)}, u32[]{:S(2)}) collective-permute-start(bf16[64,2048]{1,0:T(8,128)(2,1)S(1)} %get-tuple-element.38.refs_0_), channel_id=1, source_target_pairs={{0,2},{1,9},{2,4},{3,11},{4,6},{5,13},{6,0},{7,15},{8,10},{9,17},{... | collective-permute-start | bytes 786440 | tf_op jit(solution)/shard_map/ppermute | solution.py:40
  60.1 5.9 %copy-start.4 = (bf16[448,448]{1,0:T(8,128)(2,1)S(1)}, bf16[448,448]{1,0:T(8,128)(2,1)}, u32[]{:S(2)}) copy-start(bf16[448,448]{1,0:T(8,128)(2,1)} %refs_4_.3) | copy-start | bytes 1204228
  60.1 9.3 %collective-permute-start.21 = (bf16[256,2048]{1,0:T(8,128)(2,1)S(1)}, bf16[256,2048]{1,0:T(8,128)(2,1)S(1)}, u32[]{:S(2)}, u32[]{:S(2)}) collective-permute-start(bf16[256,2048]{1,0:T(8,128)(2,1)S(1)} %stack.6.refs_0_), channel_id=1, source_target_pairs={{0,1},{1,0},{2,3},{3,2},{4,5},{5,4},{6,7},{7,6},{8,9},{9,8},{10,11... | collective-permute-start | bytes 3145736 | tf_op jit(solution)/shard_map/ppermute | solution.py:40
  72.8 9.6 %collective-permute-start.22 = (bf16[256,448]{1,0:T(8,128)(2,1)S(1)}, bf16[256,448]{1,0:T(8,128)(2,1)S(1)}, u32[]{:S(2)}, u32[]{:S(2)}) collective-permute-start(bf16[256,448]{1,0:T(8,128)(2,1)S(1)} %gate_up.7), channel_id=1, source_target_pairs={{0,1},{1,0},{2,3},{3,2},{4,5},{5,4},{6,7},{7,6},{8,9},{9,8},{10,11... | collective-permute-start | bytes 688136 | tf_op jit(solution)/shard_map/ppermute | solution.py:40
  73.4 11.5 %collective-permute-start.15 = (bf16[256,448]{1,0:T(8,128)(2,1)S(1)}, bf16[256,448]{1,0:T(8,128)(2,1)S(1)}, u32[]{:S(2)}, u32[]{:S(2)}) collective-permute-start(bf16[256,448]{1,0:T(8,128)(2,1)S(1)} %gate_up.6.own), channel_id=1, source_target_pairs={{0,24},{1,7},{2,26},{3,1},{4,28},{5,3},{6,30},{7,5},{8,0},{9,15},{... | collective-permute-start | bytes 688136 | tf_op jit(solution)/shard_map/ppermute | solution.py:40
  74.0 10.9 %collective-permute-start.16 = (bf16[256,448]{1,0:T(8,128)(2,1)S(1)}, bf16[256,448]{1,0:T(8,128)(2,1)S(1)}, u32[]{:S(2)}, u32[]{:S(2)}) collective-permute-start(bf16[256,448]{1,0:T(8,128)(2,1)S(1)} %gate_up.6.own), channel_id=1, source_target_pairs={{0,16},{1,5},{2,18},{3,7},{4,20},{5,1},{6,22},{7,3},{8,24},{9,13},... | collective-permute-start | bytes 688136 | tf_op jit(solution)/shard_map/ppermute | solution.py:40
  74.8 10.1 %collective-permute-start.17 = (bf16[256,448]{1,0:T(8,128)(2,1)S(1)}, bf16[256,448]{1,0:T(8,128)(2,1)S(1)}, u32[]{:S(2)}, u32[]{:S(2)}) collective-permute-start(bf16[256,448]{1,0:T(8,128)(2,1)S(1)} %gate_up.6.own), channel_id=1, source_target_pairs={{0,8},{1,3},{2,10},{3,5},{4,12},{5,7},{6,14},{7,1},{8,16},{9,11},{... | collective-permute-start | bytes 688136 | tf_op jit(solution)/shard_map/ppermute | solution.py:40
  78.7 3.0 %copy-start = (bf16[448,8192]{1,0:T(8,128)(2,1)}, bf16[448,8192]{1,0:T(8,128)(2,1)S(1)}, u32[]{:S(2)}) copy-start(bf16[448,8192]{1,0:T(8,128)(2,1)S(1)} %load.1.loaded) | copy-start | bytes 22020100
  82.4 7.5 %collective-permute-start.23 = (bf16[256,448]{1,0:T(8,128)(2,1)S(1)}, bf16[256,448]{1,0:T(8,128)(2,1)S(1)}, u32[]{:S(2)}, u32[]{:S(2)}) collective-permute-start(bf16[256,448]{1,0:T(8,128)(2,1)S(1)} %collective-permute-done.22.own), channel_id=1, source_target_pairs={{0,24},{1,7},{2,26},{3,1},{4,28},{5,3},{6,30},{7,5},{8,0},{9,15},{... | collective-permute-start | bytes 688136 | tf_op jit(solution)/shard_map/ppermute | solution.py:40
  85.6 10.3 %collective-permute-start.24 = (bf16[256,448]{1,0:T(8,128)(2,1)S(1)}, bf16[256,448]{1,0:T(8,128)(2,1)S(1)}, u32[]{:S(2)}, u32[]{:S(2)}) collective-permute-start(bf16[256,448]{1,0:T(8,128)(2,1)S(1)} %collective-permute-done.22.own), channel_id=1, source_target_pairs={{0,16},{1,5},{2,18},{3,7},{4,20},{5,1},{6,22},{7,3},{8,24},{9,13},... | collective-permute-start | bytes 688136 | tf_op jit(solution)/shard_map/ppermute | solution.py:40
  87.2 14.8 %collective-permute-start.25 = (bf16[256,448]{1,0:T(8,128)(2,1)S(1)}, bf16[256,448]{1,0:T(8,128)(2,1)S(1)}, u32[]{:S(2)}, u32[]{:S(2)}) collective-permute-start(bf16[256,448]{1,0:T(8,128)(2,1)S(1)} %collective-permute-done.22.own), channel_id=1, source_target_pairs={{0,8},{1,3},{2,10},{3,5},{4,12},{5,7},{6,14},{7,1},{8,16},{9,11},{... | collective-permute-start | bytes 688136 | tf_op jit(solution)/shard_map/ppermute | solution.py:40
  88.6 15.3 %collective-permute-start.18 = (bf16[256,448]{1,0:T(8,128)(2,1)S(1)}, bf16[256,448]{1,0:T(8,128)(2,1)S(1)}, u32[]{:S(2)}, u32[]{:S(2)}) collective-permute-start(bf16[256,448]{1,0:T(8,128)(2,1)S(1)} %first_ring.2.refs_0_), channel_id=1, source_target_pairs={{0,6},{1,25},{2,0},{3,27},{4,2},{5,29},{6,4},{7,31},{8,14},{9,1},{... | collective-permute-start | bytes 688136 | tf_op jit(solution)/shard_map/ppermute | solution.py:40
  89.2 15.7 %collective-permute-start.19 = (bf16[256,448]{1,0:T(8,128)(2,1)S(1)}, bf16[256,448]{1,0:T(8,128)(2,1)S(1)}, u32[]{:S(2)}, u32[]{:S(2)}) collective-permute-start(bf16[256,448]{1,0:T(8,128)(2,1)S(1)} %first_ring.2.refs_0_), channel_id=1, source_target_pairs={{0,4},{1,17},{2,6},{3,19},{4,0},{5,21},{6,2},{7,23},{8,12},{9,25},... | collective-permute-start | bytes 688136 | tf_op jit(solution)/shard_map/ppermute | solution.py:40
  90.0 14.9 %collective-permute-start.20 = (bf16[256,448]{1,0:T(8,128)(2,1)S(1)}, bf16[256,448]{1,0:T(8,128)(2,1)S(1)}, u32[]{:S(2)}, u32[]{:S(2)}) collective-permute-start(bf16[256,448]{1,0:T(8,128)(2,1)S(1)} %first_ring.2.refs_0_), channel_id=1, source_target_pairs={{0,2},{1,9},{2,4},{3,11},{4,6},{5,13},{6,0},{7,15},{8,10},{9,17},{... | collective-permute-start | bytes 688136 | tf_op jit(solution)/shard_map/ppermute | solution.py:40
  102.8 6.4 %collective-permute-start.26 = (bf16[256,448]{1,0:T(8,128)(2,1)S(1)}, bf16[256,448]{1,0:T(8,128)(2,1)S(1)}, u32[]{:S(2)}, u32[]{:S(2)}) collective-permute-start(bf16[256,448]{1,0:T(8,128)(2,1)S(1)} %first_ring.3.refs_4_), channel_id=1, source_target_pairs={{0,6},{1,25},{2,0},{3,27},{4,2},{5,29},{6,4},{7,31},{8,14},{9,1},{... | collective-permute-start | bytes 688136 | tf_op jit(solution)/shard_map/ppermute | solution.py:40
  102.9 8.1 %collective-permute-start.27 = (bf16[256,448]{1,0:T(8,128)(2,1)S(1)}, bf16[256,448]{1,0:T(8,128)(2,1)S(1)}, u32[]{:S(2)}, u32[]{:S(2)}) collective-permute-start(bf16[256,448]{1,0:T(8,128)(2,1)S(1)} %first_ring.3.refs_4_), channel_id=1, source_target_pairs={{0,4},{1,17},{2,6},{3,19},{4,0},{5,21},{6,2},{7,23},{8,12},{9,25},... | collective-permute-start | bytes 688136 | tf_op jit(solution)/shard_map/ppermute | solution.py:40
  103.9 9.7 %collective-permute-start.28 = (bf16[256,448]{1,0:T(8,128)(2,1)S(1)}, bf16[256,448]{1,0:T(8,128)(2,1)S(1)}, u32[]{:S(2)}, u32[]{:S(2)}) collective-permute-start(bf16[256,448]{1,0:T(8,128)(2,1)S(1)} %first_ring.3.refs_4_), channel_id=1, source_target_pairs={{0,2},{1,9},{2,4},{3,11},{4,6},{5,13},{6,0},{7,15},{8,10},{9,17},{... | collective-permute-start | bytes 688136 | tf_op jit(solution)/shard_map/ppermute | solution.py:40
  114.6 3.1 %copy-start.1 = (bf16[448,8192]{1,0:T(8,128)(2,1)S(1)}, bf16[448,8192]{1,0:T(8,128)(2,1)}, u32[]{:S(2)}) copy-start(bf16[448,8192]{1,0:T(8,128)(2,1)} %copy-done) | copy-start | bytes 22020100
  117.7 3.1 %copy-start.3 = (bf16[448,8192]{1,0:T(8,128)(2,1)S(1)}, bf16[448,8192]{1,0:T(8,128)(2,1)}, u32[]{:S(2)}) copy-start(bf16[448,8192]{1,0:T(8,128)(2,1)} %copy-done.2) | copy-start | bytes 22020100
  123.1 16.1 %collective-permute-start.32 = (bf16[64,4096]{1,0:T(8,128)(2,1)S(1)}, bf16[64,4096]{1,0:T(8,128)(2,1)S(1)}, u32[]{:S(2)}, u32[]{:S(2)}) collective-permute-start(bf16[64,4096]{1,0:T(8,128)(2,1)S(1)} %get-tuple-element.54), channel_id=1, source_target_pairs={{0,2},{1,9},{2,4},{3,11},{4,6},{5,13},{6,0},{7,15},{8,10},{9,17},{... | collective-permute-start | bytes 1572872 | tf_op jit(solution)/shard_map/ppermute | solution.py:40
  123.2 16.0 %collective-permute-start.33 = (bf16[64,4096]{1,0:T(8,128)(2,1)S(1)}, bf16[64,4096]{1,0:T(8,128)(2,1)S(1)}, u32[]{:S(2)}, u32[]{:S(2)}) collective-permute-start(bf16[64,4096]{1,0:T(8,128)(2,1)S(1)} %get-tuple-element.55), channel_id=1, source_target_pairs={{0,4},{1,17},{2,6},{3,19},{4,0},{5,21},{6,2},{7,23},{8,12},{9,25},... | collective-permute-start | bytes 1572872 | tf_op jit(solution)/shard_map/ppermute | solution.py:40
  125.7 14.4 %collective-permute-start.34 = (bf16[64,4096]{1,0:T(8,128)(2,1)S(1)}, bf16[64,4096]{1,0:T(8,128)(2,1)S(1)}, u32[]{:S(2)}, u32[]{:S(2)}) collective-permute-start(bf16[64,4096]{1,0:T(8,128)(2,1)S(1)} %get-tuple-element.56), channel_id=1, source_target_pairs={{0,6},{1,25},{2,0},{3,27},{4,2},{5,29},{6,4},{7,31},{8,14},{9,1},{... | collective-permute-start | bytes 1572872 | tf_op jit(solution)/shard_map/ppermute | solution.py:40
  129.2 21.2 %collective-permute-start.29 = (bf16[64,4096]{1,0:T(8,128)(2,1)S(1)}, bf16[64,4096]{1,0:T(8,128)(2,1)S(1)}, u32[]{:S(2)}, u32[]{:S(2)}) collective-permute-start(bf16[64,4096]{1,0:T(8,128)(2,1)S(1)} %get-tuple-element.50), channel_id=1, source_target_pairs={{0,2},{1,9},{2,4},{3,11},{4,6},{5,13},{6,0},{7,15},{8,10},{9,17},{... | collective-permute-start | bytes 1572872 | tf_op jit(solution)/shard_map/ppermute | solution.py:40
  130.2 21.2 %collective-permute-start.30 = (bf16[64,4096]{1,0:T(8,128)(2,1)S(1)}, bf16[64,4096]{1,0:T(8,128)(2,1)S(1)}, u32[]{:S(2)}, u32[]{:S(2)}) collective-permute-start(bf16[64,4096]{1,0:T(8,128)(2,1)S(1)} %get-tuple-element.51), channel_id=1, source_target_pairs={{0,4},{1,17},{2,6},{3,19},{4,0},{5,21},{6,2},{7,23},{8,12},{9,25},... | collective-permute-start | bytes 1572872 | tf_op jit(solution)/shard_map/ppermute | solution.py:40
  139.2 15.2 %collective-permute-start.31 = (bf16[64,4096]{1,0:T(8,128)(2,1)S(1)}, bf16[64,4096]{1,0:T(8,128)(2,1)S(1)}, u32[]{:S(2)}, u32[]{:S(2)}) collective-permute-start(bf16[64,4096]{1,0:T(8,128)(2,1)S(1)} %get-tuple-element.52), channel_id=1, source_target_pairs={{0,6},{1,25},{2,0},{3,27},{4,2},{5,29},{6,4},{7,31},{8,14},{9,1},{... | collective-permute-start | bytes 1572872 | tf_op jit(solution)/shard_map/ppermute | solution.py:40
  154.9 10.5 %collective-permute-start.35 = (bf16[16,8192]{1,0:T(8,128)(2,1)S(1)}, bf16[16,8192]{1,0:T(8,128)(2,1)S(1)}, u32[]{:S(2)}, u32[]{:S(2)}) collective-permute-start(bf16[16,8192]{1,0:T(8,128)(2,1)S(1)} %get-tuple-element.58), channel_id=1, source_target_pairs={{0,8},{1,3},{2,10},{3,5},{4,12},{5,7},{6,14},{7,1},{8,16},{9,11},{... | collective-permute-start | bytes 786440 | tf_op jit(solution)/shard_map/ppermute | solution.py:40
  155.0 10.4 %collective-permute-start.36 = (bf16[16,8192]{1,0:T(8,128)(2,1)S(1)}, bf16[16,8192]{1,0:T(8,128)(2,1)S(1)}, u32[]{:S(2)}, u32[]{:S(2)}) collective-permute-start(bf16[16,8192]{1,0:T(8,128)(2,1)S(1)} %get-tuple-element.59), channel_id=1, source_target_pairs={{0,16},{1,5},{2,18},{3,7},{4,20},{5,1},{6,22},{7,3},{8,24},{9,13},... | collective-permute-start | bytes 786440 | tf_op jit(solution)/shard_map/ppermute | solution.py:40
  157.7 8.5 %collective-permute-start.37 = (bf16[16,8192]{1,0:T(8,128)(2,1)S(1)}, bf16[16,8192]{1,0:T(8,128)(2,1)S(1)}, u32[]{:S(2)}, u32[]{:S(2)}) collective-permute-start(bf16[16,8192]{1,0:T(8,128)(2,1)S(1)} %get-tuple-element.60), channel_id=1, source_target_pairs={{0,24},{1,7},{2,26},{3,1},{4,28},{5,3},{6,30},{7,5},{8,0},{9,15},{... | collective-permute-start | bytes 786440 | tf_op jit(solution)/shard_map/ppermute | solution.py:40

commit v5 on v4

v5 whole, which is shorter than its diff:
```python
import math

import jax
import jax.numpy as jnp
import numpy as np
from jax import lax
from jax.experimental import pallas as pl
from jax.experimental.pallas import tpu as pltpu
from jax.sharding import PartitionSpec as P

RING = 4
PLACES = [(x, y, c) for x in range(RING) for y in range(RING) for c in range(2)]
GATHER_SPANS = (1, 1)
LIMIT = 40 * 2**20
BY_ROWS = (((1,), (1,)), ((), ()))


def place(x, y, c):
    return (x % RING) * RING * 2 + (y % RING) * 2 + c


def along_first(d):
    return [
        (place(x, y, c), place(x + d, y, c) if c == 0 else place(x, y + d, c))
        for x, y, c in PLACES
    ]


def along_second(d):
    return [
        (place(x, y, c), place(x + d, y, c) if c == 1 else place(x, y + d, c))
        for x, y, c in PLACES
    ]


SIBLING = [(place(x, y, c), place(x, y, 1 - c)) for x, y, c in PLACES]


def send(value, pairs):
    return lax.ppermute(value, "tensor", pairs)


def from_steps(value, along):
    return send(value, along(-1)), send(value, along(2)), send(value, along(1))


def after(value, *others):
    return lax.optimization_barrier((value, *others))[0]


def dot(a, b):
    return jnp.dot(a, b, preferred_element_type=jnp.float32)


def scalar_table():
    def sign(row, column):
        return 1.0 - 2.0 * (bin(row & column).count("1") % 2)

    rows = []
    for x, y, c in PLACES:
        first, second = (x, y) if c == 0 else (y, x)
        row = [1.0 - 2.0 * c]
        row += [sign(first, (first + s) % RING) for s in range(RING)]
        row += [
            sign(second, (second + s) % RING) / math.sqrt(2 * RING * RING) for s in range(RING)
        ]
        rows.append(row + [0.0] * (16 - len(row)))
    return np.array(rows, np.float32)


def cuts_of(shares, total):
    widths = [w * total // sum(shares) for w in shares]
    starts = [sum(widths[:n]) for n in range(len(widths))]
    return list(zip(starts, widths))


VMEM = pl.BlockSpec(memory_space=pltpu.VMEM)
SCALARS = pl.BlockSpec(memory_space=pltpu.SMEM)


def call(kernel, name, flops, size, operands, outs, specs=None, out_specs=None, **kwargs):
    return pl.pallas_call(
        kernel,
        name=name,
        compiler_params=pltpu.CompilerParams(vmem_limit_bytes=LIMIT),
        cost_estimate=pl.CostEstimate(flops=flops, bytes_accessed=size, transcendentals=0),
        in_specs=specs or [VMEM] * len(operands),
        out_specs=out_specs or [VMEM] * len(outs),
        out_shape=outs,
        **kwargs,
    )(*operands)


def in_hbm(value):
    return pltpu.with_memory_space_constraint(value, pltpu.HBM)


def stack(parts, cuts):
    rows = parts[0].shape[0]

    def kernel(*refs):
        ins, outs = refs[: len(parts)], refs[len(parts) :]
        for (at, span), out in zip(cuts, outs):
            for n, part in enumerate(ins):
                out[n * rows : (n + 1) * rows] = part[:, at : at + span]

    return call(
        kernel,
        "stack",
        0,
        sum(4 * rows * len(parts) * span for _, span in cuts),
        parts,
        [jax.ShapeDtypeStruct((rows * len(parts), span), jnp.bfloat16) for _, span in cuts],
    )


def gate_up(pieces, weights, at, span, sums, finish):
    group = pieces[0].shape[0]
    rows = RING * group
    units = weights[0].shape[0]
    block = math.gcd(span, 1024)
    steps = span // block
    opening, closing = sums is None, finish is not None

    def kernel(*refs):
        refs = list(refs)
        parts, loads, refs = refs[:RING], refs[RING : RING + 4], refs[RING + 4 :]
        before = None if opening else refs.pop(0)
        if closing:
            mixing, scalars, out, total, x = refs
        else:
            total, x = refs
        step = pl.program_id(0)

        @pl.when(step == 0)
        def _():
            total[...] = jnp.zeros(total.shape, total.dtype) if opening else before[...]

        for n, part in enumerate(parts):
            x[n * group : (n + 1) * group] = part[...]
        for n, weight in enumerate(loads):
            total[n] += lax.dot_general(
                x[...], weight[...], BY_ROWS, preferred_element_type=jnp.float32
            )

        if closing:

            @pl.when(step == steps - 1)
            def _():
                local = []
                for n in (0, 2):
                    gate, up = total[n], total[n + 1]
                    hidden = (gate / (1.0 + jnp.exp(-gate)) * up).astype(jnp.bfloat16)
                    local.append(dot(hidden, mixing[...]))
                own, other = local
                turn = scalars[0]
                out[:, :units] = (other + turn * own).astype(jnp.bfloat16)
                out[:, units:] = (own - turn * other).astype(jnp.bfloat16)

    operands = [*pieces, *[in_hbm(w) for w in weights]]
    specs = [pl.BlockSpec((group, block), lambda k: (0, k))] * RING
    specs += [pl.BlockSpec((units, block), lambda k: (0, k + at // block))] * 4
    scratch = [pltpu.VMEM((rows, block), jnp.bfloat16)]
    if not opening:
        operands.append(sums)
        specs.append(VMEM)
    if closing:
        operands += finish
        specs += [VMEM, SCALARS]
        out = jax.ShapeDtypeStruct((rows, 2 * units), jnp.bfloat16)
        scratch = [pltpu.VMEM((4, rows, units), jnp.float32)] + scratch
    else:
        out = jax.ShapeDtypeStruct((4, rows, units), jnp.float32)
    return call(
        kernel,
        "gate_up",
        8 * rows * units * span,
        8 * units * span,
        operands,
        [out],
        specs,
        grid=(steps,),
        scratch_shapes=scratch,
    )[0]


def combine(parts, scalars, first_scalar, major):
    rows, width = parts[0].shape
    slot = rows // (RING * RING)

    def kernel(*refs):
        came, factors, out = refs[:RING], refs[RING], refs[RING + 1]
        for i in range(RING):
            for j in range(RING):
                total = 0.0
                for s in range(RING):
                    where = ((i - s) % RING, j) if major else (i, (j - s) % RING)
                    at = (where[0] * RING + where[1]) * slot
                    total = total + factors[first_scalar + s] * came[s][at : at + slot].astype(
                        jnp.float32
                    )
                at = (i * RING + j) * slot
                out[at : at + slot] = total.astype(jnp.bfloat16)

    return call(
        kernel,
        "combine",
        0,
        10 * rows * width,
        [*parts, scalars],
        [jax.ShapeDtypeStruct((rows, width), jnp.bfloat16)],
        [VMEM] * RING + [SCALARS],
    )[0]


def down(value, weights, at, span):
    rows, units = value.shape[0], weights[0].shape[0]
    group = rows // RING
    block = math.gcd(span, 2048)

    def kernel(held, loaded, loaded_other, *outs):
        product = dot(held[:, :units], loaded[...]) + dot(held[:, units:], loaded_other[...])
        product = product.astype(jnp.bfloat16)
        for n, out in enumerate(outs):
            out[...] = product[n * group : (n + 1) * group]

    return call(
        kernel,
        "down",
        4 * rows * units * span,
        4 * units * span,
        [value, *[in_hbm(w) for w in weights]],
        [jax.ShapeDtypeStruct((group, span), jnp.bfloat16)] * RING,
        [pl.BlockSpec(value.shape, lambda k: (0, 0))]
        + [pl.BlockSpec((units, block), lambda k: (0, k + at // block))] * 2,
        grid=(span // block,),
        out_specs=[pl.BlockSpec((group, block), lambda k: (0, k))] * RING,
    )


def fold(sides):
    count = len(sides[0])
    group = sides[0][0].shape[0]
    rows = group // RING
    width = sum(parts[0].shape[1] for parts in sides)

    def kernel(*refs):
        ins, outs = refs[: count * len(sides)], refs[count * len(sides) :]
        start = 0
        for n in range(len(sides)):
            parts = ins[count * n : count * (n + 1)]
            stop = start + parts[0].shape[1]
            for m, out in enumerate(outs):
                at = slice(m * rows, (m + 1) * rows)
                total = sum(part[at].astype(jnp.float32) for part in parts)
                out[:, start:stop] = total.astype(jnp.bfloat16)
            start = stop

    return call(
        kernel,
        "fold",
        0,
        10 * group * width,
        [part for parts in sides for part in parts],
        [jax.ShapeDtypeStruct((rows, width), jnp.bfloat16)] * RING,
    )


def to_steps(parts, along):
    return parts[0], send(parts[1], along(1)), send(parts[2], along(2)), send(parts[3], along(-1))


def body(tokens, gate_weight, up_weight, down_weight, mixing):
    width = tokens.shape[1]
    index = lax.axis_index("tensor")
    scalars = lax.dynamic_index_in_dim(jnp.asarray(scalar_table()), index, keepdims=False)

    gate, up = gate_weight.T, up_weight.T
    weights = (gate, up, send(gate, SIBLING), send(up, SIBLING))

    cuts = cuts_of(GATHER_SPANS, width)
    blocks = stack((tokens, *from_steps(tokens, along_first)), cuts)
    value = None
    for n, (at, span) in enumerate(cuts):
        pieces = (blocks[n], *from_steps(blocks[n], along_second))
        finish = (mixing, scalars) if n == len(cuts) - 1 else None
        value = gate_up(pieces, weights, at, span, value, finish)

    down_other = send(after(down_weight, value), SIBLING)

    value = combine((value, *from_steps(value, along_first)), scalars, 1, False)
    value = combine((value, *from_steps(value, along_second)), scalars, 1 + RING, True)

    half = width // 2
    sides = [
        to_steps(down(value, (down_weight, down_other), at, half), along_second)
        for at in (0, half)
    ]
    parts = to_steps(fold(sides), along_first)
    return sum(part.astype(jnp.float32) for part in parts).astype(jnp.bfloat16)


def solution(mesh):
    in_specs = (
        P(("dp", "tensor"), None),
        P(None, "tensor"),
        P(None, "tensor"),
        P("tensor", None),
        P(),
    )
    out_specs = P(("dp", "tensor"), None)
    return jax.shard_map(body, mesh=mesh, in_specs=in_specs, out_specs=out_specs, check_vma=False)
```

time: 169 us -> 138 us (0.82)
  waiting for transfers between devices: 85.3 us -> 63.3 us
  local copies, waits for them, and re-layouts: 13.7 us -> 4.56 us
    ppermute x38 -> x27, waiting for transfers between devices: 85.3 us -> 63.3 us  [send(): return lax.ppermute(value, 'tensor', pairs)]
    unnamed x12 -> x10, local copies, waits for them, and re-layouts: 13 us -> 3.87 us
    pallas_call x14 -> x8, Pallas kernels: 26.4 us -> 29.8 us  [call(): pl.pallas_call(kernel, name=name, compiler_params=pltpu.CompilerParams(vm...]
    pallas_call x1 -> x0, Pallas kernels: 3.09 us -> none  [load(): pl.pallas_call(kernel, name='load', compiler_params=pltpu.CompilerParams(...]
    ppermute x38 -> x27, starting transfers between devices: 37.6 us -> 38.6 us  [send(): return lax.ppermute(value, 'tensor', pairs)]
  transfers between devices with their start and end apart: 38 -> 27, of which waited for: 23 -> 17; matrix products, arithmetic and copies ran while one was open for 0% -> 1% of each run, Pallas kernels for 13% -> 11%
where the time goes in v5:
time: 138 us; the launch traced here: 137 us
  waiting for transfers between devices  63.3 us (46%)
  starting transfers between devices  38.6 us (28%)
  Pallas kernels  29.8 us (22%)
  local copies, waits for them, and re-layouts  4.56 us (3%)
    ppermute x27, waiting for transfers between devices, send(): return lax.ppermute(value, 'tensor', pairs)  63.3 us
    ppermute x27, starting transfers between devices, send(): return lax.ppermute(value, 'tensor', pairs)  38.6 us
    pallas_call x8, Pallas kernels, call(): pl.pallas_call(kernel, name=name, compiler_params=pltpu.CompilerParams(vm...  29.8 us
    unnamed x10, local copies, waits for them, and re-layouts  3.87 us
  transfers between devices with their start and end apart: 27, of which 17 were waited for; matrix products, arithmetic and copies ran while one was open for 1% of the time, Pallas kernels for 11%

profile of v5, /device:TPU:0, one launch (start us, length us, event | category | flops | bytes accessed | tf_op | source)
XLA Modules:
  0.0 137.2 jit_solution(14849189213978141831)
XLA Ops:
  0.0 0.5 collective-permute-start.7
  0.5 2.8 %collective-permute-start = (bf16[16,8192]{1,0:T(8,128)(2,1)}, bf16[16,8192]{1,0:T(8,128)(2,1)S(1)}, u32[]{:S(2)}, u32[]{:S(2)}) collective-permute-start(bf16[16,8192]{1,0:T(8,128)(2,1)} %refs_0_.1), channel_id=1, source_target_pairs={{0,24},{1,7},{2,26},{3,1},{4,28},{5,3},{6,30},{7,5},{8,0},{9,15},{... | collective-permute-start | bytes 786440 | tf_op jit(solution)/shard_map/ppermute | solution.py:40
  3.4 0.8 collective-permute-start.1
  4.2 0.9 collective-permute-start.2
  5.0 5.3 %collective-permute-done.refs_1_ = bf16[16,8192]{1,0:T(8,128)(2,1)S(1)} collective-permute-done((bf16[16,8192]{1,0:T(8,128)(2,1)}, bf16[16,8192]{1,0:T(8,128)(2,1)S(1)}, u32[]{:S(2)}, u32[]{:S(2)}) %collective-permute-start) | collective-permute-done | bytes 262176 | tf_op jit(solution)/shard_map/ppermute | solution.py:40
  10.4 1.2 collective-permute-done.1.refs_2_
  11.5 2.7 %collective-permute-done.2.refs_3_ = bf16[16,8192]{1,0:T(8,128)(2,1)S(1)} collective-permute-done((bf16[16,8192]{1,0:T(8,128)(2,1)}, bf16[16,8192]{1,0:T(8,128)(2,1)S(1)}, u32[]{:S(2)}, u32[]{:S(2)}) %collective-permute-start.2) | collective-permute-done | bytes 262176 | tf_op jit(solution)/shard_map/ppermute | solution.py:40
  14.3 0.9 copy-done.1
  15.2 0.1 stack.1
  15.3 1.6 %collective-permute-start.10 = (bf16[64,4096]{1,0:T(8,128)(2,1)S(1)}, bf16[64,4096]{1,0:T(8,128)(2,1)S(1)}, u32[]{:S(2)}, u32[]{:S(2)}) collective-permute-start(bf16[64,4096]{1,0:T(8,128)(2,1)S(1)} %get-tuple-element.21.refs_0_), channel_id=1, source_target_pairs={{0,2},{1,9},{2,4},{3,11},{4,6},{5,13},{6,0},{7,15},{8,10},{9,17},{... | collective-permute-start | bytes 1572872 | tf_op jit(solution)/shard_map/ppermute | solution.py:40
  16.9 1.7 %collective-permute-start.8 = (bf16[64,4096]{1,0:T(8,128)(2,1)S(1)}, bf16[64,4096]{1,0:T(8,128)(2,1)S(1)}, u32[]{:S(2)}, u32[]{:S(2)}) collective-permute-start(bf16[64,4096]{1,0:T(8,128)(2,1)S(1)} %get-tuple-element.21.refs_0_), channel_id=1, source_target_pairs={{0,6},{1,25},{2,0},{3,27},{4,2},{5,29},{6,4},{7,31},{8,14},{9,1},{... | collective-permute-start | bytes 1572872 | tf_op jit(solution)/shard_map/ppermute | solution.py:40
  18.6 2.0 %collective-permute-start.9 = (bf16[64,4096]{1,0:T(8,128)(2,1)S(1)}, bf16[64,4096]{1,0:T(8,128)(2,1)S(1)}, u32[]{:S(2)}, u32[]{:S(2)}) collective-permute-start(bf16[64,4096]{1,0:T(8,128)(2,1)S(1)} %get-tuple-element.21.refs_0_), channel_id=1, source_target_pairs={{0,4},{1,17},{2,6},{3,19},{4,0},{5,21},{6,2},{7,23},{8,12},{9,25},... | collective-permute-start | bytes 1572872 | tf_op jit(solution)/shard_map/ppermute | solution.py:40
  20.6 5.2 %collective-permute-done.10.refs_3_ = bf16[64,4096]{1,0:T(8,128)(2,1)S(1)} collective-permute-done((bf16[64,4096]{1,0:T(8,128)(2,1)S(1)}, bf16[64,4096]{1,0:T(8,128)(2,1)S(1)}, u32[]{:S(2)}, u32[]{:S(2)}) %collective-permute-start.10) | collective-permute-done | bytes 524320 | tf_op jit(solution)/shard_map/ppermute | solution.py:40
  25.7 1.8 %collective-permute-start.3 = (bf16[64,4096]{1,0:T(8,128)(2,1)S(1)}, bf16[64,4096]{1,0:T(8,128)(2,1)S(1)}, u32[]{:S(2)}, u32[]{:S(2)}) collective-permute-start(bf16[64,4096]{1,0:T(8,128)(2,1)S(1)} %get-tuple-element.20.refs_0_), channel_id=1, source_target_pairs={{0,6},{1,25},{2,0},{3,27},{4,2},{5,29},{6,4},{7,31},{8,14},{9,1},{... | collective-permute-start | bytes 1572872 | tf_op jit(solution)/shard_map/ppermute | solution.py:40
  27.5 0.0 collective-permute-done.8.refs_1_
  27.5 5.8 %collective-permute-start.4 = (bf16[64,4096]{1,0:T(8,128)(2,1)S(1)}, bf16[64,4096]{1,0:T(8,128)(2,1)}, u32[]{:S(2)}, u32[]{:S(2)}) collective-permute-start(bf16[64,4096]{1,0:T(8,128)(2,1)S(1)} %get-tuple-element.20.refs_0_), channel_id=1, source_target_pairs={{0,4},{1,17},{2,6},{3,19},{4,0},{5,21},{6,2},{7,23},{8,12},{9,25},... | collective-permute-start | bytes 1572872 | tf_op jit(solution)/shard_map/ppermute | solution.py:40
  33.3 0.0 collective-permute-done.9.refs_2_
  33.3 2.1 %collective-permute-start.5 = (bf16[64,4096]{1,0:T(8,128)(2,1)S(1)}, bf16[64,4096]{1,0:T(8,128)(2,1)}, u32[]{:S(2)}, u32[]{:S(2)}) collective-permute-start(bf16[64,4096]{1,0:T(8,128)(2,1)S(1)} %get-tuple-element.20.refs_0_), channel_id=1, source_target_pairs={{0,2},{1,9},{2,4},{3,11},{4,6},{5,13},{6,0},{7,15},{8,10},{9,17},{... | collective-permute-start | bytes 1572872 | tf_op jit(solution)/shard_map/ppermute | solution.py:40
  35.5 0.7 dynamic-slice_bitcast_fusion.refs_10_.refs_4_
  36.2 0.0 slice-start
  36.2 8.7 %gate_up.2.refs_8_ = f32[4,256,448]{2,1,0:T(8,128)S(1)} custom-call(bf16[64,4096]{1,0:T(8,128)(2,1)S(1)} %get-tuple-element.21.refs_0_, bf16[64,4096]{1,0:T(8,128)(2,1)S(1)} %collective-permute-done.8.refs_1_, bf16[64,4096]{1,0:T(8,128)(2,1)S(1)} %collective-permute-done.9.refs_2_, bf16[64,4096]{1,0:T(8,128)(2,1)S(1)} %collective-permute-done.10.refs_3_, ...), custom_call_target="tpu_custom_call" | custom-call | flops 3758096384 | bytes 14680064 | tf_op jit(solution)/shard_map/gate_up/pallas_call | solution.py:82
  44.8 0.0 slice-start.1
  44.9 0.0 collective-permute-done.3.refs_1_
  44.9 0.0 collective-permute-done.4.refs_2_
  44.9 1.3 collective-permute-done.5.refs_3_
  46.2 9.2 %gate_up.3.refs_0_ = bf16[256,896]{1,0:T(8,128)(2,1)S(1)} custom-call(bf16[64,4096]{1,0:T(8,128)(2,1)S(1)} %get-tuple-element.20.refs_0_, bf16[64,4096]{1,0:T(8,128)(2,1)S(1)} %collective-permute-done.3.refs_1_, bf16[64,4096]{1,0:T(8,128)(2,1)} %collective-permute-done.4.refs_2_, bf16[64,4096]{1,0:T(8,128)(2,1)} %collective-permute-done.5.refs_3_, ...), custom_call_target="tpu_custom_call" | custom-call | flops 3758096384 | bytes 14680064 | tf_op jit(solution)/shard_map/gate_up/pallas_call | solution.py:82
  55.4 0.1 collective-permute-start.17
  55.5 0.7 collective-permute-start.11
  56.2 0.8 collective-permute-start.12
  57.0 0.8 collective-permute-start.13
  57.8 6.3 %collective-permute-done.11.refs_1_ = bf16[256,896]{1,0:T(8,128)(2,1)S(1)} collective-permute-done((bf16[256,896]{1,0:T(8,128)(2,1)S(1)}, bf16[256,896]{1,0:T(8,128)(2,1)S(1)}, u32[]{:S(2)}, u32[]{:S(2)}) %collective-permute-start.11) | collective-permute-done | bytes 458784 | tf_op jit(solution)/shard_map/ppermute | solution.py:40
  64.1 2.2 %collective-permute-done.12.refs_2_ = bf16[256,896]{1,0:T(8,128)(2,1)S(1)} collective-permute-done((bf16[256,896]{1,0:T(8,128)(2,1)S(1)}, bf16[256,896]{1,0:T(8,128)(2,1)S(1)}, u32[]{:S(2)}, u32[]{:S(2)}) %collective-permute-start.12) | collective-permute-done | bytes 458784 | tf_op jit(solution)/shard_map/ppermute | solution.py:40
  66.3 4.8 %collective-permute-done.13.refs_3_ = bf16[256,896]{1,0:T(8,128)(2,1)S(1)} collective-permute-done((bf16[256,896]{1,0:T(8,128)(2,1)S(1)}, bf16[256,896]{1,0:T(8,128)(2,1)S(1)}, u32[]{:S(2)}, u32[]{:S(2)}) %collective-permute-start.13) | collective-permute-done | bytes 458784 | tf_op jit(solution)/shard_map/ppermute | solution.py:40
  71.1 0.9 combine.2.refs_0_
  72.0 0.7 collective-permute-start.14
  72.7 3.5 %collective-permute-start.15 = (bf16[256,896]{1,0:T(8,128)(2,1)S(1)}, bf16[256,896]{1,0:T(8,128)(2,1)S(1)}, u32[]{:S(2)}, u32[]{:S(2)}) collective-permute-start(bf16[256,896]{1,0:T(8,128)(2,1)S(1)} %combine.2.refs_0_), channel_id=1, source_target_pairs={{0,4},{1,17},{2,6},{3,19},{4,0},{5,21},{6,2},{7,23},{8,12},{9,25},... | collective-permute-start | bytes 1376264 | tf_op jit(solution)/shard_map/ppermute | solution.py:40
  76.2 0.8 collective-permute-start.16
  77.0 3.6 %collective-permute-done.14.refs_1_ = bf16[256,896]{1,0:T(8,128)(2,1)S(1)} collective-permute-done((bf16[256,896]{1,0:T(8,128)(2,1)S(1)}, bf16[256,896]{1,0:T(8,128)(2,1)S(1)}, u32[]{:S(2)}, u32[]{:S(2)}) %collective-permute-start.14) | collective-permute-done | bytes 458784 | tf_op jit(solution)/shard_map/ppermute | solution.py:40
  80.6 2.2 %collective-permute-done.15.refs_2_ = bf16[256,896]{1,0:T(8,128)(2,1)S(1)} collective-permute-done((bf16[256,896]{1,0:T(8,128)(2,1)S(1)}, bf16[256,896]{1,0:T(8,128)(2,1)S(1)}, u32[]{:S(2)}, u32[]{:S(2)}) %collective-permute-start.15) | collective-permute-done | bytes 458784 | tf_op jit(solution)/shard_map/ppermute | solution.py:40
  82.8 4.8 %collective-permute-done.16.refs_3_ = bf16[256,896]{1,0:T(8,128)(2,1)S(1)} collective-permute-done((bf16[256,896]{1,0:T(8,128)(2,1)S(1)}, bf16[256,896]{1,0:T(8,128)(2,1)S(1)}, u32[]{:S(2)}, u32[]{:S(2)}) %collective-permute-start.16) | collective-permute-done | bytes 458784 | tf_op jit(solution)/shard_map/ppermute | solution.py:40
  87.6 0.9 combine.3.held
  88.5 0.0 collective-permute-done.17.loaded_other
  88.5 2.9 %copy-done.2 = bf16[448,8192]{1,0:T(8,128)(2,1)} copy-done((bf16[448,8192]{1,0:T(8,128)(2,1)}, bf16[448,8192]{1,0:T(8,128)(2,1)S(1)}, u32[]{:S(2)}) %copy-start.2) | copy-done | bytes 7340056
  91.4 4.8 %down.3 = (bf16[64,4096]{1,0:T(8,128)(2,1)S(1)}, bf16[64,4096]{1,0:T(8,128)(2,1)S(1)}, bf16[64,4096]{1,0:T(8,128)(2,1)S(1)}, bf16[64,4096]{1,0:T(8,128)(2,1)S(1)}) custom-call(bf16[256,896]{1,0:T(8,128)(2,1)S(1)} %combine.3.held, bf16[448,8192]{1,0:T(8,128)(2,1)} %loaded.3, bf16[448,8192]{1,0:T(8,128)(2,1)} %copy-done.2), custom_call_target="tpu_custom_call" | custom-call | flops 1879048192 | bytes 7340032 | tf_op jit(solution)/shard_map/down/pallas_call | solution.py:82
  96.2 2.1 %collective-permute-start.21 = (bf16[64,4096]{1,0:T(8,128)(2,1)S(1)}, bf16[64,4096]{1,0:T(8,128)(2,1)S(1)}, u32[]{:S(2)}, u32[]{:S(2)}) collective-permute-start(bf16[64,4096]{1,0:T(8,128)(2,1)S(1)} %get-tuple-element.28), channel_id=1, source_target_pairs={{0,2},{1,9},{2,4},{3,11},{4,6},{5,13},{6,0},{7,15},{8,10},{9,17},{... | collective-permute-start | bytes 1572872 | tf_op jit(solution)/shard_map/ppermute | solution.py:40
  98.3 0.9 collective-permute-start.22
  99.2 2.5 %collective-permute-start.23 = (bf16[64,4096]{1,0:T(8,128)(2,1)S(1)}, bf16[64,4096]{1,0:T(8,128)(2,1)S(1)}, u32[]{:S(2)}, u32[]{:S(2)}) collective-permute-start(bf16[64,4096]{1,0:T(8,128)(2,1)S(1)} %get-tuple-element.30), channel_id=1, source_target_pairs={{0,6},{1,25},{2,0},{3,27},{4,2},{5,29},{6,4},{7,31},{8,14},{9,1},{... | collective-permute-start | bytes 1572872 | tf_op jit(solution)/shard_map/ppermute | solution.py:40
  101.8 4.8 %down.2 = (bf16[64,4096]{1,0:T(8,128)(2,1)S(1)}, bf16[64,4096]{1,0:T(8,128)(2,1)S(1)}, bf16[64,4096]{1,0:T(8,128)(2,1)S(1)}, bf16[64,4096]{1,0:T(8,128)(2,1)S(1)}) custom-call(bf16[256,896]{1,0:T(8,128)(2,1)S(1)} %combine.3.held, bf16[448,8192]{1,0:T(8,128)(2,1)} %loaded.3, bf16[448,8192]{1,0:T(8,128)(2,1)} %copy-done.2), custom_call_target="tpu_custom_call" | custom-call | flops 1879048192 | bytes 7340032 | tf_op jit(solution)/shard_map/down/pallas_call | solution.py:82
  106.6 0.1 collective-permute-start.18
  106.6 2.1 %collective-permute-start.19 = (bf16[64,4096]{1,0:T(8,128)(2,1)S(1)}, bf16[64,4096]{1,0:T(8,128)(2,1)S(1)}, u32[]{:S(2)}, u32[]{:S(2)}) collective-permute-start(bf16[64,4096]{1,0:T(8,128)(2,1)S(1)} %get-tuple-element.25), channel_id=1, source_target_pairs={{0,4},{1,17},{2,6},{3,19},{4,0},{5,21},{6,2},{7,23},{8,12},{9,25},... | collective-permute-start | bytes 1572872 | tf_op jit(solution)/shard_map/ppermute | solution.py:40
  108.7 3.6 %collective-permute-done.21.refs_5_ = bf16[64,4096]{1,0:T(8,128)(2,1)S(1)} collective-permute-done((bf16[64,4096]{1,0:T(8,128)(2,1)S(1)}, bf16[64,4096]{1,0:T(8,128)(2,1)S(1)}, u32[]{:S(2)}, u32[]{:S(2)}) %collective-permute-start.21) | collective-permute-done | bytes 524320 | tf_op jit(solution)/shard_map/ppermute | solution.py:40
  112.3 0.0 collective-permute-start.20
  112.3 0.0 collective-permute-done.22.refs_6_
  112.3 0.9 collective-permute-done.23.refs_7_
  113.2 10.3 %collective-permute-done.18.refs_1_ = bf16[64,4096]{1,0:T(8,128)(2,1)S(1)} collective-permute-done((bf16[64,4096]{1,0:T(8,128)(2,1)S(1)}, bf16[64,4096]{1,0:T(8,128)(2,1)S(1)}, u32[]{:S(2)}, u32[]{:S(2)}) %collective-permute-start.18) | collective-permute-done | bytes 524320 | tf_op jit(solution)/shard_map/ppermute | solution.py:40
  123.5 0.0 collective-permute-done.19.refs_2_
  123.5 0.9 collective-permute-done.20.refs_3_
  124.5 0.5 fold.1
  125.0 0.1 collective-permute-start.24
  125.1 2.1 %collective-permute-start.25 = (bf16[16,8192]{1,0:T(8,128)(2,1)S(1)}, bf16[16,8192]{1,0:T(8,128)(2,1)S(1)}, u32[]{:S(2)}, u32[]{:S(2)}) collective-permute-start(bf16[16,8192]{1,0:T(8,128)(2,1)S(1)} %get-tuple-element.33), channel_id=1, source_target_pairs={{0,16},{1,5},{2,18},{3,7},{4,20},{5,1},{6,22},{7,3},{8,24},{9,13},... | collective-permute-start | bytes 786440 | tf_op jit(solution)/shard_map/ppermute | solution.py:40
  127.1 1.3 collective-permute-start.26
  128.5 7.0 %collective-permute-done.24 = bf16[16,8192]{1,0:T(8,128)(2,1)S(1)} collective-permute-done((bf16[16,8192]{1,0:T(8,128)(2,1)S(1)}, bf16[16,8192]{1,0:T(8,128)(2,1)S(1)}, u32[]{:S(2)}, u32[]{:S(2)}) %collective-permute-start.24) | collective-permute-done | bytes 262176 | tf_op jit(solution)/shard_map/ppermute | solution.py:40
  135.5 0.9 collective-permute-done.26
  136.4 0.8 add_convert_fusion
  (11 shorter events, 0.0 us)
Async XLA Ops:
  0.0 36.1 %collective-permute-start.6 = (bf16[448,8192]{1,0:T(8,128)(2,1)}, bf16[448,8192]{1,0:T(8,128)(2,1)}, u32[]{:S(2)}, u32[]{:S(2)}) collective-permute-start(bf16[448,8192]{1,0:T(8,128)(2,1)} %bitcast.4), channel_id=1, source_target_pairs={{0,1},{1,0},{2,3},{3,2},{4,5},{5,4},{6,7},{7,6},{8,9},{9,8},{10,11... | collective-permute-start | bytes 22020104 | tf_op jit(solution)/shard_map/ppermute | solution.py:40
  0.0 36.1 %collective-permute-start.7 = (bf16[448,8192]{1,0:T(8,128)(2,1)}, bf16[448,8192]{1,0:T(8,128)(2,1)}, u32[]{:S(2)}, u32[]{:S(2)}) collective-permute-start(bf16[448,8192]{1,0:T(8,128)(2,1)} %bitcast.7), channel_id=1, source_target_pairs={{0,1},{1,0},{2,3},{3,2},{4,5},{5,4},{6,7},{7,6},{8,9},{9,8},{10,11... | collective-permute-start | bytes 22020104 | tf_op jit(solution)/shard_map/ppermute | solution.py:40
  0.5 9.9 %collective-permute-start = (bf16[16,8192]{1,0:T(8,128)(2,1)}, bf16[16,8192]{1,0:T(8,128)(2,1)S(1)}, u32[]{:S(2)}, u32[]{:S(2)}) collective-permute-start(bf16[16,8192]{1,0:T(8,128)(2,1)} %refs_0_.1), channel_id=1, source_target_pairs={{0,24},{1,7},{2,26},{3,1},{4,28},{5,3},{6,30},{7,5},{8,0},{9,15},{... | collective-permute-start | bytes 786440 | tf_op jit(solution)/shard_map/ppermute | solution.py:40
  3.4 8.2 %collective-permute-start.1 = (bf16[16,8192]{1,0:T(8,128)(2,1)}, bf16[16,8192]{1,0:T(8,128)(2,1)S(1)}, u32[]{:S(2)}, u32[]{:S(2)}) collective-permute-start(bf16[16,8192]{1,0:T(8,128)(2,1)} %refs_0_.1), channel_id=1, source_target_pairs={{0,16},{1,5},{2,18},{3,7},{4,20},{5,1},{6,22},{7,3},{8,24},{9,13},... | collective-permute-start | bytes 786440 | tf_op jit(solution)/shard_map/ppermute | solution.py:40
  4.2 10.1 %collective-permute-start.2 = (bf16[16,8192]{1,0:T(8,128)(2,1)}, bf16[16,8192]{1,0:T(8,128)(2,1)S(1)}, u32[]{:S(2)}, u32[]{:S(2)}) collective-permute-start(bf16[16,8192]{1,0:T(8,128)(2,1)} %refs_0_.1), channel_id=1, source_target_pairs={{0,8},{1,3},{2,10},{3,5},{4,12},{5,7},{6,14},{7,1},{8,16},{9,11},{... | collective-permute-start | bytes 786440 | tf_op jit(solution)/shard_map/ppermute | solution.py:40
  14.2 1.0 copy-start.1
  15.3 10.5 %collective-permute-start.10 = (bf16[64,4096]{1,0:T(8,128)(2,1)S(1)}, bf16[64,4096]{1,0:T(8,128)(2,1)S(1)}, u32[]{:S(2)}, u32[]{:S(2)}) collective-permute-start(bf16[64,4096]{1,0:T(8,128)(2,1)S(1)} %get-tuple-element.21.refs_0_), channel_id=1, source_target_pairs={{0,2},{1,9},{2,4},{3,11},{4,6},{5,13},{6,0},{7,15},{8,10},{9,17},{... | collective-permute-start | bytes 1572872 | tf_op jit(solution)/shard_map/ppermute | solution.py:40
  16.9 10.6 %collective-permute-start.8 = (bf16[64,4096]{1,0:T(8,128)(2,1)S(1)}, bf16[64,4096]{1,0:T(8,128)(2,1)S(1)}, u32[]{:S(2)}, u32[]{:S(2)}) collective-permute-start(bf16[64,4096]{1,0:T(8,128)(2,1)S(1)} %get-tuple-element.21.refs_0_), channel_id=1, source_target_pairs={{0,6},{1,25},{2,0},{3,27},{4,2},{5,29},{6,4},{7,31},{8,14},{9,1},{... | collective-permute-start | bytes 1572872 | tf_op jit(solution)/shard_map/ppermute | solution.py:40
  18.6 14.8 %collective-permute-start.9 = (bf16[64,4096]{1,0:T(8,128)(2,1)S(1)}, bf16[64,4096]{1,0:T(8,128)(2,1)S(1)}, u32[]{:S(2)}, u32[]{:S(2)}) collective-permute-start(bf16[64,4096]{1,0:T(8,128)(2,1)S(1)} %get-tuple-element.21.refs_0_), channel_id=1, source_target_pairs={{0,4},{1,17},{2,6},{3,19},{4,0},{5,21},{6,2},{7,23},{8,12},{9,25},... | collective-permute-start | bytes 1572872 | tf_op jit(solution)/shard_map/ppermute | solution.py:40
  25.7 19.1 %collective-permute-start.3 = (bf16[64,4096]{1,0:T(8,128)(2,1)S(1)}, bf16[64,4096]{1,0:T(8,128)(2,1)S(1)}, u32[]{:S(2)}, u32[]{:S(2)}) collective-permute-start(bf16[64,4096]{1,0:T(8,128)(2,1)S(1)} %get-tuple-element.20.refs_0_), channel_id=1, source_target_pairs={{0,6},{1,25},{2,0},{3,27},{4,2},{5,29},{6,4},{7,31},{8,14},{9,1},{... | collective-permute-start | bytes 1572872 | tf_op jit(solution)/shard_map/ppermute | solution.py:40
  27.5 17.3 %collective-permute-start.4 = (bf16[64,4096]{1,0:T(8,128)(2,1)S(1)}, bf16[64,4096]{1,0:T(8,128)(2,1)}, u32[]{:S(2)}, u32[]{:S(2)}) collective-permute-start(bf16[64,4096]{1,0:T(8,128)(2,1)S(1)} %get-tuple-element.20.refs_0_), channel_id=1, source_target_pairs={{0,4},{1,17},{2,6},{3,19},{4,0},{5,21},{6,2},{7,23},{8,12},{9,25},... | collective-permute-start | bytes 1572872 | tf_op jit(solution)/shard_map/ppermute | solution.py:40
  33.3 12.9 %collective-permute-start.5 = (bf16[64,4096]{1,0:T(8,128)(2,1)S(1)}, bf16[64,4096]{1,0:T(8,128)(2,1)}, u32[]{:S(2)}, u32[]{:S(2)}) collective-permute-start(bf16[64,4096]{1,0:T(8,128)(2,1)S(1)} %get-tuple-element.20.refs_0_), channel_id=1, source_target_pairs={{0,2},{1,9},{2,4},{3,11},{4,6},{5,13},{6,0},{7,15},{8,10},{9,17},{... | collective-permute-start | bytes 1572872 | tf_op jit(solution)/shard_map/ppermute | solution.py:40
  36.1 10.1 %copy-start = (bf16[448,448]{1,0:T(8,128)(2,1)S(1)}, bf16[448,448]{1,0:T(8,128)(2,1)}, u32[]{:S(2)}) copy-start(bf16[448,448]{1,0:T(8,128)(2,1)} %refs_9_.1) | copy-start | bytes 1204228
  36.2 19.2 %slice-start = ((s8[7340032]{0:T(1024)(128)(4,1)}), s8[4194304]{0:T(1024)(128)(4,1)S(1)}, s32[]{:S(2)}) async-start(s8[7340032]{0:T(1024)(128)(4,1)} %bitcast.10), calls=%async_computation | async-start | bytes 8388608
  44.8 10.6 %slice-start.1 = ((s8[7340032]{0:T(1024)(128)(4,1)}), s8[3145728]{0:T(1024)(128)(4,1)S(1)}, s32[]{:S(2)}) async-start(s8[7340032]{0:T(1024)(128)(4,1)} %bitcast.10), calls=%async_computation.1 | async-start | bytes 6291456
  55.4 33.1 %collective-permute-start.17 = (bf16[448,8192]{1,0:T(8,128)(2,1)S(1)}, bf16[448,8192]{1,0:T(8,128)(2,1)S(1)}, u32[]{:S(2)}, u32[]{:S(2)}) collective-permute-start(bf16[448,8192]{1,0:T(8,128)(2,1)S(1)} %bitcast.11), channel_id=1, source_target_pairs={{0,1},{1,0},{2,3},{3,2},{4,5},{5,4},{6,7},{7,6},{8,9},{9,8},{10,11... | collective-permute-start | bytes 22020104 | tf_op jit(solution)/shard_map/ppermute | solution.py:40
  55.5 8.5 %collective-permute-start.11 = (bf16[256,896]{1,0:T(8,128)(2,1)S(1)}, bf16[256,896]{1,0:T(8,128)(2,1)S(1)}, u32[]{:S(2)}, u32[]{:S(2)}) collective-permute-start(bf16[256,896]{1,0:T(8,128)(2,1)S(1)} %gate_up.3.refs_0_), channel_id=1, source_target_pairs={{0,24},{1,7},{2,26},{3,1},{4,28},{5,3},{6,30},{7,5},{8,0},{9,15},{... | collective-permute-start | bytes 1376264 | tf_op jit(solution)/shard_map/ppermute | solution.py:40
  56.2 10.1 %collective-permute-start.12 = (bf16[256,896]{1,0:T(8,128)(2,1)S(1)}, bf16[256,896]{1,0:T(8,128)(2,1)S(1)}, u32[]{:S(2)}, u32[]{:S(2)}) collective-permute-start(bf16[256,896]{1,0:T(8,128)(2,1)S(1)} %gate_up.3.refs_0_), channel_id=1, source_target_pairs={{0,16},{1,5},{2,18},{3,7},{4,20},{5,1},{6,22},{7,3},{8,24},{9,13},... | collective-permute-start | bytes 1376264 | tf_op jit(solution)/shard_map/ppermute | solution.py:40
  57.0 14.1 %collective-permute-start.13 = (bf16[256,896]{1,0:T(8,128)(2,1)S(1)}, bf16[256,896]{1,0:T(8,128)(2,1)S(1)}, u32[]{:S(2)}, u32[]{:S(2)}) collective-permute-start(bf16[256,896]{1,0:T(8,128)(2,1)S(1)} %gate_up.3.refs_0_), channel_id=1, source_target_pairs={{0,8},{1,3},{2,10},{3,5},{4,12},{5,7},{6,14},{7,1},{8,16},{9,11},{... | collective-permute-start | bytes 1376264 | tf_op jit(solution)/shard_map/ppermute | solution.py:40
  72.0 8.6 %collective-permute-start.14 = (bf16[256,896]{1,0:T(8,128)(2,1)S(1)}, bf16[256,896]{1,0:T(8,128)(2,1)S(1)}, u32[]{:S(2)}, u32[]{:S(2)}) collective-permute-start(bf16[256,896]{1,0:T(8,128)(2,1)S(1)} %combine.2.refs_0_), channel_id=1, source_target_pairs={{0,6},{1,25},{2,0},{3,27},{4,2},{5,29},{6,4},{7,31},{8,14},{9,1},{... | collective-permute-start | bytes 1376264 | tf_op jit(solution)/shard_map/ppermute | solution.py:40
  72.7 10.1 %collective-permute-start.15 = (bf16[256,896]{1,0:T(8,128)(2,1)S(1)}, bf16[256,896]{1,0:T(8,128)(2,1)S(1)}, u32[]{:S(2)}, u32[]{:S(2)}) collective-permute-start(bf16[256,896]{1,0:T(8,128)(2,1)S(1)} %combine.2.refs_0_), channel_id=1, source_target_pairs={{0,4},{1,17},{2,6},{3,19},{4,0},{5,21},{6,2},{7,23},{8,12},{9,25},... | collective-permute-start | bytes 1376264 | tf_op jit(solution)/shard_map/ppermute | solution.py:40
  76.2 11.4 %collective-permute-start.16 = (bf16[256,896]{1,0:T(8,128)(2,1)S(1)}, bf16[256,896]{1,0:T(8,128)(2,1)S(1)}, u32[]{:S(2)}, u32[]{:S(2)}) collective-permute-start(bf16[256,896]{1,0:T(8,128)(2,1)S(1)} %combine.2.refs_0_), channel_id=1, source_target_pairs={{0,2},{1,9},{2,4},{3,11},{4,6},{5,13},{6,0},{7,15},{8,10},{9,17},{... | collective-permute-start | bytes 1376264 | tf_op jit(solution)/shard_map/ppermute | solution.py:40
  88.5 2.9 %copy-start.2 = (bf16[448,8192]{1,0:T(8,128)(2,1)}, bf16[448,8192]{1,0:T(8,128)(2,1)S(1)}, u32[]{:S(2)}) copy-start(bf16[448,8192]{1,0:T(8,128)(2,1)S(1)} %collective-permute-done.17.loaded_other) | copy-start | bytes 22020100
  96.2 16.1 %collective-permute-start.21 = (bf16[64,4096]{1,0:T(8,128)(2,1)S(1)}, bf16[64,4096]{1,0:T(8,128)(2,1)S(1)}, u32[]{:S(2)}, u32[]{:S(2)}) collective-permute-start(bf16[64,4096]{1,0:T(8,128)(2,1)S(1)} %get-tuple-element.28), channel_id=1, source_target_pairs={{0,2},{1,9},{2,4},{3,11},{4,6},{5,13},{6,0},{7,15},{8,10},{9,17},{... | collective-permute-start | bytes 1572872 | tf_op jit(solution)/shard_map/ppermute | solution.py:40
  98.3 14.0 %collective-permute-start.22 = (bf16[64,4096]{1,0:T(8,128)(2,1)S(1)}, bf16[64,4096]{1,0:T(8,128)(2,1)S(1)}, u32[]{:S(2)}, u32[]{:S(2)}) collective-permute-start(bf16[64,4096]{1,0:T(8,128)(2,1)S(1)} %get-tuple-element.29), channel_id=1, source_target_pairs={{0,4},{1,17},{2,6},{3,19},{4,0},{5,21},{6,2},{7,23},{8,12},{9,25},... | collective-permute-start | bytes 1572872 | tf_op jit(solution)/shard_map/ppermute | solution.py:40
  99.2 14.0 %collective-permute-start.23 = (bf16[64,4096]{1,0:T(8,128)(2,1)S(1)}, bf16[64,4096]{1,0:T(8,128)(2,1)S(1)}, u32[]{:S(2)}, u32[]{:S(2)}) collective-permute-start(bf16[64,4096]{1,0:T(8,128)(2,1)S(1)} %get-tuple-element.30), channel_id=1, source_target_pairs={{0,6},{1,25},{2,0},{3,27},{4,2},{5,29},{6,4},{7,31},{8,14},{9,1},{... | collective-permute-start | bytes 1572872 | tf_op jit(solution)/shard_map/ppermute | solution.py:40
  106.6 17.0 %collective-permute-start.18 = (bf16[64,4096]{1,0:T(8,128)(2,1)S(1)}, bf16[64,4096]{1,0:T(8,128)(2,1)S(1)}, u32[]{:S(2)}, u32[]{:S(2)}) collective-permute-start(bf16[64,4096]{1,0:T(8,128)(2,1)S(1)} %get-tuple-element.24), channel_id=1, source_target_pairs={{0,2},{1,9},{2,4},{3,11},{4,6},{5,13},{6,0},{7,15},{8,10},{9,17},{... | collective-permute-start | bytes 1572872 | tf_op jit(solution)/shard_map/ppermute | solution.py:40
  106.6 16.9 %collective-permute-start.19 = (bf16[64,4096]{1,0:T(8,128)(2,1)S(1)}, bf16[64,4096]{1,0:T(8,128)(2,1)S(1)}, u32[]{:S(2)}, u32[]{:S(2)}) collective-permute-start(bf16[64,4096]{1,0:T(8,128)(2,1)S(1)} %get-tuple-element.25), channel_id=1, source_target_pairs={{0,4},{1,17},{2,6},{3,19},{4,0},{5,21},{6,2},{7,23},{8,12},{9,25},... | collective-permute-start | bytes 1572872 | tf_op jit(solution)/shard_map/ppermute | solution.py:40
  112.3 12.2 %collective-permute-start.20 = (bf16[64,4096]{1,0:T(8,128)(2,1)S(1)}, bf16[64,4096]{1,0:T(8,128)(2,1)S(1)}, u32[]{:S(2)}, u32[]{:S(2)}) collective-permute-start(bf16[64,4096]{1,0:T(8,128)(2,1)S(1)} %get-tuple-element.26), channel_id=1, source_target_pairs={{0,6},{1,25},{2,0},{3,27},{4,2},{5,29},{6,4},{7,31},{8,14},{9,1},{... | collective-permute-start | bytes 1572872 | tf_op jit(solution)/shard_map/ppermute | solution.py:40
  125.0 10.5 %collective-permute-start.24 = (bf16[16,8192]{1,0:T(8,128)(2,1)S(1)}, bf16[16,8192]{1,0:T(8,128)(2,1)S(1)}, u32[]{:S(2)}, u32[]{:S(2)}) collective-permute-start(bf16[16,8192]{1,0:T(8,128)(2,1)S(1)} %get-tuple-element.32), channel_id=1, source_target_pairs={{0,8},{1,3},{2,10},{3,5},{4,12},{5,7},{6,14},{7,1},{8,16},{9,11},{... | collective-permute-start | bytes 786440 | tf_op jit(solution)/shard_map/ppermute | solution.py:40
  125.1 10.4 %collective-permute-start.25 = (bf16[16,8192]{1,0:T(8,128)(2,1)S(1)}, bf16[16,8192]{1,0:T(8,128)(2,1)S(1)}, u32[]{:S(2)}, u32[]{:S(2)}) collective-permute-start(bf16[16,8192]{1,0:T(8,128)(2,1)S(1)} %get-tuple-element.33), channel_id=1, source_target_pairs={{0,16},{1,5},{2,18},{3,7},{4,20},{5,1},{6,22},{7,3},{8,24},{9,13},... | collective-permute-start | bytes 786440 | tf_op jit(solution)/shard_map/ppermute | solution.py:40
  127.1 9.2 %collective-permute-start.26 = (bf16[16,8192]{1,0:T(8,128)(2,1)S(1)}, bf16[16,8192]{1,0:T(8,128)(2,1)S(1)}, u32[]{:S(2)}, u32[]{:S(2)}) collective-permute-start(bf16[16,8192]{1,0:T(8,128)(2,1)S(1)} %get-tuple-element.34), channel_id=1, source_target_pairs={{0,24},{1,7},{2,26},{3,1},{4,28},{5,3},{6,30},{7,5},{8,0},{9,15},{... | collective-permute-start | bytes 786440 | tf_op jit(solution)/shard_map/ppermute | solution.py:40

commit v6 on v5

--- a/solution.py
+++ b/solution.py
@@ -12,6 +12,7 @@
 PLACES = [(x, y, c) for x in range(RING) for y in range(RING) for c in range(2)]
 GATHER_SPANS = (1, 1)
 LIMIT = 40 * 2**20
+SMALL = 16 * 2**20
 BY_ROWS = (((1,), (1,)), ((), ()))
 
 
@@ -78,14 +79,14 @@
 SCALARS = pl.BlockSpec(memory_space=pltpu.SMEM)
 
 
-def call(kernel, name, flops, size, operands, outs, specs=None, out_specs=None, **kwargs):
+def call(kernel, name, flops, size, operands, outs, specs=None, limit=SMALL, **kwargs):
     return pl.pallas_call(
         kernel,
         name=name,
-        compiler_params=pltpu.CompilerParams(vmem_limit_bytes=LIMIT),
+        compiler_params=pltpu.CompilerParams(vmem_limit_bytes=limit),
         cost_estimate=pl.CostEstimate(flops=flops, bytes_accessed=size, transcendentals=0),
         in_specs=specs or [VMEM] * len(operands),
-        out_specs=out_specs or [VMEM] * len(outs),
+        out_specs=[VMEM] * len(outs),
         out_shape=outs,
         **kwargs,
     )(*operands)
@@ -93,6 +94,26 @@
 
 def in_hbm(value):
     return pltpu.with_memory_space_constraint(value, pltpu.HBM)
+
+
+def load(value, at, span):
+    def kernel(value, out, sem):
+        copy = pltpu.make_async_copy(value.at[:, pl.ds(at, span)], out, sem)
+        copy.start()
+        copy.wait()
+
+    return pl.pallas_call(
+        kernel,
+        name="load",
+        compiler_params=pltpu.CompilerParams(vmem_limit_bytes=SMALL),
+        cost_estimate=pl.CostEstimate(
+            flops=0, bytes_accessed=4 * value.shape[0] * span, transcendentals=0
+        ),
+        in_specs=[pl.BlockSpec(memory_space=pltpu.HBM)],
+        out_specs=VMEM,
+        out_shape=pltpu.VMEM((value.shape[0], span), value.dtype),
+        scratch_shapes=[pltpu.SemaphoreType.DMA],
+    )(in_hbm(value))
 
 
 def stack(parts, cuts):
@@ -114,7 +135,7 @@
     )
 
 
-def gate_up(pieces, weights, at, span, sums, finish):
+def gate_up(pieces, close, weights, at, span, sums, finish):
     group = pieces[0].shape[0]
     rows = RING * group
     units = weights[0].shape[0]
@@ -138,9 +159,13 @@
 
         for n, part in enumerate(parts):
             x[n * group : (n + 1) * group] = part[...]
+        here = pl.ds(pl.multiple_of(step * block, block), block)
         for n, weight in enumerate(loads):
             total[n] += lax.dot_general(
-                x[...], weight[...], BY_ROWS, preferred_element_type=jnp.float32
+                x[...],
+                weight[:, here] if n < len(close) else weight[...],
+                BY_ROWS,
+                preferred_element_type=jnp.float32,
             )
 
         if closing:
@@ -157,9 +182,11 @@
                 out[:, :units] = (other + turn * own).astype(jnp.bfloat16)
                 out[:, units:] = (own - turn * other).astype(jnp.bfloat16)
 
-    operands = [*pieces, *[in_hbm(w) for w in weights]]
+    operands = [*pieces, *close, *[in_hbm(w) for w in weights[len(close) :]]]
     specs = [pl.BlockSpec((group, block), lambda k: (0, k))] * RING
-    specs += [pl.BlockSpec((units, block), lambda k: (0, k + at // block))] * 4
+    specs += [VMEM] * len(close)
+    streamed = pl.BlockSpec((units, block), lambda k: (0, k + at // block))
+    specs += [streamed] * (4 - len(close))
     scratch = [pltpu.VMEM((rows, block), jnp.bfloat16)]
     if not opening:
         operands.append(sums)
@@ -179,6 +206,7 @@
         operands,
         [out],
         specs,
+        LIMIT,
         grid=(steps,),
         scratch_shapes=scratch,
     )[0]
@@ -216,25 +244,25 @@
 def down(value, weights, at, span):
     rows, units = value.shape[0], weights[0].shape[0]
     group = rows // RING
-    block = math.gcd(span, 2048)
+    block = min(span, 512)
 
     def kernel(held, loaded, loaded_other, *outs):
-        product = dot(held[:, :units], loaded[...]) + dot(held[:, units:], loaded_other[...])
-        product = product.astype(jnp.bfloat16)
-        for n, out in enumerate(outs):
-            out[...] = product[n * group : (n + 1) * group]
+        for start in range(0, span, block):
+            where = slice(at + start, at + start + block)
+            product = dot(held[:, :units], loaded[:, where]) + dot(
+                held[:, units:], loaded_other[:, where]
+            )
+            product = product.astype(jnp.bfloat16)
+            for n, out in enumerate(outs):
+                out[:, start : start + block] = product[n * group : (n + 1) * group]
 
     return call(
         kernel,
         "down",
         4 * rows * units * span,
         4 * units * span,
-        [value, *[in_hbm(w) for w in weights]],
+        [value, *weights],
         [jax.ShapeDtypeStruct((group, span), jnp.bfloat16)] * RING,
-        [pl.BlockSpec(value.shape, lambda k: (0, 0))]
-        + [pl.BlockSpec((units, block), lambda k: (0, k + at // block))] * 2,
-        grid=(span // block,),
-        out_specs=[pl.BlockSpec((group, block), lambda k: (0, k))] * RING,
     )
 
 
@@ -276,24 +304,28 @@
     scalars = lax.dynamic_index_in_dim(jnp.asarray(scalar_table()), index, keepdims=False)
 
     gate, up = gate_weight.T, up_weight.T
-    weights = (gate, up, send(gate, SIBLING), send(up, SIBLING))
-
     cuts = cuts_of(GATHER_SPANS, width)
-    blocks = stack((tokens, *from_steps(tokens, along_first)), cuts)
+    held = [load(gate, *cuts[-1]), load(up, *cuts[-1])]
+    weights = [gate, up, send(gate, SIBLING), send(up, SIBLING)]
+
+    near = from_steps(tokens, along_first)
+    blocks = stack((after(tokens, *held), *near), cuts)
     value = None
     for n, (at, span) in enumerate(cuts):
         pieces = (blocks[n], *from_steps(blocks[n], along_second))
         finish = (mixing, scalars) if n == len(cuts) - 1 else None
-        value = gate_up(pieces, weights, at, span, value, finish)
+        value = gate_up(pieces, held if finish else [], weights, at, span, value, finish)
 
     down_other = send(after(down_weight, value), SIBLING)
 
     value = combine((value, *from_steps(value, along_first)), scalars, 1, False)
+    down_own = load(down_weight, 0, width)
+    value = after(value, down_own)
     value = combine((value, *from_steps(value, along_second)), scalars, 1 + RING, True)
 
     half = width // 2
     sides = [
-        to_steps(down(value, (down_weight, down_other), at, half), along_second)
+        to_steps(down(value, (down_own, down_other), at, half), along_second)
         for at in (0, half)
     ]
     parts = to_steps(fold(sides), along_first)

time: 138 us -> 131 us (0.949)
  waiting for transfers between devices: 63.3 us -> 53.6 us
  Pallas kernels: 29.8 us -> 31.5 us
    ppermute x27, waiting for transfers between devices: 63.3 us -> 53.6 us  [send(): return lax.ppermute(value, 'tensor', pairs)]
    pallas_call x0 -> x3, Pallas kernels: none -> 7.23 us  [load(): pl.pallas_call(kernel, name='load', compiler_params=pltpu.CompilerParams(...]
    pallas_call x8, Pallas kernels: 29.8 us -> 24.2 us  [call(): pl.pallas_call(kernel, name=name, compiler_params=pltpu.CompilerParams(vm...]
    unnamed x10 -> x12, local copies, waits for them, and re-layouts: 3.87 us -> 3.66 us
  transfers between devices with their start and end apart: 27 -> 27, of which waited for: 17 -> 15; matrix products, arithmetic and copies ran while one was open for 1% -> 1% of each run, Pallas kernels for 11% -> 16%
where the time goes in v6:
time: 131 us; the launch traced here: 130 us
  waiting for transfers between devices  53.6 us (41%)
  starting transfers between devices  39.9 us (30%)
  Pallas kernels  31.5 us (24%)
  local copies, waits for them, and re-layouts  4.35 us (3%)
    ppermute x27, waiting for transfers between devices, send(): return lax.ppermute(value, 'tensor', pairs)  53.6 us
    ppermute x27, starting transfers between devices, send(): return lax.ppermute(value, 'tensor', pairs)  39.9 us
    pallas_call x8, Pallas kernels, call(): pl.pallas_call(kernel, name=name, compiler_params=pltpu.CompilerParams(vm...  24.2 us
    pallas_call x3, Pallas kernels, load(): pl.pallas_call(kernel, name='load', compiler_params=pltpu.CompilerParams(...  7.23 us
    unnamed x12, local copies, waits for them, and re-layouts  3.66 us
  transfers between devices with their start and end apart: 27, of which 15 were waited for; matrix products, arithmetic and copies ran while one was open for 1% of the time, Pallas kernels for 16%

profile of v6, /device:TPU:0, one launch (start us, length us, event | category | flops | bytes accessed | tf_op | source)
XLA Modules:
  0.0 130.3 jit_solution(9646486891993496746)
XLA Ops:
  0.0 0.0 collective-permute-start.6
  0.0 0.5 collective-permute-start.7
  0.5 2.8 %collective-permute-start = (bf16[16,8192]{1,0:T(8,128)(2,1)}, bf16[16,8192]{1,0:T(8,128)(2,1)S(1)}, u32[]{:S(2)}, u32[]{:S(2)}) collective-permute-start(bf16[16,8192]{1,0:T(8,128)(2,1)} %refs_0_), channel_id=1, source_target_pairs={{0,24},{1,7},{2,26},{3,1},{4,28},{5,3},{6,30},{7,5},{8,0},{9,15},{... | collective-permute-start | bytes 786440 | tf_op jit(solution)/shard_map/ppermute | solution.py:41
  3.4 0.8 collective-permute-start.1
  4.2 0.9 collective-permute-start.2
  5.0 2.0 %load.3.refs_4_ = bf16[448,4096]{1,0:T(8,128)(2,1)S(1)} custom-call(bf16[448,8192]{1,0:T(8,128)(2,1)} %bitcast.5), custom_call_target="tpu_custom_call" | custom-call | bytes 7340032 | tf_op jit(solution)/shard_map/load/pallas_call | solution.py:105
  7.1 1.8 %copy-done = bf16[448,4096]{1,0:T(8,128)(2,1)} copy-done((bf16[448,4096]{1,0:T(8,128)(2,1)}, bf16[448,4096]{1,0:T(8,128)(2,1)S(1)}, u32[]{:S(2)}) %copy-start) | copy-done | bytes 3670040
  8.9 2.1 %load.4.refs_5_ = bf16[448,4096]{1,0:T(8,128)(2,1)S(1)} custom-call(bf16[448,8192]{1,0:T(8,128)(2,1)} %bitcast.8), custom_call_target="tpu_custom_call" | custom-call | bytes 7340032 | tf_op jit(solution)/shard_map/load/pallas_call | solution.py:105
  11.0 1.9 %copy-done.2 = bf16[448,4096]{1,0:T(8,128)(2,1)} copy-done((bf16[448,4096]{1,0:T(8,128)(2,1)}, bf16[448,4096]{1,0:T(8,128)(2,1)S(1)}, u32[]{:S(2)}) %copy-start.2) | copy-done | bytes 3670040
  12.9 0.0 collective-permute-done.refs_1_
  12.9 0.0 collective-permute-done.1.refs_2_
  12.9 1.4 %collective-permute-done.2.refs_3_ = bf16[16,8192]{1,0:T(8,128)(2,1)S(1)} collective-permute-done((bf16[16,8192]{1,0:T(8,128)(2,1)}, bf16[16,8192]{1,0:T(8,128)(2,1)S(1)}, u32[]{:S(2)}, u32[]{:S(2)}) %collective-permute-start.2) | collective-permute-done | bytes 262176 | tf_op jit(solution)/shard_map/ppermute | solution.py:41
  14.3 0.1 stack.1
  14.3 1.6 %collective-permute-start.10 = (bf16[64,4096]{1,0:T(8,128)(2,1)S(1)}, bf16[64,4096]{1,0:T(8,128)(2,1)S(1)}, u32[]{:S(2)}, u32[]{:S(2)}) collective-permute-start(bf16[64,4096]{1,0:T(8,128)(2,1)S(1)} %get-tuple-element.24.refs_0_), channel_id=1, source_target_pairs={{0,2},{1,9},{2,4},{3,11},{4,6},{5,13},{6,0},{7,15},{8,10},{9,17},{... | collective-permute-start | bytes 1572872 | tf_op jit(solution)/shard_map/ppermute | solution.py:41
  16.0 1.7 %collective-permute-start.8 = (bf16[64,4096]{1,0:T(8,128)(2,1)S(1)}, bf16[64,4096]{1,0:T(8,128)(2,1)S(1)}, u32[]{:S(2)}, u32[]{:S(2)}) collective-permute-start(bf16[64,4096]{1,0:T(8,128)(2,1)S(1)} %get-tuple-element.24.refs_0_), channel_id=1, source_target_pairs={{0,6},{1,25},{2,0},{3,27},{4,2},{5,29},{6,4},{7,31},{8,14},{9,1},{... | collective-permute-start | bytes 1572872 | tf_op jit(solution)/shard_map/ppermute | solution.py:41
  17.6 2.0 %collective-permute-start.9 = (bf16[64,4096]{1,0:T(8,128)(2,1)S(1)}, bf16[64,4096]{1,0:T(8,128)(2,1)S(1)}, u32[]{:S(2)}, u32[]{:S(2)}) collective-permute-start(bf16[64,4096]{1,0:T(8,128)(2,1)S(1)} %get-tuple-element.24.refs_0_), channel_id=1, source_target_pairs={{0,4},{1,17},{2,6},{3,19},{4,0},{5,21},{6,2},{7,23},{8,12},{9,25},... | collective-permute-start | bytes 1572872 | tf_op jit(solution)/shard_map/ppermute | solution.py:41
  19.6 5.2 %collective-permute-done.10.refs_3_ = bf16[64,4096]{1,0:T(8,128)(2,1)S(1)} collective-permute-done((bf16[64,4096]{1,0:T(8,128)(2,1)S(1)}, bf16[64,4096]{1,0:T(8,128)(2,1)S(1)}, u32[]{:S(2)}, u32[]{:S(2)}) %collective-permute-start.10) | collective-permute-done | bytes 524320 | tf_op jit(solution)/shard_map/ppermute | solution.py:41
  24.8 1.8 %collective-permute-start.3 = (bf16[64,4096]{1,0:T(8,128)(2,1)S(1)}, bf16[64,4096]{1,0:T(8,128)(2,1)S(1)}, u32[]{:S(2)}, u32[]{:S(2)}) collective-permute-start(bf16[64,4096]{1,0:T(8,128)(2,1)S(1)} %get-tuple-element.23.refs_0_), channel_id=1, source_target_pairs={{0,6},{1,25},{2,0},{3,27},{4,2},{5,29},{6,4},{7,31},{8,14},{9,1},{... | collective-permute-start | bytes 1572872 | tf_op jit(solution)/shard_map/ppermute | solution.py:41
  26.6 0.0 collective-permute-done.8.refs_1_
  26.6 5.8 %collective-permute-start.4 = (bf16[64,4096]{1,0:T(8,128)(2,1)S(1)}, bf16[64,4096]{1,0:T(8,128)(2,1)}, u32[]{:S(2)}, u32[]{:S(2)}) collective-permute-start(bf16[64,4096]{1,0:T(8,128)(2,1)S(1)} %get-tuple-element.23.refs_0_), channel_id=1, source_target_pairs={{0,4},{1,17},{2,6},{3,19},{4,0},{5,21},{6,2},{7,23},{8,12},{9,25},... | collective-permute-start | bytes 1572872 | tf_op jit(solution)/shard_map/ppermute | solution.py:41
  32.4 0.0 collective-permute-done.9.refs_2_
  32.4 2.1 %collective-permute-start.5 = (bf16[64,4096]{1,0:T(8,128)(2,1)S(1)}, bf16[64,4096]{1,0:T(8,128)(2,1)}, u32[]{:S(2)}, u32[]{:S(2)}) collective-permute-start(bf16[64,4096]{1,0:T(8,128)(2,1)S(1)} %get-tuple-element.23.refs_0_), channel_id=1, source_target_pairs={{0,2},{1,9},{2,4},{3,11},{4,6},{5,13},{6,0},{7,15},{8,10},{9,17},{... | collective-permute-start | bytes 1572872 | tf_op jit(solution)/shard_map/ppermute | solution.py:41
  34.5 0.7 dynamic-slice_bitcast_fusion.refs_10_.refs_4_
  35.2 0.0 collective-permute-done.6.refs_6_
  35.2 0.0 collective-permute-done.7.refs_7_
  35.2 9.1 %gate_up.2.refs_8_ = f32[4,256,448]{2,1,0:T(8,128)S(1)} custom-call(bf16[64,4096]{1,0:T(8,128)(2,1)S(1)} %get-tuple-element.24.refs_0_, bf16[64,4096]{1,0:T(8,128)(2,1)S(1)} %collective-permute-done.8.refs_1_, bf16[64,4096]{1,0:T(8,128)(2,1)S(1)} %collective-permute-done.9.refs_2_, bf16[64,4096]{1,0:T(8,128)(2,1)S(1)} %collective-permute-done.10.refs_3_, ...), custom_call_target="tpu_custom_call" | custom-call | flops 3758096384 | bytes 14680064 | tf_op jit(solution)/shard_map/gate_up/pallas_call | solution.py:83
  44.3 0.0 collective-permute-done.3.refs_1_
  44.4 0.9 collective-permute-done.5.refs_3_
  45.3 8.0 %gate_up.3.refs_0_ = bf16[256,896]{1,0:T(8,128)(2,1)S(1)} custom-call(bf16[64,4096]{1,0:T(8,128)(2,1)S(1)} %get-tuple-element.23.refs_0_, bf16[64,4096]{1,0:T(8,128)(2,1)S(1)} %collective-permute-done.3.refs_1_, bf16[64,4096]{1,0:T(8,128)(2,1)} %collective-permute-done.4.refs_2_, bf16[64,4096]{1,0:T(8,128)(2,1)} %collective-permute-done.5.refs_3_, ...), custom_call_target="tpu_custom_call" | custom-call | flops 3758096384 | bytes 14680064 | tf_op jit(solution)/shard_map/gate_up/pallas_call | solution.py:83
  53.3 0.1 collective-permute-start.17
  53.4 1.1 collective-permute-start.11
  54.5 1.5 %collective-permute-start.12 = (bf16[256,896]{1,0:T(8,128)(2,1)S(1)}, bf16[256,896]{1,0:T(8,128)(2,1)S(1)}, u32[]{:S(2)}, u32[]{:S(2)}) collective-permute-start(bf16[256,896]{1,0:T(8,128)(2,1)S(1)} %gate_up.3.refs_0_), channel_id=1, source_target_pairs={{0,16},{1,5},{2,18},{3,7},{4,20},{5,1},{6,22},{7,3},{8,24},{9,13},... | collective-permute-start | bytes 1376264 | tf_op jit(solution)/shard_map/ppermute | solution.py:41
  56.0 3.1 %load.5.loaded = bf16[448,8192]{1,0:T(8,128)(2,1)S(1)} custom-call(bf16[448,8192]{1,0:T(8,128)(2,1)} %value.1), custom_call_target="tpu_custom_call" | custom-call | bytes 14680064 | tf_op jit(solution)/shard_map/load/pallas_call | solution.py:105
  59.1 2.9 %collective-permute-done.11.refs_1_ = bf16[256,896]{1,0:T(8,128)(2,1)S(1)} collective-permute-done((bf16[256,896]{1,0:T(8,128)(2,1)S(1)}, bf16[256,896]{1,0:T(8,128)(2,1)S(1)}, u32[]{:S(2)}, u32[]{:S(2)}) %collective-permute-start.11) | collective-permute-done | bytes 458784 | tf_op jit(solution)/shard_map/ppermute | solution.py:41
  62.0 2.6 %collective-permute-done.12.refs_2_ = bf16[256,896]{1,0:T(8,128)(2,1)S(1)} collective-permute-done((bf16[256,896]{1,0:T(8,128)(2,1)S(1)}, bf16[256,896]{1,0:T(8,128)(2,1)S(1)}, u32[]{:S(2)}, u32[]{:S(2)}) %collective-permute-start.12) | collective-permute-done | bytes 458784 | tf_op jit(solution)/shard_map/ppermute | solution.py:41
  64.6 4.8 %collective-permute-done.13.refs_3_ = bf16[256,896]{1,0:T(8,128)(2,1)S(1)} collective-permute-done((bf16[256,896]{1,0:T(8,128)(2,1)S(1)}, bf16[256,896]{1,0:T(8,128)(2,1)S(1)}, u32[]{:S(2)}, u32[]{:S(2)}) %collective-permute-start.13) | collective-permute-done | bytes 458784 | tf_op jit(solution)/shard_map/ppermute | solution.py:41
  69.4 0.9 combine.2.refs_0_
  70.3 0.7 collective-permute-start.14
  70.9 3.5 %collective-permute-start.15 = (bf16[256,896]{1,0:T(8,128)(2,1)S(1)}, bf16[256,896]{1,0:T(8,128)(2,1)S(1)}, u32[]{:S(2)}, u32[]{:S(2)}) collective-permute-start(bf16[256,896]{1,0:T(8,128)(2,1)S(1)} %combine.2.refs_0_), channel_id=1, source_target_pairs={{0,4},{1,17},{2,6},{3,19},{4,0},{5,21},{6,2},{7,23},{8,12},{9,25},... | collective-permute-start | bytes 1376264 | tf_op jit(solution)/shard_map/ppermute | solution.py:41
  74.5 0.8 collective-permute-start.16
  75.3 3.6 %collective-permute-done.14.refs_1_ = bf16[256,896]{1,0:T(8,128)(2,1)S(1)} collective-permute-done((bf16[256,896]{1,0:T(8,128)(2,1)S(1)}, bf16[256,896]{1,0:T(8,128)(2,1)S(1)}, u32[]{:S(2)}, u32[]{:S(2)}) %collective-permute-start.14) | collective-permute-done | bytes 458784 | tf_op jit(solution)/shard_map/ppermute | solution.py:41
  78.9 2.2 %collective-permute-done.15.refs_2_ = bf16[256,896]{1,0:T(8,128)(2,1)S(1)} collective-permute-done((bf16[256,896]{1,0:T(8,128)(2,1)S(1)}, bf16[256,896]{1,0:T(8,128)(2,1)S(1)}, u32[]{:S(2)}, u32[]{:S(2)}) %collective-permute-start.15) | collective-permute-done | bytes 458784 | tf_op jit(solution)/shard_map/ppermute | solution.py:41
  81.0 4.8 %collective-permute-done.16.refs_3_ = bf16[256,896]{1,0:T(8,128)(2,1)S(1)} collective-permute-done((bf16[256,896]{1,0:T(8,128)(2,1)S(1)}, bf16[256,896]{1,0:T(8,128)(2,1)S(1)}, u32[]{:S(2)}, u32[]{:S(2)}) %collective-permute-start.16) | collective-permute-done | bytes 458784 | tf_op jit(solution)/shard_map/ppermute | solution.py:41
  85.8 0.9 combine.3.held
  86.7 2.4 %down.3 = (bf16[64,4096]{1,0:T(8,128)(2,1)S(1)}, bf16[64,4096]{1,0:T(8,128)(2,1)S(1)}, bf16[64,4096]{1,0:T(8,128)(2,1)S(1)}, bf16[64,4096]{1,0:T(8,128)(2,1)S(1)}) custom-call(bf16[256,896]{1,0:T(8,128)(2,1)S(1)} %combine.3.held, bf16[448,8192]{1,0:T(8,128)(2,1)S(1)} %load.5.loaded, bf16[448,8192]{1,0:T(8,128)(2,1)S(1)} %collective-permute-done.17.loaded_other), custom_call_target="tpu_custom_call" | custom-call | flops 1879048192 | bytes 7340032 | tf_op jit(solution)/shard_map/down/pallas_call | solution.py:83
  89.1 2.3 %collective-permute-start.21 = (bf16[64,4096]{1,0:T(8,128)(2,1)S(1)}, bf16[64,4096]{1,0:T(8,128)(2,1)S(1)}, u32[]{:S(2)}, u32[]{:S(2)}) collective-permute-start(bf16[64,4096]{1,0:T(8,128)(2,1)S(1)} %get-tuple-element.32), channel_id=1, source_target_pairs={{0,2},{1,9},{2,4},{3,11},{4,6},{5,13},{6,0},{7,15},{8,10},{9,17},{... | collective-permute-start | bytes 1572872 | tf_op jit(solution)/shard_map/ppermute | solution.py:41
  91.4 0.9 collective-permute-start.22
  92.3 2.5 %collective-permute-start.23 = (bf16[64,4096]{1,0:T(8,128)(2,1)S(1)}, bf16[64,4096]{1,0:T(8,128)(2,1)S(1)}, u32[]{:S(2)}, u32[]{:S(2)}) collective-permute-start(bf16[64,4096]{1,0:T(8,128)(2,1)S(1)} %get-tuple-element.34), channel_id=1, source_target_pairs={{0,6},{1,25},{2,0},{3,27},{4,2},{5,29},{6,4},{7,31},{8,14},{9,1},{... | collective-permute-start | bytes 1572872 | tf_op jit(solution)/shard_map/ppermute | solution.py:41
  94.9 2.4 %down.2 = (bf16[64,4096]{1,0:T(8,128)(2,1)S(1)}, bf16[64,4096]{1,0:T(8,128)(2,1)S(1)}, bf16[64,4096]{1,0:T(8,128)(2,1)S(1)}, bf16[64,4096]{1,0:T(8,128)(2,1)S(1)}) custom-call(bf16[256,896]{1,0:T(8,128)(2,1)S(1)} %combine.3.held, bf16[448,8192]{1,0:T(8,128)(2,1)S(1)} %load.5.loaded, bf16[448,8192]{1,0:T(8,128)(2,1)S(1)} %collective-permute-done.17.loaded_other), custom_call_target="tpu_custom_call" | custom-call | flops 1879048192 | bytes 7340032 | tf_op jit(solution)/shard_map/down/pallas_call | solution.py:83
  97.3 0.1 collective-permute-start.18
  97.3 2.1 %collective-permute-start.19 = (bf16[64,4096]{1,0:T(8,128)(2,1)S(1)}, bf16[64,4096]{1,0:T(8,128)(2,1)S(1)}, u32[]{:S(2)}, u32[]{:S(2)}) collective-permute-start(bf16[64,4096]{1,0:T(8,128)(2,1)S(1)} %get-tuple-element.29), channel_id=1, source_target_pairs={{0,4},{1,17},{2,6},{3,19},{4,0},{5,21},{6,2},{7,23},{8,12},{9,25},... | collective-permute-start | bytes 1572872 | tf_op jit(solution)/shard_map/ppermute | solution.py:41
  99.4 5.9 %collective-permute-done.21.refs_5_ = bf16[64,4096]{1,0:T(8,128)(2,1)S(1)} collective-permute-done((bf16[64,4096]{1,0:T(8,128)(2,1)S(1)}, bf16[64,4096]{1,0:T(8,128)(2,1)S(1)}, u32[]{:S(2)}, u32[]{:S(2)}) %collective-permute-start.21) | collective-permute-done | bytes 524320 | tf_op jit(solution)/shard_map/ppermute | solution.py:41
  105.4 0.0 collective-permute-done.22.refs_6_
  105.4 0.9 collective-permute-done.23.refs_7_
  106.3 10.3 %collective-permute-done.18.refs_1_ = bf16[64,4096]{1,0:T(8,128)(2,1)S(1)} collective-permute-done((bf16[64,4096]{1,0:T(8,128)(2,1)S(1)}, bf16[64,4096]{1,0:T(8,128)(2,1)S(1)}, u32[]{:S(2)}, u32[]{:S(2)}) %collective-permute-start.18) | collective-permute-done | bytes 524320 | tf_op jit(solution)/shard_map/ppermute | solution.py:41
  116.6 0.9 collective-permute-done.20.refs_3_
  117.6 0.5 fold.1
  118.1 0.1 collective-permute-start.24
  118.2 2.0 %collective-permute-start.25 = (bf16[16,8192]{1,0:T(8,128)(2,1)S(1)}, bf16[16,8192]{1,0:T(8,128)(2,1)S(1)}, u32[]{:S(2)}, u32[]{:S(2)}) collective-permute-start(bf16[16,8192]{1,0:T(8,128)(2,1)S(1)} %get-tuple-element.37), channel_id=1, source_target_pairs={{0,16},{1,5},{2,18},{3,7},{4,20},{5,1},{6,22},{7,3},{8,24},{9,13},... | collective-permute-start | bytes 786440 | tf_op jit(solution)/shard_map/ppermute | solution.py:41
  120.2 2.1 %collective-permute-start.26 = (bf16[16,8192]{1,0:T(8,128)(2,1)S(1)}, bf16[16,8192]{1,0:T(8,128)(2,1)S(1)}, u32[]{:S(2)}, u32[]{:S(2)}) collective-permute-start(bf16[16,8192]{1,0:T(8,128)(2,1)S(1)} %get-tuple-element.38), channel_id=1, source_target_pairs={{0,24},{1,7},{2,26},{3,1},{4,28},{5,3},{6,30},{7,5},{8,0},{9,15},{... | collective-permute-start | bytes 786440 | tf_op jit(solution)/shard_map/ppermute | solution.py:41
  122.3 6.2 %collective-permute-done.24 = bf16[16,8192]{1,0:T(8,128)(2,1)S(1)} collective-permute-done((bf16[16,8192]{1,0:T(8,128)(2,1)S(1)}, bf16[16,8192]{1,0:T(8,128)(2,1)S(1)}, u32[]{:S(2)}, u32[]{:S(2)}) %collective-permute-start.24) | collective-permute-done | bytes 262176 | tf_op jit(solution)/shard_map/ppermute | solution.py:41
  128.5 0.0 collective-permute-done.25
  128.5 0.9 collective-permute-done.26
  129.4 0.8 add_convert_fusion
  (15 shorter events, 0.0 us)
Async XLA Ops:
  0.0 35.2 %collective-permute-start.6 = (bf16[448,8192]{1,0:T(8,128)(2,1)}, bf16[448,8192]{1,0:T(8,128)(2,1)}, u32[]{:S(2)}, u32[]{:S(2)}) collective-permute-start(bf16[448,8192]{1,0:T(8,128)(2,1)} %bitcast.4), channel_id=1, source_target_pairs={{0,1},{1,0},{2,3},{3,2},{4,5},{5,4},{6,7},{7,6},{8,9},{9,8},{10,11... | collective-permute-start | bytes 22020104 | tf_op jit(solution)/shard_map/ppermute | solution.py:41
  0.0 35.2 %collective-permute-start.7 = (bf16[448,8192]{1,0:T(8,128)(2,1)}, bf16[448,8192]{1,0:T(8,128)(2,1)}, u32[]{:S(2)}, u32[]{:S(2)}) collective-permute-start(bf16[448,8192]{1,0:T(8,128)(2,1)} %bitcast.7), channel_id=1, source_target_pairs={{0,1},{1,0},{2,3},{3,2},{4,5},{5,4},{6,7},{7,6},{8,9},{9,8},{10,11... | collective-permute-start | bytes 22020104 | tf_op jit(solution)/shard_map/ppermute | solution.py:41
  0.5 12.3 %collective-permute-start = (bf16[16,8192]{1,0:T(8,128)(2,1)}, bf16[16,8192]{1,0:T(8,128)(2,1)S(1)}, u32[]{:S(2)}, u32[]{:S(2)}) collective-permute-start(bf16[16,8192]{1,0:T(8,128)(2,1)} %refs_0_), channel_id=1, source_target_pairs={{0,24},{1,7},{2,26},{3,1},{4,28},{5,3},{6,30},{7,5},{8,0},{9,15},{... | collective-permute-start | bytes 786440 | tf_op jit(solution)/shard_map/ppermute | solution.py:41
  3.4 9.5 %collective-permute-start.1 = (bf16[16,8192]{1,0:T(8,128)(2,1)}, bf16[16,8192]{1,0:T(8,128)(2,1)S(1)}, u32[]{:S(2)}, u32[]{:S(2)}) collective-permute-start(bf16[16,8192]{1,0:T(8,128)(2,1)} %refs_0_), channel_id=1, source_target_pairs={{0,16},{1,5},{2,18},{3,7},{4,20},{5,1},{6,22},{7,3},{8,24},{9,13},... | collective-permute-start | bytes 786440 | tf_op jit(solution)/shard_map/ppermute | solution.py:41
  4.2 10.1 %collective-permute-start.2 = (bf16[16,8192]{1,0:T(8,128)(2,1)}, bf16[16,8192]{1,0:T(8,128)(2,1)S(1)}, u32[]{:S(2)}, u32[]{:S(2)}) collective-permute-start(bf16[16,8192]{1,0:T(8,128)(2,1)} %refs_0_), channel_id=1, source_target_pairs={{0,8},{1,3},{2,10},{3,5},{4,12},{5,7},{6,14},{7,1},{8,16},{9,11},{... | collective-permute-start | bytes 786440 | tf_op jit(solution)/shard_map/ppermute | solution.py:41
  7.1 1.8 %copy-start = (bf16[448,4096]{1,0:T(8,128)(2,1)}, bf16[448,4096]{1,0:T(8,128)(2,1)S(1)}, u32[]{:S(2)}) copy-start(bf16[448,4096]{1,0:T(8,128)(2,1)S(1)} %load.3.refs_4_) | copy-start | bytes 11010052
  8.9 5.4 %copy-start.5 = (bf16[16,8192]{1,0:T(8,128)(2,1)S(1)}, bf16[16,8192]{1,0:T(8,128)(2,1)}, u32[]{:S(2)}) copy-start(bf16[16,8192]{1,0:T(8,128)(2,1)} %refs_0_) | copy-start | bytes 786436
  11.0 1.9 %copy-start.2 = (bf16[448,4096]{1,0:T(8,128)(2,1)}, bf16[448,4096]{1,0:T(8,128)(2,1)S(1)}, u32[]{:S(2)}) copy-start(bf16[448,4096]{1,0:T(8,128)(2,1)S(1)} %load.4.refs_5_) | copy-start | bytes 11010052
  14.3 10.5 %collective-permute-start.10 = (bf16[64,4096]{1,0:T(8,128)(2,1)S(1)}, bf16[64,4096]{1,0:T(8,128)(2,1)S(1)}, u32[]{:S(2)}, u32[]{:S(2)}) collective-permute-start(bf16[64,4096]{1,0:T(8,128)(2,1)S(1)} %get-tuple-element.24.refs_0_), channel_id=1, source_target_pairs={{0,2},{1,9},{2,4},{3,11},{4,6},{5,13},{6,0},{7,15},{8,10},{9,17},{... | collective-permute-start | bytes 1572872 | tf_op jit(solution)/shard_map/ppermute | solution.py:41
  16.0 10.6 %collective-permute-start.8 = (bf16[64,4096]{1,0:T(8,128)(2,1)S(1)}, bf16[64,4096]{1,0:T(8,128)(2,1)S(1)}, u32[]{:S(2)}, u32[]{:S(2)}) collective-permute-start(bf16[64,4096]{1,0:T(8,128)(2,1)S(1)} %get-tuple-element.24.refs_0_), channel_id=1, source_target_pairs={{0,6},{1,25},{2,0},{3,27},{4,2},{5,29},{6,4},{7,31},{8,14},{9,1},{... | collective-permute-start | bytes 1572872 | tf_op jit(solution)/shard_map/ppermute | solution.py:41
  17.6 14.8 %collective-permute-start.9 = (bf16[64,4096]{1,0:T(8,128)(2,1)S(1)}, bf16[64,4096]{1,0:T(8,128)(2,1)S(1)}, u32[]{:S(2)}, u32[]{:S(2)}) collective-permute-start(bf16[64,4096]{1,0:T(8,128)(2,1)S(1)} %get-tuple-element.24.refs_0_), channel_id=1, source_target_pairs={{0,4},{1,17},{2,6},{3,19},{4,0},{5,21},{6,2},{7,23},{8,12},{9,25},... | collective-permute-start | bytes 1572872 | tf_op jit(solution)/shard_map/ppermute | solution.py:41
  24.8 19.6 %collective-permute-start.3 = (bf16[64,4096]{1,0:T(8,128)(2,1)S(1)}, bf16[64,4096]{1,0:T(8,128)(2,1)S(1)}, u32[]{:S(2)}, u32[]{:S(2)}) collective-permute-start(bf16[64,4096]{1,0:T(8,128)(2,1)S(1)} %get-tuple-element.23.refs_0_), channel_id=1, source_target_pairs={{0,6},{1,25},{2,0},{3,27},{4,2},{5,29},{6,4},{7,31},{8,14},{9,1},{... | collective-permute-start | bytes 1572872 | tf_op jit(solution)/shard_map/ppermute | solution.py:41
  26.6 17.8 %collective-permute-start.4 = (bf16[64,4096]{1,0:T(8,128)(2,1)S(1)}, bf16[64,4096]{1,0:T(8,128)(2,1)}, u32[]{:S(2)}, u32[]{:S(2)}) collective-permute-start(bf16[64,4096]{1,0:T(8,128)(2,1)S(1)} %get-tuple-element.23.refs_0_), channel_id=1, source_target_pairs={{0,4},{1,17},{2,6},{3,19},{4,0},{5,21},{6,2},{7,23},{8,12},{9,25},... | collective-permute-start | bytes 1572872 | tf_op jit(solution)/shard_map/ppermute | solution.py:41
  32.4 12.9 %collective-permute-start.5 = (bf16[64,4096]{1,0:T(8,128)(2,1)S(1)}, bf16[64,4096]{1,0:T(8,128)(2,1)}, u32[]{:S(2)}, u32[]{:S(2)}) collective-permute-start(bf16[64,4096]{1,0:T(8,128)(2,1)S(1)} %get-tuple-element.23.refs_0_), channel_id=1, source_target_pairs={{0,2},{1,9},{2,4},{3,11},{4,6},{5,13},{6,0},{7,15},{8,10},{9,17},{... | collective-permute-start | bytes 1572872 | tf_op jit(solution)/shard_map/ppermute | solution.py:41
  35.2 10.1 %copy-start.1 = (bf16[448,4096]{1,0:T(8,128)(2,1)S(1)}, bf16[448,4096]{1,0:T(8,128)(2,1)}, u32[]{:S(2)}) copy-start(bf16[448,4096]{1,0:T(8,128)(2,1)} %copy-done) | copy-start | bytes 11010052
  35.2 10.1 %copy-start.3 = (bf16[448,4096]{1,0:T(8,128)(2,1)S(1)}, bf16[448,4096]{1,0:T(8,128)(2,1)}, u32[]{:S(2)}) copy-start(bf16[448,4096]{1,0:T(8,128)(2,1)} %copy-done.2) | copy-start | bytes 11010052
  35.2 10.1 %copy-start.4 = (bf16[448,448]{1,0:T(8,128)(2,1)S(1)}, bf16[448,448]{1,0:T(8,128)(2,1)}, u32[]{:S(2)}) copy-start(bf16[448,448]{1,0:T(8,128)(2,1)} %refs_9_.1) | copy-start | bytes 1204228
  53.3 33.4 %collective-permute-start.17 = (bf16[448,8192]{1,0:T(8,128)(2,1)}, bf16[448,8192]{1,0:T(8,128)(2,1)S(1)}, u32[]{:S(2)}, u32[]{:S(2)}) collective-permute-start(bf16[448,8192]{1,0:T(8,128)(2,1)} %value.1), channel_id=1, source_target_pairs={{0,1},{1,0},{2,3},{3,2},{4,5},{5,4},{6,7},{7,6},{8,9},{9,8},{10,11... | collective-permute-start | bytes 22020104 | tf_op jit(solution)/shard_map/ppermute | solution.py:41
  53.4 8.5 %collective-permute-start.11 = (bf16[256,896]{1,0:T(8,128)(2,1)S(1)}, bf16[256,896]{1,0:T(8,128)(2,1)S(1)}, u32[]{:S(2)}, u32[]{:S(2)}) collective-permute-start(bf16[256,896]{1,0:T(8,128)(2,1)S(1)} %gate_up.3.refs_0_), channel_id=1, source_target_pairs={{0,24},{1,7},{2,26},{3,1},{4,28},{5,3},{6,30},{7,5},{8,0},{9,15},{... | collective-permute-start | bytes 1376264 | tf_op jit(solution)/shard_map/ppermute | solution.py:41
  54.5 10.1 %collective-permute-start.12 = (bf16[256,896]{1,0:T(8,128)(2,1)S(1)}, bf16[256,896]{1,0:T(8,128)(2,1)S(1)}, u32[]{:S(2)}, u32[]{:S(2)}) collective-permute-start(bf16[256,896]{1,0:T(8,128)(2,1)S(1)} %gate_up.3.refs_0_), channel_id=1, source_target_pairs={{0,16},{1,5},{2,18},{3,7},{4,20},{5,1},{6,22},{7,3},{8,24},{9,13},... | collective-permute-start | bytes 1376264 | tf_op jit(solution)/shard_map/ppermute | solution.py:41
  56.0 13.4 %collective-permute-start.13 = (bf16[256,896]{1,0:T(8,128)(2,1)S(1)}, bf16[256,896]{1,0:T(8,128)(2,1)S(1)}, u32[]{:S(2)}, u32[]{:S(2)}) collective-permute-start(bf16[256,896]{1,0:T(8,128)(2,1)S(1)} %gate_up.3.refs_0_), channel_id=1, source_target_pairs={{0,8},{1,3},{2,10},{3,5},{4,12},{5,7},{6,14},{7,1},{8,16},{9,11},{... | collective-permute-start | bytes 1376264 | tf_op jit(solution)/shard_map/ppermute | solution.py:41
  70.3 8.6 %collective-permute-start.14 = (bf16[256,896]{1,0:T(8,128)(2,1)S(1)}, bf16[256,896]{1,0:T(8,128)(2,1)S(1)}, u32[]{:S(2)}, u32[]{:S(2)}) collective-permute-start(bf16[256,896]{1,0:T(8,128)(2,1)S(1)} %combine.2.refs_0_), channel_id=1, source_target_pairs={{0,6},{1,25},{2,0},{3,27},{4,2},{5,29},{6,4},{7,31},{8,14},{9,1},{... | collective-permute-start | bytes 1376264 | tf_op jit(solution)/shard_map/ppermute | solution.py:41
  70.9 10.1 %collective-permute-start.15 = (bf16[256,896]{1,0:T(8,128)(2,1)S(1)}, bf16[256,896]{1,0:T(8,128)(2,1)S(1)}, u32[]{:S(2)}, u32[]{:S(2)}) collective-permute-start(bf16[256,896]{1,0:T(8,128)(2,1)S(1)} %combine.2.refs_0_), channel_id=1, source_target_pairs={{0,4},{1,17},{2,6},{3,19},{4,0},{5,21},{6,2},{7,23},{8,12},{9,25},... | collective-permute-start | bytes 1376264 | tf_op jit(solution)/shard_map/ppermute | solution.py:41
  74.5 11.4 %collective-permute-start.16 = (bf16[256,896]{1,0:T(8,128)(2,1)S(1)}, bf16[256,896]{1,0:T(8,128)(2,1)S(1)}, u32[]{:S(2)}, u32[]{:S(2)}) collective-permute-start(bf16[256,896]{1,0:T(8,128)(2,1)S(1)} %combine.2.refs_0_), channel_id=1, source_target_pairs={{0,2},{1,9},{2,4},{3,11},{4,6},{5,13},{6,0},{7,15},{8,10},{9,17},{... | collective-permute-start | bytes 1376264 | tf_op jit(solution)/shard_map/ppermute | solution.py:41
  89.1 16.3 %collective-permute-start.21 = (bf16[64,4096]{1,0:T(8,128)(2,1)S(1)}, bf16[64,4096]{1,0:T(8,128)(2,1)S(1)}, u32[]{:S(2)}, u32[]{:S(2)}) collective-permute-start(bf16[64,4096]{1,0:T(8,128)(2,1)S(1)} %get-tuple-element.32), channel_id=1, source_target_pairs={{0,2},{1,9},{2,4},{3,11},{4,6},{5,13},{6,0},{7,15},{8,10},{9,17},{... | collective-permute-start | bytes 1572872 | tf_op jit(solution)/shard_map/ppermute | solution.py:41
  91.4 13.9 %collective-permute-start.22 = (bf16[64,4096]{1,0:T(8,128)(2,1)S(1)}, bf16[64,4096]{1,0:T(8,128)(2,1)S(1)}, u32[]{:S(2)}, u32[]{:S(2)}) collective-permute-start(bf16[64,4096]{1,0:T(8,128)(2,1)S(1)} %get-tuple-element.33), channel_id=1, source_target_pairs={{0,4},{1,17},{2,6},{3,19},{4,0},{5,21},{6,2},{7,23},{8,12},{9,25},... | collective-permute-start | bytes 1572872 | tf_op jit(solution)/shard_map/ppermute | solution.py:41
  92.3 13.9 %collective-permute-start.23 = (bf16[64,4096]{1,0:T(8,128)(2,1)S(1)}, bf16[64,4096]{1,0:T(8,128)(2,1)S(1)}, u32[]{:S(2)}, u32[]{:S(2)}) collective-permute-start(bf16[64,4096]{1,0:T(8,128)(2,1)S(1)} %get-tuple-element.34), channel_id=1, source_target_pairs={{0,6},{1,25},{2,0},{3,27},{4,2},{5,29},{6,4},{7,31},{8,14},{9,1},{... | collective-permute-start | bytes 1572872 | tf_op jit(solution)/shard_map/ppermute | solution.py:41
  97.3 19.4 %collective-permute-start.18 = (bf16[64,4096]{1,0:T(8,128)(2,1)S(1)}, bf16[64,4096]{1,0:T(8,128)(2,1)S(1)}, u32[]{:S(2)}, u32[]{:S(2)}) collective-permute-start(bf16[64,4096]{1,0:T(8,128)(2,1)S(1)} %get-tuple-element.28), channel_id=1, source_target_pairs={{0,2},{1,9},{2,4},{3,11},{4,6},{5,13},{6,0},{7,15},{8,10},{9,17},{... | collective-permute-start | bytes 1572872 | tf_op jit(solution)/shard_map/ppermute | solution.py:41
  97.3 19.3 %collective-permute-start.19 = (bf16[64,4096]{1,0:T(8,128)(2,1)S(1)}, bf16[64,4096]{1,0:T(8,128)(2,1)S(1)}, u32[]{:S(2)}, u32[]{:S(2)}) collective-permute-start(bf16[64,4096]{1,0:T(8,128)(2,1)S(1)} %get-tuple-element.29), channel_id=1, source_target_pairs={{0,4},{1,17},{2,6},{3,19},{4,0},{5,21},{6,2},{7,23},{8,12},{9,25},... | collective-permute-start | bytes 1572872 | tf_op jit(solution)/shard_map/ppermute | solution.py:41
  105.4 12.2 %collective-permute-start.20 = (bf16[64,4096]{1,0:T(8,128)(2,1)S(1)}, bf16[64,4096]{1,0:T(8,128)(2,1)S(1)}, u32[]{:S(2)}, u32[]{:S(2)}) collective-permute-start(bf16[64,4096]{1,0:T(8,128)(2,1)S(1)} %get-tuple-element.30), channel_id=1, source_target_pairs={{0,6},{1,25},{2,0},{3,27},{4,2},{5,29},{6,4},{7,31},{8,14},{9,1},{... | collective-permute-start | bytes 1572872 | tf_op jit(solution)/shard_map/ppermute | solution.py:41
  118.1 10.5 %collective-permute-start.24 = (bf16[16,8192]{1,0:T(8,128)(2,1)S(1)}, bf16[16,8192]{1,0:T(8,128)(2,1)S(1)}, u32[]{:S(2)}, u32[]{:S(2)}) collective-permute-start(bf16[16,8192]{1,0:T(8,128)(2,1)S(1)} %get-tuple-element.36), channel_id=1, source_target_pairs={{0,8},{1,3},{2,10},{3,5},{4,12},{5,7},{6,14},{7,1},{8,16},{9,11},{... | collective-permute-start | bytes 786440 | tf_op jit(solution)/shard_map/ppermute | solution.py:41
  118.2 10.3 %collective-permute-start.25 = (bf16[16,8192]{1,0:T(8,128)(2,1)S(1)}, bf16[16,8192]{1,0:T(8,128)(2,1)S(1)}, u32[]{:S(2)}, u32[]{:S(2)}) collective-permute-start(bf16[16,8192]{1,0:T(8,128)(2,1)S(1)} %get-tuple-element.37), channel_id=1, source_target_pairs={{0,16},{1,5},{2,18},{3,7},{4,20},{5,1},{6,22},{7,3},{8,24},{9,13},... | collective-permute-start | bytes 786440 | tf_op jit(solution)/shard_map/ppermute | solution.py:41
  120.2 9.2 %collective-permute-start.26 = (bf16[16,8192]{1,0:T(8,128)(2,1)S(1)}, bf16[16,8192]{1,0:T(8,128)(2,1)S(1)}, u32[]{:S(2)}, u32[]{:S(2)}) collective-permute-start(bf16[16,8192]{1,0:T(8,128)(2,1)S(1)} %get-tuple-element.38), channel_id=1, source_target_pairs={{0,24},{1,7},{2,26},{3,1},{4,28},{5,3},{6,30},{7,5},{8,0},{9,15},{... | collective-permute-start | bytes 786440 | tf_op jit(solution)/shard_map/ppermute | solution.py:41

commit v7 on v6

--- a/solution.py
+++ b/solution.py
@@ -9,9 +9,11 @@
 from jax.sharding import PartitionSpec as P
 
 RING = 4
+ORDER = (0, 2, 1, 3)
 PLACES = [(x, y, c) for x in range(RING) for y in range(RING) for c in range(2)]
 GATHER_SPANS = (1, 1)
-LIMIT = 40 * 2**20
+OUT_SPANS = (1, 1)
+LIMIT = 24 * 2**20
 SMALL = 16 * 2**20
 BY_ROWS = (((1,), (1,)), ((), ()))
 
@@ -42,7 +44,7 @@
 
 
 def from_steps(value, along):
-    return send(value, along(-1)), send(value, along(2)), send(value, along(1))
+    return send(value, along(2)), send(value, along(-1)), send(value, along(1))
 
 
 def after(value, *others):
@@ -96,24 +98,34 @@
     return pltpu.with_memory_space_constraint(value, pltpu.HBM)
 
 
-def load(value, at, span):
-    def kernel(value, out, sem):
-        copy = pltpu.make_async_copy(value.at[:, pl.ds(at, span)], out, sem)
-        copy.start()
-        copy.wait()
+def load(values, at, span):
+    count = len(values)
+
+    def kernel(*refs):
+        sems = refs[-1]
+        copies = [
+            pltpu.make_async_copy(refs[n].at[:, pl.ds(at, span)], refs[count + n], sems.at[n])
+            for n in range(count)
+        ]
+        for copy in copies:
+            copy.start()
+        for copy in copies:
+            copy.wait()
 
     return pl.pallas_call(
         kernel,
         name="load",
         compiler_params=pltpu.CompilerParams(vmem_limit_bytes=SMALL),
         cost_estimate=pl.CostEstimate(
-            flops=0, bytes_accessed=4 * value.shape[0] * span, transcendentals=0
+            flops=0,
+            bytes_accessed=sum(4 * value.shape[0] * span for value in values),
+            transcendentals=0,
         ),
-        in_specs=[pl.BlockSpec(memory_space=pltpu.HBM)],
-        out_specs=VMEM,
-        out_shape=pltpu.VMEM((value.shape[0], span), value.dtype),
-        scratch_shapes=[pltpu.SemaphoreType.DMA],
-    )(in_hbm(value))
+        in_specs=[pl.BlockSpec(memory_space=pltpu.HBM)] * count,
+        out_specs=[VMEM] * count,
+        out_shape=[pltpu.VMEM((value.shape[0], span), value.dtype) for value in values],
+        scratch_shapes=[pltpu.SemaphoreType.DMA((count,))],
+    )(*[in_hbm(value) for value in values])
 
 
 def stack(parts, cuts):
@@ -122,7 +134,7 @@
     def kernel(*refs):
         ins, outs = refs[: len(parts)], refs[len(parts) :]
         for (at, span), out in zip(cuts, outs):
-            for n, part in enumerate(ins):
+            for n, part in zip(ORDER, ins):
                 out[n * rows : (n + 1) * rows] = part[:, at : at + span]
 
     return call(
@@ -139,55 +151,70 @@
     group = pieces[0].shape[0]
     rows = RING * group
     units = weights[0].shape[0]
-    block = math.gcd(span, 1024)
+    block = math.gcd(span, 2048)
     steps = span // block
     opening, closing = sums is None, finish is not None
+    count = len(close)
 
     def kernel(*refs):
         refs = list(refs)
-        parts, loads, refs = refs[:RING], refs[RING : RING + 4], refs[RING + 4 :]
+        parts, near = refs[:RING], refs[RING : RING + count]
+        far = refs[RING + count : RING + 4]
+        refs = refs[RING + 4 :]
+        x, held, sems, refs = refs[-3], refs[-2], refs[-1], refs[:-3]
         before = None if opening else refs.pop(0)
         if closing:
-            mixing, scalars, out, total, x = refs
+            mixing, scalars, out, total = refs
         else:
-            total, x = refs
-        step = pl.program_id(0)
-
-        @pl.when(step == 0)
-        def _():
-            total[...] = jnp.zeros(total.shape, total.dtype) if opening else before[...]
-
-        for n, part in enumerate(parts):
+            (total,) = refs
+        copies = [
+            [
+                pltpu.make_async_copy(
+                    load.at[:, pl.ds(at + step * block, block)], held.at[step, n], sems.at[step, n]
+                )
+                for step in range(steps)
+            ]
+            for n, load in enumerate(far)
+        ]
+        for step in range(steps):
+            for n in range(4 - count):
+                copies[n][step].start()
+        for n, part in zip(ORDER, parts):
             x[n * group : (n + 1) * group] = part[...]
-        here = pl.ds(pl.multiple_of(step * block, block), block)
-        for n, weight in enumerate(loads):
-            total[n] += lax.dot_general(
-                x[...],
-                weight[:, here] if n < len(close) else weight[...],
-                BY_ROWS,
-                preferred_element_type=jnp.float32,
+        for n in range(count):
+            product = lax.dot_general(
+                x[...], near[n][...], BY_ROWS, preferred_element_type=jnp.float32
             )
-
+            total[n] = product if opening else before[n] + product
+        for step in range(steps):
+            here = x[:, step * block : (step + 1) * block]
+            for n in range(4 - count):
+                copies[n][step].wait()
+                product = lax.dot_general(
+                    here, held[step, n], BY_ROWS, preferred_element_type=jnp.float32
+                )
+                if step > 0:
+                    total[count + n] += product
+                else:
+                    total[count + n] = product if opening else before[count + n] + product
         if closing:
-
-            @pl.when(step == steps - 1)
-            def _():
-                local = []
-                for n in (0, 2):
-                    gate, up = total[n], total[n + 1]
-                    hidden = (gate / (1.0 + jnp.exp(-gate)) * up).astype(jnp.bfloat16)
-                    local.append(dot(hidden, mixing[...]))
-                own, other = local
-                turn = scalars[0]
-                out[:, :units] = (other + turn * own).astype(jnp.bfloat16)
-                out[:, units:] = (own - turn * other).astype(jnp.bfloat16)
-
-    operands = [*pieces, *close, *[in_hbm(w) for w in weights[len(close) :]]]
-    specs = [pl.BlockSpec((group, block), lambda k: (0, k))] * RING
-    specs += [VMEM] * len(close)
-    streamed = pl.BlockSpec((units, block), lambda k: (0, k + at // block))
-    specs += [streamed] * (4 - len(close))
-    scratch = [pltpu.VMEM((rows, block), jnp.bfloat16)]
+            local = []
+            for n in (0, 2):
+                gate, up = total[n], total[n + 1]
+                hidden = (gate / (1.0 + jnp.exp(-gate)) * up).astype(jnp.bfloat16)
+                local.append(dot(hidden, mixing[...]))
+            own, other = local
+            turn = scalars[0]
+            out[:, :units] = (other + turn * own).astype(jnp.bfloat16)
+            out[:, units:] = (own - turn * other).astype(jnp.bfloat16)
+
+    operands = [*pieces, *close, *[in_hbm(w) for w in weights]]
+    specs = [VMEM] * (RING + count) + [pl.BlockSpec(memory_space=pltpu.HBM)] * (4 - count)
+    scratch = [
+        pltpu.VMEM((rows, span), jnp.bfloat16),
+        pltpu.VMEM((steps, 4 - count, units, block), jnp.bfloat16),
+        pltpu.SemaphoreType.DMA((steps, 4 - count)),
+    ]
     if not opening:
         operands.append(sums)
         specs.append(VMEM)
@@ -207,7 +234,6 @@
         [out],
         specs,
         LIMIT,
-        grid=(steps,),
         scratch_shapes=scratch,
     )[0]
 
@@ -217,7 +243,8 @@
     slot = rows // (RING * RING)
 
     def kernel(*refs):
-        came, factors, out = refs[:RING], refs[RING], refs[RING + 1]
+        came = dict(zip(ORDER, refs[:RING]))
+        factors, out = refs[RING], refs[RING + 1]
         for i in range(RING):
             for j in range(RING):
                 total = 0.0
@@ -295,7 +322,7 @@
 
 
 def to_steps(parts, along):
-    return parts[0], send(parts[1], along(1)), send(parts[2], along(2)), send(parts[3], along(-1))
+    return parts[0], send(parts[2], along(2)), send(parts[1], along(1)), send(parts[3], along(-1))
 
 
 def body(tokens, gate_weight, up_weight, down_weight, mixing):
@@ -305,28 +332,30 @@
 
     gate, up = gate_weight.T, up_weight.T
     cuts = cuts_of(GATHER_SPANS, width)
-    held = [load(gate, *cuts[-1]), load(up, *cuts[-1])]
-    weights = [gate, up, send(gate, SIBLING), send(up, SIBLING)]
+    others = send(gate, SIBLING), send(up, SIBLING)
 
     near = from_steps(tokens, along_first)
-    blocks = stack((after(tokens, *held), *near), cuts)
+    (own,) = load((tokens,), 0, width)
+    blocks = stack((own, *near), cuts)
     value = None
     for n, (at, span) in enumerate(cuts):
         pieces = (blocks[n], *from_steps(blocks[n], along_second))
         finish = (mixing, scalars) if n == len(cuts) - 1 else None
-        value = gate_up(pieces, held if finish else [], weights, at, span, value, finish)
+        if n == 0:
+            value = gate_up(pieces, (), (gate, up, *others), at, span, value, finish)
+        else:
+            close = load((after(gate, value), up), at, span)
+            value = gate_up(pieces, close, others, at, span, value, finish)
 
     down_other = send(after(down_weight, value), SIBLING)
-
+    (down_own,) = load((down_weight,), 0, width)
     value = combine((value, *from_steps(value, along_first)), scalars, 1, False)
-    down_own = load(down_weight, 0, width)
     value = after(value, down_own)
     value = combine((value, *from_steps(value, along_second)), scalars, 1 + RING, True)
 
-    half = width // 2
     sides = [
-        to_steps(down(value, (down_own, down_other), at, half), along_second)
-        for at in (0, half)
+        to_steps(down(value, (down_own, down_other), at, span), along_second)
+        for at, span in cuts_of(OUT_SPANS, width)
     ]
     parts = to_steps(fold(sides), along_first)
     return sum(part.astype(jnp.float32) for part in parts).astype(jnp.bfloat16)

time: 131 us -> 126 us (0.962)
  local copies, waits for them, and re-layouts: 4.35 us -> 0.71 us
  waiting for transfers between devices: 53.6 us -> 55.9 us
  Pallas kernels: 31.5 us -> 29.6 us
  starting transfers between devices: 39.9 us -> 38.5 us
    unnamed x12 -> x6, local copies, waits for them, and re-layouts: 3.66 us -> 0.02 us
    ppermute x27, waiting for transfers between devices: 53.6 us -> 55.9 us  [send(): return lax.ppermute(value, 'tensor', pairs)]
    pallas_call x8, Pallas kernels: 24.2 us -> 22.2 us  [call(): pl.pallas_call(kernel, name=name, compiler_params=pltpu.CompilerParams(vm...]
    ppermute x27, starting transfers between devices: 39.9 us -> 38.5 us  [send(): return lax.ppermute(value, 'tensor', pairs)]
  transfers between devices with their start and end apart: 27 -> 27, of which waited for: 15 -> 16; matrix products, arithmetic and copies ran while one was open for 1% -> 1% of each run, Pallas kernels for 16% -> 15%
where the time goes in v7:
time: 126 us
  waiting for transfers between devices  55.9 us (44%)
  starting transfers between devices  38.5 us (31%)
  Pallas kernels  29.6 us (23%)
    ppermute x27, waiting for transfers between devices, send(): return lax.ppermute(value, 'tensor', pairs)  55.9 us
    ppermute x27, starting transfers between devices, send(): return lax.ppermute(value, 'tensor', pairs)  38.5 us
    pallas_call x8, Pallas kernels, call(): pl.pallas_call(kernel, name=name, compiler_params=pltpu.CompilerParams(vm...  22.2 us
    pallas_call x3, Pallas kernels, load(): pl.pallas_call(kernel, name='load', compiler_params=pltpu.CompilerParams(...  7.4 us
  transfers between devices with their start and end apart: 27, of which 16 were waited for; matrix products, arithmetic and copies ran while one was open for 1% of the time, Pallas kernels for 15%

profile of v7, /device:TPU:0, one launch (start us, length us, event | category | flops | bytes accessed | tf_op | source)
XLA Modules:
  0.0 125.9 jit_solution(12421794693982726532)
XLA Ops:
  0.0 0.5 collective-permute-start.9
  0.5 3.1 %collective-permute-start = (bf16[16,8192]{1,0:T(8,128)(2,1)}, bf16[16,8192]{1,0:T(8,128)(2,1)S(1)}, u32[]{:S(2)}, u32[]{:S(2)}) collective-permute-start(bf16[16,8192]{1,0:T(8,128)(2,1)} %refs_0_.2), channel_id=1, source_target_pairs={{0,16},{1,5},{2,18},{3,7},{4,20},{5,1},{6,22},{7,3},{8,24},{9,13},... | collective-permute-start | bytes 786440 | tf_op jit(solution)/shard_map/ppermute | solution.py:43
  3.6 1.1 collective-permute-start.1
  4.8 0.9 collective-permute-start.2
  5.6 1.0 load.3.refs_0_
  6.6 2.0 %collective-permute-done.refs_1_ = bf16[16,8192]{1,0:T(8,128)(2,1)S(1)} collective-permute-done((bf16[16,8192]{1,0:T(8,128)(2,1)}, bf16[16,8192]{1,0:T(8,128)(2,1)S(1)}, u32[]{:S(2)}, u32[]{:S(2)}) %collective-permute-start) | collective-permute-done | bytes 262176 | tf_op jit(solution)/shard_map/ppermute | solution.py:43
  8.6 3.0 %collective-permute-done.1.refs_2_ = bf16[16,8192]{1,0:T(8,128)(2,1)S(1)} collective-permute-done((bf16[16,8192]{1,0:T(8,128)(2,1)}, bf16[16,8192]{1,0:T(8,128)(2,1)S(1)}, u32[]{:S(2)}, u32[]{:S(2)}) %collective-permute-start.1) | collective-permute-done | bytes 262176 | tf_op jit(solution)/shard_map/ppermute | solution.py:43
  11.6 1.0 collective-permute-done.2.refs_3_
  12.6 0.1 stack.1
  12.6 3.3 %collective-permute-start.6 = (bf16[64,4096]{1,0:T(8,128)(2,1)S(1)}, bf16[64,4096]{1,0:T(8,128)(2,1)S(1)}, u32[]{:S(2)}, u32[]{:S(2)}) collective-permute-start(bf16[64,4096]{1,0:T(8,128)(2,1)S(1)} %get-tuple-element.25.refs_0_), channel_id=1, source_target_pairs={{0,4},{1,17},{2,6},{3,19},{4,0},{5,21},{6,2},{7,23},{8,12},{9,25},... | collective-permute-start | bytes 1572872 | tf_op jit(solution)/shard_map/ppermute | solution.py:43
  15.9 1.1 collective-permute-start.7
  17.0 1.0 collective-permute-start.8
  17.9 5.6 %collective-permute-done.6.refs_1_ = bf16[64,4096]{1,0:T(8,128)(2,1)S(1)} collective-permute-done((bf16[64,4096]{1,0:T(8,128)(2,1)S(1)}, bf16[64,4096]{1,0:T(8,128)(2,1)S(1)}, u32[]{:S(2)}, u32[]{:S(2)}) %collective-permute-start.6) | collective-permute-done | bytes 524320 | tf_op jit(solution)/shard_map/ppermute | solution.py:43
  23.5 3.2 %collective-permute-start.3 = (bf16[64,4096]{1,0:T(8,128)(2,1)S(1)}, bf16[64,4096]{1,0:T(8,128)(2,1)S(1)}, u32[]{:S(2)}, u32[]{:S(2)}) collective-permute-start(bf16[64,4096]{1,0:T(8,128)(2,1)S(1)} %get-tuple-element.24.refs_0_), channel_id=1, source_target_pairs={{0,4},{1,17},{2,6},{3,19},{4,0},{5,21},{6,2},{7,23},{8,12},{9,25},... | collective-permute-start | bytes 1572872 | tf_op jit(solution)/shard_map/ppermute | solution.py:43
  26.7 2.7 %collective-permute-done.7.refs_2_ = bf16[64,4096]{1,0:T(8,128)(2,1)S(1)} collective-permute-done((bf16[64,4096]{1,0:T(8,128)(2,1)S(1)}, bf16[64,4096]{1,0:T(8,128)(2,1)S(1)}, u32[]{:S(2)}, u32[]{:S(2)}) %collective-permute-start.7) | collective-permute-done | bytes 524320 | tf_op jit(solution)/shard_map/ppermute | solution.py:43
  29.4 2.6 %collective-permute-start.4 = (bf16[64,4096]{1,0:T(8,128)(2,1)S(1)}, bf16[64,4096]{1,0:T(8,128)(2,1)}, u32[]{:S(2)}, u32[]{:S(2)}) collective-permute-start(bf16[64,4096]{1,0:T(8,128)(2,1)S(1)} %get-tuple-element.24.refs_0_), channel_id=1, source_target_pairs={{0,6},{1,25},{2,0},{3,27},{4,2},{5,29},{6,4},{7,31},{8,14},{9,1},{... | collective-permute-start | bytes 1572872 | tf_op jit(solution)/shard_map/ppermute | solution.py:43
  32.0 0.0 collective-permute-done.8.refs_3_
  32.0 0.0 collective-permute-start.5
  32.0 0.7 dynamic-slice_bitcast_fusion.refs_10_.refs_4_
  32.7 0.0 collective-permute-done.10.refs_7_
  32.7 0.0 collective-permute-done.9.refs_6_
  32.7 7.4 %gate_up.2.refs_8_ = f32[4,256,448]{2,1,0:T(8,128)S(1)} custom-call(bf16[64,4096]{1,0:T(8,128)(2,1)S(1)} %get-tuple-element.25.refs_0_, bf16[64,4096]{1,0:T(8,128)(2,1)S(1)} %collective-permute-done.6.refs_1_, bf16[64,4096]{1,0:T(8,128)(2,1)S(1)} %collective-permute-done.7.refs_2_, bf16[64,4096]{1,0:T(8,128)(2,1)S(1)} %collective-permute-done.8.refs_3_, ...), custom_call_target="tpu_custom_call" | custom-call | flops 3758096384 | bytes 14680064 | tf_op jit(solution)/shard_map/gate_up/pallas_call | solution.py:85
  40.2 0.0 copy-start
  40.2 0.0 slice-start
  40.2 3.3 %load.4 = (bf16[448,4096]{1,0:T(8,128)(2,1)S(1)}, bf16[448,4096]{1,0:T(8,128)(2,1)S(1)}) custom-call(bf16[448,8192]{1,0:T(8,128)(2,1)} %bitcast.6, bf16[448,8192]{1,0:T(8,128)(2,1)} %bitcast.9), custom_call_target="tpu_custom_call" | custom-call | bytes 14680064 | tf_op jit(solution)/shard_map/load/pallas_call | solution.py:115
  43.5 0.0 collective-permute-done.3.refs_1_
  43.5 0.0 collective-permute-done.5.refs_3_
  43.6 0.0 slice-start.1
  43.6 7.6 %gate_up.3.refs_0_ = bf16[256,896]{1,0:T(8,128)(2,1)S(1)} custom-call(bf16[64,4096]{1,0:T(8,128)(2,1)S(1)} %get-tuple-element.24.refs_0_, bf16[64,4096]{1,0:T(8,128)(2,1)S(1)} %collective-permute-done.3.refs_1_, bf16[64,4096]{1,0:T(8,128)(2,1)} %collective-permute-done.4.refs_2_, bf16[64,4096]{1,0:T(8,128)(2,1)} %collective-permute-done.5.refs_3_, ...), custom_call_target="tpu_custom_call" | custom-call | flops 3758096384 | bytes 14680064 | tf_op jit(solution)/shard_map/gate_up/pallas_call | solution.py:85
  51.2 0.1 collective-permute-start.17
  51.3 2.1 %collective-permute-start.11 = (bf16[256,896]{1,0:T(8,128)(2,1)S(1)}, bf16[256,896]{1,0:T(8,128)(2,1)S(1)}, u32[]{:S(2)}, u32[]{:S(2)}) collective-permute-start(bf16[256,896]{1,0:T(8,128)(2,1)S(1)} %gate_up.3.refs_0_), channel_id=1, source_target_pairs={{0,16},{1,5},{2,18},{3,7},{4,20},{5,1},{6,22},{7,3},{8,24},{9,13},... | collective-permute-start | bytes 1376264 | tf_op jit(solution)/shard_map/ppermute | solution.py:43
  53.4 1.2 collective-permute-start.12
  54.5 0.8 collective-permute-start.13
  55.4 3.1 %load.5.loaded = bf16[448,8192]{1,0:T(8,128)(2,1)S(1)} custom-call(bf16[448,8192]{1,0:T(8,128)(2,1)} %refs_0_.3), custom_call_target="tpu_custom_call" | custom-call | bytes 14680064 | tf_op jit(solution)/shard_map/load/pallas_call | solution.py:115
  58.5 3.0 %collective-permute-done.11.refs_1_ = bf16[256,896]{1,0:T(8,128)(2,1)S(1)} collective-permute-done((bf16[256,896]{1,0:T(8,128)(2,1)S(1)}, bf16[256,896]{1,0:T(8,128)(2,1)S(1)}, u32[]{:S(2)}, u32[]{:S(2)}) %collective-permute-start.11) | collective-permute-done | bytes 458784 | tf_op jit(solution)/shard_map/ppermute | solution.py:43
  61.5 3.9 %collective-permute-done.12.refs_2_ = bf16[256,896]{1,0:T(8,128)(2,1)S(1)} collective-permute-done((bf16[256,896]{1,0:T(8,128)(2,1)S(1)}, bf16[256,896]{1,0:T(8,128)(2,1)S(1)}, u32[]{:S(2)}, u32[]{:S(2)}) %collective-permute-start.12) | collective-permute-done | bytes 458784 | tf_op jit(solution)/shard_map/ppermute | solution.py:43
  65.4 0.9 collective-permute-done.13.refs_3_
  66.3 0.9 combine.2.refs_0_
  67.2 1.5 %collective-permute-start.14 = (bf16[256,896]{1,0:T(8,128)(2,1)S(1)}, bf16[256,896]{1,0:T(8,128)(2,1)S(1)}, u32[]{:S(2)}, u32[]{:S(2)}) collective-permute-start(bf16[256,896]{1,0:T(8,128)(2,1)S(1)} %combine.2.refs_0_), channel_id=1, source_target_pairs={{0,4},{1,17},{2,6},{3,19},{4,0},{5,21},{6,2},{7,23},{8,12},{9,25},... | collective-permute-start | bytes 1376264 | tf_op jit(solution)/shard_map/ppermute | solution.py:43
  68.7 1.9 %collective-permute-start.15 = (bf16[256,896]{1,0:T(8,128)(2,1)S(1)}, bf16[256,896]{1,0:T(8,128)(2,1)S(1)}, u32[]{:S(2)}, u32[]{:S(2)}) collective-permute-start(bf16[256,896]{1,0:T(8,128)(2,1)S(1)} %combine.2.refs_0_), channel_id=1, source_target_pairs={{0,6},{1,25},{2,0},{3,27},{4,2},{5,29},{6,4},{7,31},{8,14},{9,1},{... | collective-permute-start | bytes 1376264 | tf_op jit(solution)/shard_map/ppermute | solution.py:43
  70.6 0.8 collective-permute-start.16
  71.4 6.0 %collective-permute-done.14.refs_1_ = bf16[256,896]{1,0:T(8,128)(2,1)S(1)} collective-permute-done((bf16[256,896]{1,0:T(8,128)(2,1)S(1)}, bf16[256,896]{1,0:T(8,128)(2,1)S(1)}, u32[]{:S(2)}, u32[]{:S(2)}) %collective-permute-start.14) | collective-permute-done | bytes 458784 | tf_op jit(solution)/shard_map/ppermute | solution.py:43
  77.3 5.4 %collective-permute-done.15.refs_2_ = bf16[256,896]{1,0:T(8,128)(2,1)S(1)} collective-permute-done((bf16[256,896]{1,0:T(8,128)(2,1)S(1)}, bf16[256,896]{1,0:T(8,128)(2,1)S(1)}, u32[]{:S(2)}, u32[]{:S(2)}) %collective-permute-start.15) | collective-permute-done | bytes 458784 | tf_op jit(solution)/shard_map/ppermute | solution.py:43
  82.8 0.0 collective-permute-done.16.refs_3_
  82.8 0.9 combine.3.held
  83.7 2.4 %down.3 = (bf16[64,4096]{1,0:T(8,128)(2,1)S(1)}, bf16[64,4096]{1,0:T(8,128)(2,1)S(1)}, bf16[64,4096]{1,0:T(8,128)(2,1)S(1)}, bf16[64,4096]{1,0:T(8,128)(2,1)S(1)}) custom-call(bf16[256,896]{1,0:T(8,128)(2,1)S(1)} %combine.3.held, bf16[448,8192]{1,0:T(8,128)(2,1)S(1)} %load.5.loaded, bf16[448,8192]{1,0:T(8,128)(2,1)S(1)} %collective-permute-done.17.loaded_other), custom_call_target="tpu_custom_call" | custom-call | flops 1879048192 | bytes 7340032 | tf_op jit(solution)/shard_map/down/pallas_call | solution.py:85
  86.1 0.9 collective-permute-start.21
  87.0 2.4 %collective-permute-start.22 = (bf16[64,4096]{1,0:T(8,128)(2,1)S(1)}, bf16[64,4096]{1,0:T(8,128)(2,1)S(1)}, u32[]{:S(2)}, u32[]{:S(2)}) collective-permute-start(bf16[64,4096]{1,0:T(8,128)(2,1)S(1)} %get-tuple-element.37), channel_id=1, source_target_pairs={{0,2},{1,9},{2,4},{3,11},{4,6},{5,13},{6,0},{7,15},{8,10},{9,17},{... | collective-permute-start | bytes 1572872 | tf_op jit(solution)/shard_map/ppermute | solution.py:43
  89.5 0.8 collective-permute-start.23
  90.3 2.4 %down.2 = (bf16[64,4096]{1,0:T(8,128)(2,1)S(1)}, bf16[64,4096]{1,0:T(8,128)(2,1)S(1)}, bf16[64,4096]{1,0:T(8,128)(2,1)S(1)}, bf16[64,4096]{1,0:T(8,128)(2,1)S(1)}) custom-call(bf16[256,896]{1,0:T(8,128)(2,1)S(1)} %combine.3.held, bf16[448,8192]{1,0:T(8,128)(2,1)S(1)} %load.5.loaded, bf16[448,8192]{1,0:T(8,128)(2,1)S(1)} %collective-permute-done.17.loaded_other), custom_call_target="tpu_custom_call" | custom-call | flops 1879048192 | bytes 7340032 | tf_op jit(solution)/shard_map/down/pallas_call | solution.py:85
  92.7 1.6 %collective-permute-start.18 = (bf16[64,4096]{1,0:T(8,128)(2,1)S(1)}, bf16[64,4096]{1,0:T(8,128)(2,1)S(1)}, u32[]{:S(2)}, u32[]{:S(2)}) collective-permute-start(bf16[64,4096]{1,0:T(8,128)(2,1)S(1)} %get-tuple-element.32), channel_id=1, source_target_pairs={{0,4},{1,17},{2,6},{3,19},{4,0},{5,21},{6,2},{7,23},{8,12},{9,25},... | collective-permute-start | bytes 1572872 | tf_op jit(solution)/shard_map/ppermute | solution.py:43
  94.3 0.0 collective-permute-start.19
  94.3 2.7 %collective-permute-done.21.refs_5_ = bf16[64,4096]{1,0:T(8,128)(2,1)S(1)} collective-permute-done((bf16[64,4096]{1,0:T(8,128)(2,1)S(1)}, bf16[64,4096]{1,0:T(8,128)(2,1)S(1)}, u32[]{:S(2)}, u32[]{:S(2)}) %collective-permute-start.21) | collective-permute-done | bytes 524320 | tf_op jit(solution)/shard_map/ppermute | solution.py:43
  97.0 2.4 %collective-permute-start.20 = (bf16[64,4096]{1,0:T(8,128)(2,1)S(1)}, bf16[64,4096]{1,0:T(8,128)(2,1)S(1)}, u32[]{:S(2)}, u32[]{:S(2)}) collective-permute-start(bf16[64,4096]{1,0:T(8,128)(2,1)S(1)} %get-tuple-element.34), channel_id=1, source_target_pairs={{0,6},{1,25},{2,0},{3,27},{4,2},{5,29},{6,4},{7,31},{8,14},{9,1},{... | collective-permute-start | bytes 1572872 | tf_op jit(solution)/shard_map/ppermute | solution.py:43
  99.4 3.1 %collective-permute-done.22.refs_6_ = bf16[64,4096]{1,0:T(8,128)(2,1)S(1)} collective-permute-done((bf16[64,4096]{1,0:T(8,128)(2,1)S(1)}, bf16[64,4096]{1,0:T(8,128)(2,1)S(1)}, u32[]{:S(2)}, u32[]{:S(2)}) %collective-permute-start.22) | collective-permute-done | bytes 524320 | tf_op jit(solution)/shard_map/ppermute | solution.py:43
  102.5 5.8 %collective-permute-done.18.refs_1_ = bf16[64,4096]{1,0:T(8,128)(2,1)S(1)} collective-permute-done((bf16[64,4096]{1,0:T(8,128)(2,1)S(1)}, bf16[64,4096]{1,0:T(8,128)(2,1)S(1)}, u32[]{:S(2)}, u32[]{:S(2)}) %collective-permute-start.18) | collective-permute-done | bytes 524320 | tf_op jit(solution)/shard_map/ppermute | solution.py:43
  108.3 5.5 %collective-permute-done.19.refs_2_ = bf16[64,4096]{1,0:T(8,128)(2,1)S(1)} collective-permute-done((bf16[64,4096]{1,0:T(8,128)(2,1)S(1)}, bf16[64,4096]{1,0:T(8,128)(2,1)S(1)}, u32[]{:S(2)}, u32[]{:S(2)}) %collective-permute-start.19) | collective-permute-done | bytes 524320 | tf_op jit(solution)/shard_map/ppermute | solution.py:43
  113.7 0.5 fold.1
  114.2 2.0 %collective-permute-start.24 = (bf16[16,8192]{1,0:T(8,128)(2,1)S(1)}, bf16[16,8192]{1,0:T(8,128)(2,1)S(1)}, u32[]{:S(2)}, u32[]{:S(2)}) collective-permute-start(bf16[16,8192]{1,0:T(8,128)(2,1)S(1)} %get-tuple-element.40), channel_id=1, source_target_pairs={{0,16},{1,5},{2,18},{3,7},{4,20},{5,1},{6,22},{7,3},{8,24},{9,13},... | collective-permute-start | bytes 786440 | tf_op jit(solution)/shard_map/ppermute | solution.py:43
  116.3 0.6 collective-permute-start.25
  116.9 2.6 %collective-permute-start.26 = (bf16[16,8192]{1,0:T(8,128)(2,1)S(1)}, bf16[16,8192]{1,0:T(8,128)(2,1)S(1)}, u32[]{:S(2)}, u32[]{:S(2)}) collective-permute-start(bf16[16,8192]{1,0:T(8,128)(2,1)S(1)} %get-tuple-element.42), channel_id=1, source_target_pairs={{0,24},{1,7},{2,26},{3,1},{4,28},{5,3},{6,30},{7,5},{8,0},{9,15},{... | collective-permute-start | bytes 786440 | tf_op jit(solution)/shard_map/ppermute | solution.py:43
  119.5 2.8 %collective-permute-done.24 = bf16[16,8192]{1,0:T(8,128)(2,1)S(1)} collective-permute-done((bf16[16,8192]{1,0:T(8,128)(2,1)S(1)}, bf16[16,8192]{1,0:T(8,128)(2,1)S(1)}, u32[]{:S(2)}, u32[]{:S(2)}) %collective-permute-start.24) | collective-permute-done | bytes 262176 | tf_op jit(solution)/shard_map/ppermute | solution.py:43
  122.3 2.7 %collective-permute-done.25 = bf16[16,8192]{1,0:T(8,128)(2,1)S(1)} collective-permute-done((bf16[16,8192]{1,0:T(8,128)(2,1)S(1)}, bf16[16,8192]{1,0:T(8,128)(2,1)S(1)}, u32[]{:S(2)}, u32[]{:S(2)}) %collective-permute-start.25) | collective-permute-done | bytes 262176 | tf_op jit(solution)/shard_map/ppermute | solution.py:43
  125.0 0.8 add_convert_fusion
  (10 shorter events, 0.0 us)
Async XLA Ops:
  0.0 32.7 %collective-permute-start.10 = (bf16[448,8192]{1,0:T(8,128)(2,1)}, bf16[448,8192]{1,0:T(8,128)(2,1)}, u32[]{:S(2)}, u32[]{:S(2)}) collective-permute-start(bf16[448,8192]{1,0:T(8,128)(2,1)} %bitcast.7), channel_id=1, source_target_pairs={{0,1},{1,0},{2,3},{3,2},{4,5},{5,4},{6,7},{7,6},{8,9},{9,8},{10,11... | collective-permute-start | bytes 22020104 | tf_op jit(solution)/shard_map/ppermute | solution.py:43
  0.0 32.7 %collective-permute-start.9 = (bf16[448,8192]{1,0:T(8,128)(2,1)}, bf16[448,8192]{1,0:T(8,128)(2,1)}, u32[]{:S(2)}, u32[]{:S(2)}) collective-permute-start(bf16[448,8192]{1,0:T(8,128)(2,1)} %bitcast.4), channel_id=1, source_target_pairs={{0,1},{1,0},{2,3},{3,2},{4,5},{5,4},{6,7},{7,6},{8,9},{9,8},{10,11... | collective-permute-start | bytes 22020104 | tf_op jit(solution)/shard_map/ppermute | solution.py:43
  0.5 8.1 %collective-permute-start = (bf16[16,8192]{1,0:T(8,128)(2,1)}, bf16[16,8192]{1,0:T(8,128)(2,1)S(1)}, u32[]{:S(2)}, u32[]{:S(2)}) collective-permute-start(bf16[16,8192]{1,0:T(8,128)(2,1)} %refs_0_.2), channel_id=1, source_target_pairs={{0,16},{1,5},{2,18},{3,7},{4,20},{5,1},{6,22},{7,3},{8,24},{9,13},... | collective-permute-start | bytes 786440 | tf_op jit(solution)/shard_map/ppermute | solution.py:43
  3.6 8.0 %collective-permute-start.1 = (bf16[16,8192]{1,0:T(8,128)(2,1)}, bf16[16,8192]{1,0:T(8,128)(2,1)S(1)}, u32[]{:S(2)}, u32[]{:S(2)}) collective-permute-start(bf16[16,8192]{1,0:T(8,128)(2,1)} %refs_0_.2), channel_id=1, source_target_pairs={{0,24},{1,7},{2,26},{3,1},{4,28},{5,3},{6,30},{7,5},{8,0},{9,15},{... | collective-permute-start | bytes 786440 | tf_op jit(solution)/shard_map/ppermute | solution.py:43
  4.8 7.8 %collective-permute-start.2 = (bf16[16,8192]{1,0:T(8,128)(2,1)}, bf16[16,8192]{1,0:T(8,128)(2,1)S(1)}, u32[]{:S(2)}, u32[]{:S(2)}) collective-permute-start(bf16[16,8192]{1,0:T(8,128)(2,1)} %refs_0_.2), channel_id=1, source_target_pairs={{0,8},{1,3},{2,10},{3,5},{4,12},{5,7},{6,14},{7,1},{8,16},{9,11},{... | collective-permute-start | bytes 786440 | tf_op jit(solution)/shard_map/ppermute | solution.py:43
  12.6 10.9 %collective-permute-start.6 = (bf16[64,4096]{1,0:T(8,128)(2,1)S(1)}, bf16[64,4096]{1,0:T(8,128)(2,1)S(1)}, u32[]{:S(2)}, u32[]{:S(2)}) collective-permute-start(bf16[64,4096]{1,0:T(8,128)(2,1)S(1)} %get-tuple-element.25.refs_0_), channel_id=1, source_target_pairs={{0,4},{1,17},{2,6},{3,19},{4,0},{5,21},{6,2},{7,23},{8,12},{9,25},... | collective-permute-start | bytes 1572872 | tf_op jit(solution)/shard_map/ppermute | solution.py:43
  15.9 13.5 %collective-permute-start.7 = (bf16[64,4096]{1,0:T(8,128)(2,1)S(1)}, bf16[64,4096]{1,0:T(8,128)(2,1)S(1)}, u32[]{:S(2)}, u32[]{:S(2)}) collective-permute-start(bf16[64,4096]{1,0:T(8,128)(2,1)S(1)} %get-tuple-element.25.refs_0_), channel_id=1, source_target_pairs={{0,6},{1,25},{2,0},{3,27},{4,2},{5,29},{6,4},{7,31},{8,14},{9,1},{... | collective-permute-start | bytes 1572872 | tf_op jit(solution)/shard_map/ppermute | solution.py:43
  17.0 15.1 %collective-permute-start.8 = (bf16[64,4096]{1,0:T(8,128)(2,1)S(1)}, bf16[64,4096]{1,0:T(8,128)(2,1)S(1)}, u32[]{:S(2)}, u32[]{:S(2)}) collective-permute-start(bf16[64,4096]{1,0:T(8,128)(2,1)S(1)} %get-tuple-element.25.refs_0_), channel_id=1, source_target_pairs={{0,2},{1,9},{2,4},{3,11},{4,6},{5,13},{6,0},{7,15},{8,10},{9,17},{... | collective-permute-start | bytes 1572872 | tf_op jit(solution)/shard_map/ppermute | solution.py:43
  23.5 20.0 %collective-permute-start.3 = (bf16[64,4096]{1,0:T(8,128)(2,1)S(1)}, bf16[64,4096]{1,0:T(8,128)(2,1)S(1)}, u32[]{:S(2)}, u32[]{:S(2)}) collective-permute-start(bf16[64,4096]{1,0:T(8,128)(2,1)S(1)} %get-tuple-element.24.refs_0_), channel_id=1, source_target_pairs={{0,4},{1,17},{2,6},{3,19},{4,0},{5,21},{6,2},{7,23},{8,12},{9,25},... | collective-permute-start | bytes 1572872 | tf_op jit(solution)/shard_map/ppermute | solution.py:43
  29.4 14.1 %collective-permute-start.4 = (bf16[64,4096]{1,0:T(8,128)(2,1)S(1)}, bf16[64,4096]{1,0:T(8,128)(2,1)}, u32[]{:S(2)}, u32[]{:S(2)}) collective-permute-start(bf16[64,4096]{1,0:T(8,128)(2,1)S(1)} %get-tuple-element.24.refs_0_), channel_id=1, source_target_pairs={{0,6},{1,25},{2,0},{3,27},{4,2},{5,29},{6,4},{7,31},{8,14},{9,1},{... | collective-permute-start | bytes 1572872 | tf_op jit(solution)/shard_map/ppermute | solution.py:43
  32.0 11.5 %collective-permute-start.5 = (bf16[64,4096]{1,0:T(8,128)(2,1)S(1)}, bf16[64,4096]{1,0:T(8,128)(2,1)}, u32[]{:S(2)}, u32[]{:S(2)}) collective-permute-start(bf16[64,4096]{1,0:T(8,128)(2,1)S(1)} %get-tuple-element.24.refs_0_), channel_id=1, source_target_pairs={{0,2},{1,9},{2,4},{3,11},{4,6},{5,13},{6,0},{7,15},{8,10},{9,17},{... | collective-permute-start | bytes 1572872 | tf_op jit(solution)/shard_map/ppermute | solution.py:43
  40.2 3.4 %copy-start = (bf16[448,448]{1,0:T(8,128)(2,1)S(1)}, bf16[448,448]{1,0:T(8,128)(2,1)}, u32[]{:S(2)}) copy-start(bf16[448,448]{1,0:T(8,128)(2,1)} %refs_9_.1) | copy-start | bytes 1204228
  40.2 11.0 %slice-start = ((s8[7340032]{0:T(1024)(128)(4,1)}), s8[4194304]{0:T(1024)(128)(4,1)S(1)}, s32[]{:S(2)}) async-start(s8[7340032]{0:T(1024)(128)(4,1)} %bitcast.10), calls=%async_computation | async-start | bytes 8388608
  43.6 7.6 %slice-start.1 = ((s8[7340032]{0:T(1024)(128)(4,1)}), s8[3145728]{0:T(1024)(128)(4,1)S(1)}, s32[]{:S(2)}) async-start(s8[7340032]{0:T(1024)(128)(4,1)} %bitcast.10), calls=%async_computation.1 | async-start | bytes 6291456
  51.2 32.5 %collective-permute-start.17 = (bf16[448,8192]{1,0:T(8,128)(2,1)S(1)}, bf16[448,8192]{1,0:T(8,128)(2,1)S(1)}, u32[]{:S(2)}, u32[]{:S(2)}) collective-permute-start(bf16[448,8192]{1,0:T(8,128)(2,1)S(1)} %bitcast.11), channel_id=1, source_target_pairs={{0,1},{1,0},{2,3},{3,2},{4,5},{5,4},{6,7},{7,6},{8,9},{9,8},{10,11... | collective-permute-start | bytes 22020104 | tf_op jit(solution)/shard_map/ppermute | solution.py:43
  51.3 10.2 %collective-permute-start.11 = (bf16[256,896]{1,0:T(8,128)(2,1)S(1)}, bf16[256,896]{1,0:T(8,128)(2,1)S(1)}, u32[]{:S(2)}, u32[]{:S(2)}) collective-permute-start(bf16[256,896]{1,0:T(8,128)(2,1)S(1)} %gate_up.3.refs_0_), channel_id=1, source_target_pairs={{0,16},{1,5},{2,18},{3,7},{4,20},{5,1},{6,22},{7,3},{8,24},{9,13},... | collective-permute-start | bytes 1376264 | tf_op jit(solution)/shard_map/ppermute | solution.py:43
  53.4 12.0 %collective-permute-start.12 = (bf16[256,896]{1,0:T(8,128)(2,1)S(1)}, bf16[256,896]{1,0:T(8,128)(2,1)S(1)}, u32[]{:S(2)}, u32[]{:S(2)}) collective-permute-start(bf16[256,896]{1,0:T(8,128)(2,1)S(1)} %gate_up.3.refs_0_), channel_id=1, source_target_pairs={{0,24},{1,7},{2,26},{3,1},{4,28},{5,3},{6,30},{7,5},{8,0},{9,15},{... | collective-permute-start | bytes 1376264 | tf_op jit(solution)/shard_map/ppermute | solution.py:43
  54.5 11.7 %collective-permute-start.13 = (bf16[256,896]{1,0:T(8,128)(2,1)S(1)}, bf16[256,896]{1,0:T(8,128)(2,1)S(1)}, u32[]{:S(2)}, u32[]{:S(2)}) collective-permute-start(bf16[256,896]{1,0:T(8,128)(2,1)S(1)} %gate_up.3.refs_0_), channel_id=1, source_target_pairs={{0,8},{1,3},{2,10},{3,5},{4,12},{5,7},{6,14},{7,1},{8,16},{9,11},{... | collective-permute-start | bytes 1376264 | tf_op jit(solution)/shard_map/ppermute | solution.py:43
  67.2 10.2 %collective-permute-start.14 = (bf16[256,896]{1,0:T(8,128)(2,1)S(1)}, bf16[256,896]{1,0:T(8,128)(2,1)S(1)}, u32[]{:S(2)}, u32[]{:S(2)}) collective-permute-start(bf16[256,896]{1,0:T(8,128)(2,1)S(1)} %combine.2.refs_0_), channel_id=1, source_target_pairs={{0,4},{1,17},{2,6},{3,19},{4,0},{5,21},{6,2},{7,23},{8,12},{9,25},... | collective-permute-start | bytes 1376264 | tf_op jit(solution)/shard_map/ppermute | solution.py:43
  68.7 14.0 %collective-permute-start.15 = (bf16[256,896]{1,0:T(8,128)(2,1)S(1)}, bf16[256,896]{1,0:T(8,128)(2,1)S(1)}, u32[]{:S(2)}, u32[]{:S(2)}) collective-permute-start(bf16[256,896]{1,0:T(8,128)(2,1)S(1)} %combine.2.refs_0_), channel_id=1, source_target_pairs={{0,6},{1,25},{2,0},{3,27},{4,2},{5,29},{6,4},{7,31},{8,14},{9,1},{... | collective-permute-start | bytes 1376264 | tf_op jit(solution)/shard_map/ppermute | solution.py:43
  70.6 12.2 %collective-permute-start.16 = (bf16[256,896]{1,0:T(8,128)(2,1)S(1)}, bf16[256,896]{1,0:T(8,128)(2,1)S(1)}, u32[]{:S(2)}, u32[]{:S(2)}) collective-permute-start(bf16[256,896]{1,0:T(8,128)(2,1)S(1)} %combine.2.refs_0_), channel_id=1, source_target_pairs={{0,2},{1,9},{2,4},{3,11},{4,6},{5,13},{6,0},{7,15},{8,10},{9,17},{... | collective-permute-start | bytes 1376264 | tf_op jit(solution)/shard_map/ppermute | solution.py:43
  86.1 10.9 %collective-permute-start.21 = (bf16[64,4096]{1,0:T(8,128)(2,1)S(1)}, bf16[64,4096]{1,0:T(8,128)(2,1)S(1)}, u32[]{:S(2)}, u32[]{:S(2)}) collective-permute-start(bf16[64,4096]{1,0:T(8,128)(2,1)S(1)} %get-tuple-element.36), channel_id=1, source_target_pairs={{0,4},{1,17},{2,6},{3,19},{4,0},{5,21},{6,2},{7,23},{8,12},{9,25},... | collective-permute-start | bytes 1572872 | tf_op jit(solution)/shard_map/ppermute | solution.py:43
  87.0 15.5 %collective-permute-start.22 = (bf16[64,4096]{1,0:T(8,128)(2,1)S(1)}, bf16[64,4096]{1,0:T(8,128)(2,1)S(1)}, u32[]{:S(2)}, u32[]{:S(2)}) collective-permute-start(bf16[64,4096]{1,0:T(8,128)(2,1)S(1)} %get-tuple-element.37), channel_id=1, source_target_pairs={{0,2},{1,9},{2,4},{3,11},{4,6},{5,13},{6,0},{7,15},{8,10},{9,17},{... | collective-permute-start | bytes 1572872 | tf_op jit(solution)/shard_map/ppermute | solution.py:43
  89.5 13.0 %collective-permute-start.23 = (bf16[64,4096]{1,0:T(8,128)(2,1)S(1)}, bf16[64,4096]{1,0:T(8,128)(2,1)S(1)}, u32[]{:S(2)}, u32[]{:S(2)}) collective-permute-start(bf16[64,4096]{1,0:T(8,128)(2,1)S(1)} %get-tuple-element.38), channel_id=1, source_target_pairs={{0,6},{1,25},{2,0},{3,27},{4,2},{5,29},{6,4},{7,31},{8,14},{9,1},{... | collective-permute-start | bytes 1572872 | tf_op jit(solution)/shard_map/ppermute | solution.py:43
  92.7 15.6 %collective-permute-start.18 = (bf16[64,4096]{1,0:T(8,128)(2,1)S(1)}, bf16[64,4096]{1,0:T(8,128)(2,1)S(1)}, u32[]{:S(2)}, u32[]{:S(2)}) collective-permute-start(bf16[64,4096]{1,0:T(8,128)(2,1)S(1)} %get-tuple-element.32), channel_id=1, source_target_pairs={{0,4},{1,17},{2,6},{3,19},{4,0},{5,21},{6,2},{7,23},{8,12},{9,25},... | collective-permute-start | bytes 1572872 | tf_op jit(solution)/shard_map/ppermute | solution.py:43
  94.3 19.5 %collective-permute-start.19 = (bf16[64,4096]{1,0:T(8,128)(2,1)S(1)}, bf16[64,4096]{1,0:T(8,128)(2,1)S(1)}, u32[]{:S(2)}, u32[]{:S(2)}) collective-permute-start(bf16[64,4096]{1,0:T(8,128)(2,1)S(1)} %get-tuple-element.33), channel_id=1, source_target_pairs={{0,2},{1,9},{2,4},{3,11},{4,6},{5,13},{6,0},{7,15},{8,10},{9,17},{... | collective-permute-start | bytes 1572872 | tf_op jit(solution)/shard_map/ppermute | solution.py:43
  97.0 16.8 %collective-permute-start.20 = (bf16[64,4096]{1,0:T(8,128)(2,1)S(1)}, bf16[64,4096]{1,0:T(8,128)(2,1)S(1)}, u32[]{:S(2)}, u32[]{:S(2)}) collective-permute-start(bf16[64,4096]{1,0:T(8,128)(2,1)S(1)} %get-tuple-element.34), channel_id=1, source_target_pairs={{0,6},{1,25},{2,0},{3,27},{4,2},{5,29},{6,4},{7,31},{8,14},{9,1},{... | collective-permute-start | bytes 1572872 | tf_op jit(solution)/shard_map/ppermute | solution.py:43
  114.2 8.1 %collective-permute-start.24 = (bf16[16,8192]{1,0:T(8,128)(2,1)S(1)}, bf16[16,8192]{1,0:T(8,128)(2,1)S(1)}, u32[]{:S(2)}, u32[]{:S(2)}) collective-permute-start(bf16[16,8192]{1,0:T(8,128)(2,1)S(1)} %get-tuple-element.40), channel_id=1, source_target_pairs={{0,16},{1,5},{2,18},{3,7},{4,20},{5,1},{6,22},{7,3},{8,24},{9,13},... | collective-permute-start | bytes 786440 | tf_op jit(solution)/shard_map/ppermute | solution.py:43
  116.3 8.7 %collective-permute-start.25 = (bf16[16,8192]{1,0:T(8,128)(2,1)S(1)}, bf16[16,8192]{1,0:T(8,128)(2,1)S(1)}, u32[]{:S(2)}, u32[]{:S(2)}) collective-permute-start(bf16[16,8192]{1,0:T(8,128)(2,1)S(1)} %get-tuple-element.41), channel_id=1, source_target_pairs={{0,8},{1,3},{2,10},{3,5},{4,12},{5,7},{6,14},{7,1},{8,16},{9,11},{... | collective-permute-start | bytes 786440 | tf_op jit(solution)/shard_map/ppermute | solution.py:43
  116.9 8.1 %collective-permute-start.26 = (bf16[16,8192]{1,0:T(8,128)(2,1)S(1)}, bf16[16,8192]{1,0:T(8,128)(2,1)S(1)}, u32[]{:S(2)}, u32[]{:S(2)}) collective-permute-start(bf16[16,8192]{1,0:T(8,128)(2,1)S(1)} %get-tuple-element.42), channel_id=1, source_target_pairs={{0,24},{1,7},{2,26},{3,1},{4,28},{5,3},{6,30},{7,5},{8,0},{9,15},{... | collective-permute-start | bytes 786440 | tf_op jit(solution)/shard_map/ppermute | solution.py:43

commit v8 on v7

--- a/solution.py
+++ b/solution.py
@@ -9,7 +9,8 @@
 from jax.sharding import PartitionSpec as P
 
 RING = 4
-ORDER = (0, 2, 1, 3)
+TOKEN_ORDER = (0, 2, 1, 3)
+ORDER = (0, 1, 3, 2)
 PLACES = [(x, y, c) for x in range(RING) for y in range(RING) for c in range(2)]
 GATHER_SPANS = (1, 1)
 OUT_SPANS = (1, 1)
@@ -43,8 +44,8 @@
     return lax.ppermute(value, "tensor", pairs)
 
 
-def from_steps(value, along):
-    return send(value, along(2)), send(value, along(-1)), send(value, along(1))
+def from_steps(value, along, order):
+    return [send(value, along({1: -1, 2: 2, 3: 1}[step])) for step in order[1:]]
 
 
 def after(value, *others):
@@ -134,7 +135,7 @@
     def kernel(*refs):
         ins, outs = refs[: len(parts)], refs[len(parts) :]
         for (at, span), out in zip(cuts, outs):
-            for n, part in zip(ORDER, ins):
+            for n, part in zip(TOKEN_ORDER, ins):
                 out[n * rows : (n + 1) * rows] = part[:, at : at + span]
 
     return call(
@@ -145,6 +146,11 @@
         parts,
         [jax.ShapeDtypeStruct((rows * len(parts), span), jnp.bfloat16) for _, span in cuts],
     )
+
+
+def local(gate, up, mixing):
+    hidden = (gate / (1.0 + jnp.exp(-gate)) * up).astype(jnp.bfloat16)
+    return dot(hidden, mixing[...])
 
 
 def gate_up(pieces, close, weights, at, span, sums, finish):
@@ -186,6 +192,8 @@
                 x[...], near[n][...], BY_ROWS, preferred_element_type=jnp.float32
             )
             total[n] = product if opening else before[n] + product
+        if closing and count == 2:
+            own = local(total[0], total[1], mixing)
         for step in range(steps):
             here = x[:, step * block : (step + 1) * block]
             for n in range(4 - count):
@@ -198,12 +206,9 @@
                 else:
                     total[count + n] = product if opening else before[count + n] + product
         if closing:
-            local = []
-            for n in (0, 2):
-                gate, up = total[n], total[n + 1]
-                hidden = (gate / (1.0 + jnp.exp(-gate)) * up).astype(jnp.bfloat16)
-                local.append(dot(hidden, mixing[...]))
-            own, other = local
+            if count != 2:
+                own = local(total[0], total[1], mixing)
+            other = local(total[2], total[3], mixing)
             turn = scalars[0]
             out[:, :units] = (other + turn * own).astype(jnp.bfloat16)
             out[:, units:] = (own - turn * other).astype(jnp.bfloat16)
@@ -233,29 +238,46 @@
         operands,
         [out],
         specs,
-        LIMIT,
+        LIMIT if opening else SMALL,
         scratch_shapes=scratch,
     )[0]
 
 
+def turn_rows(came, factors, first_scalar, major, out):
+    slot = out.shape[0] // (RING * RING)
+    for i in range(RING):
+        for j in range(RING):
+            total = 0.0
+            for s in range(RING):
+                where = ((i - s) % RING, j) if major else (i, (j - s) % RING)
+                at = (where[0] * RING + where[1]) * slot
+                total = total + factors[first_scalar + s] * came[s][at : at + slot].astype(
+                    jnp.float32
+                )
+            at = (i * RING + j) * slot
+            out[at : at + slot] = total.astype(jnp.bfloat16)
+
+
+def down_rows(held, loaded, loaded_other, at, span, outs):
+    units = loaded.shape[0]
+    group = held.shape[0] // RING
+    block = min(span, 512)
+    for start in range(0, span, block):
+        where = slice(at + start, at + start + block)
+        product = dot(held[:, :units], loaded[:, where]) + dot(
+            held[:, units:], loaded_other[:, where]
+        )
+        product = product.astype(jnp.bfloat16)
+        for n, out in enumerate(outs):
+            out[:, start : start + block] = product[n * group : (n + 1) * group]
+
+
 def combine(parts, scalars, first_scalar, major):
     rows, width = parts[0].shape
-    slot = rows // (RING * RING)
 
     def kernel(*refs):
         came = dict(zip(ORDER, refs[:RING]))
-        factors, out = refs[RING], refs[RING + 1]
-        for i in range(RING):
-            for j in range(RING):
-                total = 0.0
-                for s in range(RING):
-                    where = ((i - s) % RING, j) if major else (i, (j - s) % RING)
-                    at = (where[0] * RING + where[1]) * slot
-                    total = total + factors[first_scalar + s] * came[s][at : at + slot].astype(
-                        jnp.float32
-                    )
-                at = (i * RING + j) * slot
-                out[at : at + slot] = total.astype(jnp.bfloat16)
+        turn_rows(came, refs[RING], first_scalar, major, refs[RING + 1])
 
     return call(
         kernel,
@@ -268,28 +290,41 @@
     )[0]
 
 
+def combine_down(parts, scalars, first_scalar, major, weights, at, span):
+    rows, width = parts[0].shape
+
+    def kernel(*refs):
+        came = dict(zip(ORDER, refs[:RING]))
+        factors, loaded, loaded_other, value, *outs = refs[RING:]
+        turn_rows(came, factors, first_scalar, major, value)
+        down_rows(value, loaded, loaded_other, at, span, outs)
+
+    value, *outs = call(
+        kernel,
+        "combine_down",
+        2 * rows * width * span,
+        2 * width * span,
+        [*parts, scalars, *weights],
+        [jax.ShapeDtypeStruct((rows, width), jnp.bfloat16)]
+        + [jax.ShapeDtypeStruct((rows // RING, span), jnp.bfloat16)] * RING,
+        [VMEM] * RING + [SCALARS] + [VMEM] * 2,
+    )
+    return value, outs
+
+
 def down(value, weights, at, span):
-    rows, units = value.shape[0], weights[0].shape[0]
-    group = rows // RING
-    block = min(span, 512)
+    rows, width = value.shape
 
     def kernel(held, loaded, loaded_other, *outs):
-        for start in range(0, span, block):
-            where = slice(at + start, at + start + block)
-            product = dot(held[:, :units], loaded[:, where]) + dot(
-                held[:, units:], loaded_other[:, where]
-            )
-            product = product.astype(jnp.bfloat16)
-            for n, out in enumerate(outs):
-                out[:, start : start + block] = product[n * group : (n + 1) * group]
+        down_rows(held, loaded, loaded_other, at, span, outs)
 
     return call(
         kernel,
         "down",
-        4 * rows * units * span,
-        4 * units * span,
+        2 * rows * width * span,
+        2 * width * span,
         [value, *weights],
-        [jax.ShapeDtypeStruct((group, span), jnp.bfloat16)] * RING,
+        [jax.ShapeDtypeStruct((rows // RING, span), jnp.bfloat16)] * RING,
     )
 
 
@@ -334,12 +369,13 @@
     cuts = cuts_of(GATHER_SPANS, width)
     others = send(gate, SIBLING), send(up, SIBLING)
 
-    near = from_steps(tokens, along_first)
+    near = from_steps(tokens, along_first, TOKEN_ORDER)
     (own,) = load((tokens,), 0, width)
+    own = after(own, scalars)
     blocks = stack((own, *near), cuts)
     value = None
     for n, (at, span) in enumerate(cuts):
-        pieces = (blocks[n], *from_steps(blocks[n], along_second))
+        pieces = (blocks[n], *from_steps(blocks[n], along_second, ORDER))
         finish = (mixing, scalars) if n == len(cuts) - 1 else None
         if n == 0:
             value = gate_up(pieces, (), (gate, up, *others), at, span, value, finish)
@@ -347,16 +383,15 @@
             close = load((after(gate, value), up), at, span)
             value = gate_up(pieces, close, others, at, span, value, finish)
 
-    down_other = send(after(down_weight, value), SIBLING)
-    (down_own,) = load((down_weight,), 0, width)
-    value = combine((value, *from_steps(value, along_first)), scalars, 1, False)
-    value = after(value, down_own)
-    value = combine((value, *from_steps(value, along_second)), scalars, 1 + RING, True)
-
-    sides = [
-        to_steps(down(value, (down_own, down_other), at, span), along_second)
-        for at, span in cuts_of(OUT_SPANS, width)
-    ]
+    down_own = after(down_weight, value)
+    down_other = send(down_own, SIBLING)
+    value = combine((value, *from_steps(value, along_first, ORDER)), scalars, 1, False)
+    left, right = cuts_of(OUT_SPANS, width)
+    weights = (down_own, down_other)
+    parts = (value, *from_steps(value, along_second, ORDER))
+    value, partial = combine_down(parts, scalars, 1 + RING, True, weights, *left)
+    sides = [to_steps(partial, along_second)]
+    sides.append(to_steps(down(value, weights, *right), along_second))
     parts = to_steps(fold(sides), along_first)
     return sum(part.astype(jnp.float32) for part in parts).astype(jnp.bfloat16)
 

time: 126 us -> 123 us (0.976)
  Pallas kernels: 29.6 us -> 25.6 us
  starting transfers between devices: 38.5 us -> 41.7 us
  waiting for transfers between devices: 55.9 us -> 54.3 us
    ppermute x27, starting transfers between devices: 38.5 us -> 41.7 us  [send(): return lax.ppermute(value, 'tensor', pairs)]
    pallas_call x3 -> x2, Pallas kernels: 7.4 us -> 4.31 us  [load(): pl.pallas_call(kernel, name='load', compiler_params=pltpu.CompilerParams(...]
    ppermute x27, waiting for transfers between devices: 55.9 us -> 54.3 us  [send(): return lax.ppermute(value, 'tensor', pairs)]
    pallas_call x8 -> x7, Pallas kernels: 22.2 us -> 21.3 us  [call(): pl.pallas_call(kernel, name=name, compiler_params=pltpu.CompilerParams(vm...]
  transfers between devices with their start and end apart: 27 -> 27, of which waited for: 16 -> 15; matrix products, arithmetic and copies ran while one was open for 1% -> 1% of each run, Pallas kernels for 15% -> 12%
where the time goes in v8:
time: 123 us
  waiting for transfers between devices  54.3 us (44%)
  starting transfers between devices  41.7 us (34%)
  Pallas kernels  25.6 us (21%)
    ppermute x27, waiting for transfers between devices, send(): return lax.ppermute(value, 'tensor', pairs)  54.3 us
    ppermute x27, starting transfers between devices, send(): return lax.ppermute(value, 'tensor', pairs)  41.7 us
    pallas_call x7, Pallas kernels, call(): pl.pallas_call(kernel, name=name, compiler_params=pltpu.CompilerParams(vm...  21.3 us
    pallas_call x2, Pallas kernels, load(): pl.pallas_call(kernel, name='load', compiler_params=pltpu.CompilerParams(...  4.31 us
  transfers between devices with their start and end apart: 27, of which 15 were waited for; matrix products, arithmetic and copies ran while one was open for 1% of the time, Pallas kernels for 12%

profile of v8, /device:TPU:0, one launch (start us, length us, event | category | flops | bytes accessed | tf_op | source)
XLA Modules:
  0.0 123.3 jit_solution(4352252512417070592)
XLA Ops:
  0.0 0.0 collective-permute-start.9
  0.0 0.5 collective-permute-start.10
  0.5 3.1 %collective-permute-start = (bf16[16,8192]{1,0:T(8,128)(2,1)}, bf16[16,8192]{1,0:T(8,128)(2,1)S(1)}, u32[]{:S(2)}, u32[]{:S(2)}) collective-permute-start(bf16[16,8192]{1,0:T(8,128)(2,1)} %refs_0_.1), channel_id=1, source_target_pairs={{0,16},{1,5},{2,18},{3,7},{4,20},{5,1},{6,22},{7,3},{8,24},{9,13},... | collective-permute-start | bytes 786440 | tf_op jit(solution)/shard_map/ppermute | solution.py:44
  3.6 0.6 collective-permute-start.2
  4.2 2.6 %collective-permute-start.1 = (bf16[16,8192]{1,0:T(8,128)(2,1)}, bf16[16,8192]{1,0:T(8,128)(2,1)S(1)}, u32[]{:S(2)}, u32[]{:S(2)}) collective-permute-start(bf16[16,8192]{1,0:T(8,128)(2,1)} %refs_0_.1), channel_id=1, source_target_pairs={{0,24},{1,7},{2,26},{3,1},{4,28},{5,3},{6,30},{7,5},{8,0},{9,15},{... | collective-permute-start | bytes 786440 | tf_op jit(solution)/shard_map/ppermute | solution.py:44
  6.9 1.0 load.2.refs_0_
  7.9 0.7 dynamic-slice_bitcast_fusion.refs_10_.refs_4_
  8.6 0.0 collective-permute-done.refs_1_
  8.6 2.8 %collective-permute-done.2.refs_3_ = bf16[16,8192]{1,0:T(8,128)(2,1)S(1)} collective-permute-done((bf16[16,8192]{1,0:T(8,128)(2,1)}, bf16[16,8192]{1,0:T(8,128)(2,1)S(1)}, u32[]{:S(2)}, u32[]{:S(2)}) %collective-permute-start.2) | collective-permute-done | bytes 262176 | tf_op jit(solution)/shard_map/ppermute | solution.py:44
  11.4 0.2 collective-permute-done.1.refs_2_
  11.6 0.1 stack.1
  11.6 3.3 %collective-permute-start.8 = (bf16[64,4096]{1,0:T(8,128)(2,1)S(1)}, bf16[64,4096]{1,0:T(8,128)(2,1)S(1)}, u32[]{:S(2)}, u32[]{:S(2)}) collective-permute-start(bf16[64,4096]{1,0:T(8,128)(2,1)S(1)} %get-tuple-element.27.refs_0_), channel_id=1, source_target_pairs={{0,4},{1,17},{2,6},{3,19},{4,0},{5,21},{6,2},{7,23},{8,12},{9,25},... | collective-permute-start | bytes 1572872 | tf_op jit(solution)/shard_map/ppermute | solution.py:44
  14.9 0.7 collective-permute-start.7
  15.6 2.6 %collective-permute-start.6 = (bf16[64,4096]{1,0:T(8,128)(2,1)S(1)}, bf16[64,4096]{1,0:T(8,128)(2,1)S(1)}, u32[]{:S(2)}, u32[]{:S(2)}) collective-permute-start(bf16[64,4096]{1,0:T(8,128)(2,1)S(1)} %get-tuple-element.27.refs_0_), channel_id=1, source_target_pairs={{0,6},{1,25},{2,0},{3,27},{4,2},{5,29},{6,4},{7,31},{8,14},{9,1},{... | collective-permute-start | bytes 1572872 | tf_op jit(solution)/shard_map/ppermute | solution.py:44
  18.2 4.4 %collective-permute-done.8.refs_3_ = bf16[64,4096]{1,0:T(8,128)(2,1)S(1)} collective-permute-done((bf16[64,4096]{1,0:T(8,128)(2,1)S(1)}, bf16[64,4096]{1,0:T(8,128)(2,1)S(1)}, u32[]{:S(2)}, u32[]{:S(2)}) %collective-permute-start.8) | collective-permute-done | bytes 524320 | tf_op jit(solution)/shard_map/ppermute | solution.py:44
  22.5 3.2 %collective-permute-start.5 = (bf16[64,4096]{1,0:T(8,128)(2,1)S(1)}, bf16[64,4096]{1,0:T(8,128)(2,1)S(1)}, u32[]{:S(2)}, u32[]{:S(2)}) collective-permute-start(bf16[64,4096]{1,0:T(8,128)(2,1)S(1)} %get-tuple-element.26.refs_0_), channel_id=1, source_target_pairs={{0,4},{1,17},{2,6},{3,19},{4,0},{5,21},{6,2},{7,23},{8,12},{9,25},... | collective-permute-start | bytes 1572872 | tf_op jit(solution)/shard_map/ppermute | solution.py:44
  25.7 2.3 %collective-permute-done.7.refs_2_ = bf16[64,4096]{1,0:T(8,128)(2,1)S(1)} collective-permute-done((bf16[64,4096]{1,0:T(8,128)(2,1)S(1)}, bf16[64,4096]{1,0:T(8,128)(2,1)S(1)}, u32[]{:S(2)}, u32[]{:S(2)}) %collective-permute-start.7) | collective-permute-done | bytes 524320 | tf_op jit(solution)/shard_map/ppermute | solution.py:44
  28.0 1.7 %collective-permute-start.4 = (bf16[64,4096]{1,0:T(8,128)(2,1)S(1)}, bf16[64,4096]{1,0:T(8,128)(2,1)S(1)}, u32[]{:S(2)}, u32[]{:S(2)}) collective-permute-start(bf16[64,4096]{1,0:T(8,128)(2,1)S(1)} %get-tuple-element.26.refs_0_), channel_id=1, source_target_pairs={{0,2},{1,9},{2,4},{3,11},{4,6},{5,13},{6,0},{7,15},{8,10},{9,17},{... | collective-permute-start | bytes 1572872 | tf_op jit(solution)/shard_map/ppermute | solution.py:44
  29.8 0.0 collective-permute-done.6.refs_1_
  29.8 1.5 %collective-permute-start.3 = (bf16[64,4096]{1,0:T(8,128)(2,1)S(1)}, bf16[64,4096]{1,0:T(8,128)(2,1)S(1)}, u32[]{:S(2)}, u32[]{:S(2)}) collective-permute-start(bf16[64,4096]{1,0:T(8,128)(2,1)S(1)} %get-tuple-element.26.refs_0_), channel_id=1, source_target_pairs={{0,6},{1,25},{2,0},{3,27},{4,2},{5,29},{6,4},{7,31},{8,14},{9,1},{... | collective-permute-start | bytes 1572872 | tf_op jit(solution)/shard_map/ppermute | solution.py:44
  31.3 0.0 collective-permute-done.9.refs_6_
  31.3 0.0 collective-permute-done.10.refs_7_
  31.3 7.4 %gate_up.2.refs_8_ = f32[4,256,448]{2,1,0:T(8,128)S(1)} custom-call(bf16[64,4096]{1,0:T(8,128)(2,1)S(1)} %get-tuple-element.27.refs_0_, bf16[64,4096]{1,0:T(8,128)(2,1)S(1)} %collective-permute-done.6.refs_1_, bf16[64,4096]{1,0:T(8,128)(2,1)S(1)} %collective-permute-done.7.refs_2_, bf16[64,4096]{1,0:T(8,128)(2,1)S(1)} %collective-permute-done.8.refs_3_, ...), custom_call_target="tpu_custom_call" | custom-call | flops 3758096384 | bytes 14680064 | tf_op jit(solution)/shard_map/gate_up/pallas_call | solution.py:86
  38.7 0.0 copy-start
  38.7 0.0 slice-start
  38.8 3.3 %load.3 = (bf16[448,4096]{1,0:T(8,128)(2,1)S(1)}, bf16[448,4096]{1,0:T(8,128)(2,1)S(1)}) custom-call(bf16[448,8192]{1,0:T(8,128)(2,1)} %bitcast.8, bf16[448,8192]{1,0:T(8,128)(2,1)} %bitcast.11), custom_call_target="tpu_custom_call" | custom-call | bytes 14680064 | tf_op jit(solution)/shard_map/load/pallas_call | solution.py:116
  42.1 0.0 collective-permute-done.5.refs_3_
  42.1 0.0 collective-permute-done.3.refs_1_
  42.1 0.0 slice-start.1
  42.1 6.8 %gate_up.3.refs_0_ = bf16[256,896]{1,0:T(8,128)(2,1)S(1)} custom-call(bf16[64,4096]{1,0:T(8,128)(2,1)S(1)} %get-tuple-element.26.refs_0_, bf16[64,4096]{1,0:T(8,128)(2,1)S(1)} %collective-permute-done.3.refs_1_, bf16[64,4096]{1,0:T(8,128)(2,1)S(1)} %collective-permute-done.4.refs_2_, bf16[64,4096]{1,0:T(8,128)(2,1)S(1)} %collective-permute-done.5.refs_3_, ...), custom_call_target="tpu_custom_call" | custom-call | flops 3758096384 | bytes 14680064 | tf_op jit(solution)/shard_map/gate_up/pallas_call | solution.py:86
  49.0 0.1 collective-permute-start.17
  49.1 2.2 %collective-permute-start.13 = (bf16[256,896]{1,0:T(8,128)(2,1)S(1)}, bf16[256,896]{1,0:T(8,128)(2,1)S(1)}, u32[]{:S(2)}, u32[]{:S(2)}) collective-permute-start(bf16[256,896]{1,0:T(8,128)(2,1)S(1)} %gate_up.3.refs_0_), channel_id=1, source_target_pairs={{0,16},{1,5},{2,18},{3,7},{4,20},{5,1},{6,22},{7,3},{8,24},{9,13},... | collective-permute-start | bytes 1376264 | tf_op jit(solution)/shard_map/ppermute | solution.py:44
  51.3 1.8 %collective-permute-start.12 = (bf16[256,896]{1,0:T(8,128)(2,1)S(1)}, bf16[256,896]{1,0:T(8,128)(2,1)S(1)}, u32[]{:S(2)}, u32[]{:S(2)}) collective-permute-start(bf16[256,896]{1,0:T(8,128)(2,1)S(1)} %gate_up.3.refs_0_), channel_id=1, source_target_pairs={{0,8},{1,3},{2,10},{3,5},{4,12},{5,7},{6,14},{7,1},{8,16},{9,11},{... | collective-permute-start | bytes 1376264 | tf_op jit(solution)/shard_map/ppermute | solution.py:44
  53.1 1.4 %collective-permute-start.11 = (bf16[256,896]{1,0:T(8,128)(2,1)S(1)}, bf16[256,896]{1,0:T(8,128)(2,1)S(1)}, u32[]{:S(2)}, u32[]{:S(2)}) collective-permute-start(bf16[256,896]{1,0:T(8,128)(2,1)S(1)} %gate_up.3.refs_0_), channel_id=1, source_target_pairs={{0,24},{1,7},{2,26},{3,1},{4,28},{5,3},{6,30},{7,5},{8,0},{9,15},{... | collective-permute-start | bytes 1376264 | tf_op jit(solution)/shard_map/ppermute | solution.py:44
  54.5 4.8 %collective-permute-done.13.refs_3_ = bf16[256,896]{1,0:T(8,128)(2,1)S(1)} collective-permute-done((bf16[256,896]{1,0:T(8,128)(2,1)S(1)}, bf16[256,896]{1,0:T(8,128)(2,1)S(1)}, u32[]{:S(2)}, u32[]{:S(2)}) %collective-permute-start.13) | collective-permute-done | bytes 458784 | tf_op jit(solution)/shard_map/ppermute | solution.py:44
  59.3 4.8 %collective-permute-done.12.refs_2_ = bf16[256,896]{1,0:T(8,128)(2,1)S(1)} collective-permute-done((bf16[256,896]{1,0:T(8,128)(2,1)S(1)}, bf16[256,896]{1,0:T(8,128)(2,1)S(1)}, u32[]{:S(2)}, u32[]{:S(2)}) %collective-permute-start.12) | collective-permute-done | bytes 458784 | tf_op jit(solution)/shard_map/ppermute | solution.py:44
  64.1 0.4 collective-permute-done.11.refs_1_
  64.5 0.9 combine.1.refs_0_
  65.4 1.3 %collective-permute-start.16 = (bf16[256,896]{1,0:T(8,128)(2,1)S(1)}, bf16[256,896]{1,0:T(8,128)(2,1)S(1)}, u32[]{:S(2)}, u32[]{:S(2)}) collective-permute-start(bf16[256,896]{1,0:T(8,128)(2,1)S(1)} %combine.1.refs_0_), channel_id=1, source_target_pairs={{0,4},{1,17},{2,6},{3,19},{4,0},{5,21},{6,2},{7,23},{8,12},{9,25},... | collective-permute-start | bytes 1376264 | tf_op jit(solution)/shard_map/ppermute | solution.py:44
  66.7 0.0 collective-permute-start.15
  66.7 3.2 %collective-permute-start.14 = (bf16[256,896]{1,0:T(8,128)(2,1)S(1)}, bf16[256,896]{1,0:T(8,128)(2,1)S(1)}, u32[]{:S(2)}, u32[]{:S(2)}) collective-permute-start(bf16[256,896]{1,0:T(8,128)(2,1)S(1)} %combine.1.refs_0_), channel_id=1, source_target_pairs={{0,6},{1,25},{2,0},{3,27},{4,2},{5,29},{6,4},{7,31},{8,14},{9,1},{... | collective-permute-start | bytes 1376264 | tf_op jit(solution)/shard_map/ppermute | solution.py:44
  69.9 5.6 %collective-permute-done.16.refs_3_ = bf16[256,896]{1,0:T(8,128)(2,1)S(1)} collective-permute-done((bf16[256,896]{1,0:T(8,128)(2,1)S(1)}, bf16[256,896]{1,0:T(8,128)(2,1)S(1)}, u32[]{:S(2)}, u32[]{:S(2)}) %collective-permute-start.16) | collective-permute-done | bytes 458784 | tf_op jit(solution)/shard_map/ppermute | solution.py:44
  75.6 4.8 %collective-permute-done.15.refs_2_ = bf16[256,896]{1,0:T(8,128)(2,1)S(1)} collective-permute-done((bf16[256,896]{1,0:T(8,128)(2,1)S(1)}, bf16[256,896]{1,0:T(8,128)(2,1)S(1)}, u32[]{:S(2)}, u32[]{:S(2)}) %collective-permute-start.15) | collective-permute-done | bytes 458784 | tf_op jit(solution)/shard_map/ppermute | solution.py:44
  80.4 0.0 collective-permute-done.14.refs_1_
  80.4 3.2 %combine_down.1 = (bf16[256,896]{1,0:T(8,128)(2,1)S(1)}, bf16[64,4096]{1,0:T(8,128)(2,1)S(1)}, bf16[64,4096]{1,0:T(8,128)(2,1)S(1)}, bf16[64,4096]{1,0:T(8,128)(2,1)S(1)}, bf16[64,4096]{1,0:T(8,128)(2,1)S(1)}) custom-call(bf16[256,896]{1,0:T(8,128)(2,1)S(1)} %combine.1.refs_0_, bf16[256,896]{1,0:T(8,128)(2,1)S(1)} %collective-permute-done.14.refs_1_, ...), custom_call_target="tpu_custom_call" | custom-call | flops 1879048192 | bytes 7340032 | tf_op jit(solution)/shard_map/combine_down/pallas_call | solution.py:86
  83.6 1.3 %collective-permute-start.18 = (bf16[64,4096]{1,0:T(8,128)(2,1)S(1)}, bf16[64,4096]{1,0:T(8,128)(2,1)S(1)}, u32[]{:S(2)}, u32[]{:S(2)}) collective-permute-start(bf16[64,4096]{1,0:T(8,128)(2,1)S(1)} %get-tuple-element.33), channel_id=1, source_target_pairs={{0,4},{1,17},{2,6},{3,19},{4,0},{5,21},{6,2},{7,23},{8,12},{9,25},... | collective-permute-start | bytes 1572872 | tf_op jit(solution)/shard_map/ppermute | solution.py:44
  84.9 0.3 collective-permute-start.19
  85.1 3.0 %collective-permute-start.20 = (bf16[64,4096]{1,0:T(8,128)(2,1)S(1)}, bf16[64,4096]{1,0:T(8,128)(2,1)S(1)}, u32[]{:S(2)}, u32[]{:S(2)}) collective-permute-start(bf16[64,4096]{1,0:T(8,128)(2,1)S(1)} %get-tuple-element.35), channel_id=1, source_target_pairs={{0,6},{1,25},{2,0},{3,27},{4,2},{5,29},{6,4},{7,31},{8,14},{9,1},{... | collective-permute-start | bytes 1572872 | tf_op jit(solution)/shard_map/ppermute | solution.py:44
  88.1 2.4 %down.1 = (bf16[64,4096]{1,0:T(8,128)(2,1)S(1)}, bf16[64,4096]{1,0:T(8,128)(2,1)S(1)}, bf16[64,4096]{1,0:T(8,128)(2,1)S(1)}, bf16[64,4096]{1,0:T(8,128)(2,1)S(1)}) custom-call(bf16[256,896]{1,0:T(8,128)(2,1)S(1)} %get-tuple-element.36.held, bf16[448,8192]{1,0:T(8,128)(2,1)S(1)} %bitcast.5, bf16[448,8192]{1,0:T(8,128)(2,1)S(1)} %collective-permute-done.17.refs_6_.loaded_other), custom_call_target="tpu_custom_call" | custom-call | flops 1879048192 | bytes 7340032 | tf_op jit(solution)/shard_map/down/pallas_call | solution.py:86
  90.5 1.2 collective-permute-start.21
  91.7 0.5 collective-permute-start.22
  92.2 2.3 %collective-permute-done.18.refs_1_ = bf16[64,4096]{1,0:T(8,128)(2,1)S(1)} collective-permute-done((bf16[64,4096]{1,0:T(8,128)(2,1)S(1)}, bf16[64,4096]{1,0:T(8,128)(2,1)S(1)}, u32[]{:S(2)}, u32[]{:S(2)}) %collective-permute-start.18) | collective-permute-done | bytes 524320 | tf_op jit(solution)/shard_map/ppermute | solution.py:44
  94.4 0.6 collective-permute-start.23
  95.0 4.9 %collective-permute-done.19.refs_2_ = bf16[64,4096]{1,0:T(8,128)(2,1)S(1)} collective-permute-done((bf16[64,4096]{1,0:T(8,128)(2,1)S(1)}, bf16[64,4096]{1,0:T(8,128)(2,1)S(1)}, u32[]{:S(2)}, u32[]{:S(2)}) %collective-permute-start.19) | collective-permute-done | bytes 524320 | tf_op jit(solution)/shard_map/ppermute | solution.py:44
  100.0 5.8 %collective-permute-done.21.refs_5_ = bf16[64,4096]{1,0:T(8,128)(2,1)S(1)} collective-permute-done((bf16[64,4096]{1,0:T(8,128)(2,1)S(1)}, bf16[64,4096]{1,0:T(8,128)(2,1)S(1)}, u32[]{:S(2)}, u32[]{:S(2)}) %collective-permute-start.21) | collective-permute-done | bytes 524320 | tf_op jit(solution)/shard_map/ppermute | solution.py:44
  105.7 5.5 %collective-permute-done.22.refs_6_ = bf16[64,4096]{1,0:T(8,128)(2,1)S(1)} collective-permute-done((bf16[64,4096]{1,0:T(8,128)(2,1)S(1)}, bf16[64,4096]{1,0:T(8,128)(2,1)S(1)}, u32[]{:S(2)}, u32[]{:S(2)}) %collective-permute-start.22) | collective-permute-done | bytes 524320 | tf_op jit(solution)/shard_map/ppermute | solution.py:44
  111.2 0.5 fold.1
  111.7 1.8 %collective-permute-start.24 = (bf16[16,8192]{1,0:T(8,128)(2,1)S(1)}, bf16[16,8192]{1,0:T(8,128)(2,1)S(1)}, u32[]{:S(2)}, u32[]{:S(2)}) collective-permute-start(bf16[16,8192]{1,0:T(8,128)(2,1)S(1)} %get-tuple-element.42), channel_id=1, source_target_pairs={{0,16},{1,5},{2,18},{3,7},{4,20},{5,1},{6,22},{7,3},{8,24},{9,13},... | collective-permute-start | bytes 786440 | tf_op jit(solution)/shard_map/ppermute | solution.py:44
  113.5 1.8 %collective-permute-start.25 = (bf16[16,8192]{1,0:T(8,128)(2,1)S(1)}, bf16[16,8192]{1,0:T(8,128)(2,1)S(1)}, u32[]{:S(2)}, u32[]{:S(2)}) collective-permute-start(bf16[16,8192]{1,0:T(8,128)(2,1)S(1)} %get-tuple-element.43), channel_id=1, source_target_pairs={{0,8},{1,3},{2,10},{3,5},{4,12},{5,7},{6,14},{7,1},{8,16},{9,11},{... | collective-permute-start | bytes 786440 | tf_op jit(solution)/shard_map/ppermute | solution.py:44
  115.3 1.4 %collective-permute-start.26 = (bf16[16,8192]{1,0:T(8,128)(2,1)S(1)}, bf16[16,8192]{1,0:T(8,128)(2,1)S(1)}, u32[]{:S(2)}, u32[]{:S(2)}) collective-permute-start(bf16[16,8192]{1,0:T(8,128)(2,1)S(1)} %get-tuple-element.44), channel_id=1, source_target_pairs={{0,24},{1,7},{2,26},{3,1},{4,28},{5,3},{6,30},{7,5},{8,0},{9,15},{... | collective-permute-start | bytes 786440 | tf_op jit(solution)/shard_map/ppermute | solution.py:44
  116.7 3.1 %collective-permute-done.24 = bf16[16,8192]{1,0:T(8,128)(2,1)S(1)} collective-permute-done((bf16[16,8192]{1,0:T(8,128)(2,1)S(1)}, bf16[16,8192]{1,0:T(8,128)(2,1)S(1)}, u32[]{:S(2)}, u32[]{:S(2)}) %collective-permute-start.24) | collective-permute-done | bytes 262176 | tf_op jit(solution)/shard_map/ppermute | solution.py:44
  119.8 2.7 %collective-permute-done.25 = bf16[16,8192]{1,0:T(8,128)(2,1)S(1)} collective-permute-done((bf16[16,8192]{1,0:T(8,128)(2,1)S(1)}, bf16[16,8192]{1,0:T(8,128)(2,1)S(1)}, u32[]{:S(2)}, u32[]{:S(2)}) %collective-permute-start.25) | collective-permute-done | bytes 262176 | tf_op jit(solution)/shard_map/ppermute | solution.py:44
  122.5 0.0 collective-permute-done.26
  122.5 0.8 add_convert_fusion
  (8 shorter events, 0.0 us)
Async XLA Ops:
  0.0 31.3 %collective-permute-start.9 = (bf16[448,8192]{1,0:T(8,128)(2,1)}, bf16[448,8192]{1,0:T(8,128)(2,1)}, u32[]{:S(2)}, u32[]{:S(2)}) collective-permute-start(bf16[448,8192]{1,0:T(8,128)(2,1)} %bitcast.6), channel_id=1, source_target_pairs={{0,1},{1,0},{2,3},{3,2},{4,5},{5,4},{6,7},{7,6},{8,9},{9,8},{10,11... | collective-permute-start | bytes 22020104 | tf_op jit(solution)/shard_map/ppermute | solution.py:44
  0.0 31.3 %collective-permute-start.10 = (bf16[448,8192]{1,0:T(8,128)(2,1)}, bf16[448,8192]{1,0:T(8,128)(2,1)}, u32[]{:S(2)}, u32[]{:S(2)}) collective-permute-start(bf16[448,8192]{1,0:T(8,128)(2,1)} %bitcast.9), channel_id=1, source_target_pairs={{0,1},{1,0},{2,3},{3,2},{4,5},{5,4},{6,7},{7,6},{8,9},{9,8},{10,11... | collective-permute-start | bytes 22020104 | tf_op jit(solution)/shard_map/ppermute | solution.py:44
  0.5 8.1 %collective-permute-start = (bf16[16,8192]{1,0:T(8,128)(2,1)}, bf16[16,8192]{1,0:T(8,128)(2,1)S(1)}, u32[]{:S(2)}, u32[]{:S(2)}) collective-permute-start(bf16[16,8192]{1,0:T(8,128)(2,1)} %refs_0_.1), channel_id=1, source_target_pairs={{0,16},{1,5},{2,18},{3,7},{4,20},{5,1},{6,22},{7,3},{8,24},{9,13},... | collective-permute-start | bytes 786440 | tf_op jit(solution)/shard_map/ppermute | solution.py:44
  3.6 7.8 %collective-permute-start.2 = (bf16[16,8192]{1,0:T(8,128)(2,1)}, bf16[16,8192]{1,0:T(8,128)(2,1)S(1)}, u32[]{:S(2)}, u32[]{:S(2)}) collective-permute-start(bf16[16,8192]{1,0:T(8,128)(2,1)} %refs_0_.1), channel_id=1, source_target_pairs={{0,8},{1,3},{2,10},{3,5},{4,12},{5,7},{6,14},{7,1},{8,16},{9,11},{... | collective-permute-start | bytes 786440 | tf_op jit(solution)/shard_map/ppermute | solution.py:44
  4.2 7.4 %collective-permute-start.1 = (bf16[16,8192]{1,0:T(8,128)(2,1)}, bf16[16,8192]{1,0:T(8,128)(2,1)S(1)}, u32[]{:S(2)}, u32[]{:S(2)}) collective-permute-start(bf16[16,8192]{1,0:T(8,128)(2,1)} %refs_0_.1), channel_id=1, source_target_pairs={{0,24},{1,7},{2,26},{3,1},{4,28},{5,3},{6,30},{7,5},{8,0},{9,15},{... | collective-permute-start | bytes 786440 | tf_op jit(solution)/shard_map/ppermute | solution.py:44
  11.6 10.9 %collective-permute-start.8 = (bf16[64,4096]{1,0:T(8,128)(2,1)S(1)}, bf16[64,4096]{1,0:T(8,128)(2,1)S(1)}, u32[]{:S(2)}, u32[]{:S(2)}) collective-permute-start(bf16[64,4096]{1,0:T(8,128)(2,1)S(1)} %get-tuple-element.27.refs_0_), channel_id=1, source_target_pairs={{0,4},{1,17},{2,6},{3,19},{4,0},{5,21},{6,2},{7,23},{8,12},{9,25},... | collective-permute-start | bytes 1572872 | tf_op jit(solution)/shard_map/ppermute | solution.py:44
  14.9 13.1 %collective-permute-start.7 = (bf16[64,4096]{1,0:T(8,128)(2,1)S(1)}, bf16[64,4096]{1,0:T(8,128)(2,1)S(1)}, u32[]{:S(2)}, u32[]{:S(2)}) collective-permute-start(bf16[64,4096]{1,0:T(8,128)(2,1)S(1)} %get-tuple-element.27.refs_0_), channel_id=1, source_target_pairs={{0,2},{1,9},{2,4},{3,11},{4,6},{5,13},{6,0},{7,15},{8,10},{9,17},{... | collective-permute-start | bytes 1572872 | tf_op jit(solution)/shard_map/ppermute | solution.py:44
  15.6 14.2 %collective-permute-start.6 = (bf16[64,4096]{1,0:T(8,128)(2,1)S(1)}, bf16[64,4096]{1,0:T(8,128)(2,1)S(1)}, u32[]{:S(2)}, u32[]{:S(2)}) collective-permute-start(bf16[64,4096]{1,0:T(8,128)(2,1)S(1)} %get-tuple-element.27.refs_0_), channel_id=1, source_target_pairs={{0,6},{1,25},{2,0},{3,27},{4,2},{5,29},{6,4},{7,31},{8,14},{9,1},{... | collective-permute-start | bytes 1572872 | tf_op jit(solution)/shard_map/ppermute | solution.py:44
  22.5 19.6 %collective-permute-start.5 = (bf16[64,4096]{1,0:T(8,128)(2,1)S(1)}, bf16[64,4096]{1,0:T(8,128)(2,1)S(1)}, u32[]{:S(2)}, u32[]{:S(2)}) collective-permute-start(bf16[64,4096]{1,0:T(8,128)(2,1)S(1)} %get-tuple-element.26.refs_0_), channel_id=1, source_target_pairs={{0,4},{1,17},{2,6},{3,19},{4,0},{5,21},{6,2},{7,23},{8,12},{9,25},... | collective-permute-start | bytes 1572872 | tf_op jit(solution)/shard_map/ppermute | solution.py:44
  28.0 14.1 %collective-permute-start.4 = (bf16[64,4096]{1,0:T(8,128)(2,1)S(1)}, bf16[64,4096]{1,0:T(8,128)(2,1)S(1)}, u32[]{:S(2)}, u32[]{:S(2)}) collective-permute-start(bf16[64,4096]{1,0:T(8,128)(2,1)S(1)} %get-tuple-element.26.refs_0_), channel_id=1, source_target_pairs={{0,2},{1,9},{2,4},{3,11},{4,6},{5,13},{6,0},{7,15},{8,10},{9,17},{... | collective-permute-start | bytes 1572872 | tf_op jit(solution)/shard_map/ppermute | solution.py:44
  29.8 12.3 %collective-permute-start.3 = (bf16[64,4096]{1,0:T(8,128)(2,1)S(1)}, bf16[64,4096]{1,0:T(8,128)(2,1)S(1)}, u32[]{:S(2)}, u32[]{:S(2)}) collective-permute-start(bf16[64,4096]{1,0:T(8,128)(2,1)S(1)} %get-tuple-element.26.refs_0_), channel_id=1, source_target_pairs={{0,6},{1,25},{2,0},{3,27},{4,2},{5,29},{6,4},{7,31},{8,14},{9,1},{... | collective-permute-start | bytes 1572872 | tf_op jit(solution)/shard_map/ppermute | solution.py:44
  38.7 3.4 %copy-start = (bf16[448,448]{1,0:T(8,128)(2,1)S(1)}, bf16[448,448]{1,0:T(8,128)(2,1)}, u32[]{:S(2)}) copy-start(bf16[448,448]{1,0:T(8,128)(2,1)} %refs_9_.1) | copy-start | bytes 1204228
  38.7 10.2 %slice-start = ((s8[7340032]{0:T(1024)(128)(4,1)}), s8[4194304]{0:T(1024)(128)(4,1)S(1)}, s32[]{:S(2)}) async-start(s8[7340032]{0:T(1024)(128)(4,1)} %bitcast.4), calls=%async_computation | async-start | bytes 8388608
  42.1 6.9 %slice-start.1 = ((s8[7340032]{0:T(1024)(128)(4,1)}), s8[3145728]{0:T(1024)(128)(4,1)S(1)}, s32[]{:S(2)}) async-start(s8[7340032]{0:T(1024)(128)(4,1)} %bitcast.4), calls=%async_computation.1 | async-start | bytes 6291456
  49.0 31.4 %collective-permute-start.17 = (bf16[448,8192]{1,0:T(8,128)(2,1)S(1)}, bf16[448,8192]{1,0:T(8,128)(2,1)S(1)}, u32[]{:S(2)}, u32[]{:S(2)}) collective-permute-start(bf16[448,8192]{1,0:T(8,128)(2,1)S(1)} %bitcast.5), channel_id=1, source_target_pairs={{0,1},{1,0},{2,3},{3,2},{4,5},{5,4},{6,7},{7,6},{8,9},{9,8},{10,11... | collective-permute-start | bytes 22020104 | tf_op jit(solution)/shard_map/ppermute | solution.py:44
  49.1 10.2 %collective-permute-start.13 = (bf16[256,896]{1,0:T(8,128)(2,1)S(1)}, bf16[256,896]{1,0:T(8,128)(2,1)S(1)}, u32[]{:S(2)}, u32[]{:S(2)}) collective-permute-start(bf16[256,896]{1,0:T(8,128)(2,1)S(1)} %gate_up.3.refs_0_), channel_id=1, source_target_pairs={{0,16},{1,5},{2,18},{3,7},{4,20},{5,1},{6,22},{7,3},{8,24},{9,13},... | collective-permute-start | bytes 1376264 | tf_op jit(solution)/shard_map/ppermute | solution.py:44
  51.3 12.8 %collective-permute-start.12 = (bf16[256,896]{1,0:T(8,128)(2,1)S(1)}, bf16[256,896]{1,0:T(8,128)(2,1)S(1)}, u32[]{:S(2)}, u32[]{:S(2)}) collective-permute-start(bf16[256,896]{1,0:T(8,128)(2,1)S(1)} %gate_up.3.refs_0_), channel_id=1, source_target_pairs={{0,8},{1,3},{2,10},{3,5},{4,12},{5,7},{6,14},{7,1},{8,16},{9,11},{... | collective-permute-start | bytes 1376264 | tf_op jit(solution)/shard_map/ppermute | solution.py:44
  53.1 11.4 %collective-permute-start.11 = (bf16[256,896]{1,0:T(8,128)(2,1)S(1)}, bf16[256,896]{1,0:T(8,128)(2,1)S(1)}, u32[]{:S(2)}, u32[]{:S(2)}) collective-permute-start(bf16[256,896]{1,0:T(8,128)(2,1)S(1)} %gate_up.3.refs_0_), channel_id=1, source_target_pairs={{0,24},{1,7},{2,26},{3,1},{4,28},{5,3},{6,30},{7,5},{8,0},{9,15},{... | collective-permute-start | bytes 1376264 | tf_op jit(solution)/shard_map/ppermute | solution.py:44
  65.4 10.2 %collective-permute-start.16 = (bf16[256,896]{1,0:T(8,128)(2,1)S(1)}, bf16[256,896]{1,0:T(8,128)(2,1)S(1)}, u32[]{:S(2)}, u32[]{:S(2)}) collective-permute-start(bf16[256,896]{1,0:T(8,128)(2,1)S(1)} %combine.1.refs_0_), channel_id=1, source_target_pairs={{0,4},{1,17},{2,6},{3,19},{4,0},{5,21},{6,2},{7,23},{8,12},{9,25},... | collective-permute-start | bytes 1376264 | tf_op jit(solution)/shard_map/ppermute | solution.py:44
  66.7 13.7 %collective-permute-start.15 = (bf16[256,896]{1,0:T(8,128)(2,1)S(1)}, bf16[256,896]{1,0:T(8,128)(2,1)S(1)}, u32[]{:S(2)}, u32[]{:S(2)}) collective-permute-start(bf16[256,896]{1,0:T(8,128)(2,1)S(1)} %combine.1.refs_0_), channel_id=1, source_target_pairs={{0,2},{1,9},{2,4},{3,11},{4,6},{5,13},{6,0},{7,15},{8,10},{9,17},{... | collective-permute-start | bytes 1376264 | tf_op jit(solution)/shard_map/ppermute | solution.py:44
  66.7 13.7 %collective-permute-start.14 = (bf16[256,896]{1,0:T(8,128)(2,1)S(1)}, bf16[256,896]{1,0:T(8,128)(2,1)S(1)}, u32[]{:S(2)}, u32[]{:S(2)}) collective-permute-start(bf16[256,896]{1,0:T(8,128)(2,1)S(1)} %combine.1.refs_0_), channel_id=1, source_target_pairs={{0,6},{1,25},{2,0},{3,27},{4,2},{5,29},{6,4},{7,31},{8,14},{9,1},{... | collective-permute-start | bytes 1376264 | tf_op jit(solution)/shard_map/ppermute | solution.py:44
  83.6 10.9 %collective-permute-start.18 = (bf16[64,4096]{1,0:T(8,128)(2,1)S(1)}, bf16[64,4096]{1,0:T(8,128)(2,1)S(1)}, u32[]{:S(2)}, u32[]{:S(2)}) collective-permute-start(bf16[64,4096]{1,0:T(8,128)(2,1)S(1)} %get-tuple-element.33), channel_id=1, source_target_pairs={{0,4},{1,17},{2,6},{3,19},{4,0},{5,21},{6,2},{7,23},{8,12},{9,25},... | collective-permute-start | bytes 1572872 | tf_op jit(solution)/shard_map/ppermute | solution.py:44
  84.9 15.1 %collective-permute-start.19 = (bf16[64,4096]{1,0:T(8,128)(2,1)S(1)}, bf16[64,4096]{1,0:T(8,128)(2,1)S(1)}, u32[]{:S(2)}, u32[]{:S(2)}) collective-permute-start(bf16[64,4096]{1,0:T(8,128)(2,1)S(1)} %get-tuple-element.34), channel_id=1, source_target_pairs={{0,2},{1,9},{2,4},{3,11},{4,6},{5,13},{6,0},{7,15},{8,10},{9,17},{... | collective-permute-start | bytes 1572872 | tf_op jit(solution)/shard_map/ppermute | solution.py:44
  85.1 14.8 %collective-permute-start.20 = (bf16[64,4096]{1,0:T(8,128)(2,1)S(1)}, bf16[64,4096]{1,0:T(8,128)(2,1)S(1)}, u32[]{:S(2)}, u32[]{:S(2)}) collective-permute-start(bf16[64,4096]{1,0:T(8,128)(2,1)S(1)} %get-tuple-element.35), channel_id=1, source_target_pairs={{0,6},{1,25},{2,0},{3,27},{4,2},{5,29},{6,4},{7,31},{8,14},{9,1},{... | collective-permute-start | bytes 1572872 | tf_op jit(solution)/shard_map/ppermute | solution.py:44
  90.5 15.3 %collective-permute-start.21 = (bf16[64,4096]{1,0:T(8,128)(2,1)S(1)}, bf16[64,4096]{1,0:T(8,128)(2,1)S(1)}, u32[]{:S(2)}, u32[]{:S(2)}) collective-permute-start(bf16[64,4096]{1,0:T(8,128)(2,1)S(1)} %get-tuple-element.38), channel_id=1, source_target_pairs={{0,4},{1,17},{2,6},{3,19},{4,0},{5,21},{6,2},{7,23},{8,12},{9,25},... | collective-permute-start | bytes 1572872 | tf_op jit(solution)/shard_map/ppermute | solution.py:44
  91.7 19.5 %collective-permute-start.22 = (bf16[64,4096]{1,0:T(8,128)(2,1)S(1)}, bf16[64,4096]{1,0:T(8,128)(2,1)S(1)}, u32[]{:S(2)}, u32[]{:S(2)}) collective-permute-start(bf16[64,4096]{1,0:T(8,128)(2,1)S(1)} %get-tuple-element.39), channel_id=1, source_target_pairs={{0,2},{1,9},{2,4},{3,11},{4,6},{5,13},{6,0},{7,15},{8,10},{9,17},{... | collective-permute-start | bytes 1572872 | tf_op jit(solution)/shard_map/ppermute | solution.py:44
  94.4 16.8 %collective-permute-start.23 = (bf16[64,4096]{1,0:T(8,128)(2,1)S(1)}, bf16[64,4096]{1,0:T(8,128)(2,1)S(1)}, u32[]{:S(2)}, u32[]{:S(2)}) collective-permute-start(bf16[64,4096]{1,0:T(8,128)(2,1)S(1)} %get-tuple-element.40), channel_id=1, source_target_pairs={{0,6},{1,25},{2,0},{3,27},{4,2},{5,29},{6,4},{7,31},{8,14},{9,1},{... | collective-permute-start | bytes 1572872 | tf_op jit(solution)/shard_map/ppermute | solution.py:44
  111.7 8.1 %collective-permute-start.24 = (bf16[16,8192]{1,0:T(8,128)(2,1)S(1)}, bf16[16,8192]{1,0:T(8,128)(2,1)S(1)}, u32[]{:S(2)}, u32[]{:S(2)}) collective-permute-start(bf16[16,8192]{1,0:T(8,128)(2,1)S(1)} %get-tuple-element.42), channel_id=1, source_target_pairs={{0,16},{1,5},{2,18},{3,7},{4,20},{5,1},{6,22},{7,3},{8,24},{9,13},... | collective-permute-start | bytes 786440 | tf_op jit(solution)/shard_map/ppermute | solution.py:44
  113.5 9.0 %collective-permute-start.25 = (bf16[16,8192]{1,0:T(8,128)(2,1)S(1)}, bf16[16,8192]{1,0:T(8,128)(2,1)S(1)}, u32[]{:S(2)}, u32[]{:S(2)}) collective-permute-start(bf16[16,8192]{1,0:T(8,128)(2,1)S(1)} %get-tuple-element.43), channel_id=1, source_target_pairs={{0,8},{1,3},{2,10},{3,5},{4,12},{5,7},{6,14},{7,1},{8,16},{9,11},{... | collective-permute-start | bytes 786440 | tf_op jit(solution)/shard_map/ppermute | solution.py:44
  115.3 7.2 %collective-permute-start.26 = (bf16[16,8192]{1,0:T(8,128)(2,1)S(1)}, bf16[16,8192]{1,0:T(8,128)(2,1)S(1)}, u32[]{:S(2)}, u32[]{:S(2)}) collective-permute-start(bf16[16,8192]{1,0:T(8,128)(2,1)S(1)} %get-tuple-element.44), channel_id=1, source_target_pairs={{0,24},{1,7},{2,26},{3,1},{4,28},{5,3},{6,30},{7,5},{8,0},{9,15},{... | collective-permute-start | bytes 786440 | tf_op jit(solution)/shard_map/ppermute | solution.py:44

commit v9 on v8

--- a/solution.py
+++ b/solution.py
@@ -13,7 +13,7 @@
 ORDER = (0, 1, 3, 2)
 PLACES = [(x, y, c) for x in range(RING) for y in range(RING) for c in range(2)]
 GATHER_SPANS = (1, 1)
-OUT_SPANS = (1, 1)
+OUT_SPANS = (3, 5)
 LIMIT = 24 * 2**20
 SMALL = 16 * 2**20
 BY_ROWS = (((1,), (1,)), ((), ()))

time: 123 us -> 123 us (level)
  waiting for transfers between devices: 54.3 us -> 50.5 us
  starting transfers between devices: 41.7 us -> 45 us
    ppermute x27, waiting for transfers between devices: 54.3 us -> 50.5 us  [send(): return lax.ppermute(value, 'tensor', pairs)]
    ppermute x27, starting transfers between devices: 41.7 us -> 45 us  [send(): return lax.ppermute(value, 'tensor', pairs)]
  transfers between devices with their start and end apart: 27 -> 27, of which waited for: 15 -> 12; matrix products, arithmetic and copies ran while one was open for 1% -> 1% of each run, Pallas kernels for 12% -> 13%
where the time goes in v9:
time: 123 us
  waiting for transfers between devices  50.5 us (41%)
  starting transfers between devices  45 us (37%)
  Pallas kernels  25.6 us (21%)
    ppermute x27, waiting for transfers between devices, send(): return lax.ppermute(value, 'tensor', pairs)  50.5 us
    ppermute x27, starting transfers between devices, send(): return lax.ppermute(value, 'tensor', pairs)  45 us
    pallas_call x7, Pallas kernels, call(): pl.pallas_call(kernel, name=name, compiler_params=pltpu.CompilerParams(vm...  21.3 us
    pallas_call x2, Pallas kernels, load(): pl.pallas_call(kernel, name='load', compiler_params=pltpu.CompilerParams(...  4.31 us
  transfers between devices with their start and end apart: 27, of which 12 were waited for; matrix products, arithmetic and copies ran while one was open for 1% of the time, Pallas kernels for 13%

profile of v9, /device:TPU:0, one launch (start us, length us, event | category | flops | bytes accessed | tf_op | source)
XLA Modules:
  0.0 122.8 jit_solution(7071650069959980481)
XLA Ops:
  0.0 0.0 collective-permute-start.9
  0.0 0.5 collective-permute-start.10
  0.5 3.1 %collective-permute-start = (bf16[16,8192]{1,0:T(8,128)(2,1)}, bf16[16,8192]{1,0:T(8,128)(2,1)S(1)}, u32[]{:S(2)}, u32[]{:S(2)}) collective-permute-start(bf16[16,8192]{1,0:T(8,128)(2,1)} %refs_0_.1), channel_id=1, source_target_pairs={{0,16},{1,5},{2,18},{3,7},{4,20},{5,1},{6,22},{7,3},{8,24},{9,13},... | collective-permute-start | bytes 786440 | tf_op jit(solution)/shard_map/ppermute | solution.py:44
  3.6 0.6 collective-permute-start.2
  4.2 2.6 %collective-permute-start.1 = (bf16[16,8192]{1,0:T(8,128)(2,1)}, bf16[16,8192]{1,0:T(8,128)(2,1)S(1)}, u32[]{:S(2)}, u32[]{:S(2)}) collective-permute-start(bf16[16,8192]{1,0:T(8,128)(2,1)} %refs_0_.1), channel_id=1, source_target_pairs={{0,24},{1,7},{2,26},{3,1},{4,28},{5,3},{6,30},{7,5},{8,0},{9,15},{... | collective-permute-start | bytes 786440 | tf_op jit(solution)/shard_map/ppermute | solution.py:44
  6.9 1.0 load.2.refs_0_
  7.9 0.7 dynamic-slice_bitcast_fusion.refs_10_.refs_4_
  8.6 0.0 collective-permute-done.refs_1_
  8.6 2.8 %collective-permute-done.2.refs_3_ = bf16[16,8192]{1,0:T(8,128)(2,1)S(1)} collective-permute-done((bf16[16,8192]{1,0:T(8,128)(2,1)}, bf16[16,8192]{1,0:T(8,128)(2,1)S(1)}, u32[]{:S(2)}, u32[]{:S(2)}) %collective-permute-start.2) | collective-permute-done | bytes 262176 | tf_op jit(solution)/shard_map/ppermute | solution.py:44
  11.4 0.2 collective-permute-done.1.refs_2_
  11.6 0.1 stack.1
  11.6 3.3 %collective-permute-start.8 = (bf16[64,4096]{1,0:T(8,128)(2,1)S(1)}, bf16[64,4096]{1,0:T(8,128)(2,1)S(1)}, u32[]{:S(2)}, u32[]{:S(2)}) collective-permute-start(bf16[64,4096]{1,0:T(8,128)(2,1)S(1)} %get-tuple-element.27.refs_0_), channel_id=1, source_target_pairs={{0,4},{1,17},{2,6},{3,19},{4,0},{5,21},{6,2},{7,23},{8,12},{9,25},... | collective-permute-start | bytes 1572872 | tf_op jit(solution)/shard_map/ppermute | solution.py:44
  14.9 0.7 collective-permute-start.7
  15.6 2.6 %collective-permute-start.6 = (bf16[64,4096]{1,0:T(8,128)(2,1)S(1)}, bf16[64,4096]{1,0:T(8,128)(2,1)S(1)}, u32[]{:S(2)}, u32[]{:S(2)}) collective-permute-start(bf16[64,4096]{1,0:T(8,128)(2,1)S(1)} %get-tuple-element.27.refs_0_), channel_id=1, source_target_pairs={{0,6},{1,25},{2,0},{3,27},{4,2},{5,29},{6,4},{7,31},{8,14},{9,1},{... | collective-permute-start | bytes 1572872 | tf_op jit(solution)/shard_map/ppermute | solution.py:44
  18.2 4.4 %collective-permute-done.8.refs_3_ = bf16[64,4096]{1,0:T(8,128)(2,1)S(1)} collective-permute-done((bf16[64,4096]{1,0:T(8,128)(2,1)S(1)}, bf16[64,4096]{1,0:T(8,128)(2,1)S(1)}, u32[]{:S(2)}, u32[]{:S(2)}) %collective-permute-start.8) | collective-permute-done | bytes 524320 | tf_op jit(solution)/shard_map/ppermute | solution.py:44
  22.5 3.2 %collective-permute-start.5 = (bf16[64,4096]{1,0:T(8,128)(2,1)S(1)}, bf16[64,4096]{1,0:T(8,128)(2,1)S(1)}, u32[]{:S(2)}, u32[]{:S(2)}) collective-permute-start(bf16[64,4096]{1,0:T(8,128)(2,1)S(1)} %get-tuple-element.26.refs_0_), channel_id=1, source_target_pairs={{0,4},{1,17},{2,6},{3,19},{4,0},{5,21},{6,2},{7,23},{8,12},{9,25},... | collective-permute-start | bytes 1572872 | tf_op jit(solution)/shard_map/ppermute | solution.py:44
  25.7 2.3 %collective-permute-done.7.refs_2_ = bf16[64,4096]{1,0:T(8,128)(2,1)S(1)} collective-permute-done((bf16[64,4096]{1,0:T(8,128)(2,1)S(1)}, bf16[64,4096]{1,0:T(8,128)(2,1)S(1)}, u32[]{:S(2)}, u32[]{:S(2)}) %collective-permute-start.7) | collective-permute-done | bytes 524320 | tf_op jit(solution)/shard_map/ppermute | solution.py:44
  28.0 1.7 %collective-permute-start.4 = (bf16[64,4096]{1,0:T(8,128)(2,1)S(1)}, bf16[64,4096]{1,0:T(8,128)(2,1)S(1)}, u32[]{:S(2)}, u32[]{:S(2)}) collective-permute-start(bf16[64,4096]{1,0:T(8,128)(2,1)S(1)} %get-tuple-element.26.refs_0_), channel_id=1, source_target_pairs={{0,2},{1,9},{2,4},{3,11},{4,6},{5,13},{6,0},{7,15},{8,10},{9,17},{... | collective-permute-start | bytes 1572872 | tf_op jit(solution)/shard_map/ppermute | solution.py:44
  29.8 0.0 collective-permute-done.6.refs_1_
  29.8 1.5 %collective-permute-start.3 = (bf16[64,4096]{1,0:T(8,128)(2,1)S(1)}, bf16[64,4096]{1,0:T(8,128)(2,1)S(1)}, u32[]{:S(2)}, u32[]{:S(2)}) collective-permute-start(bf16[64,4096]{1,0:T(8,128)(2,1)S(1)} %get-tuple-element.26.refs_0_), channel_id=1, source_target_pairs={{0,6},{1,25},{2,0},{3,27},{4,2},{5,29},{6,4},{7,31},{8,14},{9,1},{... | collective-permute-start | bytes 1572872 | tf_op jit(solution)/shard_map/ppermute | solution.py:44
  31.3 0.0 collective-permute-done.9.refs_6_
  31.3 0.0 collective-permute-done.10.refs_7_
  31.3 7.4 %gate_up.2.refs_8_ = f32[4,256,448]{2,1,0:T(8,128)S(1)} custom-call(bf16[64,4096]{1,0:T(8,128)(2,1)S(1)} %get-tuple-element.27.refs_0_, bf16[64,4096]{1,0:T(8,128)(2,1)S(1)} %collective-permute-done.6.refs_1_, bf16[64,4096]{1,0:T(8,128)(2,1)S(1)} %collective-permute-done.7.refs_2_, bf16[64,4096]{1,0:T(8,128)(2,1)S(1)} %collective-permute-done.8.refs_3_, ...), custom_call_target="tpu_custom_call" | custom-call | flops 3758096384 | bytes 14680064 | tf_op jit(solution)/shard_map/gate_up/pallas_call | solution.py:86
  38.7 0.0 copy-start
  38.7 0.0 slice-start
  38.8 3.3 %load.3 = (bf16[448,4096]{1,0:T(8,128)(2,1)S(1)}, bf16[448,4096]{1,0:T(8,128)(2,1)S(1)}) custom-call(bf16[448,8192]{1,0:T(8,128)(2,1)} %bitcast.8, bf16[448,8192]{1,0:T(8,128)(2,1)} %bitcast.11), custom_call_target="tpu_custom_call" | custom-call | bytes 14680064 | tf_op jit(solution)/shard_map/load/pallas_call | solution.py:116
  42.1 0.0 collective-permute-done.3.refs_1_
  42.1 0.0 slice-start.1
  42.1 6.8 %gate_up.3.refs_0_ = bf16[256,896]{1,0:T(8,128)(2,1)S(1)} custom-call(bf16[64,4096]{1,0:T(8,128)(2,1)S(1)} %get-tuple-element.26.refs_0_, bf16[64,4096]{1,0:T(8,128)(2,1)S(1)} %collective-permute-done.3.refs_1_, bf16[64,4096]{1,0:T(8,128)(2,1)S(1)} %collective-permute-done.4.refs_2_, bf16[64,4096]{1,0:T(8,128)(2,1)S(1)} %collective-permute-done.5.refs_3_, ...), custom_call_target="tpu_custom_call" | custom-call | flops 3758096384 | bytes 14680064 | tf_op jit(solution)/shard_map/gate_up/pallas_call | solution.py:86
  49.0 0.1 collective-permute-start.17
  49.1 2.2 %collective-permute-start.13 = (bf16[256,896]{1,0:T(8,128)(2,1)S(1)}, bf16[256,896]{1,0:T(8,128)(2,1)S(1)}, u32[]{:S(2)}, u32[]{:S(2)}) collective-permute-start(bf16[256,896]{1,0:T(8,128)(2,1)S(1)} %gate_up.3.refs_0_), channel_id=1, source_target_pairs={{0,16},{1,5},{2,18},{3,7},{4,20},{5,1},{6,22},{7,3},{8,24},{9,13},... | collective-permute-start | bytes 1376264 | tf_op jit(solution)/shard_map/ppermute | solution.py:44
  51.3 1.8 %collective-permute-start.12 = (bf16[256,896]{1,0:T(8,128)(2,1)S(1)}, bf16[256,896]{1,0:T(8,128)(2,1)S(1)}, u32[]{:S(2)}, u32[]{:S(2)}) collective-permute-start(bf16[256,896]{1,0:T(8,128)(2,1)S(1)} %gate_up.3.refs_0_), channel_id=1, source_target_pairs={{0,8},{1,3},{2,10},{3,5},{4,12},{5,7},{6,14},{7,1},{8,16},{9,11},{... | collective-permute-start | bytes 1376264 | tf_op jit(solution)/shard_map/ppermute | solution.py:44
  53.1 1.4 %collective-permute-start.11 = (bf16[256,896]{1,0:T(8,128)(2,1)S(1)}, bf16[256,896]{1,0:T(8,128)(2,1)S(1)}, u32[]{:S(2)}, u32[]{:S(2)}) collective-permute-start(bf16[256,896]{1,0:T(8,128)(2,1)S(1)} %gate_up.3.refs_0_), channel_id=1, source_target_pairs={{0,24},{1,7},{2,26},{3,1},{4,28},{5,3},{6,30},{7,5},{8,0},{9,15},{... | collective-permute-start | bytes 1376264 | tf_op jit(solution)/shard_map/ppermute | solution.py:44
  54.5 4.8 %collective-permute-done.13.refs_3_ = bf16[256,896]{1,0:T(8,128)(2,1)S(1)} collective-permute-done((bf16[256,896]{1,0:T(8,128)(2,1)S(1)}, bf16[256,896]{1,0:T(8,128)(2,1)S(1)}, u32[]{:S(2)}, u32[]{:S(2)}) %collective-permute-start.13) | collective-permute-done | bytes 458784 | tf_op jit(solution)/shard_map/ppermute | solution.py:44
  59.3 4.8 %collective-permute-done.12.refs_2_ = bf16[256,896]{1,0:T(8,128)(2,1)S(1)} collective-permute-done((bf16[256,896]{1,0:T(8,128)(2,1)S(1)}, bf16[256,896]{1,0:T(8,128)(2,1)S(1)}, u32[]{:S(2)}, u32[]{:S(2)}) %collective-permute-start.12) | collective-permute-done | bytes 458784 | tf_op jit(solution)/shard_map/ppermute | solution.py:44
  64.1 0.4 collective-permute-done.11.refs_1_
  64.5 0.9 combine.1.refs_0_
  65.4 1.3 %collective-permute-start.16 = (bf16[256,896]{1,0:T(8,128)(2,1)S(1)}, bf16[256,896]{1,0:T(8,128)(2,1)S(1)}, u32[]{:S(2)}, u32[]{:S(2)}) collective-permute-start(bf16[256,896]{1,0:T(8,128)(2,1)S(1)} %combine.1.refs_0_), channel_id=1, source_target_pairs={{0,4},{1,17},{2,6},{3,19},{4,0},{5,21},{6,2},{7,23},{8,12},{9,25},... | collective-permute-start | bytes 1376264 | tf_op jit(solution)/shard_map/ppermute | solution.py:44
  66.7 0.0 collective-permute-start.15
  66.7 3.2 %collective-permute-start.14 = (bf16[256,896]{1,0:T(8,128)(2,1)S(1)}, bf16[256,896]{1,0:T(8,128)(2,1)S(1)}, u32[]{:S(2)}, u32[]{:S(2)}) collective-permute-start(bf16[256,896]{1,0:T(8,128)(2,1)S(1)} %combine.1.refs_0_), channel_id=1, source_target_pairs={{0,6},{1,25},{2,0},{3,27},{4,2},{5,29},{6,4},{7,31},{8,14},{9,1},{... | collective-permute-start | bytes 1376264 | tf_op jit(solution)/shard_map/ppermute | solution.py:44
  69.9 5.6 %collective-permute-done.16.refs_3_ = bf16[256,896]{1,0:T(8,128)(2,1)S(1)} collective-permute-done((bf16[256,896]{1,0:T(8,128)(2,1)S(1)}, bf16[256,896]{1,0:T(8,128)(2,1)S(1)}, u32[]{:S(2)}, u32[]{:S(2)}) %collective-permute-start.16) | collective-permute-done | bytes 458784 | tf_op jit(solution)/shard_map/ppermute | solution.py:44
  75.6 4.8 %collective-permute-done.15.refs_2_ = bf16[256,896]{1,0:T(8,128)(2,1)S(1)} collective-permute-done((bf16[256,896]{1,0:T(8,128)(2,1)S(1)}, bf16[256,896]{1,0:T(8,128)(2,1)S(1)}, u32[]{:S(2)}, u32[]{:S(2)}) %collective-permute-start.15) | collective-permute-done | bytes 458784 | tf_op jit(solution)/shard_map/ppermute | solution.py:44
  80.4 0.0 collective-permute-done.14.refs_1_
  80.4 2.6 %combine_down.1 = (bf16[256,896]{1,0:T(8,128)(2,1)S(1)}, bf16[64,3072]{1,0:T(8,128)(2,1)S(1)}, bf16[64,3072]{1,0:T(8,128)(2,1)S(1)}, bf16[64,3072]{1,0:T(8,128)(2,1)S(1)}, bf16[64,3072]{1,0:T(8,128)(2,1)S(1)}) custom-call(bf16[256,896]{1,0:T(8,128)(2,1)S(1)} %combine.1.refs_0_, bf16[256,896]{1,0:T(8,128)(2,1)S(1)} %collective-permute-done.14.refs_1_, ...), custom_call_target="tpu_custom_call" | custom-call | flops 1409286144 | bytes 5505024 | tf_op jit(solution)/shard_map/combine_down/pallas_call | solution.py:86
  83.0 1.3 %collective-permute-start.18 = (bf16[64,3072]{1,0:T(8,128)(2,1)S(1)}, bf16[64,3072]{1,0:T(8,128)(2,1)S(1)}, u32[]{:S(2)}, u32[]{:S(2)}) collective-permute-start(bf16[64,3072]{1,0:T(8,128)(2,1)S(1)} %get-tuple-element.33), channel_id=1, source_target_pairs={{0,4},{1,17},{2,6},{3,19},{4,0},{5,21},{6,2},{7,23},{8,12},{9,25},... | collective-permute-start | bytes 1179656 | tf_op jit(solution)/shard_map/ppermute | solution.py:44
  84.3 2.9 %down.1 = (bf16[64,5120]{1,0:T(8,128)(2,1)S(1)}, bf16[64,5120]{1,0:T(8,128)(2,1)S(1)}, bf16[64,5120]{1,0:T(8,128)(2,1)S(1)}, bf16[64,5120]{1,0:T(8,128)(2,1)S(1)}) custom-call(bf16[256,896]{1,0:T(8,128)(2,1)S(1)} %get-tuple-element.36.held, bf16[448,8192]{1,0:T(8,128)(2,1)S(1)} %bitcast.5, bf16[448,8192]{1,0:T(8,128)(2,1)S(1)} %collective-permute-done.17.refs_6_.loaded_other), custom_call_target="tpu_custom_call" | custom-call | flops 2348810240 | bytes 9175040 | tf_op jit(solution)/shard_map/down/pallas_call | solution.py:86
  87.2 2.4 %collective-permute-start.21 = (bf16[64,5120]{1,0:T(8,128)(2,1)S(1)}, bf16[64,5120]{1,0:T(8,128)(2,1)S(1)}, u32[]{:S(2)}, u32[]{:S(2)}) collective-permute-start(bf16[64,5120]{1,0:T(8,128)(2,1)S(1)} %get-tuple-element.38), channel_id=1, source_target_pairs={{0,4},{1,17},{2,6},{3,19},{4,0},{5,21},{6,2},{7,23},{8,12},{9,25},... | collective-permute-start | bytes 1966088 | tf_op jit(solution)/shard_map/ppermute | solution.py:44
  89.6 0.5 collective-permute-start.22
  90.2 2.7 %collective-permute-start.23 = (bf16[64,5120]{1,0:T(8,128)(2,1)S(1)}, bf16[64,5120]{1,0:T(8,128)(2,1)S(1)}, u32[]{:S(2)}, u32[]{:S(2)}) collective-permute-start(bf16[64,5120]{1,0:T(8,128)(2,1)S(1)} %get-tuple-element.40), channel_id=1, source_target_pairs={{0,6},{1,25},{2,0},{3,27},{4,2},{5,29},{6,4},{7,31},{8,14},{9,1},{... | collective-permute-start | bytes 1966088 | tf_op jit(solution)/shard_map/ppermute | solution.py:44
  92.9 0.0 collective-permute-start.19
  92.9 0.0 collective-permute-done.18.refs_1_
  92.9 3.2 %collective-permute-start.20 = (bf16[64,3072]{1,0:T(8,128)(2,1)S(1)}, bf16[64,3072]{1,0:T(8,128)(2,1)S(1)}, u32[]{:S(2)}, u32[]{:S(2)}) collective-permute-start(bf16[64,3072]{1,0:T(8,128)(2,1)S(1)} %get-tuple-element.35), channel_id=1, source_target_pairs={{0,6},{1,25},{2,0},{3,27},{4,2},{5,29},{6,4},{7,31},{8,14},{9,1},{... | collective-permute-start | bytes 1179656 | tf_op jit(solution)/shard_map/ppermute | solution.py:44
  96.1 14.5 %collective-permute-done.19.refs_2_ = bf16[64,3072]{1,0:T(8,128)(2,1)S(1)} collective-permute-done((bf16[64,3072]{1,0:T(8,128)(2,1)S(1)}, bf16[64,3072]{1,0:T(8,128)(2,1)S(1)}, u32[]{:S(2)}, u32[]{:S(2)}) %collective-permute-start.19) | collective-permute-done | bytes 393248 | tf_op jit(solution)/shard_map/ppermute | solution.py:44
  110.6 0.0 collective-permute-done.20.refs_3_
  110.7 0.0 collective-permute-done.21.refs_5_
  110.7 0.0 collective-permute-done.22.refs_6_
  110.7 0.0 collective-permute-done.23.refs_7_
  110.7 0.5 fold.1
  111.2 1.8 %collective-permute-start.24 = (bf16[16,8192]{1,0:T(8,128)(2,1)S(1)}, bf16[16,8192]{1,0:T(8,128)(2,1)S(1)}, u32[]{:S(2)}, u32[]{:S(2)}) collective-permute-start(bf16[16,8192]{1,0:T(8,128)(2,1)S(1)} %get-tuple-element.42), channel_id=1, source_target_pairs={{0,16},{1,5},{2,18},{3,7},{4,20},{5,1},{6,22},{7,3},{8,24},{9,13},... | collective-permute-start | bytes 786440 | tf_op jit(solution)/shard_map/ppermute | solution.py:44
  113.0 1.8 %collective-permute-start.25 = (bf16[16,8192]{1,0:T(8,128)(2,1)S(1)}, bf16[16,8192]{1,0:T(8,128)(2,1)S(1)}, u32[]{:S(2)}, u32[]{:S(2)}) collective-permute-start(bf16[16,8192]{1,0:T(8,128)(2,1)S(1)} %get-tuple-element.43), channel_id=1, source_target_pairs={{0,8},{1,3},{2,10},{3,5},{4,12},{5,7},{6,14},{7,1},{8,16},{9,11},{... | collective-permute-start | bytes 786440 | tf_op jit(solution)/shard_map/ppermute | solution.py:44
  114.8 1.4 %collective-permute-start.26 = (bf16[16,8192]{1,0:T(8,128)(2,1)S(1)}, bf16[16,8192]{1,0:T(8,128)(2,1)S(1)}, u32[]{:S(2)}, u32[]{:S(2)}) collective-permute-start(bf16[16,8192]{1,0:T(8,128)(2,1)S(1)} %get-tuple-element.44), channel_id=1, source_target_pairs={{0,24},{1,7},{2,26},{3,1},{4,28},{5,3},{6,30},{7,5},{8,0},{9,15},{... | collective-permute-start | bytes 786440 | tf_op jit(solution)/shard_map/ppermute | solution.py:44
  116.2 3.1 %collective-permute-done.24 = bf16[16,8192]{1,0:T(8,128)(2,1)S(1)} collective-permute-done((bf16[16,8192]{1,0:T(8,128)(2,1)S(1)}, bf16[16,8192]{1,0:T(8,128)(2,1)S(1)}, u32[]{:S(2)}, u32[]{:S(2)}) %collective-permute-start.24) | collective-permute-done | bytes 262176 | tf_op jit(solution)/shard_map/ppermute | solution.py:44
  119.3 2.7 %collective-permute-done.25 = bf16[16,8192]{1,0:T(8,128)(2,1)S(1)} collective-permute-done((bf16[16,8192]{1,0:T(8,128)(2,1)S(1)}, bf16[16,8192]{1,0:T(8,128)(2,1)S(1)}, u32[]{:S(2)}, u32[]{:S(2)}) %collective-permute-start.25) | collective-permute-done | bytes 262176 | tf_op jit(solution)/shard_map/ppermute | solution.py:44
  122.0 0.8 add_convert_fusion
  (8 shorter events, 0.0 us)
Async XLA Ops:
  0.0 31.3 %collective-permute-start.9 = (bf16[448,8192]{1,0:T(8,128)(2,1)}, bf16[448,8192]{1,0:T(8,128)(2,1)}, u32[]{:S(2)}, u32[]{:S(2)}) collective-permute-start(bf16[448,8192]{1,0:T(8,128)(2,1)} %bitcast.6), channel_id=1, source_target_pairs={{0,1},{1,0},{2,3},{3,2},{4,5},{5,4},{6,7},{7,6},{8,9},{9,8},{10,11... | collective-permute-start | bytes 22020104 | tf_op jit(solution)/shard_map/ppermute | solution.py:44
  0.0 31.3 %collective-permute-start.10 = (bf16[448,8192]{1,0:T(8,128)(2,1)}, bf16[448,8192]{1,0:T(8,128)(2,1)}, u32[]{:S(2)}, u32[]{:S(2)}) collective-permute-start(bf16[448,8192]{1,0:T(8,128)(2,1)} %bitcast.9), channel_id=1, source_target_pairs={{0,1},{1,0},{2,3},{3,2},{4,5},{5,4},{6,7},{7,6},{8,9},{9,8},{10,11... | collective-permute-start | bytes 22020104 | tf_op jit(solution)/shard_map/ppermute | solution.py:44
  0.5 8.1 %collective-permute-start = (bf16[16,8192]{1,0:T(8,128)(2,1)}, bf16[16,8192]{1,0:T(8,128)(2,1)S(1)}, u32[]{:S(2)}, u32[]{:S(2)}) collective-permute-start(bf16[16,8192]{1,0:T(8,128)(2,1)} %refs_0_.1), channel_id=1, source_target_pairs={{0,16},{1,5},{2,18},{3,7},{4,20},{5,1},{6,22},{7,3},{8,24},{9,13},... | collective-permute-start | bytes 786440 | tf_op jit(solution)/shard_map/ppermute | solution.py:44
  3.6 7.8 %collective-permute-start.2 = (bf16[16,8192]{1,0:T(8,128)(2,1)}, bf16[16,8192]{1,0:T(8,128)(2,1)S(1)}, u32[]{:S(2)}, u32[]{:S(2)}) collective-permute-start(bf16[16,8192]{1,0:T(8,128)(2,1)} %refs_0_.1), channel_id=1, source_target_pairs={{0,8},{1,3},{2,10},{3,5},{4,12},{5,7},{6,14},{7,1},{8,16},{9,11},{... | collective-permute-start | bytes 786440 | tf_op jit(solution)/shard_map/ppermute | solution.py:44
  4.2 7.4 %collective-permute-start.1 = (bf16[16,8192]{1,0:T(8,128)(2,1)}, bf16[16,8192]{1,0:T(8,128)(2,1)S(1)}, u32[]{:S(2)}, u32[]{:S(2)}) collective-permute-start(bf16[16,8192]{1,0:T(8,128)(2,1)} %refs_0_.1), channel_id=1, source_target_pairs={{0,24},{1,7},{2,26},{3,1},{4,28},{5,3},{6,30},{7,5},{8,0},{9,15},{... | collective-permute-start | bytes 786440 | tf_op jit(solution)/shard_map/ppermute | solution.py:44
  11.6 10.9 %collective-permute-start.8 = (bf16[64,4096]{1,0:T(8,128)(2,1)S(1)}, bf16[64,4096]{1,0:T(8,128)(2,1)S(1)}, u32[]{:S(2)}, u32[]{:S(2)}) collective-permute-start(bf16[64,4096]{1,0:T(8,128)(2,1)S(1)} %get-tuple-element.27.refs_0_), channel_id=1, source_target_pairs={{0,4},{1,17},{2,6},{3,19},{4,0},{5,21},{6,2},{7,23},{8,12},{9,25},... | collective-permute-start | bytes 1572872 | tf_op jit(solution)/shard_map/ppermute | solution.py:44
  14.9 13.1 %collective-permute-start.7 = (bf16[64,4096]{1,0:T(8,128)(2,1)S(1)}, bf16[64,4096]{1,0:T(8,128)(2,1)S(1)}, u32[]{:S(2)}, u32[]{:S(2)}) collective-permute-start(bf16[64,4096]{1,0:T(8,128)(2,1)S(1)} %get-tuple-element.27.refs_0_), channel_id=1, source_target_pairs={{0,2},{1,9},{2,4},{3,11},{4,6},{5,13},{6,0},{7,15},{8,10},{9,17},{... | collective-permute-start | bytes 1572872 | tf_op jit(solution)/shard_map/ppermute | solution.py:44
  15.6 14.2 %collective-permute-start.6 = (bf16[64,4096]{1,0:T(8,128)(2,1)S(1)}, bf16[64,4096]{1,0:T(8,128)(2,1)S(1)}, u32[]{:S(2)}, u32[]{:S(2)}) collective-permute-start(bf16[64,4096]{1,0:T(8,128)(2,1)S(1)} %get-tuple-element.27.refs_0_), channel_id=1, source_target_pairs={{0,6},{1,25},{2,0},{3,27},{4,2},{5,29},{6,4},{7,31},{8,14},{9,1},{... | collective-permute-start | bytes 1572872 | tf_op jit(solution)/shard_map/ppermute | solution.py:44
  22.5 19.6 %collective-permute-start.5 = (bf16[64,4096]{1,0:T(8,128)(2,1)S(1)}, bf16[64,4096]{1,0:T(8,128)(2,1)S(1)}, u32[]{:S(2)}, u32[]{:S(2)}) collective-permute-start(bf16[64,4096]{1,0:T(8,128)(2,1)S(1)} %get-tuple-element.26.refs_0_), channel_id=1, source_target_pairs={{0,4},{1,17},{2,6},{3,19},{4,0},{5,21},{6,2},{7,23},{8,12},{9,25},... | collective-permute-start | bytes 1572872 | tf_op jit(solution)/shard_map/ppermute | solution.py:44
  28.0 14.1 %collective-permute-start.4 = (bf16[64,4096]{1,0:T(8,128)(2,1)S(1)}, bf16[64,4096]{1,0:T(8,128)(2,1)S(1)}, u32[]{:S(2)}, u32[]{:S(2)}) collective-permute-start(bf16[64,4096]{1,0:T(8,128)(2,1)S(1)} %get-tuple-element.26.refs_0_), channel_id=1, source_target_pairs={{0,2},{1,9},{2,4},{3,11},{4,6},{5,13},{6,0},{7,15},{8,10},{9,17},{... | collective-permute-start | bytes 1572872 | tf_op jit(solution)/shard_map/ppermute | solution.py:44
  29.8 12.3 %collective-permute-start.3 = (bf16[64,4096]{1,0:T(8,128)(2,1)S(1)}, bf16[64,4096]{1,0:T(8,128)(2,1)S(1)}, u32[]{:S(2)}, u32[]{:S(2)}) collective-permute-start(bf16[64,4096]{1,0:T(8,128)(2,1)S(1)} %get-tuple-element.26.refs_0_), channel_id=1, source_target_pairs={{0,6},{1,25},{2,0},{3,27},{4,2},{5,29},{6,4},{7,31},{8,14},{9,1},{... | collective-permute-start | bytes 1572872 | tf_op jit(solution)/shard_map/ppermute | solution.py:44
  38.7 3.4 %copy-start = (bf16[448,448]{1,0:T(8,128)(2,1)S(1)}, bf16[448,448]{1,0:T(8,128)(2,1)}, u32[]{:S(2)}) copy-start(bf16[448,448]{1,0:T(8,128)(2,1)} %refs_9_.1) | copy-start | bytes 1204228
  38.7 10.2 %slice-start = ((s8[7340032]{0:T(1024)(128)(4,1)}), s8[4194304]{0:T(1024)(128)(4,1)S(1)}, s32[]{:S(2)}) async-start(s8[7340032]{0:T(1024)(128)(4,1)} %bitcast.4), calls=%async_computation | async-start | bytes 8388608
  42.1 6.9 %slice-start.1 = ((s8[7340032]{0:T(1024)(128)(4,1)}), s8[3145728]{0:T(1024)(128)(4,1)S(1)}, s32[]{:S(2)}) async-start(s8[7340032]{0:T(1024)(128)(4,1)} %bitcast.4), calls=%async_computation.1 | async-start | bytes 6291456
  49.0 31.4 %collective-permute-start.17 = (bf16[448,8192]{1,0:T(8,128)(2,1)S(1)}, bf16[448,8192]{1,0:T(8,128)(2,1)S(1)}, u32[]{:S(2)}, u32[]{:S(2)}) collective-permute-start(bf16[448,8192]{1,0:T(8,128)(2,1)S(1)} %bitcast.5), channel_id=1, source_target_pairs={{0,1},{1,0},{2,3},{3,2},{4,5},{5,4},{6,7},{7,6},{8,9},{9,8},{10,11... | collective-permute-start | bytes 22020104 | tf_op jit(solution)/shard_map/ppermute | solution.py:44
  49.1 10.2 %collective-permute-start.13 = (bf16[256,896]{1,0:T(8,128)(2,1)S(1)}, bf16[256,896]{1,0:T(8,128)(2,1)S(1)}, u32[]{:S(2)}, u32[]{:S(2)}) collective-permute-start(bf16[256,896]{1,0:T(8,128)(2,1)S(1)} %gate_up.3.refs_0_), channel_id=1, source_target_pairs={{0,16},{1,5},{2,18},{3,7},{4,20},{5,1},{6,22},{7,3},{8,24},{9,13},... | collective-permute-start | bytes 1376264 | tf_op jit(solution)/shard_map/ppermute | solution.py:44
  51.3 12.8 %collective-permute-start.12 = (bf16[256,896]{1,0:T(8,128)(2,1)S(1)}, bf16[256,896]{1,0:T(8,128)(2,1)S(1)}, u32[]{:S(2)}, u32[]{:S(2)}) collective-permute-start(bf16[256,896]{1,0:T(8,128)(2,1)S(1)} %gate_up.3.refs_0_), channel_id=1, source_target_pairs={{0,8},{1,3},{2,10},{3,5},{4,12},{5,7},{6,14},{7,1},{8,16},{9,11},{... | collective-permute-start | bytes 1376264 | tf_op jit(solution)/shard_map/ppermute | solution.py:44
  53.1 11.4 %collective-permute-start.11 = (bf16[256,896]{1,0:T(8,128)(2,1)S(1)}, bf16[256,896]{1,0:T(8,128)(2,1)S(1)}, u32[]{:S(2)}, u32[]{:S(2)}) collective-permute-start(bf16[256,896]{1,0:T(8,128)(2,1)S(1)} %gate_up.3.refs_0_), channel_id=1, source_target_pairs={{0,24},{1,7},{2,26},{3,1},{4,28},{5,3},{6,30},{7,5},{8,0},{9,15},{... | collective-permute-start | bytes 1376264 | tf_op jit(solution)/shard_map/ppermute | solution.py:44
  65.4 10.2 %collective-permute-start.16 = (bf16[256,896]{1,0:T(8,128)(2,1)S(1)}, bf16[256,896]{1,0:T(8,128)(2,1)S(1)}, u32[]{:S(2)}, u32[]{:S(2)}) collective-permute-start(bf16[256,896]{1,0:T(8,128)(2,1)S(1)} %combine.1.refs_0_), channel_id=1, source_target_pairs={{0,4},{1,17},{2,6},{3,19},{4,0},{5,21},{6,2},{7,23},{8,12},{9,25},... | collective-permute-start | bytes 1376264 | tf_op jit(solution)/shard_map/ppermute | solution.py:44
  66.7 13.7 %collective-permute-start.15 = (bf16[256,896]{1,0:T(8,128)(2,1)S(1)}, bf16[256,896]{1,0:T(8,128)(2,1)S(1)}, u32[]{:S(2)}, u32[]{:S(2)}) collective-permute-start(bf16[256,896]{1,0:T(8,128)(2,1)S(1)} %combine.1.refs_0_), channel_id=1, source_target_pairs={{0,2},{1,9},{2,4},{3,11},{4,6},{5,13},{6,0},{7,15},{8,10},{9,17},{... | collective-permute-start | bytes 1376264 | tf_op jit(solution)/shard_map/ppermute | solution.py:44
  66.7 13.7 %collective-permute-start.14 = (bf16[256,896]{1,0:T(8,128)(2,1)S(1)}, bf16[256,896]{1,0:T(8,128)(2,1)S(1)}, u32[]{:S(2)}, u32[]{:S(2)}) collective-permute-start(bf16[256,896]{1,0:T(8,128)(2,1)S(1)} %combine.1.refs_0_), channel_id=1, source_target_pairs={{0,6},{1,25},{2,0},{3,27},{4,2},{5,29},{6,4},{7,31},{8,14},{9,1},{... | collective-permute-start | bytes 1376264 | tf_op jit(solution)/shard_map/ppermute | solution.py:44
  83.0 9.8 %collective-permute-start.18 = (bf16[64,3072]{1,0:T(8,128)(2,1)S(1)}, bf16[64,3072]{1,0:T(8,128)(2,1)S(1)}, u32[]{:S(2)}, u32[]{:S(2)}) collective-permute-start(bf16[64,3072]{1,0:T(8,128)(2,1)S(1)} %get-tuple-element.33), channel_id=1, source_target_pairs={{0,4},{1,17},{2,6},{3,19},{4,0},{5,21},{6,2},{7,23},{8,12},{9,25},... | collective-permute-start | bytes 1179656 | tf_op jit(solution)/shard_map/ppermute | solution.py:44
  87.2 23.4 %collective-permute-start.21 = (bf16[64,5120]{1,0:T(8,128)(2,1)S(1)}, bf16[64,5120]{1,0:T(8,128)(2,1)S(1)}, u32[]{:S(2)}, u32[]{:S(2)}) collective-permute-start(bf16[64,5120]{1,0:T(8,128)(2,1)S(1)} %get-tuple-element.38), channel_id=1, source_target_pairs={{0,4},{1,17},{2,6},{3,19},{4,0},{5,21},{6,2},{7,23},{8,12},{9,25},... | collective-permute-start | bytes 1966088 | tf_op jit(solution)/shard_map/ppermute | solution.py:44
  89.6 21.0 %collective-permute-start.22 = (bf16[64,5120]{1,0:T(8,128)(2,1)S(1)}, bf16[64,5120]{1,0:T(8,128)(2,1)S(1)}, u32[]{:S(2)}, u32[]{:S(2)}) collective-permute-start(bf16[64,5120]{1,0:T(8,128)(2,1)S(1)} %get-tuple-element.39), channel_id=1, source_target_pairs={{0,2},{1,9},{2,4},{3,11},{4,6},{5,13},{6,0},{7,15},{8,10},{9,17},{... | collective-permute-start | bytes 1966088 | tf_op jit(solution)/shard_map/ppermute | solution.py:44
  90.2 20.5 %collective-permute-start.23 = (bf16[64,5120]{1,0:T(8,128)(2,1)S(1)}, bf16[64,5120]{1,0:T(8,128)(2,1)S(1)}, u32[]{:S(2)}, u32[]{:S(2)}) collective-permute-start(bf16[64,5120]{1,0:T(8,128)(2,1)S(1)} %get-tuple-element.40), channel_id=1, source_target_pairs={{0,6},{1,25},{2,0},{3,27},{4,2},{5,29},{6,4},{7,31},{8,14},{9,1},{... | collective-permute-start | bytes 1966088 | tf_op jit(solution)/shard_map/ppermute | solution.py:44
  92.9 17.8 %collective-permute-start.19 = (bf16[64,3072]{1,0:T(8,128)(2,1)S(1)}, bf16[64,3072]{1,0:T(8,128)(2,1)S(1)}, u32[]{:S(2)}, u32[]{:S(2)}) collective-permute-start(bf16[64,3072]{1,0:T(8,128)(2,1)S(1)} %get-tuple-element.34), channel_id=1, source_target_pairs={{0,2},{1,9},{2,4},{3,11},{4,6},{5,13},{6,0},{7,15},{8,10},{9,17},{... | collective-permute-start | bytes 1179656 | tf_op jit(solution)/shard_map/ppermute | solution.py:44
  92.9 17.8 %collective-permute-start.20 = (bf16[64,3072]{1,0:T(8,128)(2,1)S(1)}, bf16[64,3072]{1,0:T(8,128)(2,1)S(1)}, u32[]{:S(2)}, u32[]{:S(2)}) collective-permute-start(bf16[64,3072]{1,0:T(8,128)(2,1)S(1)} %get-tuple-element.35), channel_id=1, source_target_pairs={{0,6},{1,25},{2,0},{3,27},{4,2},{5,29},{6,4},{7,31},{8,14},{9,1},{... | collective-permute-start | bytes 1179656 | tf_op jit(solution)/shard_map/ppermute | solution.py:44
  111.2 8.1 %collective-permute-start.24 = (bf16[16,8192]{1,0:T(8,128)(2,1)S(1)}, bf16[16,8192]{1,0:T(8,128)(2,1)S(1)}, u32[]{:S(2)}, u32[]{:S(2)}) collective-permute-start(bf16[16,8192]{1,0:T(8,128)(2,1)S(1)} %get-tuple-element.42), channel_id=1, source_target_pairs={{0,16},{1,5},{2,18},{3,7},{4,20},{5,1},{6,22},{7,3},{8,24},{9,13},... | collective-permute-start | bytes 786440 | tf_op jit(solution)/shard_map/ppermute | solution.py:44
  113.0 9.0 %collective-permute-start.25 = (bf16[16,8192]{1,0:T(8,128)(2,1)S(1)}, bf16[16,8192]{1,0:T(8,128)(2,1)S(1)}, u32[]{:S(2)}, u32[]{:S(2)}) collective-permute-start(bf16[16,8192]{1,0:T(8,128)(2,1)S(1)} %get-tuple-element.43), channel_id=1, source_target_pairs={{0,8},{1,3},{2,10},{3,5},{4,12},{5,7},{6,14},{7,1},{8,16},{9,11},{... | collective-permute-start | bytes 786440 | tf_op jit(solution)/shard_map/ppermute | solution.py:44
  114.8 7.2 %collective-permute-start.26 = (bf16[16,8192]{1,0:T(8,128)(2,1)S(1)}, bf16[16,8192]{1,0:T(8,128)(2,1)S(1)}, u32[]{:S(2)}, u32[]{:S(2)}) collective-permute-start(bf16[16,8192]{1,0:T(8,128)(2,1)S(1)} %get-tuple-element.44), channel_id=1, source_target_pairs={{0,24},{1,7},{2,26},{3,1},{4,28},{5,3},{6,30},{7,5},{8,0},{9,15},{... | collective-permute-start | bytes 786440 | tf_op jit(solution)/shard_map/ppermute | solution.py:44

commit v10 on v9

--- a/solution.py
+++ b/solution.py
@@ -157,7 +157,7 @@
     group = pieces[0].shape[0]
     rows = RING * group
     units = weights[0].shape[0]
-    block = math.gcd(span, 2048)
+    block = math.gcd(span, 4096)
     steps = span // block
     opening, closing = sums is None, finish is not None
     count = len(close)

time: 123 us -> 123 us (level)
  no operation moved by 1% of the time
where the time goes in v10:
time: 123 us; the launch traced here: 122 us
  waiting for transfers between devices  50.5 us (41%)
  starting transfers between devices  45.2 us (37%)
  Pallas kernels  25.1 us (20%)
    ppermute x27, waiting for transfers between devices, send(): return lax.ppermute(value, 'tensor', pairs)  50.5 us
    ppermute x27, starting transfers between devices, send(): return lax.ppermute(value, 'tensor', pairs)  45.2 us
    pallas_call x7, Pallas kernels, call(): pl.pallas_call(kernel, name=name, compiler_params=pltpu.CompilerParams(vm...  20.7 us
    pallas_call x2, Pallas kernels, load(): pl.pallas_call(kernel, name='load', compiler_params=pltpu.CompilerParams(...  4.31 us
  transfers between devices with their start and end apart: 27, of which 12 were waited for; matrix products, arithmetic and copies ran while one was open for 1% of the time, Pallas kernels for 13%

profile of v10, /device:TPU:0, one launch (start us, length us, event | category | flops | bytes accessed | tf_op | source)
XLA Modules:
  0.0 122.4 jit_solution(2510657609130072892)
XLA Ops:
  0.0 0.0 collective-permute-start.9
  0.0 0.5 collective-permute-start.10
  0.5 3.1 %collective-permute-start = (bf16[16,8192]{1,0:T(8,128)(2,1)}, bf16[16,8192]{1,0:T(8,128)(2,1)S(1)}, u32[]{:S(2)}, u32[]{:S(2)}) collective-permute-start(bf16[16,8192]{1,0:T(8,128)(2,1)} %refs_0_.1), channel_id=1, source_target_pairs={{0,16},{1,5},{2,18},{3,7},{4,20},{5,1},{6,22},{7,3},{8,24},{9,13},... | collective-permute-start | bytes 786440 | tf_op jit(solution)/shard_map/ppermute | solution.py:44
  3.6 0.6 collective-permute-start.2
  4.2 2.6 %collective-permute-start.1 = (bf16[16,8192]{1,0:T(8,128)(2,1)}, bf16[16,8192]{1,0:T(8,128)(2,1)S(1)}, u32[]{:S(2)}, u32[]{:S(2)}) collective-permute-start(bf16[16,8192]{1,0:T(8,128)(2,1)} %refs_0_.1), channel_id=1, source_target_pairs={{0,24},{1,7},{2,26},{3,1},{4,28},{5,3},{6,30},{7,5},{8,0},{9,15},{... | collective-permute-start | bytes 786440 | tf_op jit(solution)/shard_map/ppermute | solution.py:44
  6.9 1.0 load.2.refs_0_
  7.9 0.7 dynamic-slice_bitcast_fusion.refs_10_.refs_4_
  8.6 0.0 collective-permute-done.refs_1_
  8.6 2.8 %collective-permute-done.2.refs_3_ = bf16[16,8192]{1,0:T(8,128)(2,1)S(1)} collective-permute-done((bf16[16,8192]{1,0:T(8,128)(2,1)}, bf16[16,8192]{1,0:T(8,128)(2,1)S(1)}, u32[]{:S(2)}, u32[]{:S(2)}) %collective-permute-start.2) | collective-permute-done | bytes 262176 | tf_op jit(solution)/shard_map/ppermute | solution.py:44
  11.4 0.2 collective-permute-done.1.refs_2_
  11.6 0.1 stack.1
  11.6 3.3 %collective-permute-start.8 = (bf16[64,4096]{1,0:T(8,128)(2,1)S(1)}, bf16[64,4096]{1,0:T(8,128)(2,1)S(1)}, u32[]{:S(2)}, u32[]{:S(2)}) collective-permute-start(bf16[64,4096]{1,0:T(8,128)(2,1)S(1)} %get-tuple-element.27.refs_0_), channel_id=1, source_target_pairs={{0,4},{1,17},{2,6},{3,19},{4,0},{5,21},{6,2},{7,23},{8,12},{9,25},... | collective-permute-start | bytes 1572872 | tf_op jit(solution)/shard_map/ppermute | solution.py:44
  14.9 0.7 collective-permute-start.7
  15.6 2.6 %collective-permute-start.6 = (bf16[64,4096]{1,0:T(8,128)(2,1)S(1)}, bf16[64,4096]{1,0:T(8,128)(2,1)S(1)}, u32[]{:S(2)}, u32[]{:S(2)}) collective-permute-start(bf16[64,4096]{1,0:T(8,128)(2,1)S(1)} %get-tuple-element.27.refs_0_), channel_id=1, source_target_pairs={{0,6},{1,25},{2,0},{3,27},{4,2},{5,29},{6,4},{7,31},{8,14},{9,1},{... | collective-permute-start | bytes 1572872 | tf_op jit(solution)/shard_map/ppermute | solution.py:44
  18.2 4.4 %collective-permute-done.8.refs_3_ = bf16[64,4096]{1,0:T(8,128)(2,1)S(1)} collective-permute-done((bf16[64,4096]{1,0:T(8,128)(2,1)S(1)}, bf16[64,4096]{1,0:T(8,128)(2,1)S(1)}, u32[]{:S(2)}, u32[]{:S(2)}) %collective-permute-start.8) | collective-permute-done | bytes 524320 | tf_op jit(solution)/shard_map/ppermute | solution.py:44
  22.5 3.2 %collective-permute-start.5 = (bf16[64,4096]{1,0:T(8,128)(2,1)S(1)}, bf16[64,4096]{1,0:T(8,128)(2,1)S(1)}, u32[]{:S(2)}, u32[]{:S(2)}) collective-permute-start(bf16[64,4096]{1,0:T(8,128)(2,1)S(1)} %get-tuple-element.26.refs_0_), channel_id=1, source_target_pairs={{0,4},{1,17},{2,6},{3,19},{4,0},{5,21},{6,2},{7,23},{8,12},{9,25},... | collective-permute-start | bytes 1572872 | tf_op jit(solution)/shard_map/ppermute | solution.py:44
  25.7 2.3 %collective-permute-done.7.refs_2_ = bf16[64,4096]{1,0:T(8,128)(2,1)S(1)} collective-permute-done((bf16[64,4096]{1,0:T(8,128)(2,1)S(1)}, bf16[64,4096]{1,0:T(8,128)(2,1)S(1)}, u32[]{:S(2)}, u32[]{:S(2)}) %collective-permute-start.7) | collective-permute-done | bytes 524320 | tf_op jit(solution)/shard_map/ppermute | solution.py:44
  28.0 1.7 %collective-permute-start.4 = (bf16[64,4096]{1,0:T(8,128)(2,1)S(1)}, bf16[64,4096]{1,0:T(8,128)(2,1)S(1)}, u32[]{:S(2)}, u32[]{:S(2)}) collective-permute-start(bf16[64,4096]{1,0:T(8,128)(2,1)S(1)} %get-tuple-element.26.refs_0_), channel_id=1, source_target_pairs={{0,2},{1,9},{2,4},{3,11},{4,6},{5,13},{6,0},{7,15},{8,10},{9,17},{... | collective-permute-start | bytes 1572872 | tf_op jit(solution)/shard_map/ppermute | solution.py:44
  29.8 0.0 collective-permute-done.6.refs_1_
  29.8 1.5 %collective-permute-start.3 = (bf16[64,4096]{1,0:T(8,128)(2,1)S(1)}, bf16[64,4096]{1,0:T(8,128)(2,1)S(1)}, u32[]{:S(2)}, u32[]{:S(2)}) collective-permute-start(bf16[64,4096]{1,0:T(8,128)(2,1)S(1)} %get-tuple-element.26.refs_0_), channel_id=1, source_target_pairs={{0,6},{1,25},{2,0},{3,27},{4,2},{5,29},{6,4},{7,31},{8,14},{9,1},{... | collective-permute-start | bytes 1572872 | tf_op jit(solution)/shard_map/ppermute | solution.py:44
  31.3 0.0 collective-permute-done.9.refs_6_
  31.3 0.0 collective-permute-done.10.refs_7_
  31.3 7.2 %gate_up.2.refs_8_ = f32[4,256,448]{2,1,0:T(8,128)S(1)} custom-call(bf16[64,4096]{1,0:T(8,128)(2,1)S(1)} %get-tuple-element.27.refs_0_, bf16[64,4096]{1,0:T(8,128)(2,1)S(1)} %collective-permute-done.6.refs_1_, bf16[64,4096]{1,0:T(8,128)(2,1)S(1)} %collective-permute-done.7.refs_2_, bf16[64,4096]{1,0:T(8,128)(2,1)S(1)} %collective-permute-done.8.refs_3_, ...), custom_call_target="tpu_custom_call" | custom-call | flops 3758096384 | bytes 14680064 | tf_op jit(solution)/shard_map/gate_up/pallas_call | solution.py:86
  38.4 0.0 copy-start
  38.5 0.0 slice-start
  38.5 3.3 %load.3 = (bf16[448,4096]{1,0:T(8,128)(2,1)S(1)}, bf16[448,4096]{1,0:T(8,128)(2,1)S(1)}) custom-call(bf16[448,8192]{1,0:T(8,128)(2,1)} %bitcast.8, bf16[448,8192]{1,0:T(8,128)(2,1)} %bitcast.11), custom_call_target="tpu_custom_call" | custom-call | bytes 14680064 | tf_op jit(solution)/shard_map/load/pallas_call | solution.py:116
  41.8 0.0 collective-permute-done.5.refs_3_
  41.8 0.0 collective-permute-done.4.refs_2_
  41.8 0.0 collective-permute-done.3.refs_1_
  41.8 0.0 slice-start.1
  41.9 6.6 %gate_up.3.refs_0_ = bf16[256,896]{1,0:T(8,128)(2,1)S(1)} custom-call(bf16[64,4096]{1,0:T(8,128)(2,1)S(1)} %get-tuple-element.26.refs_0_, bf16[64,4096]{1,0:T(8,128)(2,1)S(1)} %collective-permute-done.3.refs_1_, bf16[64,4096]{1,0:T(8,128)(2,1)S(1)} %collective-permute-done.4.refs_2_, bf16[64,4096]{1,0:T(8,128)(2,1)S(1)} %collective-permute-done.5.refs_3_, ...), custom_call_target="tpu_custom_call" | custom-call | flops 3758096384 | bytes 14680064 | tf_op jit(solution)/shard_map/gate_up/pallas_call | solution.py:86
  48.5 0.3 collective-permute-start.17
  48.7 2.2 %collective-permute-start.13 = (bf16[256,896]{1,0:T(8,128)(2,1)S(1)}, bf16[256,896]{1,0:T(8,128)(2,1)S(1)}, u32[]{:S(2)}, u32[]{:S(2)}) collective-permute-start(bf16[256,896]{1,0:T(8,128)(2,1)S(1)} %gate_up.3.refs_0_), channel_id=1, source_target_pairs={{0,16},{1,5},{2,18},{3,7},{4,20},{5,1},{6,22},{7,3},{8,24},{9,13},... | collective-permute-start | bytes 1376264 | tf_op jit(solution)/shard_map/ppermute | solution.py:44
  50.9 1.8 %collective-permute-start.12 = (bf16[256,896]{1,0:T(8,128)(2,1)S(1)}, bf16[256,896]{1,0:T(8,128)(2,1)S(1)}, u32[]{:S(2)}, u32[]{:S(2)}) collective-permute-start(bf16[256,896]{1,0:T(8,128)(2,1)S(1)} %gate_up.3.refs_0_), channel_id=1, source_target_pairs={{0,8},{1,3},{2,10},{3,5},{4,12},{5,7},{6,14},{7,1},{8,16},{9,11},{... | collective-permute-start | bytes 1376264 | tf_op jit(solution)/shard_map/ppermute | solution.py:44
  52.8 1.4 %collective-permute-start.11 = (bf16[256,896]{1,0:T(8,128)(2,1)S(1)}, bf16[256,896]{1,0:T(8,128)(2,1)S(1)}, u32[]{:S(2)}, u32[]{:S(2)}) collective-permute-start(bf16[256,896]{1,0:T(8,128)(2,1)S(1)} %gate_up.3.refs_0_), channel_id=1, source_target_pairs={{0,24},{1,7},{2,26},{3,1},{4,28},{5,3},{6,30},{7,5},{8,0},{9,15},{... | collective-permute-start | bytes 1376264 | tf_op jit(solution)/shard_map/ppermute | solution.py:44
  54.2 4.7 %collective-permute-done.13.refs_3_ = bf16[256,896]{1,0:T(8,128)(2,1)S(1)} collective-permute-done((bf16[256,896]{1,0:T(8,128)(2,1)S(1)}, bf16[256,896]{1,0:T(8,128)(2,1)S(1)}, u32[]{:S(2)}, u32[]{:S(2)}) %collective-permute-start.13) | collective-permute-done | bytes 458784 | tf_op jit(solution)/shard_map/ppermute | solution.py:44
  58.9 4.8 %collective-permute-done.12.refs_2_ = bf16[256,896]{1,0:T(8,128)(2,1)S(1)} collective-permute-done((bf16[256,896]{1,0:T(8,128)(2,1)S(1)}, bf16[256,896]{1,0:T(8,128)(2,1)S(1)}, u32[]{:S(2)}, u32[]{:S(2)}) %collective-permute-start.12) | collective-permute-done | bytes 458784 | tf_op jit(solution)/shard_map/ppermute | solution.py:44
  63.7 0.4 collective-permute-done.11.refs_1_
  64.2 0.9 combine.1.refs_0_
  65.1 1.3 %collective-permute-start.16 = (bf16[256,896]{1,0:T(8,128)(2,1)S(1)}, bf16[256,896]{1,0:T(8,128)(2,1)S(1)}, u32[]{:S(2)}, u32[]{:S(2)}) collective-permute-start(bf16[256,896]{1,0:T(8,128)(2,1)S(1)} %combine.1.refs_0_), channel_id=1, source_target_pairs={{0,4},{1,17},{2,6},{3,19},{4,0},{5,21},{6,2},{7,23},{8,12},{9,25},... | collective-permute-start | bytes 1376264 | tf_op jit(solution)/shard_map/ppermute | solution.py:44
  66.3 0.1 collective-permute-start.15
  66.5 3.1 %collective-permute-start.14 = (bf16[256,896]{1,0:T(8,128)(2,1)S(1)}, bf16[256,896]{1,0:T(8,128)(2,1)S(1)}, u32[]{:S(2)}, u32[]{:S(2)}) collective-permute-start(bf16[256,896]{1,0:T(8,128)(2,1)S(1)} %combine.1.refs_0_), channel_id=1, source_target_pairs={{0,6},{1,25},{2,0},{3,27},{4,2},{5,29},{6,4},{7,31},{8,14},{9,1},{... | collective-permute-start | bytes 1376264 | tf_op jit(solution)/shard_map/ppermute | solution.py:44
  69.6 5.6 %collective-permute-done.16.refs_3_ = bf16[256,896]{1,0:T(8,128)(2,1)S(1)} collective-permute-done((bf16[256,896]{1,0:T(8,128)(2,1)S(1)}, bf16[256,896]{1,0:T(8,128)(2,1)S(1)}, u32[]{:S(2)}, u32[]{:S(2)}) %collective-permute-start.16) | collective-permute-done | bytes 458784 | tf_op jit(solution)/shard_map/ppermute | solution.py:44
  75.2 4.8 %collective-permute-done.15.refs_2_ = bf16[256,896]{1,0:T(8,128)(2,1)S(1)} collective-permute-done((bf16[256,896]{1,0:T(8,128)(2,1)S(1)}, bf16[256,896]{1,0:T(8,128)(2,1)S(1)}, u32[]{:S(2)}, u32[]{:S(2)}) %collective-permute-start.15) | collective-permute-done | bytes 458784 | tf_op jit(solution)/shard_map/ppermute | solution.py:44
  80.0 0.0 collective-permute-done.14.refs_1_
  80.1 2.6 %combine_down.1 = (bf16[256,896]{1,0:T(8,128)(2,1)S(1)}, bf16[64,3072]{1,0:T(8,128)(2,1)S(1)}, bf16[64,3072]{1,0:T(8,128)(2,1)S(1)}, bf16[64,3072]{1,0:T(8,128)(2,1)S(1)}, bf16[64,3072]{1,0:T(8,128)(2,1)S(1)}) custom-call(bf16[256,896]{1,0:T(8,128)(2,1)S(1)} %combine.1.refs_0_, bf16[256,896]{1,0:T(8,128)(2,1)S(1)} %collective-permute-done.14.refs_1_, ...), custom_call_target="tpu_custom_call" | custom-call | flops 1409286144 | bytes 5505024 | tf_op jit(solution)/shard_map/combine_down/pallas_call | solution.py:86
  82.7 1.3 %collective-permute-start.18 = (bf16[64,3072]{1,0:T(8,128)(2,1)S(1)}, bf16[64,3072]{1,0:T(8,128)(2,1)S(1)}, u32[]{:S(2)}, u32[]{:S(2)}) collective-permute-start(bf16[64,3072]{1,0:T(8,128)(2,1)S(1)} %get-tuple-element.33), channel_id=1, source_target_pairs={{0,4},{1,17},{2,6},{3,19},{4,0},{5,21},{6,2},{7,23},{8,12},{9,25},... | collective-permute-start | bytes 1179656 | tf_op jit(solution)/shard_map/ppermute | solution.py:44
  84.0 2.9 %down.1 = (bf16[64,5120]{1,0:T(8,128)(2,1)S(1)}, bf16[64,5120]{1,0:T(8,128)(2,1)S(1)}, bf16[64,5120]{1,0:T(8,128)(2,1)S(1)}, bf16[64,5120]{1,0:T(8,128)(2,1)S(1)}) custom-call(bf16[256,896]{1,0:T(8,128)(2,1)S(1)} %get-tuple-element.36.held, bf16[448,8192]{1,0:T(8,128)(2,1)S(1)} %bitcast.5, bf16[448,8192]{1,0:T(8,128)(2,1)S(1)} %collective-permute-done.17.refs_6_.loaded_other), custom_call_target="tpu_custom_call" | custom-call | flops 2348810240 | bytes 9175040 | tf_op jit(solution)/shard_map/down/pallas_call | solution.py:86
  86.9 2.4 %collective-permute-start.21 = (bf16[64,5120]{1,0:T(8,128)(2,1)S(1)}, bf16[64,5120]{1,0:T(8,128)(2,1)S(1)}, u32[]{:S(2)}, u32[]{:S(2)}) collective-permute-start(bf16[64,5120]{1,0:T(8,128)(2,1)S(1)} %get-tuple-element.38), channel_id=1, source_target_pairs={{0,4},{1,17},{2,6},{3,19},{4,0},{5,21},{6,2},{7,23},{8,12},{9,25},... | collective-permute-start | bytes 1966088 | tf_op jit(solution)/shard_map/ppermute | solution.py:44
  89.3 0.5 collective-permute-start.22
  89.8 2.7 %collective-permute-start.23 = (bf16[64,5120]{1,0:T(8,128)(2,1)S(1)}, bf16[64,5120]{1,0:T(8,128)(2,1)S(1)}, u32[]{:S(2)}, u32[]{:S(2)}) collective-permute-start(bf16[64,5120]{1,0:T(8,128)(2,1)S(1)} %get-tuple-element.40), channel_id=1, source_target_pairs={{0,6},{1,25},{2,0},{3,27},{4,2},{5,29},{6,4},{7,31},{8,14},{9,1},{... | collective-permute-start | bytes 1966088 | tf_op jit(solution)/shard_map/ppermute | solution.py:44
  92.5 0.0 collective-permute-done.18.refs_1_
  92.5 3.2 %collective-permute-start.20 = (bf16[64,3072]{1,0:T(8,128)(2,1)S(1)}, bf16[64,3072]{1,0:T(8,128)(2,1)S(1)}, u32[]{:S(2)}, u32[]{:S(2)}) collective-permute-start(bf16[64,3072]{1,0:T(8,128)(2,1)S(1)} %get-tuple-element.35), channel_id=1, source_target_pairs={{0,6},{1,25},{2,0},{3,27},{4,2},{5,29},{6,4},{7,31},{8,14},{9,1},{... | collective-permute-start | bytes 1179656 | tf_op jit(solution)/shard_map/ppermute | solution.py:44
  95.8 14.5 %collective-permute-done.19.refs_2_ = bf16[64,3072]{1,0:T(8,128)(2,1)S(1)} collective-permute-done((bf16[64,3072]{1,0:T(8,128)(2,1)S(1)}, bf16[64,3072]{1,0:T(8,128)(2,1)S(1)}, u32[]{:S(2)}, u32[]{:S(2)}) %collective-permute-start.19) | collective-permute-done | bytes 393248 | tf_op jit(solution)/shard_map/ppermute | solution.py:44
  110.3 0.0 collective-permute-done.22.refs_6_
  110.3 0.0 collective-permute-done.23.refs_7_
  110.3 0.5 fold.1
  110.8 1.8 %collective-permute-start.24 = (bf16[16,8192]{1,0:T(8,128)(2,1)S(1)}, bf16[16,8192]{1,0:T(8,128)(2,1)S(1)}, u32[]{:S(2)}, u32[]{:S(2)}) collective-permute-start(bf16[16,8192]{1,0:T(8,128)(2,1)S(1)} %get-tuple-element.42), channel_id=1, source_target_pairs={{0,16},{1,5},{2,18},{3,7},{4,20},{5,1},{6,22},{7,3},{8,24},{9,13},... | collective-permute-start | bytes 786440 | tf_op jit(solution)/shard_map/ppermute | solution.py:44
  112.6 1.8 %collective-permute-start.25 = (bf16[16,8192]{1,0:T(8,128)(2,1)S(1)}, bf16[16,8192]{1,0:T(8,128)(2,1)S(1)}, u32[]{:S(2)}, u32[]{:S(2)}) collective-permute-start(bf16[16,8192]{1,0:T(8,128)(2,1)S(1)} %get-tuple-element.43), channel_id=1, source_target_pairs={{0,8},{1,3},{2,10},{3,5},{4,12},{5,7},{6,14},{7,1},{8,16},{9,11},{... | collective-permute-start | bytes 786440 | tf_op jit(solution)/shard_map/ppermute | solution.py:44
  114.4 1.4 %collective-permute-start.26 = (bf16[16,8192]{1,0:T(8,128)(2,1)S(1)}, bf16[16,8192]{1,0:T(8,128)(2,1)S(1)}, u32[]{:S(2)}, u32[]{:S(2)}) collective-permute-start(bf16[16,8192]{1,0:T(8,128)(2,1)S(1)} %get-tuple-element.44), channel_id=1, source_target_pairs={{0,24},{1,7},{2,26},{3,1},{4,28},{5,3},{6,30},{7,5},{8,0},{9,15},{... | collective-permute-start | bytes 786440 | tf_op jit(solution)/shard_map/ppermute | solution.py:44
  115.8 3.1 %collective-permute-done.24 = bf16[16,8192]{1,0:T(8,128)(2,1)S(1)} collective-permute-done((bf16[16,8192]{1,0:T(8,128)(2,1)S(1)}, bf16[16,8192]{1,0:T(8,128)(2,1)S(1)}, u32[]{:S(2)}, u32[]{:S(2)}) %collective-permute-start.24) | collective-permute-done | bytes 262176 | tf_op jit(solution)/shard_map/ppermute | solution.py:44
  118.9 2.7 %collective-permute-done.25 = bf16[16,8192]{1,0:T(8,128)(2,1)S(1)} collective-permute-done((bf16[16,8192]{1,0:T(8,128)(2,1)S(1)}, bf16[16,8192]{1,0:T(8,128)(2,1)S(1)}, u32[]{:S(2)}, u32[]{:S(2)}) %collective-permute-start.25) | collective-permute-done | bytes 262176 | tf_op jit(solution)/shard_map/ppermute | solution.py:44
  121.6 0.0 collective-permute-done.26
  121.6 0.8 add_convert_fusion
  (8 shorter events, 0.0 us)
Async XLA Ops:
  0.0 31.3 %collective-permute-start.9 = (bf16[448,8192]{1,0:T(8,128)(2,1)}, bf16[448,8192]{1,0:T(8,128)(2,1)}, u32[]{:S(2)}, u32[]{:S(2)}) collective-permute-start(bf16[448,8192]{1,0:T(8,128)(2,1)} %bitcast.6), channel_id=1, source_target_pairs={{0,1},{1,0},{2,3},{3,2},{4,5},{5,4},{6,7},{7,6},{8,9},{9,8},{10,11... | collective-permute-start | bytes 22020104 | tf_op jit(solution)/shard_map/ppermute | solution.py:44
  0.0 31.3 %collective-permute-start.10 = (bf16[448,8192]{1,0:T(8,128)(2,1)}, bf16[448,8192]{1,0:T(8,128)(2,1)}, u32[]{:S(2)}, u32[]{:S(2)}) collective-permute-start(bf16[448,8192]{1,0:T(8,128)(2,1)} %bitcast.9), channel_id=1, source_target_pairs={{0,1},{1,0},{2,3},{3,2},{4,5},{5,4},{6,7},{7,6},{8,9},{9,8},{10,11... | collective-permute-start | bytes 22020104 | tf_op jit(solution)/shard_map/ppermute | solution.py:44
  0.5 8.1 %collective-permute-start = (bf16[16,8192]{1,0:T(8,128)(2,1)}, bf16[16,8192]{1,0:T(8,128)(2,1)S(1)}, u32[]{:S(2)}, u32[]{:S(2)}) collective-permute-start(bf16[16,8192]{1,0:T(8,128)(2,1)} %refs_0_.1), channel_id=1, source_target_pairs={{0,16},{1,5},{2,18},{3,7},{4,20},{5,1},{6,22},{7,3},{8,24},{9,13},... | collective-permute-start | bytes 786440 | tf_op jit(solution)/shard_map/ppermute | solution.py:44
  3.6 7.8 %collective-permute-start.2 = (bf16[16,8192]{1,0:T(8,128)(2,1)}, bf16[16,8192]{1,0:T(8,128)(2,1)S(1)}, u32[]{:S(2)}, u32[]{:S(2)}) collective-permute-start(bf16[16,8192]{1,0:T(8,128)(2,1)} %refs_0_.1), channel_id=1, source_target_pairs={{0,8},{1,3},{2,10},{3,5},{4,12},{5,7},{6,14},{7,1},{8,16},{9,11},{... | collective-permute-start | bytes 786440 | tf_op jit(solution)/shard_map/ppermute | solution.py:44
  4.2 7.4 %collective-permute-start.1 = (bf16[16,8192]{1,0:T(8,128)(2,1)}, bf16[16,8192]{1,0:T(8,128)(2,1)S(1)}, u32[]{:S(2)}, u32[]{:S(2)}) collective-permute-start(bf16[16,8192]{1,0:T(8,128)(2,1)} %refs_0_.1), channel_id=1, source_target_pairs={{0,24},{1,7},{2,26},{3,1},{4,28},{5,3},{6,30},{7,5},{8,0},{9,15},{... | collective-permute-start | bytes 786440 | tf_op jit(solution)/shard_map/ppermute | solution.py:44
  11.6 10.9 %collective-permute-start.8 = (bf16[64,4096]{1,0:T(8,128)(2,1)S(1)}, bf16[64,4096]{1,0:T(8,128)(2,1)S(1)}, u32[]{:S(2)}, u32[]{:S(2)}) collective-permute-start(bf16[64,4096]{1,0:T(8,128)(2,1)S(1)} %get-tuple-element.27.refs_0_), channel_id=1, source_target_pairs={{0,4},{1,17},{2,6},{3,19},{4,0},{5,21},{6,2},{7,23},{8,12},{9,25},... | collective-permute-start | bytes 1572872 | tf_op jit(solution)/shard_map/ppermute | solution.py:44
  14.9 13.1 %collective-permute-start.7 = (bf16[64,4096]{1,0:T(8,128)(2,1)S(1)}, bf16[64,4096]{1,0:T(8,128)(2,1)S(1)}, u32[]{:S(2)}, u32[]{:S(2)}) collective-permute-start(bf16[64,4096]{1,0:T(8,128)(2,1)S(1)} %get-tuple-element.27.refs_0_), channel_id=1, source_target_pairs={{0,2},{1,9},{2,4},{3,11},{4,6},{5,13},{6,0},{7,15},{8,10},{9,17},{... | collective-permute-start | bytes 1572872 | tf_op jit(solution)/shard_map/ppermute | solution.py:44
  15.6 14.2 %collective-permute-start.6 = (bf16[64,4096]{1,0:T(8,128)(2,1)S(1)}, bf16[64,4096]{1,0:T(8,128)(2,1)S(1)}, u32[]{:S(2)}, u32[]{:S(2)}) collective-permute-start(bf16[64,4096]{1,0:T(8,128)(2,1)S(1)} %get-tuple-element.27.refs_0_), channel_id=1, source_target_pairs={{0,6},{1,25},{2,0},{3,27},{4,2},{5,29},{6,4},{7,31},{8,14},{9,1},{... | collective-permute-start | bytes 1572872 | tf_op jit(solution)/shard_map/ppermute | solution.py:44
  22.5 19.3 %collective-permute-start.5 = (bf16[64,4096]{1,0:T(8,128)(2,1)S(1)}, bf16[64,4096]{1,0:T(8,128)(2,1)S(1)}, u32[]{:S(2)}, u32[]{:S(2)}) collective-permute-start(bf16[64,4096]{1,0:T(8,128)(2,1)S(1)} %get-tuple-element.26.refs_0_), channel_id=1, source_target_pairs={{0,4},{1,17},{2,6},{3,19},{4,0},{5,21},{6,2},{7,23},{8,12},{9,25},... | collective-permute-start | bytes 1572872 | tf_op jit(solution)/shard_map/ppermute | solution.py:44
  28.0 13.8 %collective-permute-start.4 = (bf16[64,4096]{1,0:T(8,128)(2,1)S(1)}, bf16[64,4096]{1,0:T(8,128)(2,1)S(1)}, u32[]{:S(2)}, u32[]{:S(2)}) collective-permute-start(bf16[64,4096]{1,0:T(8,128)(2,1)S(1)} %get-tuple-element.26.refs_0_), channel_id=1, source_target_pairs={{0,2},{1,9},{2,4},{3,11},{4,6},{5,13},{6,0},{7,15},{8,10},{9,17},{... | collective-permute-start | bytes 1572872 | tf_op jit(solution)/shard_map/ppermute | solution.py:44
  29.8 12.0 %collective-permute-start.3 = (bf16[64,4096]{1,0:T(8,128)(2,1)S(1)}, bf16[64,4096]{1,0:T(8,128)(2,1)S(1)}, u32[]{:S(2)}, u32[]{:S(2)}) collective-permute-start(bf16[64,4096]{1,0:T(8,128)(2,1)S(1)} %get-tuple-element.26.refs_0_), channel_id=1, source_target_pairs={{0,6},{1,25},{2,0},{3,27},{4,2},{5,29},{6,4},{7,31},{8,14},{9,1},{... | collective-permute-start | bytes 1572872 | tf_op jit(solution)/shard_map/ppermute | solution.py:44
  38.4 3.4 %copy-start = (bf16[448,448]{1,0:T(8,128)(2,1)S(1)}, bf16[448,448]{1,0:T(8,128)(2,1)}, u32[]{:S(2)}) copy-start(bf16[448,448]{1,0:T(8,128)(2,1)} %refs_9_.1) | copy-start | bytes 1204228
  38.5 10.0 %slice-start = ((s8[7340032]{0:T(1024)(128)(4,1)}), s8[4194304]{0:T(1024)(128)(4,1)S(1)}, s32[]{:S(2)}) async-start(s8[7340032]{0:T(1024)(128)(4,1)} %bitcast.4), calls=%async_computation | async-start | bytes 8388608
  41.8 6.6 %slice-start.1 = ((s8[7340032]{0:T(1024)(128)(4,1)}), s8[3145728]{0:T(1024)(128)(4,1)S(1)}, s32[]{:S(2)}) async-start(s8[7340032]{0:T(1024)(128)(4,1)} %bitcast.4), calls=%async_computation.1 | async-start | bytes 6291456
  48.5 31.6 %collective-permute-start.17 = (bf16[448,8192]{1,0:T(8,128)(2,1)S(1)}, bf16[448,8192]{1,0:T(8,128)(2,1)S(1)}, u32[]{:S(2)}, u32[]{:S(2)}) collective-permute-start(bf16[448,8192]{1,0:T(8,128)(2,1)S(1)} %bitcast.5), channel_id=1, source_target_pairs={{0,1},{1,0},{2,3},{3,2},{4,5},{5,4},{6,7},{7,6},{8,9},{9,8},{10,11... | collective-permute-start | bytes 22020104 | tf_op jit(solution)/shard_map/ppermute | solution.py:44
  48.7 10.2 %collective-permute-start.13 = (bf16[256,896]{1,0:T(8,128)(2,1)S(1)}, bf16[256,896]{1,0:T(8,128)(2,1)S(1)}, u32[]{:S(2)}, u32[]{:S(2)}) collective-permute-start(bf16[256,896]{1,0:T(8,128)(2,1)S(1)} %gate_up.3.refs_0_), channel_id=1, source_target_pairs={{0,16},{1,5},{2,18},{3,7},{4,20},{5,1},{6,22},{7,3},{8,24},{9,13},... | collective-permute-start | bytes 1376264 | tf_op jit(solution)/shard_map/ppermute | solution.py:44
  50.9 12.8 %collective-permute-start.12 = (bf16[256,896]{1,0:T(8,128)(2,1)S(1)}, bf16[256,896]{1,0:T(8,128)(2,1)S(1)}, u32[]{:S(2)}, u32[]{:S(2)}) collective-permute-start(bf16[256,896]{1,0:T(8,128)(2,1)S(1)} %gate_up.3.refs_0_), channel_id=1, source_target_pairs={{0,8},{1,3},{2,10},{3,5},{4,12},{5,7},{6,14},{7,1},{8,16},{9,11},{... | collective-permute-start | bytes 1376264 | tf_op jit(solution)/shard_map/ppermute | solution.py:44
  52.8 11.4 %collective-permute-start.11 = (bf16[256,896]{1,0:T(8,128)(2,1)S(1)}, bf16[256,896]{1,0:T(8,128)(2,1)S(1)}, u32[]{:S(2)}, u32[]{:S(2)}) collective-permute-start(bf16[256,896]{1,0:T(8,128)(2,1)S(1)} %gate_up.3.refs_0_), channel_id=1, source_target_pairs={{0,24},{1,7},{2,26},{3,1},{4,28},{5,3},{6,30},{7,5},{8,0},{9,15},{... | collective-permute-start | bytes 1376264 | tf_op jit(solution)/shard_map/ppermute | solution.py:44
  65.1 10.2 %collective-permute-start.16 = (bf16[256,896]{1,0:T(8,128)(2,1)S(1)}, bf16[256,896]{1,0:T(8,128)(2,1)S(1)}, u32[]{:S(2)}, u32[]{:S(2)}) collective-permute-start(bf16[256,896]{1,0:T(8,128)(2,1)S(1)} %combine.1.refs_0_), channel_id=1, source_target_pairs={{0,4},{1,17},{2,6},{3,19},{4,0},{5,21},{6,2},{7,23},{8,12},{9,25},... | collective-permute-start | bytes 1376264 | tf_op jit(solution)/shard_map/ppermute | solution.py:44
  66.3 13.7 %collective-permute-start.15 = (bf16[256,896]{1,0:T(8,128)(2,1)S(1)}, bf16[256,896]{1,0:T(8,128)(2,1)S(1)}, u32[]{:S(2)}, u32[]{:S(2)}) collective-permute-start(bf16[256,896]{1,0:T(8,128)(2,1)S(1)} %combine.1.refs_0_), channel_id=1, source_target_pairs={{0,2},{1,9},{2,4},{3,11},{4,6},{5,13},{6,0},{7,15},{8,10},{9,17},{... | collective-permute-start | bytes 1376264 | tf_op jit(solution)/shard_map/ppermute | solution.py:44
  66.5 13.6 %collective-permute-start.14 = (bf16[256,896]{1,0:T(8,128)(2,1)S(1)}, bf16[256,896]{1,0:T(8,128)(2,1)S(1)}, u32[]{:S(2)}, u32[]{:S(2)}) collective-permute-start(bf16[256,896]{1,0:T(8,128)(2,1)S(1)} %combine.1.refs_0_), channel_id=1, source_target_pairs={{0,6},{1,25},{2,0},{3,27},{4,2},{5,29},{6,4},{7,31},{8,14},{9,1},{... | collective-permute-start | bytes 1376264 | tf_op jit(solution)/shard_map/ppermute | solution.py:44
  82.7 9.8 %collective-permute-start.18 = (bf16[64,3072]{1,0:T(8,128)(2,1)S(1)}, bf16[64,3072]{1,0:T(8,128)(2,1)S(1)}, u32[]{:S(2)}, u32[]{:S(2)}) collective-permute-start(bf16[64,3072]{1,0:T(8,128)(2,1)S(1)} %get-tuple-element.33), channel_id=1, source_target_pairs={{0,4},{1,17},{2,6},{3,19},{4,0},{5,21},{6,2},{7,23},{8,12},{9,25},... | collective-permute-start | bytes 1179656 | tf_op jit(solution)/shard_map/ppermute | solution.py:44
  86.9 23.4 %collective-permute-start.21 = (bf16[64,5120]{1,0:T(8,128)(2,1)S(1)}, bf16[64,5120]{1,0:T(8,128)(2,1)S(1)}, u32[]{:S(2)}, u32[]{:S(2)}) collective-permute-start(bf16[64,5120]{1,0:T(8,128)(2,1)S(1)} %get-tuple-element.38), channel_id=1, source_target_pairs={{0,4},{1,17},{2,6},{3,19},{4,0},{5,21},{6,2},{7,23},{8,12},{9,25},... | collective-permute-start | bytes 1966088 | tf_op jit(solution)/shard_map/ppermute | solution.py:44
  89.3 21.0 %collective-permute-start.22 = (bf16[64,5120]{1,0:T(8,128)(2,1)S(1)}, bf16[64,5120]{1,0:T(8,128)(2,1)S(1)}, u32[]{:S(2)}, u32[]{:S(2)}) collective-permute-start(bf16[64,5120]{1,0:T(8,128)(2,1)S(1)} %get-tuple-element.39), channel_id=1, source_target_pairs={{0,2},{1,9},{2,4},{3,11},{4,6},{5,13},{6,0},{7,15},{8,10},{9,17},{... | collective-permute-start | bytes 1966088 | tf_op jit(solution)/shard_map/ppermute | solution.py:44
  89.8 20.5 %collective-permute-start.23 = (bf16[64,5120]{1,0:T(8,128)(2,1)S(1)}, bf16[64,5120]{1,0:T(8,128)(2,1)S(1)}, u32[]{:S(2)}, u32[]{:S(2)}) collective-permute-start(bf16[64,5120]{1,0:T(8,128)(2,1)S(1)} %get-tuple-element.40), channel_id=1, source_target_pairs={{0,6},{1,25},{2,0},{3,27},{4,2},{5,29},{6,4},{7,31},{8,14},{9,1},{... | collective-permute-start | bytes 1966088 | tf_op jit(solution)/shard_map/ppermute | solution.py:44
  92.5 17.8 %collective-permute-start.19 = (bf16[64,3072]{1,0:T(8,128)(2,1)S(1)}, bf16[64,3072]{1,0:T(8,128)(2,1)S(1)}, u32[]{:S(2)}, u32[]{:S(2)}) collective-permute-start(bf16[64,3072]{1,0:T(8,128)(2,1)S(1)} %get-tuple-element.34), channel_id=1, source_target_pairs={{0,2},{1,9},{2,4},{3,11},{4,6},{5,13},{6,0},{7,15},{8,10},{9,17},{... | collective-permute-start | bytes 1179656 | tf_op jit(solution)/shard_map/ppermute | solution.py:44
  92.5 17.8 %collective-permute-start.20 = (bf16[64,3072]{1,0:T(8,128)(2,1)S(1)}, bf16[64,3072]{1,0:T(8,128)(2,1)S(1)}, u32[]{:S(2)}, u32[]{:S(2)}) collective-permute-start(bf16[64,3072]{1,0:T(8,128)(2,1)S(1)} %get-tuple-element.35), channel_id=1, source_target_pairs={{0,6},{1,25},{2,0},{3,27},{4,2},{5,29},{6,4},{7,31},{8,14},{9,1},{... | collective-permute-start | bytes 1179656 | tf_op jit(solution)/shard_map/ppermute | solution.py:44
  110.8 8.1 %collective-permute-start.24 = (bf16[16,8192]{1,0:T(8,128)(2,1)S(1)}, bf16[16,8192]{1,0:T(8,128)(2,1)S(1)}, u32[]{:S(2)}, u32[]{:S(2)}) collective-permute-start(bf16[16,8192]{1,0:T(8,128)(2,1)S(1)} %get-tuple-element.42), channel_id=1, source_target_pairs={{0,16},{1,5},{2,18},{3,7},{4,20},{5,1},{6,22},{7,3},{8,24},{9,13},... | collective-permute-start | bytes 786440 | tf_op jit(solution)/shard_map/ppermute | solution.py:44
  112.6 9.0 %collective-permute-start.25 = (bf16[16,8192]{1,0:T(8,128)(2,1)S(1)}, bf16[16,8192]{1,0:T(8,128)(2,1)S(1)}, u32[]{:S(2)}, u32[]{:S(2)}) collective-permute-start(bf16[16,8192]{1,0:T(8,128)(2,1)S(1)} %get-tuple-element.43), channel_id=1, source_target_pairs={{0,8},{1,3},{2,10},{3,5},{4,12},{5,7},{6,14},{7,1},{8,16},{9,11},{... | collective-permute-start | bytes 786440 | tf_op jit(solution)/shard_map/ppermute | solution.py:44
  114.4 7.2 %collective-permute-start.26 = (bf16[16,8192]{1,0:T(8,128)(2,1)S(1)}, bf16[16,8192]{1,0:T(8,128)(2,1)S(1)}, u32[]{:S(2)}, u32[]{:S(2)}) collective-permute-start(bf16[16,8192]{1,0:T(8,128)(2,1)S(1)} %get-tuple-element.44), channel_id=1, source_target_pairs={{0,24},{1,7},{2,26},{3,1},{4,28},{5,3},{6,30},{7,5},{8,0},{9,15},{... | collective-permute-start | bytes 786440 | tf_op jit(solution)/shard_map/ppermute | solution.py:44
